TPU v7x, 32 devices: a whole 2x2x4 slice. The times are simulated.
32 devices in a mesh: parts: 2 (over x), row: 2 (over core), col: 8 (over z, y).
Axes of the slice: x: 2, y: 2, z: 4, core: 2. Of those that a mesh axis runs over, the one named last changes fastest.
Arguments:
- pair_state: bfloat16 [224, 112, 128], P(('parts', 'row'), 'col'), parts along dimension 0, may hold values from -6 to 6
- valid_length: int32 [2], P('parts'), parts along dimension 0, may hold values from 56 to 112
- input_gain: float32 [128], replicated, may hold values from 0.1 to 1.9
- left_gate: bfloat16 [128, 128], replicated, may hold values from -0.5 to 0.5
- left_value: bfloat16 [128, 128], replicated, may hold values from -0.5 to 0.5
- right_gate: bfloat16 [128, 128], replicated, may hold values from -0.5 to 0.5
- right_value: bfloat16 [128, 128], replicated, may hold values from -0.5 to 0.5
- out_gate: bfloat16 [128, 128], replicated, may hold values from -0.5 to 0.5
- output_gain: float32 [128], replicated, may hold values from 0.1 to 1.9
- out_weight: bfloat16 [128, 128], replicated, may hold values from -0.5 to 0.5
Outputs:
- update: bfloat16 [224, 112, 128], P(('parts', 'row'), 'col'), parts along dimension 0
There are 2 independent parts, one for each index of `parts`. A program takes and returns all parts, laid end to end along the dimension named above; an argument that names none is the same for every part. Nothing has to cross between parts.
All inputs are finite; a program needn't handle non-finite values.
Results may differ from a plain program's by a relative error of at most 0.014.
Values may be sent and summed in bfloat16 or wider, within the bound.
No kernel may reach another device: no remote copies, remote signals or barrier semaphores. Data moves between devices by JAX's collectives and lax.ppermute only.
A program may use at most 128 MiB of HBM per device.

v0:
```python
import jax
import jax.numpy as jnp
from jax import lax
from jax.sharding import PartitionSpec as P


def norm_last(values, gain):
    average = jnp.mean(values, -1, keepdims=True)
    centered = values - average
    variance = jnp.mean(centered * centered, -1, keepdims=True)
    return centered * lax.rsqrt(variance + 1e-05) * gain


def local(
    pair_state,
    valid_length,
    input_gain,
    left_gate,
    left_value,
    right_gate,
    right_value,
    out_gate,
    output_gain,
    out_weight,
):
    height, width, channels = pair_state.shape
    hidden_width = left_gate.shape[1]
    row_first = lax.axis_index("row") * height
    col_first = lax.axis_index("col") * width
    normed = norm_last(pair_state.astype(jnp.float32), input_gain).astype(jnp.bfloat16)
    limit = valid_length[0]
    row_valid = (row_first + jnp.arange(height, dtype=jnp.int32) < limit).astype(jnp.float32)
    col_valid = (col_first + jnp.arange(width, dtype=jnp.int32) < limit).astype(jnp.float32)
    pair_mask = (row_valid[:, None] * col_valid[None, :])[:, :, None]

    def project(weight):
        return jnp.einsum("rjc,ch->rjh", normed, weight, preferred_element_type=jnp.float32)

    left = (jax.nn.sigmoid(project(left_gate)) * project(left_value) * pair_mask).astype(
        jnp.bfloat16
    )
    right = (jax.nn.sigmoid(project(right_gate)) * project(right_value) * pair_mask).astype(
        jnp.bfloat16
    )
    gating = jax.nn.sigmoid(project(out_gate))
    right_full = lax.all_gather(right, "row", axis=0, tiled=True)
    right_cols = lax.all_to_all(right_full, "col", split_axis=0, concat_axis=1, tiled=True)
    empty = jnp.zeros((height, width, hidden_width), jnp.float32)
    piece = lax.all_gather(left, "col", axis=1, tiled=True)
    blocks = piece.shape[1] // width

    def add_block(index, running):
        offset = index * width
        left_part = lax.dynamic_slice_in_dim(piece, offset, width, 1)
        partner = lax.dynamic_slice_in_dim(right_cols, offset, width, 1)
        term = jnp.einsum("ikc,jkc->ijc", left_part, partner, preferred_element_type=jnp.float32)
        return running + term.astype(jnp.bfloat16).astype(jnp.float32)

    combined = lax.fori_loop(0, blocks, add_block, empty)
    settled = norm_last(combined, output_gain).astype(jnp.bfloat16)
    update = gating * jnp.einsum(
        "ijc,ch->ijh", settled, out_weight, preferred_element_type=jnp.float32
    )
    return update.astype(jnp.bfloat16)


def solution(mesh):
    return jax.shard_map(
        local,
        mesh=mesh,
        in_specs=(
            P(("parts", "row"), "col", None),
            P("parts"),
            P(),
            P(),
            P(),
            P(),
            P(),
            P(),
            P(),
            P(),
        ),
        out_specs=P(("parts", "row"), "col", None),
        check_vma=False,
    )
```

profile of v0, /device:TPU:0, one launch (start us, length us, event | category | flops | bytes accessed | tf_op | source)
XLA Modules:
  0.0 92.7 jit_solution(1287902978997130300)
XLA Ops:
  7.3 1.1 %convert_reduce_fusion = f32[56,14]{0,1:T(8,128)S(1)} fusion(bf16[56,14,128]{2,0,1:T(8,128)(2,1)} %param.12), kind=kLoop, calls=%fused_computation.29 | loop fusion | flops 199920 | bytes 203840 | tf_op jit(solution)/shard_map/reduce_sum | solution.py:8
  8.4 1.3 %fusion.22 = f32[56,14]{0,1:T(8,128)S(1)} fusion(bf16[56,14,128]{2,0,1:T(8,128)(2,1)} %param.12, f32[56,14]{0,1:T(8,128)S(1)} %broadcast_multiply_fusion.2), kind=kLoop, calls=%fused_computation.34 | loop fusion | flops 400624 | bytes 206976 | tf_op jit(solution)/shard_map/reduce_sum | solution.py:10
  9.8 1.4 %fusion.5 = f32[56,14,128]{2,0,1:T(8,128)S(1)} fusion(bf16[128,128]{1,0:T(8,128)(2,1)S(1)} %copy-done, bf16[56,14,128]{2,0,1:T(8,128)(2,1)} %param.12, f32[128]{0:T(128)} %param.14, f32[56,14]{0,1:T(8,128)S(1)} %get-tuple-element.120, f32[56,14]{0,1:T(8,128)S(1)} %broadcast_multiply_fusion.2), kind=kOutput, calls=%fused_computation.10 | convolution fusion | flops 26492928 | bytes 641664 | tf_op jit(solution)/shard_map/rjc,ch->rjh/dot_general | solution.py:37
  11.2 1.1 %fusion.15 = bf16[56,14,128]{2,0,1:T(8,128)(2,1)} fusion(f32[56,14,128]{2,0,1:T(8,128)S(1)} %fusion.5, f32[56,14]{0,1:T(8,128)S(1)} %get-tuple-element.121, bf16[128,128]{1,0:T(8,128)(2,1)S(1)} %copy-done.3, bf16[56,14,128]{2,0,1:T(8,128)(2,1)S(1)} %copy-done.1, f32[128]{0:T(128)S(1)} %copy-done.5, f32[56,14]{0,1:T(8,128)S(1)} %get-tuple-element.120, ...), kind=kOutput, calls=%fused_computation.23 | convolution fusion | flops 26492928 | bytes 845504 | tf_op jit(solution)/shard_map/rjc,ch->rjh/dot_general | solution.py:37
  13.2 2.2 %all_gather.6 = bf16[112,14,128]{2,0,1:T(8,128)(2,1)S(1)} all-gather(bf16[56,14,128]{2,0,1:T(8,128)(2,1)S(1)} %fusion.16), channel_id=1, replica_groups=mesh['parts'=2,'row'=2,'col'=8] {'row'}, dimensions={0}, use_global_device_ids=true | all-gather | bytes 602112 | tf_op jit(solution)/shard_map/all_gather | solution.py:46
  15.4 0.9 copy.18
  16.3 7.2 %all-to-all-start = ((bf16[112,14,128]{2,1,0:T(8,128)(2,1)}), bf16[112,14,128]{2,1,0:T(8,128)(2,1)S(1)}, u32[]{:S(2)}, u32[]{:S(2)}) async-start(bf16[112,14,128]{2,1,0:T(8,128)(2,1)} %copy.18), calls=%async_computation | async-start | bytes 917504 | tf_op jit(solution)/shard_map/all_to_all | solution.py:47
  23.5 19.7 %all-to-all-done = bf16[112,14,128]{2,1,0:T(8,128)(2,1)S(1)} async-done(((bf16[112,14,128]{2,1,0:T(8,128)(2,1)}), bf16[112,14,128]{2,1,0:T(8,128)(2,1)S(1)}, u32[]{:S(2)}, u32[]{:S(2)}) %all-to-all-start) | async-done | bytes 401440 | tf_op jit(solution)/shard_map/all_to_all | solution.py:47
  43.4 21.2 %all-gather.2.cloned.1.call-done = bf16[56,112,128]{2,0,1:T(8,128)(2,1)} async-done(((bf16[56,14,128]{2,0,1:T(8,128)(2,1)}), bf16[56,112,128]{2,0,1:T(8,128)(2,1)}) %all-gather.2.cloned.1.call-update) | async-done | bytes 1605648 | tf_op jit(solution)/shard_map/all_gather | solution.py:49
  64.6 18.9 %while.14 = (s32[]{:T(128)}, f32[56,14,128]{0,1,2:T(8,128)S(1)}, bf16[14,112,128]{2,1,0:T(8,128)(2,1)S(1)}, bf16[56,112,128]{2,0,1:T(8,128)(2,1)}, s32[]{:T(128)}, /*index=5*/s32[]{:T(128)}, s32[]{:T(128)}, s32[]{:T(128)}) while((s32[]{:T(128)}, f32[56,14,128]{0,1,2:T(8,128)S(1)}, bf16[14,112,128]{2,1,0:T(8,128)(2,1)S(1)}, ...), condition=%wide.region_3.0_spmd.clone, body=%wide.region_2.0_spmd.clone.sunk | while | flops 3211271 | bytes 2057373 | solution.py:59
  64.6 1.0 %constant_dynamic-slice_fusion.5 = bf16[56,14,128]{2,0,1:T(8,128)(2,1)S(1)} fusion(bf16[56,112,128]{2,0,1:T(8,128)(2,1)} %get-tuple-element.166, s32[]{:T(128)S(6)} %select_n.10), kind=kLoop, calls=%fused_computation.4.clone.1 | loop fusion | bytes 401412 | tf_op jit(solution)/shard_map/while/body/eval_jaxpr/dynamic_slice | solution.py:54
  66.0 0.5 copy.32
  66.5 0.4 fusion.43
  67.0 1.0 %constant_dynamic-slice_fusion.5 = bf16[56,14,128]{2,0,1:T(8,128)(2,1)S(1)} fusion(bf16[56,112,128]{2,0,1:T(8,128)(2,1)} %get-tuple-element.166, s32[]{:T(128)S(6)} %select_n.10), kind=kLoop, calls=%fused_computation.4.clone.1 | loop fusion | bytes 401412 | tf_op jit(solution)/shard_map/while/body/eval_jaxpr/dynamic_slice | solution.py:54
  68.4 0.5 copy.32
  69.3 1.0 %constant_dynamic-slice_fusion.5 = bf16[56,14,128]{2,0,1:T(8,128)(2,1)S(1)} fusion(bf16[56,112,128]{2,0,1:T(8,128)(2,1)} %get-tuple-element.166, s32[]{:T(128)S(6)} %select_n.10), kind=kLoop, calls=%fused_computation.4.clone.1 | loop fusion | bytes 401412 | tf_op jit(solution)/shard_map/while/body/eval_jaxpr/dynamic_slice | solution.py:54
  70.7 0.5 copy.32
  71.2 0.4 fusion.43
  71.7 1.0 %constant_dynamic-slice_fusion.5 = bf16[56,14,128]{2,0,1:T(8,128)(2,1)S(1)} fusion(bf16[56,112,128]{2,0,1:T(8,128)(2,1)} %get-tuple-element.166, s32[]{:T(128)S(6)} %select_n.10), kind=kLoop, calls=%fused_computation.4.clone.1 | loop fusion | bytes 401412 | tf_op jit(solution)/shard_map/while/body/eval_jaxpr/dynamic_slice | solution.py:54
  73.1 0.5 copy.32
  73.6 0.4 fusion.43
  74.1 1.0 %constant_dynamic-slice_fusion.5 = bf16[56,14,128]{2,0,1:T(8,128)(2,1)S(1)} fusion(bf16[56,112,128]{2,0,1:T(8,128)(2,1)} %get-tuple-element.166, s32[]{:T(128)S(6)} %select_n.10), kind=kLoop, calls=%fused_computation.4.clone.1 | loop fusion | bytes 401412 | tf_op jit(solution)/shard_map/while/body/eval_jaxpr/dynamic_slice | solution.py:54
  75.5 0.5 copy.32
  76.4 1.0 %constant_dynamic-slice_fusion.5 = bf16[56,14,128]{2,0,1:T(8,128)(2,1)S(1)} fusion(bf16[56,112,128]{2,0,1:T(8,128)(2,1)} %get-tuple-element.166, s32[]{:T(128)S(6)} %select_n.10), kind=kLoop, calls=%fused_computation.4.clone.1 | loop fusion | bytes 401412 | tf_op jit(solution)/shard_map/while/body/eval_jaxpr/dynamic_slice | solution.py:54
  77.8 0.5 copy.32
  78.8 1.0 %constant_dynamic-slice_fusion.5 = bf16[56,14,128]{2,0,1:T(8,128)(2,1)S(1)} fusion(bf16[56,112,128]{2,0,1:T(8,128)(2,1)} %get-tuple-element.166, s32[]{:T(128)S(6)} %select_n.10), kind=kLoop, calls=%fused_computation.4.clone.1 | loop fusion | bytes 401412 | tf_op jit(solution)/shard_map/while/body/eval_jaxpr/dynamic_slice | solution.py:54
  80.2 0.5 copy.32
  80.6 0.4 fusion.43
  81.2 1.0 %constant_dynamic-slice_fusion.5 = bf16[56,14,128]{2,0,1:T(8,128)(2,1)S(1)} fusion(bf16[56,112,128]{2,0,1:T(8,128)(2,1)} %get-tuple-element.166, s32[]{:T(128)S(6)} %select_n.10), kind=kLoop, calls=%fused_computation.4.clone.1 | loop fusion | bytes 401412 | tf_op jit(solution)/shard_map/while/body/eval_jaxpr/dynamic_slice | solution.py:54
  82.6 0.5 copy.32
  83.0 0.4 fusion.43
  84.7 1.1 %fusion.17 = bf16[56,14,128]{2,0,1:T(8,128)(2,1)} fusion(f32[56,14,128]{2,0,1:T(8,128)S(1)} %fusion.20, bf16[128,128]{1,0:T(8,128)(2,1)S(1)} %copy-done.8, bf16[56,14,128]{2,0,1:T(8,128)(2,1)S(1)} %copy-done.1, f32[128]{0:T(128)S(1)} %copy-done.5, f32[56,14]{0,1:T(8,128)S(1)} %get-tuple-element.120, f32[56,14]{0,1:T(8,128)S(1)} %broadcast_multiply_fusion.2), kind=kOutput, calls=%fused_computation.25 | convolution fusion | flops 26693632 | bytes 842368 | tf_op jit(solution)/shard_map/rjc,ch->rjh/dot_general | solution.py:37
  (54 shorter events, 7.3 us)
Async XLA Ops:
  6.5 3.3 %copy-start = (bf16[128,128]{1,0:T(8,128)(2,1)S(1)}, bf16[128,128]{1,0:T(8,128)(2,1)}, u32[]{:S(2)}) copy-start(bf16[128,128]{1,0:T(8,128)(2,1)} %param.15) | copy-start | bytes 98308
  6.5 4.7 %copy-start.1 = (bf16[56,14,128]{2,0,1:T(8,128)(2,1)S(1)}, bf16[56,14,128]{2,0,1:T(8,128)(2,1)}, u32[]{:S(2)}) copy-start(bf16[56,14,128]{2,0,1:T(8,128)(2,1)} %param.12) | copy-start | bytes 602116
  6.5 4.7 %copy-start.5 = (f32[128]{0:T(128)S(1)}, f32[128]{0:T(128)}, u32[]{:S(2)}) copy-start(f32[128]{0:T(128)} %param.14) | copy-start | bytes 1540
  6.5 4.7 %copy-start.3 = (bf16[128,128]{1,0:T(8,128)(2,1)S(1)}, bf16[128,128]{1,0:T(8,128)(2,1)}, u32[]{:S(2)}) copy-start(bf16[128,128]{1,0:T(8,128)(2,1)} %param.16) | copy-start | bytes 98308
  6.5 58.0 %all-gather.2.cloned.1.call-start = ((), (), s32[]{:S(2)}) async-start(), calls=%async_computation.1 | async-start | bytes 1806336 | tf_op jit(solution)/shard_map/all_gather | solution.py:49
  9.7 2.6 %copy-start.7 = (bf16[128,128]{1,0:T(8,128)(2,1)S(1)}, bf16[128,128]{1,0:T(8,128)(2,1)}, u32[]{:S(2)}) copy-start(bf16[128,128]{1,0:T(8,128)(2,1)} %param.17) | copy-start | bytes 98308
  11.2 1.6 %copy-start.4 = (bf16[128,128]{1,0:T(8,128)(2,1)S(1)}, bf16[128,128]{1,0:T(8,128)(2,1)}, u32[]{:S(2)}) copy-start(bf16[128,128]{1,0:T(8,128)(2,1)} %param.18) | copy-start | bytes 98308
  16.3 26.9 %all-to-all-start = ((bf16[112,14,128]{2,1,0:T(8,128)(2,1)}), bf16[112,14,128]{2,1,0:T(8,128)(2,1)S(1)}, u32[]{:S(2)}, u32[]{:S(2)}) async-start(bf16[112,14,128]{2,1,0:T(8,128)(2,1)} %copy.18), calls=%async_computation | async-start | bytes 917504 | tf_op jit(solution)/shard_map/all_to_all | solution.py:47
  83.5 0.7 copy-start.6
  83.6 0.8 copy-start.2
  83.7 1.0 %copy-start.8 = (bf16[128,128]{1,0:T(8,128)(2,1)S(1)}, bf16[128,128]{1,0:T(8,128)(2,1)}, u32[]{:S(2)}) copy-start(bf16[128,128]{1,0:T(8,128)(2,1)} %param.19) | copy-start | bytes 98308
Sparse Core Ops, SparseCore 0:
  12.5 52.0 all-gather.1
where the time goes:
time: 93.2 us; the launch traced here: 92.7 us
  waiting for transfers between devices  40.9 us (44%)
  local copies, waits for them, and re-layouts  16.3 us (17%)
  between operations  14.3 us (15%)
  matrix products  8.26 us (9%)
  starting transfers between devices  7.23 us (8%)
  other arithmetic  3.02 us (3%)
  blocking collectives  2.17 us (2%)
    all_gather x1, waiting for transfers between devices, local(): piece = lax.all_gather(left, 'col', axis=1, tiled=True)  21.2 us
    all_to_all x1, waiting for transfers between devices, local(): lax.all_to_all(right_full, 'col', split_axis=0, concat_axis=1, tiled=True)  19.7 us
    dynamic_slice x16, local copies, waits for them, and re-layouts, add_block(): left_part = lax.dynamic_slice_in_dim(piece, offset, width, 1)  11.1 us
    all_to_all x1, starting transfers between devices, local(): lax.all_to_all(right_full, 'col', split_axis=0, concat_axis=1, tiled=True)  7.2 us
    dot_general x5, matrix products, project(): jnp.einsum('rjc,ch->rjh', normed, weight, preferred_element_type=jnp.floa...  4.41 us
    dynamic_slice x16, local copies, waits for them, and re-layouts, add_block(): partner = lax.dynamic_slice_in_dim(right_cols, offset, width, 1)  3.86 us
    dot_general x8, matrix products, add_block(): jnp.einsum('ikc,jkc->ijc', left_part, partner, preferred_element_type=jnp...  3.55 us
    all_gather x1, blocking collectives, local(): right_full = lax.all_gather(right, 'row', axis=0, tiled=True)  2.17 us
  transfers between devices with their start and end apart: 2, of which 2 were waited for; matrix products, arithmetic and copies ran while one was open for 2% of the time, Pallas kernels for 0%

commit v1 on v0

v1 whole, which is shorter than its diff:
```python
import functools

import jax
import jax.numpy as jnp
from jax import lax
from jax.experimental import pallas as pl
from jax.experimental.pallas import tpu as pltpu
from jax.sharding import PartitionSpec as P

F32 = jnp.float32
BF16 = jnp.bfloat16
LANES = 128
SUBLANES = 16
EPS = 1e-05


def round_up(value, multiple):
    return -(-value // multiple) * multiple


class Sizes:
    def __init__(self, mesh, height, width, channels, hidden):
        self.rows = mesh.shape["row"]
        self.cols = mesh.shape["col"]
        self.peers = self.rows * self.cols
        self.height, self.width = height, width
        self.channels, self.hidden = channels, hidden
        self.each = hidden // self.peers
        fits = self.rows * height <= LANES
        self.pack = self.rows if fits and width % self.rows == 0 and self.each % self.rows == 0 else 1
        self.steps = width // self.pack
        self.groups = self.each // self.pack
        self.lanes = round_up(self.pack * height, LANES)
        self.slots = round_up(width, SUBLANES)
        self.direct = self.each % 8 == 0 and self.lanes == LANES


def normalise(values):
    average = jnp.mean(values, -1, keepdims=True)
    centered = values - average
    variance = jnp.mean(centered * centered, -1, keepdims=True)
    return centered * lax.rsqrt(variance + EPS)


def sigmoid(values):
    return 0.5 * jnp.tanh(0.5 * values) + 0.5


def swap_blocks(first, second, height):
    lanes = first.shape[-1]
    low = lax.broadcasted_iota(jnp.int32, first.shape, 1) < height
    return (
        jnp.where(low, first, pltpu.roll(second, height, 1)),
        jnp.where(low, pltpu.roll(first, lanes - height, 1), second),
    )


def produce(s, pair, length, gain, left_gate, left_value, right_gate, right_value, message):
    first = lax.axis_index("row") * s.height
    second = lax.axis_index("col") * s.width
    limit = length[0]
    weights = jnp.concatenate(
        [w[...].T for w in (left_gate, left_value, right_gate, right_value)], 0
    )
    scale = gain[...]
    lane = lax.broadcasted_iota(jnp.int32, (1, s.lanes), 1)
    block = lane // s.height
    token = first + lane - block * s.height
    for step in range(s.steps):
        normed = [
            normalise(pair[at * s.steps + step].astype(F32)) * scale for at in range(s.pack)
        ]
        if s.lanes > s.pack * s.height:
            normed.append(jnp.zeros((s.lanes - s.pack * s.height, s.channels), F32))
        normed = jnp.concatenate(normed, 0).astype(BF16)
        out = lax.dot_general(weights, normed, (((1,), (1,)), ((), ())), preferred_element_type=F32)
        inner = second + block * s.steps + step
        mask = ((token < limit) & (inner < limit)).astype(F32)
        h = s.hidden
        left = sigmoid(out[:h]) * out[h : 2 * h] * mask
        right = sigmoid(out[2 * h : 3 * h]) * out[3 * h :] * mask
        if s.direct:
            split = (s.peers, s.each, s.lanes)
            both = jnp.concatenate([left.reshape(split), right.reshape(split)], 1)
            message[:, step] = both.astype(BF16)
        else:
            message[step] = jnp.concatenate([left, right], 0).astype(BF16)


def gate(s, pair, gain, out_gate, out_weight, output_gain, gating, weight, scale, wide):
    for at in range(s.width):
        normed = (normalise(pair[at].astype(F32)) * gain[...]).astype(BF16)
        gating[at] = sigmoid(jnp.dot(normed, out_gate[...], preferred_element_type=F32))
    count = s.hidden // s.pack
    wide[...] = out_weight[...].astype(F32)
    for at in range(s.pack):
        part = wide[pl.ds(at, count, stride=s.pack), :]
        weight[:, at * s.channels : (at + 1) * s.channels] = part.astype(BF16)
    wide[...] = jnp.broadcast_to(output_gain[...], (s.hidden, s.hidden)).T
    parts = [wide[pl.ds(at, count, stride=s.pack), :][:, :1] for at in range(s.pack)]
    block = lax.broadcasted_iota(jnp.int32, (count, s.lanes), 1) // s.height
    total = jnp.broadcast_to(parts[0], (count, s.lanes))
    for at in range(1, s.pack):
        total = jnp.where(block == at, parts[at], total)
    scale[...] = total


def multiply(s, received, message, wide, square):
    span = s.steps * 2 * s.each
    if s.direct:
        for peer in range(s.peers):
            wide[peer * span : (peer + 1) * span] = (
                received[peer].reshape(span, s.lanes).astype(F32)
            )
    depth = s.cols * s.steps

    def operand(side, channel):
        at = side * s.each + channel
        if s.direct:
            blocks = [
                wide[pl.ds(row * s.cols * span + at, depth, stride=2 * s.each), :]
                for row in range(s.rows)
            ]
        else:
            blocks = [received[at, row].astype(F32) for row in range(s.rows)]
        if s.pack == 1:
            return jnp.concatenate(blocks, 1).astype(BF16)
        pad = round_up(depth, 64) - depth
        blocks = swap_blocks(*blocks, s.height)
        if pad:
            empty = jnp.zeros((pad, s.lanes), F32)
            blocks = [part for block in blocks for part in (block, empty)]
        return jnp.concatenate(blocks, 0).astype(BF16)

    for group in range(s.groups):
        sums = []
        for at in range(s.pack):
            channel = group * s.pack + at
            left, right = operand(0, channel), operand(1, channel)
            sums.append(jnp.dot(right.T, left, preferred_element_type=F32))
        if s.pack == 1:
            sums = [sums[0][:, row * s.lanes : (row + 1) * s.lanes] for row in range(s.rows)]
        else:
            sums = swap_blocks(*sums, s.height)
        for row in range(s.rows):
            square[row] = sums[row]
        for row in range(s.rows):
            for col in range(s.cols):
                start = col * s.width
                if s.pack == 1:
                    start = start // s.height * s.lanes + start % s.height
                message[row * s.cols + col, group] = square[row, start : start + s.slots].astype(BF16)


def finish(s, received, gating, weight, scale, update, wide):
    count = s.hidden // s.pack
    values = received[...].reshape(count, s.slots, s.lanes).astype(F32)

    def fold(total):
        if s.pack == 1:
            return total
        low = lax.broadcasted_iota(jnp.int32, total.shape, 1) < s.height
        up = pltpu.roll(total, s.height, 1)
        down = pltpu.roll(total, s.lanes - s.height, 1)
        return total + jnp.where(low, down, up)

    average = fold(jnp.sum(values, 0)) * (1.0 / s.hidden)
    centered = values - average[None]
    variance = fold(jnp.sum(centered * centered, 0)) * (1.0 / s.hidden)
    settled = centered * lax.rsqrt(variance + EPS)[None]
    settled = settled.reshape(count * s.slots, s.lanes)
    for tile in range(s.lanes // LANES):
        wide[tile] = settled[:, tile * LANES : (tile + 1) * LANES]
    for at in range(s.width):
        rows = [
            wide[tile, pl.ds(at, count, stride=s.slots), :] for tile in range(s.lanes // LANES)
        ]
        rows = (jnp.concatenate(rows, 1) * scale[...]).astype(BF16)
        out = jnp.dot(rows.T, weight[...], preferred_element_type=F32)
        total = out[: s.height, : s.channels]
        for block in range(1, s.pack):
            total += out[
                block * s.height : (block + 1) * s.height,
                block * s.channels : (block + 1) * s.channels,
            ]
        update[at] = (gating[at] * total).astype(BF16)


def call(body, s, out_shape, scratch, flops, *operands):
    def space(operand):
        return pl.BlockSpec(memory_space=pltpu.SMEM if operand.dtype == jnp.int32 else pltpu.VMEM)

    sent = sum(o.size * o.dtype.itemsize for o in operands)
    return pl.pallas_call(
        functools.partial(body, s),
        out_shape=out_shape,
        in_specs=[space(o) for o in operands],
        out_specs=jax.tree.map(lambda _: pl.BlockSpec(memory_space=pltpu.VMEM), out_shape),
        scratch_shapes=scratch,
        compiler_params=pltpu.CompilerParams(vmem_limit_bytes=56 * 1024 * 1024),
        cost_estimate=pl.CostEstimate(flops=flops, bytes_accessed=sent, transcendentals=0),
        name=body.__name__,
    )(*operands)


def exchange(blocks):
    return lax.all_to_all(blocks, ("row", "col"), split_axis=0, concat_axis=0, tiled=True)


def local(
    mesh,
    pair_state,
    valid_length,
    input_gain,
    left_gate,
    left_value,
    right_gate,
    right_value,
    out_gate,
    output_gain,
    out_weight,
):
    height, width, channels = pair_state.shape
    hidden = left_gate.shape[1]
    s = Sizes(mesh, height, width, channels, hidden)
    shape = jax.ShapeDtypeStruct
    pair = jnp.transpose(pair_state, (1, 0, 2))
    gain = input_gain.reshape(1, channels)
    cells = height * width

    sent = (s.peers, s.steps, 2 * s.each, s.lanes)
    message = call(
        produce,
        s,
        shape(sent if s.direct else (s.steps, 2 * hidden, s.lanes), BF16),
        [],
        8 * cells * channels * hidden,
        pair,
        valid_length,
        gain,
        left_gate,
        left_value,
        right_gate,
        right_value,
    )
    if not s.direct:
        message = message.reshape(s.steps, 2, s.peers, s.each, s.lanes)
        message = message.transpose(2, 0, 1, 3, 4).reshape(sent)
    received = exchange(message)
    gating, weight, scale = call(
        gate,
        s,
        (
            shape((width, height, channels), F32),
            shape((hidden // s.pack, s.pack * channels), BF16),
            shape((hidden // s.pack, s.lanes), F32),
        ),
        [pltpu.VMEM((hidden, channels), F32)],
        2 * cells * channels * channels,
        pair,
        gain,
        out_gate,
        out_weight,
        output_gain.reshape(1, hidden),
    )
    scratch = (s.peers * s.steps * 2 * s.each, s.lanes)
    if not s.direct:
        received = received.reshape(s.rows, s.cols * s.steps, 2 * s.each, s.lanes)
        received = received.transpose(2, 0, 1, 3)
        scratch = (8, s.lanes)
    side = s.lanes if s.pack > 1 else s.rows * s.lanes
    sums = call(
        multiply,
        s,
        shape((s.peers, s.groups, s.slots, s.lanes), BF16),
        [pltpu.VMEM(scratch, F32), pltpu.VMEM((s.rows, side, s.lanes), F32)],
        2 * s.each * (s.rows * height) ** 2 * s.cols * width,
        received,
    )
    update = call(
        finish,
        s,
        shape((width, height, channels), BF16),
        [pltpu.VMEM((s.lanes // LANES, hidden // s.pack * s.slots, LANES), F32)],
        2 * cells * channels * hidden,
        exchange(sums),
        gating,
        weight,
        scale,
    )
    return jnp.transpose(update, (1, 0, 2))


def solution(mesh):
    return jax.shard_map(
        functools.partial(local, mesh),
        mesh=mesh,
        in_specs=(P(("parts", "row"), "col", None), P("parts")) + (P(),) * 8,
        out_specs=P(("parts", "row"), "col", None),
        check_vma=False,
    )
```

time: 93.2 us -> 45.3 us (0.49)
  waiting for transfers between devices: 40.9 us -> 8.07 us
  blocking collectives: 2.17 us -> 21.9 us
  local copies, waits for them, and re-layouts: 16.3 us -> 0.71 us
  between operations: 14.3 us -> 0.66 us
  Pallas kernels: 0 us -> 9.98 us
  matrix products: 8.26 us -> 0 us
  starting transfers between devices: 7.23 us -> 3.53 us
  other arithmetic: 3.02 us -> 0 us
    all_to_all x0 -> x1, blocking collectives: none -> 21.9 us  [exchange(): lax.all_to_all(blocks, ('row', 'col'), split_axis=0, concat_axis=0, tiled...]
    all_gather x1 -> x0, waiting for transfers between devices: 21.2 us -> none  [local(): piece = lax.all_gather(left, 'col', axis=1, tiled=True)]
    dynamic_slice x32 -> x0, local copies, waits for them, and re-layouts: 14.9 us -> none  [the longest x16 11.1 us: add_block(): left_part = lax.dynamic_slice_in_dim(piece, offset, width, 1)]
    all_to_all x1, waiting for transfers between devices: 19.7 us -> 8.07 us  [exchange(): lax.all_to_all(blocks, ('row', 'col'), split_axis=0, concat_axis=0, tiled...]
    pallas_call x0 -> x4, Pallas kernels: none -> 9.98 us  [call(): pl.pallas_call(functools.partial(body, s), out_shape=out_shape, in_specs=...]
    dot_general x14 -> x0, matrix products: 8.26 us -> none  [the longest x5 4.41 us: project(): jnp.einsum('rjc,ch->rjh', normed, weight, preferred_element_type=jnp.floa...]
    all_to_all x1, starting transfers between devices: 7.2 us -> 3.53 us  [exchange(): lax.all_to_all(blocks, ('row', 'col'), split_axis=0, concat_axis=0, tiled...]
    reduce_sum x4 -> x0, other arithmetic: 2.7 us -> none  [the longest x2 1.45 us: norm_last(): variance = jnp.mean(centered * centered, -1, keepdims=True)]
  transfers between devices with their start and end apart: 2 -> 1, of which waited for: 2 -> 1; matrix products, arithmetic and copies ran while one was open for 2% -> 0% of each run, Pallas kernels for 0% -> 5%
where the time goes in v1:
time: 45.3 us; the launch traced here: 44.9 us
  blocking collectives  21.9 us (48%)
  Pallas kernels  9.98 us (22%)
  waiting for transfers between devices  8.07 us (18%)
  starting transfers between devices  3.53 us (8%)
  local copies, waits for them, and re-layouts  0.71 us (2%)
  between operations  0.66 us (1%)
    all_to_all x1, blocking collectives, exchange(): lax.all_to_all(blocks, ('row', 'col'), split_axis=0, concat_axis=0, tiled...  21.9 us
    pallas_call x4, Pallas kernels, call(): pl.pallas_call(functools.partial(body, s), out_shape=out_shape, in_specs=...  9.98 us
    all_to_all x1, waiting for transfers between devices, exchange(): lax.all_to_all(blocks, ('row', 'col'), split_axis=0, concat_axis=0, tiled...  8.07 us
    all_to_all x1, starting transfers between devices, exchange(): lax.all_to_all(blocks, ('row', 'col'), split_axis=0, concat_axis=0, tiled...  3.53 us
  transfers between devices with their start and end apart: 1, of which 1 were waited for; matrix products, arithmetic and copies ran while one was open for 0% of the time, Pallas kernels for 5%

profile of v1, /device:TPU:0, one launch (start us, length us, event | category | flops | bytes accessed | tf_op | source)
XLA Modules:
  0.0 44.9 jit_solution(17027456062078068881)
XLA Ops:
  0.7 2.5 %produce.1 = bf16[16,7,16,128]{3,2,1,0:T(8,128)(2,1)} custom-call(bf16[14,56,128]{2,1,0:T(8,128)(2,1)} %bitcast.4, s32[1]{0:T(128)S(6)} %copy.11.length, f32[1,128]{1,0:T(1,128)} %bitcast.6, bf16[128,128]{1,0:T(8,128)(2,1)} %left_gate.1, bf16[128,128]{1,0:T(8,128)(2,1)} %left_value.1, bf16[128,128]{1,0:T(8,128)(2,1)} %right_gate.1, bf16[128,128]{1,0:T(8,128)(2,1)} %right_value.1), custom_call_target="tpu_custom_call" | custom-call | flops 102760448 | bytes 332292 | tf_op jit(solution)/shard_map/produce/pallas_call | solution.py:194
  3.2 21.9 %all_to_all.10.received = bf16[16,7,16,128]{3,2,1,0:T(8,128)(2,1)} all-to-all(bf16[16,7,16,128]{3,2,1,0:T(8,128)(2,1)} %produce.1), channel_id=1, replica_groups=mesh['parts'=2,'row'=2,'col'=8] {'row','col'}, dimensions={0} | all-to-all | bytes 917504 | tf_op jit(solution)/shard_map/all_to_all | solution.py:207
  25.1 2.7 %multiply.1 = bf16[16,4,16,128]{3,2,1,0:T(8,128)(2,1)} custom-call(bf16[16,7,16,128]{3,2,1,0:T(8,128)(2,1)} %all_to_all.10.received), custom_call_target="tpu_custom_call" | custom-call | flops 22478848 | bytes 458752 | tf_op jit(solution)/shard_map/multiply/pallas_call | solution.py:194
  27.8 3.5 %all-to-all-start.1 = ((bf16[16,4,16,128]{3,2,1,0:T(8,128)(2,1)}), bf16[16,4,16,128]{3,2,1,0:T(8,128)(2,1)S(1)}, u32[]{:S(2)}, u32[]{:S(2)}) async-start(bf16[16,4,16,128]{3,2,1,0:T(8,128)(2,1)} %multiply.1), calls=%async_computation.1 | async-start | bytes 524288 | tf_op jit(solution)/shard_map/all_to_all | solution.py:207
  31.3 2.2 %gate.1 = (f32[14,56,128]{2,1,0:T(8,128)}, bf16[64,256]{1,0:T(8,128)(2,1)}, f32[64,128]{1,0:T(8,128)}) custom-call(bf16[14,56,128]{2,1,0:T(8,128)(2,1)} %bitcast.5, f32[1,128]{1,0:T(1,128)} %bitcast.7, bf16[128,128]{1,0:T(8,128)(2,1)} %out_gate.1, bf16[128,128]{1,0:T(8,128)(2,1)} %out_weight.1, f32[1,128]{1,0:T(1,128)} %bitcast.8), custom_call_target="tpu_custom_call" | custom-call | flops 25690112 | bytes 267264 | tf_op jit(solution)/shard_map/gate/pallas_call | solution.py:194
  33.5 8.1 %all-to-all-done.1.received = bf16[16,4,16,128]{3,2,1,0:T(8,128)(2,1)S(1)} async-done(((bf16[16,4,16,128]{3,2,1,0:T(8,128)(2,1)}), bf16[16,4,16,128]{3,2,1,0:T(8,128)(2,1)S(1)}, u32[]{:S(2)}, u32[]{:S(2)}) %all-to-all-start.1) | async-done | bytes 262176 | tf_op jit(solution)/shard_map/all_to_all | solution.py:207
  41.6 0.0 copy-start
  41.6 0.7 %copy-done = bf16[16,4,16,128]{3,2,1,0:T(8,128)(2,1)} copy-done((bf16[16,4,16,128]{3,2,1,0:T(8,128)(2,1)}, bf16[16,4,16,128]{3,2,1,0:T(8,128)(2,1)S(1)}, u32[]{:S(2)}) %copy-start) | copy-done | bytes 262168
  42.3 2.6 %finish.1 = bf16[14,56,128]{2,1,0:T(8,128)(2,1)} custom-call(bf16[16,4,16,128]{3,2,1,0:T(8,128)(2,1)} %copy-done, f32[14,56,128]{2,1,0:T(8,128)} %get-tuple-element.8.gating, bf16[64,256]{1,0:T(8,128)(2,1)} %get-tuple-element.9.weight, f32[64,128]{1,0:T(8,128)} %get-tuple-element.10.scale), custom_call_target="tpu_custom_call" | custom-call | flops 25690112 | bytes 729088 | tf_op jit(solution)/shard_map/finish/pallas_call | solution.py:194
Async XLA Ops:
  27.8 13.8 %all-to-all-start.1 = ((bf16[16,4,16,128]{3,2,1,0:T(8,128)(2,1)}), bf16[16,4,16,128]{3,2,1,0:T(8,128)(2,1)S(1)}, u32[]{:S(2)}, u32[]{:S(2)}) async-start(bf16[16,4,16,128]{3,2,1,0:T(8,128)(2,1)} %multiply.1), calls=%async_computation.1 | async-start | bytes 524288 | tf_op jit(solution)/shard_map/all_to_all | solution.py:207
  41.6 0.7 %copy-start = (bf16[16,4,16,128]{3,2,1,0:T(8,128)(2,1)}, bf16[16,4,16,128]{3,2,1,0:T(8,128)(2,1)S(1)}, u32[]{:S(2)}) copy-start(bf16[16,4,16,128]{3,2,1,0:T(8,128)(2,1)S(1)} %all-to-all-done.1.received) | copy-start | bytes 786436

commit v2 on v1

--- a/solution.py
+++ b/solution.py
@@ -55,7 +55,8 @@
     )
 
 
-def produce(s, pair, length, gain, left_gate, left_value, right_gate, right_value, message):
+def produce(s, pair, length, gain, left_gate, left_value, right_gate, right_value, *rest):
+    *outs, message = rest
     first = lax.axis_index("row") * s.height
     second = lax.axis_index("col") * s.width
     limit = length[0]
@@ -84,7 +85,11 @@
             both = jnp.concatenate([left.reshape(split), right.reshape(split)], 1)
             message[:, step] = both.astype(BF16)
         else:
-            message[step] = jnp.concatenate([left, right], 0).astype(BF16)
+            outs[0][step] = jnp.concatenate([left, right], 0).astype(BF16)
+    if s.direct:
+        own = lax.axis_index("row") * s.cols + lax.axis_index("col")
+        for mask, out in enumerate(outs):
+            out[...] = message[own ^ mask]
 
 
 def gate(s, pair, gain, out_gate, out_weight, output_gain, gating, weight, scale, wide):
@@ -105,13 +110,16 @@
     scale[...] = total
 
 
-def multiply(s, received, message, wide, square):
+def multiply(s, *refs):
     span = s.steps * 2 * s.each
+    own = lax.axis_index("row") * s.cols + lax.axis_index("col")
     if s.direct:
-        for peer in range(s.peers):
-            wide[peer * span : (peer + 1) * span] = (
-                received[peer].reshape(span, s.lanes).astype(F32)
-            )
+        received, outs, (message, wide, square) = refs[: s.peers], refs[s.peers : -3], refs[-3:]
+        for mask in range(s.peers):
+            at = pl.multiple_of((own ^ mask) * span, span)
+            wide[pl.ds(at, span)] = received[mask][...].reshape(span, s.lanes).astype(F32)
+    else:
+        received, *outs, message, wide, square = refs
     depth = s.cols * s.steps
 
     def operand(side, channel):
@@ -150,11 +158,17 @@
                 if s.pack == 1:
                     start = start // s.height * s.lanes + start % s.height
                 message[row * s.cols + col, group] = square[row, start : start + s.slots].astype(BF16)
-
-
-def finish(s, received, gating, weight, scale, update, wide):
+    for mask, out in enumerate(outs):
+        out[...] = message[own ^ mask]
+
+
+def finish(s, *refs):
+    received, (gating, weight, scale, update, gathered, wide) = refs[: s.peers], refs[s.peers :]
+    own = lax.axis_index("row") * s.cols + lax.axis_index("col")
+    for mask in range(s.peers):
+        gathered[own ^ mask] = received[mask][...]
     count = s.hidden // s.pack
-    values = received[...].reshape(count, s.slots, s.lanes).astype(F32)
+    values = gathered[...].reshape(count, s.slots, s.lanes).astype(F32)
 
     def fold(total):
         if s.pack == 1:
@@ -197,14 +211,18 @@
         in_specs=[space(o) for o in operands],
         out_specs=jax.tree.map(lambda _: pl.BlockSpec(memory_space=pltpu.VMEM), out_shape),
         scratch_shapes=scratch,
-        compiler_params=pltpu.CompilerParams(vmem_limit_bytes=56 * 1024 * 1024),
+        compiler_params=pltpu.CompilerParams(vmem_limit_bytes=24 * 1024 * 1024),
         cost_estimate=pl.CostEstimate(flops=flops, bytes_accessed=sent, transcendentals=0),
         name=body.__name__,
     )(*operands)
 
 
 def exchange(blocks):
-    return lax.all_to_all(blocks, ("row", "col"), split_axis=0, concat_axis=0, tiled=True)
+    peers = len(blocks)
+    return [blocks[0]] + [
+        lax.ppermute(blocks[mask], ("row", "col"), [(at, at ^ mask) for at in range(peers)])
+        for mask in range(1, peers)
+    ]
 
 
 def local(
@@ -228,12 +246,12 @@
     gain = input_gain.reshape(1, channels)
     cells = height * width
 
-    sent = (s.peers, s.steps, 2 * s.each, s.lanes)
+    sent = (s.steps, 2 * s.each, s.lanes)
     message = call(
         produce,
         s,
-        shape(sent if s.direct else (s.steps, 2 * hidden, s.lanes), BF16),
-        [],
+        [shape(sent, BF16)] * s.peers if s.direct else [shape((s.steps, 2 * hidden, s.lanes), BF16)],
+        [pltpu.VMEM((s.peers if s.direct else 1, *sent), BF16)],
         8 * cells * channels * hidden,
         pair,
         valid_length,
@@ -244,8 +262,11 @@
         right_value,
     )
     if not s.direct:
-        message = message.reshape(s.steps, 2, s.peers, s.each, s.lanes)
-        message = message.transpose(2, 0, 1, 3, 4).reshape(sent)
+        message = message[0].reshape(s.steps, 2, s.peers, s.each, s.lanes)
+        message = message.transpose(2, 0, 1, 3, 4).reshape(s.peers, *sent)
+        own = lax.axis_index("row") * s.cols + lax.axis_index("col")
+        order = own ^ jnp.arange(s.peers, dtype=jnp.int32)
+        message = list(message[order])
     received = exchange(message)
     gating, weight, scale = call(
         gate,
@@ -265,25 +286,34 @@
     )
     scratch = (s.peers * s.steps * 2 * s.each, s.lanes)
     if not s.direct:
+        received = jnp.stack(received)[order]
         received = received.reshape(s.rows, s.cols * s.steps, 2 * s.each, s.lanes)
-        received = received.transpose(2, 0, 1, 3)
+        received = [received.transpose(2, 0, 1, 3)]
         scratch = (8, s.lanes)
+    back = (s.groups, s.slots, s.lanes)
     side = s.lanes if s.pack > 1 else s.rows * s.lanes
     sums = call(
         multiply,
         s,
-        shape((s.peers, s.groups, s.slots, s.lanes), BF16),
-        [pltpu.VMEM(scratch, F32), pltpu.VMEM((s.rows, side, s.lanes), F32)],
+        [shape(back, BF16)] * s.peers,
+        [
+            pltpu.VMEM((s.peers, *back), BF16),
+            pltpu.VMEM(scratch, F32),
+            pltpu.VMEM((s.rows, side, s.lanes), F32),
+        ],
         2 * s.each * (s.rows * height) ** 2 * s.cols * width,
-        received,
+        *received,
     )
     update = call(
         finish,
         s,
         shape((width, height, channels), BF16),
-        [pltpu.VMEM((s.lanes // LANES, hidden // s.pack * s.slots, LANES), F32)],
+        [
+            pltpu.VMEM((s.peers, *back), BF16),
+            pltpu.VMEM((s.lanes // LANES, hidden // s.pack * s.slots, LANES), F32),
+        ],
         2 * cells * channels * hidden,
-        exchange(sums),
+        *exchange(sums),
         gating,
         weight,
         scale,

time: 45.3 us -> 63.9 us (1.41)
  the two profiles are of different devices: /device:TPU:0 before, /device:TPU:1 now
where the time goes in v2:
time: 63.9 us; the launch traced here: 63.5 us
  starting transfers between devices  44 us (69%)
  waiting for transfers between devices  10.2 us (16%)
  local copies, waits for them, and re-layouts  4.62 us (7%)
  Pallas kernels  3.88 us (6%)
  between operations  0.76 us (1%)
    ppermute x30, starting transfers between devices, exchange(): lax.ppermute(blocks[mask], ('row', 'col'), [(at, at ^ mask) for at in ran...  44 us
    ppermute x30, waiting for transfers between devices, exchange(): lax.ppermute(blocks[mask], ('row', 'col'), [(at, at ^ mask) for at in ran...  10.2 us
    unnamed x20, local copies, waits for them, and re-layouts  4.62 us
    pallas_call x4, Pallas kernels, call(): pl.pallas_call(functools.partial(body, s), out_shape=out_shape, in_specs=...  3.88 us
  transfers between devices with their start and end apart: 30, of which 6 were waited for; matrix products, arithmetic and copies ran while one was open for 0% of the time, Pallas kernels for 1%

profile of v2, /device:TPU:1, one launch (start us, length us, event | category | flops | bytes accessed | tf_op | source)
XLA Modules:
  0.0 63.5 jit_solution(2235067282101107300)
XLA Ops:
  1.3 0.9 %copy-done = bf16[56,14,128]{2,0,1:T(8,128)(2,1)S(1)} copy-done((bf16[56,14,128]{2,0,1:T(8,128)(2,1)S(1)}, bf16[56,14,128]{2,0,1:T(8,128)(2,1)}, u32[]{:S(2)}) %copy-start) | copy-done | bytes 200728
  2.2 0.8 %copy-done.6 = bf16[128,128]{1,0:T(8,128)(2,1)S(1)} copy-done((bf16[128,128]{1,0:T(8,128)(2,1)S(1)}, bf16[128,128]{1,0:T(8,128)(2,1)}, u32[]{:S(2)}) %copy-start.6) | copy-done | bytes 32792
  3.0 0.8 %copy-done.7 = bf16[128,128]{1,0:T(8,128)(2,1)S(1)} copy-done((bf16[128,128]{1,0:T(8,128)(2,1)S(1)}, bf16[128,128]{1,0:T(8,128)(2,1)}, u32[]{:S(2)}) %copy-start.7) | copy-done | bytes 32792
  3.8 0.8 %copy-done.8 = bf16[128,128]{1,0:T(8,128)(2,1)S(1)} copy-done((bf16[128,128]{1,0:T(8,128)(2,1)S(1)}, bf16[128,128]{1,0:T(8,128)(2,1)}, u32[]{:S(2)}) %copy-start.8) | copy-done | bytes 32792
  4.5 0.8 %copy-done.9 = bf16[128,128]{1,0:T(8,128)(2,1)S(1)} copy-done((bf16[128,128]{1,0:T(8,128)(2,1)S(1)}, bf16[128,128]{1,0:T(8,128)(2,1)}, u32[]{:S(2)}) %copy-start.9) | copy-done | bytes 32792
  5.3 0.8 %produce.1 = (bf16[7,16,128]{2,1,0:T(8,128)(2,1)S(1)}, bf16[7,16,128]{2,1,0:T(8,128)(2,1)S(1)}, bf16[7,16,128]{2,1,0:T(8,128)(2,1)S(1)}, bf16[7,16,128]{2,1,0:T(...) custom-call(bf16[14,56,128]{2,1,0:T(8,128)(2,1)S(1)} %bitcast.4, ...), custom_call_target="tpu_custom_call" | custom-call | flops 102760448 | bytes 332292 | tf_op jit(solution)/shard_map/produce/pallas_call | solution.py:208
  6.1 2.1 %collective-permute-start = (bf16[7,16,128]{2,1,0:T(8,128)(2,1)S(1)}, bf16[7,16,128]{2,1,0:T(8,128)(2,1)S(1)}, u32[]{:S(2)}, u32[]{:S(2)}) collective-permute-start(bf16[7,16,128]{2,1,0:T(8,128)(2,1)S(1)} %get-tuple-element.41), channel_id=1, source_target_pairs={{0,1},{1,0},{2,3},{3,2},{4,5},{5,4},{6,7},{7,6},{8,9},{9,8},{10,11... | collective-permute-start | bytes 86024 | tf_op jit(solution)/shard_map/ppermute | solution.py:223
  8.2 1.3 %collective-permute-start.1 = (bf16[7,16,128]{2,1,0:T(8,128)(2,1)S(1)}, bf16[7,16,128]{2,1,0:T(8,128)(2,1)S(1)}, u32[]{:S(2)}, u32[]{:S(2)}) collective-permute-start(bf16[7,16,128]{2,1,0:T(8,128)(2,1)S(1)} %get-tuple-element.42), channel_id=1, source_target_pairs={{0,2},{1,3},{2,0},{3,1},{4,6},{5,7},{6,4},{7,5},{8,10},{9,11},{10,... | collective-permute-start | bytes 86024 | tf_op jit(solution)/shard_map/ppermute | solution.py:223
  9.5 2.4 %collective-permute-start.3 = (bf16[7,16,128]{2,1,0:T(8,128)(2,1)S(1)}, bf16[7,16,128]{2,1,0:T(8,128)(2,1)S(1)}, u32[]{:S(2)}, u32[]{:S(2)}) collective-permute-start(bf16[7,16,128]{2,1,0:T(8,128)(2,1)S(1)} %get-tuple-element.44), channel_id=1, source_target_pairs={{0,4},{1,5},{2,6},{3,7},{4,0},{5,1},{6,2},{7,3},{8,12},{9,13},{10,... | collective-permute-start | bytes 86024 | tf_op jit(solution)/shard_map/ppermute | solution.py:223
  11.9 1.0 %collective-permute-start.4 = (bf16[7,16,128]{2,1,0:T(8,128)(2,1)S(1)}, bf16[7,16,128]{2,1,0:T(8,128)(2,1)S(1)}, u32[]{:S(2)}, u32[]{:S(2)}) collective-permute-start(bf16[7,16,128]{2,1,0:T(8,128)(2,1)S(1)} %get-tuple-element.45), channel_id=1, source_target_pairs={{0,5},{1,4},{2,7},{3,6},{4,1},{5,0},{6,3},{7,2},{8,13},{9,12},{10,... | collective-permute-start | bytes 86024 | tf_op jit(solution)/shard_map/ppermute | solution.py:223
  12.9 3.3 %collective-permute-start.5 = (bf16[7,16,128]{2,1,0:T(8,128)(2,1)S(1)}, bf16[7,16,128]{2,1,0:T(8,128)(2,1)S(1)}, u32[]{:S(2)}, u32[]{:S(2)}) collective-permute-start(bf16[7,16,128]{2,1,0:T(8,128)(2,1)S(1)} %get-tuple-element.46), channel_id=1, source_target_pairs={{0,6},{1,7},{2,4},{3,5},{4,2},{5,3},{6,0},{7,1},{8,14},{9,15},{10,... | collective-permute-start | bytes 86024 | tf_op jit(solution)/shard_map/ppermute | solution.py:223
  16.3 2.4 %collective-permute-start.7 = (bf16[7,16,128]{2,1,0:T(8,128)(2,1)S(1)}, bf16[7,16,128]{2,1,0:T(8,128)(2,1)S(1)}, u32[]{:S(2)}, u32[]{:S(2)}) collective-permute-start(bf16[7,16,128]{2,1,0:T(8,128)(2,1)S(1)} %get-tuple-element.48), channel_id=1, source_target_pairs={{0,8},{1,9},{2,10},{3,11},{4,12},{5,13},{6,14},{7,15},{8,0},{9,1},... | collective-permute-start | bytes 86024 | tf_op jit(solution)/shard_map/ppermute | solution.py:223
  18.7 1.3 %collective-permute-start.8 = (bf16[7,16,128]{2,1,0:T(8,128)(2,1)S(1)}, bf16[7,16,128]{2,1,0:T(8,128)(2,1)S(1)}, u32[]{:S(2)}, u32[]{:S(2)}) collective-permute-start(bf16[7,16,128]{2,1,0:T(8,128)(2,1)S(1)} %get-tuple-element.49), channel_id=1, source_target_pairs={{0,9},{1,8},{2,11},{3,10},{4,13},{5,12},{6,15},{7,14},{8,1},{9,0},... | collective-permute-start | bytes 86024 | tf_op jit(solution)/shard_map/ppermute | solution.py:223
  20.6 1.0 %collective-permute-start.10 = (bf16[7,16,128]{2,1,0:T(8,128)(2,1)S(1)}, bf16[7,16,128]{2,1,0:T(8,128)(2,1)S(1)}, u32[]{:S(2)}, u32[]{:S(2)}) collective-permute-start(bf16[7,16,128]{2,1,0:T(8,128)(2,1)S(1)} %get-tuple-element.51), channel_id=1, source_target_pairs={{0,11},{1,10},{2,9},{3,8},{4,15},{5,14},{6,13},{7,12},{8,3},{9,2},... | collective-permute-start | bytes 86024 | tf_op jit(solution)/shard_map/ppermute | solution.py:223
  21.7 2.3 %collective-permute-start.11 = (bf16[7,16,128]{2,1,0:T(8,128)(2,1)S(1)}, bf16[7,16,128]{2,1,0:T(8,128)(2,1)S(1)}, u32[]{:S(2)}, u32[]{:S(2)}) collective-permute-start(bf16[7,16,128]{2,1,0:T(8,128)(2,1)S(1)} %get-tuple-element.52), channel_id=1, source_target_pairs={{0,12},{1,13},{2,14},{3,15},{4,8},{5,9},{6,10},{7,11},{8,4},{9,5},... | collective-permute-start | bytes 86024 | tf_op jit(solution)/shard_map/ppermute | solution.py:223
  24.0 1.3 %collective-permute-start.12 = (bf16[7,16,128]{2,1,0:T(8,128)(2,1)S(1)}, bf16[7,16,128]{2,1,0:T(8,128)(2,1)S(1)}, u32[]{:S(2)}, u32[]{:S(2)}) collective-permute-start(bf16[7,16,128]{2,1,0:T(8,128)(2,1)S(1)} %get-tuple-element.53), channel_id=1, source_target_pairs={{0,13},{1,12},{2,15},{3,14},{4,9},{5,8},{6,11},{7,10},{8,5},{9,4},... | collective-permute-start | bytes 86024 | tf_op jit(solution)/shard_map/ppermute | solution.py:223
  25.3 3.7 %collective-permute-start.13 = (bf16[7,16,128]{2,1,0:T(8,128)(2,1)S(1)}, bf16[7,16,128]{2,1,0:T(8,128)(2,1)S(1)}, u32[]{:S(2)}, u32[]{:S(2)}) collective-permute-start(bf16[7,16,128]{2,1,0:T(8,128)(2,1)S(1)} %get-tuple-element.54), channel_id=1, source_target_pairs={{0,14},{1,15},{2,12},{3,13},{4,10},{5,11},{6,8},{7,9},{8,6},{9,7},... | collective-permute-start | bytes 86024 | tf_op jit(solution)/shard_map/ppermute | solution.py:223
  29.1 2.0 %collective-permute-done.13.refs_14_ = bf16[7,16,128]{2,1,0:T(8,128)(2,1)S(1)} collective-permute-done((bf16[7,16,128]{2,1,0:T(8,128)(2,1)S(1)}, bf16[7,16,128]{2,1,0:T(8,128)(2,1)S(1)}, u32[]{:S(2)}, u32[]{:S(2)}) %collective-permute-start.13) | collective-permute-done | bytes 28704 | tf_op jit(solution)/shard_map/ppermute | solution.py:223
  31.1 3.8 %collective-permute-done.14.refs_15_ = bf16[7,16,128]{2,1,0:T(8,128)(2,1)S(1)} collective-permute-done((bf16[7,16,128]{2,1,0:T(8,128)(2,1)S(1)}, bf16[7,16,128]{2,1,0:T(8,128)(2,1)S(1)}, u32[]{:S(2)}, u32[]{:S(2)}) %collective-permute-start.14) | collective-permute-done | bytes 28704 | tf_op jit(solution)/shard_map/ppermute | solution.py:223
  35.0 1.0 %multiply.1 = (bf16[4,16,128]{2,1,0:T(8,128)(2,1)S(1)}, bf16[4,16,128]{2,1,0:T(8,128)(2,1)S(1)}, bf16[4,16,128]{2,1,0:T(8,128)(2,1)S(1)}, bf16[4,16,128]{2,1,0:T...) custom-call(bf16[7,16,128]{2,1,0:T(8,128)(2,1)S(1)} %get-tuple-eleme, ...), custom_call_target="tpu_custom_call" | custom-call | flops 22478848 | bytes 458752 | tf_op jit(solution)/shard_map/multiply/pallas_call | solution.py:208
  36.3 2.4 %collective-permute-start.17 = (bf16[4,16,128]{2,1,0:T(8,128)(2,1)S(1)}, bf16[4,16,128]{2,1,0:T(8,128)(2,1)S(1)}, u32[]{:S(2)}, u32[]{:S(2)}) collective-permute-start(bf16[4,16,128]{2,1,0:T(8,128)(2,1)S(1)} %get-tuple-element.59), channel_id=1, source_target_pairs={{0,3},{1,2},{2,1},{3,0},{4,7},{5,6},{6,5},{7,4},{8,11},{9,10},{10,... | collective-permute-start | bytes 49160 | tf_op jit(solution)/shard_map/ppermute | solution.py:223
  38.7 1.2 %collective-permute-start.18 = (bf16[4,16,128]{2,1,0:T(8,128)(2,1)S(1)}, bf16[4,16,128]{2,1,0:T(8,128)(2,1)S(1)}, u32[]{:S(2)}, u32[]{:S(2)}) collective-permute-start(bf16[4,16,128]{2,1,0:T(8,128)(2,1)S(1)} %get-tuple-element.60), channel_id=1, source_target_pairs={{0,4},{1,5},{2,6},{3,7},{4,0},{5,1},{6,2},{7,3},{8,12},{9,13},{10,... | collective-permute-start | bytes 49160 | tf_op jit(solution)/shard_map/ppermute | solution.py:223
  39.9 1.2 %collective-permute-start.19 = (bf16[4,16,128]{2,1,0:T(8,128)(2,1)S(1)}, bf16[4,16,128]{2,1,0:T(8,128)(2,1)S(1)}, u32[]{:S(2)}, u32[]{:S(2)}) collective-permute-start(bf16[4,16,128]{2,1,0:T(8,128)(2,1)S(1)} %get-tuple-element.61), channel_id=1, source_target_pairs={{0,5},{1,4},{2,7},{3,6},{4,1},{5,0},{6,3},{7,2},{8,13},{9,12},{10,... | collective-permute-start | bytes 49160 | tf_op jit(solution)/shard_map/ppermute | solution.py:223
  41.0 3.3 %collective-permute-start.20 = (bf16[4,16,128]{2,1,0:T(8,128)(2,1)S(1)}, bf16[4,16,128]{2,1,0:T(8,128)(2,1)S(1)}, u32[]{:S(2)}, u32[]{:S(2)}) collective-permute-start(bf16[4,16,128]{2,1,0:T(8,128)(2,1)S(1)} %get-tuple-element.62), channel_id=1, source_target_pairs={{0,6},{1,7},{2,4},{3,5},{4,2},{5,3},{6,0},{7,1},{8,14},{9,15},{10,... | collective-permute-start | bytes 49160 | tf_op jit(solution)/shard_map/ppermute | solution.py:223
  44.3 0.9 %collective-permute-start.21 = (bf16[4,16,128]{2,1,0:T(8,128)(2,1)S(1)}, bf16[4,16,128]{2,1,0:T(8,128)(2,1)S(1)}, u32[]{:S(2)}, u32[]{:S(2)}) collective-permute-start(bf16[4,16,128]{2,1,0:T(8,128)(2,1)S(1)} %get-tuple-element.63), channel_id=1, source_target_pairs={{0,7},{1,6},{2,5},{3,4},{4,3},{5,2},{6,1},{7,0},{8,15},{9,14},{10,... | collective-permute-start | bytes 49160 | tf_op jit(solution)/shard_map/ppermute | solution.py:223
  45.3 2.0 %collective-permute-start.22 = (bf16[4,16,128]{2,1,0:T(8,128)(2,1)S(1)}, bf16[4,16,128]{2,1,0:T(8,128)(2,1)S(1)}, u32[]{:S(2)}, u32[]{:S(2)}) collective-permute-start(bf16[4,16,128]{2,1,0:T(8,128)(2,1)S(1)} %get-tuple-element.64), channel_id=1, source_target_pairs={{0,8},{1,9},{2,10},{3,11},{4,12},{5,13},{6,14},{7,15},{8,0},{9,1},... | collective-permute-start | bytes 49160 | tf_op jit(solution)/shard_map/ppermute | solution.py:223
  47.6 2.6 %collective-permute-start.25 = (bf16[4,16,128]{2,1,0:T(8,128)(2,1)S(1)}, bf16[4,16,128]{2,1,0:T(8,128)(2,1)S(1)}, u32[]{:S(2)}, u32[]{:S(2)}) collective-permute-start(bf16[4,16,128]{2,1,0:T(8,128)(2,1)S(1)} %get-tuple-element.67), channel_id=1, source_target_pairs={{0,11},{1,10},{2,9},{3,8},{4,15},{5,14},{6,13},{7,12},{8,3},{9,2},... | collective-permute-start | bytes 49160 | tf_op jit(solution)/shard_map/ppermute | solution.py:223
  50.2 2.7 %collective-permute-start.27 = (bf16[4,16,128]{2,1,0:T(8,128)(2,1)S(1)}, bf16[4,16,128]{2,1,0:T(8,128)(2,1)S(1)}, u32[]{:S(2)}, u32[]{:S(2)}) collective-permute-start(bf16[4,16,128]{2,1,0:T(8,128)(2,1)S(1)} %get-tuple-element.69), channel_id=1, source_target_pairs={{0,13},{1,12},{2,15},{3,14},{4,9},{5,8},{6,11},{7,10},{8,5},{9,4},... | collective-permute-start | bytes 49160 | tf_op jit(solution)/shard_map/ppermute | solution.py:223
  52.9 3.2 %collective-permute-start.28 = (bf16[4,16,128]{2,1,0:T(8,128)(2,1)S(1)}, bf16[4,16,128]{2,1,0:T(8,128)(2,1)S(1)}, u32[]{:S(2)}, u32[]{:S(2)}) collective-permute-start(bf16[4,16,128]{2,1,0:T(8,128)(2,1)S(1)} %get-tuple-element.70), channel_id=1, source_target_pairs={{0,14},{1,15},{2,12},{3,13},{4,10},{5,11},{6,8},{7,9},{8,6},{9,7},... | collective-permute-start | bytes 49160 | tf_op jit(solution)/shard_map/ppermute | solution.py:223
  56.1 1.2 %collective-permute-start.29 = (bf16[4,16,128]{2,1,0:T(8,128)(2,1)S(1)}, bf16[4,16,128]{2,1,0:T(8,128)(2,1)S(1)}, u32[]{:S(2)}, u32[]{:S(2)}) collective-permute-start(bf16[4,16,128]{2,1,0:T(8,128)(2,1)S(1)} %get-tuple-element.71), channel_id=1, source_target_pairs={{0,15},{1,14},{2,13},{3,12},{4,11},{5,10},{6,9},{7,8},{8,7},{9,6},... | collective-permute-start | bytes 49160 | tf_op jit(solution)/shard_map/ppermute | solution.py:223
  58.0 4.0 %collective-permute-done.29.refs_15_ = bf16[4,16,128]{2,1,0:T(8,128)(2,1)S(1)} collective-permute-done((bf16[4,16,128]{2,1,0:T(8,128)(2,1)S(1)}, bf16[4,16,128]{2,1,0:T(8,128)(2,1)S(1)}, u32[]{:S(2)}, u32[]{:S(2)}) %collective-permute-start.29) | collective-permute-done | bytes 16416 | tf_op jit(solution)/shard_map/ppermute | solution.py:223
  61.9 1.6 %finish.1 = bf16[14,56,128]{2,1,0:T(8,128)(2,1)} custom-call(bf16[4,16,128]{2,1,0:T(8,128)(2,1)S(1)} %get-tuple-element.56.refs_0_, bf16[4,16,128]{2,1,0:T(8,128)(2,1)S(1)} %collective-permute-done.15.refs_1_, bf16[4,16,128]{2,1,0:T(8,128)(2,1)S(1)} %collective-permute-done.16.refs_2_, bf16[4,16,128]{2,1,0:T(8,128)(2,1)S(1)} %collective-permute-done.17.refs_3_, ...), custom_call_target="tpu_custom_call" | custom-call | flops 25690112 | bytes 729088 | tf_op jit(solution)/shard_map/finish/pallas_call | solution.py:208
  (52 shorter events, 2.8 us)
Async XLA Ops:
  6.1 6.9 %collective-permute-start = (bf16[7,16,128]{2,1,0:T(8,128)(2,1)S(1)}, bf16[7,16,128]{2,1,0:T(8,128)(2,1)S(1)}, u32[]{:S(2)}, u32[]{:S(2)}) collective-permute-start(bf16[7,16,128]{2,1,0:T(8,128)(2,1)S(1)} %get-tuple-element.41), channel_id=1, source_target_pairs={{0,1},{1,0},{2,3},{3,2},{4,5},{5,4},{6,7},{7,6},{8,9},{9,8},{10,11... | collective-permute-start | bytes 86024 | tf_op jit(solution)/shard_map/ppermute | solution.py:223
  8.2 8.1 %collective-permute-start.1 = (bf16[7,16,128]{2,1,0:T(8,128)(2,1)S(1)}, bf16[7,16,128]{2,1,0:T(8,128)(2,1)S(1)}, u32[]{:S(2)}, u32[]{:S(2)}) collective-permute-start(bf16[7,16,128]{2,1,0:T(8,128)(2,1)S(1)} %get-tuple-element.42), channel_id=1, source_target_pairs={{0,2},{1,3},{2,0},{3,1},{4,6},{5,7},{6,4},{7,5},{8,10},{9,11},{10,... | collective-permute-start | bytes 86024 | tf_op jit(solution)/shard_map/ppermute | solution.py:223
  9.5 6.8 %collective-permute-start.2 = (bf16[7,16,128]{2,1,0:T(8,128)(2,1)S(1)}, bf16[7,16,128]{2,1,0:T(8,128)(2,1)S(1)}, u32[]{:S(2)}, u32[]{:S(2)}) collective-permute-start(bf16[7,16,128]{2,1,0:T(8,128)(2,1)S(1)} %get-tuple-element.43), channel_id=1, source_target_pairs={{0,3},{1,2},{2,1},{3,0},{4,7},{5,6},{6,5},{7,4},{8,11},{9,10},{10,... | collective-permute-start | bytes 86024 | tf_op jit(solution)/shard_map/ppermute | solution.py:223
  9.5 9.2 %collective-permute-start.3 = (bf16[7,16,128]{2,1,0:T(8,128)(2,1)S(1)}, bf16[7,16,128]{2,1,0:T(8,128)(2,1)S(1)}, u32[]{:S(2)}, u32[]{:S(2)}) collective-permute-start(bf16[7,16,128]{2,1,0:T(8,128)(2,1)S(1)} %get-tuple-element.44), channel_id=1, source_target_pairs={{0,4},{1,5},{2,6},{3,7},{4,0},{5,1},{6,2},{7,3},{8,12},{9,13},{10,... | collective-permute-start | bytes 86024 | tf_op jit(solution)/shard_map/ppermute | solution.py:223
  11.9 8.1 %collective-permute-start.4 = (bf16[7,16,128]{2,1,0:T(8,128)(2,1)S(1)}, bf16[7,16,128]{2,1,0:T(8,128)(2,1)S(1)}, u32[]{:S(2)}, u32[]{:S(2)}) collective-permute-start(bf16[7,16,128]{2,1,0:T(8,128)(2,1)S(1)} %get-tuple-element.45), channel_id=1, source_target_pairs={{0,5},{1,4},{2,7},{3,6},{4,1},{5,0},{6,3},{7,2},{8,13},{9,12},{10,... | collective-permute-start | bytes 86024 | tf_op jit(solution)/shard_map/ppermute | solution.py:223
  12.9 7.6 %collective-permute-start.5 = (bf16[7,16,128]{2,1,0:T(8,128)(2,1)S(1)}, bf16[7,16,128]{2,1,0:T(8,128)(2,1)S(1)}, u32[]{:S(2)}, u32[]{:S(2)}) collective-permute-start(bf16[7,16,128]{2,1,0:T(8,128)(2,1)S(1)} %get-tuple-element.46), channel_id=1, source_target_pairs={{0,6},{1,7},{2,4},{3,5},{4,2},{5,3},{6,0},{7,1},{8,14},{9,15},{10,... | collective-permute-start | bytes 86024 | tf_op jit(solution)/shard_map/ppermute | solution.py:223
  16.3 5.4 %collective-permute-start.6 = (bf16[7,16,128]{2,1,0:T(8,128)(2,1)S(1)}, bf16[7,16,128]{2,1,0:T(8,128)(2,1)S(1)}, u32[]{:S(2)}, u32[]{:S(2)}) collective-permute-start(bf16[7,16,128]{2,1,0:T(8,128)(2,1)S(1)} %get-tuple-element.47), channel_id=1, source_target_pairs={{0,7},{1,6},{2,5},{3,4},{4,3},{5,2},{6,1},{7,0},{8,15},{9,14},{10,... | collective-permute-start | bytes 86024 | tf_op jit(solution)/shard_map/ppermute | solution.py:223
  16.3 7.7 %collective-permute-start.7 = (bf16[7,16,128]{2,1,0:T(8,128)(2,1)S(1)}, bf16[7,16,128]{2,1,0:T(8,128)(2,1)S(1)}, u32[]{:S(2)}, u32[]{:S(2)}) collective-permute-start(bf16[7,16,128]{2,1,0:T(8,128)(2,1)S(1)} %get-tuple-element.48), channel_id=1, source_target_pairs={{0,8},{1,9},{2,10},{3,11},{4,12},{5,13},{6,14},{7,15},{8,0},{9,1},... | collective-permute-start | bytes 86024 | tf_op jit(solution)/shard_map/ppermute | solution.py:223
  18.7 6.6 %collective-permute-start.8 = (bf16[7,16,128]{2,1,0:T(8,128)(2,1)S(1)}, bf16[7,16,128]{2,1,0:T(8,128)(2,1)S(1)}, u32[]{:S(2)}, u32[]{:S(2)}) collective-permute-start(bf16[7,16,128]{2,1,0:T(8,128)(2,1)S(1)} %get-tuple-element.49), channel_id=1, source_target_pairs={{0,9},{1,8},{2,11},{3,10},{4,13},{5,12},{6,15},{7,14},{8,1},{9,0},... | collective-permute-start | bytes 86024 | tf_op jit(solution)/shard_map/ppermute | solution.py:223
  20.0 9.0 %collective-permute-start.9 = (bf16[7,16,128]{2,1,0:T(8,128)(2,1)S(1)}, bf16[7,16,128]{2,1,0:T(8,128)(2,1)S(1)}, u32[]{:S(2)}, u32[]{:S(2)}) collective-permute-start(bf16[7,16,128]{2,1,0:T(8,128)(2,1)S(1)} %get-tuple-element.50), channel_id=1, source_target_pairs={{0,10},{1,11},{2,8},{3,9},{4,14},{5,15},{6,12},{7,13},{8,2},{9,3},... | collective-permute-start | bytes 86024 | tf_op jit(solution)/shard_map/ppermute | solution.py:223
  20.6 8.4 %collective-permute-start.10 = (bf16[7,16,128]{2,1,0:T(8,128)(2,1)S(1)}, bf16[7,16,128]{2,1,0:T(8,128)(2,1)S(1)}, u32[]{:S(2)}, u32[]{:S(2)}) collective-permute-start(bf16[7,16,128]{2,1,0:T(8,128)(2,1)S(1)} %get-tuple-element.51), channel_id=1, source_target_pairs={{0,11},{1,10},{2,9},{3,8},{4,15},{5,14},{6,13},{7,12},{8,3},{9,2},... | collective-permute-start | bytes 86024 | tf_op jit(solution)/shard_map/ppermute | solution.py:223
  21.7 7.3 %collective-permute-start.11 = (bf16[7,16,128]{2,1,0:T(8,128)(2,1)S(1)}, bf16[7,16,128]{2,1,0:T(8,128)(2,1)S(1)}, u32[]{:S(2)}, u32[]{:S(2)}) collective-permute-start(bf16[7,16,128]{2,1,0:T(8,128)(2,1)S(1)} %get-tuple-element.52), channel_id=1, source_target_pairs={{0,12},{1,13},{2,14},{3,15},{4,8},{5,9},{6,10},{7,11},{8,4},{9,5},... | collective-permute-start | bytes 86024 | tf_op jit(solution)/shard_map/ppermute | solution.py:223
  24.0 5.1 %collective-permute-start.12 = (bf16[7,16,128]{2,1,0:T(8,128)(2,1)S(1)}, bf16[7,16,128]{2,1,0:T(8,128)(2,1)S(1)}, u32[]{:S(2)}, u32[]{:S(2)}) collective-permute-start(bf16[7,16,128]{2,1,0:T(8,128)(2,1)S(1)} %get-tuple-element.53), channel_id=1, source_target_pairs={{0,13},{1,12},{2,15},{3,14},{4,9},{5,8},{6,11},{7,10},{8,5},{9,4},... | collective-permute-start | bytes 86024 | tf_op jit(solution)/shard_map/ppermute | solution.py:223
  25.3 5.8 %collective-permute-start.13 = (bf16[7,16,128]{2,1,0:T(8,128)(2,1)S(1)}, bf16[7,16,128]{2,1,0:T(8,128)(2,1)S(1)}, u32[]{:S(2)}, u32[]{:S(2)}) collective-permute-start(bf16[7,16,128]{2,1,0:T(8,128)(2,1)S(1)} %get-tuple-element.54), channel_id=1, source_target_pairs={{0,14},{1,15},{2,12},{3,13},{4,10},{5,11},{6,8},{7,9},{8,6},{9,7},... | collective-permute-start | bytes 86024 | tf_op jit(solution)/shard_map/ppermute | solution.py:223
  29.0 6.0 %collective-permute-start.14 = (bf16[7,16,128]{2,1,0:T(8,128)(2,1)S(1)}, bf16[7,16,128]{2,1,0:T(8,128)(2,1)S(1)}, u32[]{:S(2)}, u32[]{:S(2)}) collective-permute-start(bf16[7,16,128]{2,1,0:T(8,128)(2,1)S(1)} %get-tuple-element.55), channel_id=1, source_target_pairs={{0,15},{1,14},{2,13},{3,12},{4,11},{5,10},{6,9},{7,8},{8,7},{9,6},... | collective-permute-start | bytes 86024 | tf_op jit(solution)/shard_map/ppermute | solution.py:223
  34.9 22.3 %copy-start.2 = (bf16[128,128]{1,0:T(8,128)(2,1)S(1)}, bf16[128,128]{1,0:T(8,128)(2,1)}, u32[]{:S(2)}) copy-start(bf16[128,128]{1,0:T(8,128)(2,1)} %out_gate.1) | copy-start | bytes 98308
  35.0 22.3 %copy-start.3 = (bf16[128,128]{1,0:T(8,128)(2,1)S(1)}, bf16[128,128]{1,0:T(8,128)(2,1)}, u32[]{:S(2)}) copy-start(bf16[128,128]{1,0:T(8,128)(2,1)} %out_weight.1) | copy-start | bytes 98308
  36.0 5.0 %collective-permute-start.15 = (bf16[4,16,128]{2,1,0:T(8,128)(2,1)S(1)}, bf16[4,16,128]{2,1,0:T(8,128)(2,1)S(1)}, u32[]{:S(2)}, u32[]{:S(2)}) collective-permute-start(bf16[4,16,128]{2,1,0:T(8,128)(2,1)S(1)} %get-tuple-element.57), channel_id=1, source_target_pairs={{0,1},{1,0},{2,3},{3,2},{4,5},{5,4},{6,7},{7,6},{8,9},{9,8},{10,11... | collective-permute-start | bytes 49160 | tf_op jit(solution)/shard_map/ppermute | solution.py:223
  36.3 8.0 %collective-permute-start.16 = (bf16[4,16,128]{2,1,0:T(8,128)(2,1)S(1)}, bf16[4,16,128]{2,1,0:T(8,128)(2,1)S(1)}, u32[]{:S(2)}, u32[]{:S(2)}) collective-permute-start(bf16[4,16,128]{2,1,0:T(8,128)(2,1)S(1)} %get-tuple-element.58), channel_id=1, source_target_pairs={{0,2},{1,3},{2,0},{3,1},{4,6},{5,7},{6,4},{7,5},{8,10},{9,11},{10,... | collective-permute-start | bytes 49160 | tf_op jit(solution)/shard_map/ppermute | solution.py:223
  36.3 9.0 %collective-permute-start.17 = (bf16[4,16,128]{2,1,0:T(8,128)(2,1)S(1)}, bf16[4,16,128]{2,1,0:T(8,128)(2,1)S(1)}, u32[]{:S(2)}, u32[]{:S(2)}) collective-permute-start(bf16[4,16,128]{2,1,0:T(8,128)(2,1)S(1)} %get-tuple-element.59), channel_id=1, source_target_pairs={{0,3},{1,2},{2,1},{3,0},{4,7},{5,6},{6,5},{7,4},{8,11},{9,10},{10,... | collective-permute-start | bytes 49160 | tf_op jit(solution)/shard_map/ppermute | solution.py:223
  38.7 8.6 %collective-permute-start.18 = (bf16[4,16,128]{2,1,0:T(8,128)(2,1)S(1)}, bf16[4,16,128]{2,1,0:T(8,128)(2,1)S(1)}, u32[]{:S(2)}, u32[]{:S(2)}) collective-permute-start(bf16[4,16,128]{2,1,0:T(8,128)(2,1)S(1)} %get-tuple-element.60), channel_id=1, source_target_pairs={{0,4},{1,5},{2,6},{3,7},{4,0},{5,1},{6,2},{7,3},{8,12},{9,13},{10,... | collective-permute-start | bytes 49160 | tf_op jit(solution)/shard_map/ppermute | solution.py:223
  39.9 7.7 %collective-permute-start.19 = (bf16[4,16,128]{2,1,0:T(8,128)(2,1)S(1)}, bf16[4,16,128]{2,1,0:T(8,128)(2,1)S(1)}, u32[]{:S(2)}, u32[]{:S(2)}) collective-permute-start(bf16[4,16,128]{2,1,0:T(8,128)(2,1)S(1)} %get-tuple-element.61), channel_id=1, source_target_pairs={{0,5},{1,4},{2,7},{3,6},{4,1},{5,0},{6,3},{7,2},{8,13},{9,12},{10,... | collective-permute-start | bytes 49160 | tf_op jit(solution)/shard_map/ppermute | solution.py:223
  41.0 6.6 %collective-permute-start.20 = (bf16[4,16,128]{2,1,0:T(8,128)(2,1)S(1)}, bf16[4,16,128]{2,1,0:T(8,128)(2,1)S(1)}, u32[]{:S(2)}, u32[]{:S(2)}) collective-permute-start(bf16[4,16,128]{2,1,0:T(8,128)(2,1)S(1)} %get-tuple-element.62), channel_id=1, source_target_pairs={{0,6},{1,7},{2,4},{3,5},{4,2},{5,3},{6,0},{7,1},{8,14},{9,15},{10,... | collective-permute-start | bytes 49160 | tf_op jit(solution)/shard_map/ppermute | solution.py:223
  44.3 5.9 %collective-permute-start.21 = (bf16[4,16,128]{2,1,0:T(8,128)(2,1)S(1)}, bf16[4,16,128]{2,1,0:T(8,128)(2,1)S(1)}, u32[]{:S(2)}, u32[]{:S(2)}) collective-permute-start(bf16[4,16,128]{2,1,0:T(8,128)(2,1)S(1)} %get-tuple-element.63), channel_id=1, source_target_pairs={{0,7},{1,6},{2,5},{3,4},{4,3},{5,2},{6,1},{7,0},{8,15},{9,14},{10,... | collective-permute-start | bytes 49160 | tf_op jit(solution)/shard_map/ppermute | solution.py:223
  45.3 4.9 %collective-permute-start.22 = (bf16[4,16,128]{2,1,0:T(8,128)(2,1)S(1)}, bf16[4,16,128]{2,1,0:T(8,128)(2,1)S(1)}, u32[]{:S(2)}, u32[]{:S(2)}) collective-permute-start(bf16[4,16,128]{2,1,0:T(8,128)(2,1)S(1)} %get-tuple-element.64), channel_id=1, source_target_pairs={{0,8},{1,9},{2,10},{3,11},{4,12},{5,13},{6,14},{7,15},{8,0},{9,1},... | collective-permute-start | bytes 49160 | tf_op jit(solution)/shard_map/ppermute | solution.py:223
  47.3 5.6 %collective-permute-start.23 = (bf16[4,16,128]{2,1,0:T(8,128)(2,1)S(1)}, bf16[4,16,128]{2,1,0:T(8,128)(2,1)S(1)}, u32[]{:S(2)}, u32[]{:S(2)}) collective-permute-start(bf16[4,16,128]{2,1,0:T(8,128)(2,1)S(1)} %get-tuple-element.65), channel_id=1, source_target_pairs={{0,9},{1,8},{2,11},{3,10},{4,13},{5,12},{6,15},{7,14},{8,1},{9,0},... | collective-permute-start | bytes 49160 | tf_op jit(solution)/shard_map/ppermute | solution.py:223
  47.6 8.5 %collective-permute-start.24 = (bf16[4,16,128]{2,1,0:T(8,128)(2,1)S(1)}, bf16[4,16,128]{2,1,0:T(8,128)(2,1)S(1)}, u32[]{:S(2)}, u32[]{:S(2)}) collective-permute-start(bf16[4,16,128]{2,1,0:T(8,128)(2,1)S(1)} %get-tuple-element.66), channel_id=1, source_target_pairs={{0,10},{1,11},{2,8},{3,9},{4,14},{5,15},{6,12},{7,13},{8,2},{9,3},... | collective-permute-start | bytes 49160 | tf_op jit(solution)/shard_map/ppermute | solution.py:223
  47.6 10.2 %collective-permute-start.25 = (bf16[4,16,128]{2,1,0:T(8,128)(2,1)S(1)}, bf16[4,16,128]{2,1,0:T(8,128)(2,1)S(1)}, u32[]{:S(2)}, u32[]{:S(2)}) collective-permute-start(bf16[4,16,128]{2,1,0:T(8,128)(2,1)S(1)} %get-tuple-element.67), channel_id=1, source_target_pairs={{0,11},{1,10},{2,9},{3,8},{4,15},{5,14},{6,13},{7,12},{8,3},{9,2},... | collective-permute-start | bytes 49160 | tf_op jit(solution)/shard_map/ppermute | solution.py:223
  50.2 7.6 %collective-permute-start.26 = (bf16[4,16,128]{2,1,0:T(8,128)(2,1)S(1)}, bf16[4,16,128]{2,1,0:T(8,128)(2,1)S(1)}, u32[]{:S(2)}, u32[]{:S(2)}) collective-permute-start(bf16[4,16,128]{2,1,0:T(8,128)(2,1)S(1)} %get-tuple-element.68), channel_id=1, source_target_pairs={{0,12},{1,13},{2,14},{3,15},{4,8},{5,9},{6,10},{7,11},{8,4},{9,5},... | collective-permute-start | bytes 49160 | tf_op jit(solution)/shard_map/ppermute | solution.py:223
  50.2 7.6 %collective-permute-start.27 = (bf16[4,16,128]{2,1,0:T(8,128)(2,1)S(1)}, bf16[4,16,128]{2,1,0:T(8,128)(2,1)S(1)}, u32[]{:S(2)}, u32[]{:S(2)}) collective-permute-start(bf16[4,16,128]{2,1,0:T(8,128)(2,1)S(1)} %get-tuple-element.69), channel_id=1, source_target_pairs={{0,13},{1,12},{2,15},{3,14},{4,9},{5,8},{6,11},{7,10},{8,5},{9,4},... | collective-permute-start | bytes 49160 | tf_op jit(solution)/shard_map/ppermute | solution.py:223
  52.9 5.0 %collective-permute-start.28 = (bf16[4,16,128]{2,1,0:T(8,128)(2,1)S(1)}, bf16[4,16,128]{2,1,0:T(8,128)(2,1)S(1)}, u32[]{:S(2)}, u32[]{:S(2)}) collective-permute-start(bf16[4,16,128]{2,1,0:T(8,128)(2,1)S(1)} %get-tuple-element.70), channel_id=1, source_target_pairs={{0,14},{1,15},{2,12},{3,13},{4,10},{5,11},{6,8},{7,9},{8,6},{9,7},... | collective-permute-start | bytes 49160 | tf_op jit(solution)/shard_map/ppermute | solution.py:223
  56.1 5.9 %collective-permute-start.29 = (bf16[4,16,128]{2,1,0:T(8,128)(2,1)S(1)}, bf16[4,16,128]{2,1,0:T(8,128)(2,1)S(1)}, u32[]{:S(2)}, u32[]{:S(2)}) collective-permute-start(bf16[4,16,128]{2,1,0:T(8,128)(2,1)S(1)} %get-tuple-element.71), channel_id=1, source_target_pairs={{0,15},{1,14},{2,13},{3,12},{4,11},{5,10},{6,9},{7,8},{8,7},{9,6},... | collective-permute-start | bytes 49160 | tf_op jit(solution)/shard_map/ppermute | solution.py:223
  (8 other events, 28.2 us)

commit v3 on v1

--- a/solution.py
+++ b/solution.py
@@ -10,7 +10,6 @@
 F32 = jnp.float32
 BF16 = jnp.bfloat16
 LANES = 128
-SUBLANES = 16
 EPS = 1e-05
 
 
@@ -31,7 +30,6 @@
         self.steps = width // self.pack
         self.groups = self.each // self.pack
         self.lanes = round_up(self.pack * height, LANES)
-        self.slots = round_up(width, SUBLANES)
         self.direct = self.each % 8 == 0 and self.lanes == LANES
 
 
@@ -55,7 +53,17 @@
     )
 
 
-def produce(s, pair, length, gain, left_gate, left_value, right_gate, right_value, message):
+def produce(s, length, *refs):
+    sources, message, held, arrived = refs[:6], refs[6], refs[7:13], refs[13]
+    copies = [
+        pltpu.make_async_copy(source, target, arrived.at[at])
+        for at, (source, target) in enumerate(zip(sources, held))
+    ]
+    for copy in copies:
+        copy.start()
+    pair, gain, left_gate, left_value, right_gate, right_value = held
+    for copy in copies:
+        copy.wait()
     first = lax.axis_index("row") * s.height
     second = lax.axis_index("col") * s.width
     limit = length[0]
@@ -105,7 +113,7 @@
     scale[...] = total
 
 
-def multiply(s, received, message, wide, square):
+def multiply(s, received, message, wide, square, stage):
     span = s.steps * 2 * s.each
     if s.direct:
         for peer in range(s.peers):
@@ -143,40 +151,45 @@
         else:
             sums = swap_blocks(*sums, s.height)
         for row in range(s.rows):
-            square[row] = sums[row]
-        for row in range(s.rows):
-            for col in range(s.cols):
-                start = col * s.width
-                if s.pack == 1:
-                    start = start // s.height * s.lanes + start % s.height
-                message[row * s.cols + col, group] = square[row, start : start + s.slots].astype(BF16)
+            square[group, row] = sums[row]
+    for row in range(s.rows):
+        for col in range(s.cols):
+            peer = row * s.cols + col
+            start = col * s.width
+            if s.pack == 1:
+                start = start // s.height * s.lanes + start % s.height
+            for group in range(s.groups):
+                stage[peer, group * s.width : (group + 1) * s.width] = (
+                    square[group, row, start : start + s.width]
+                )
+            message[peer] = stage[peer].astype(BF16)
 
 
 def finish(s, received, gating, weight, scale, update, wide):
     count = s.hidden // s.pack
-    values = received[...].reshape(count, s.slots, s.lanes).astype(F32)
-
-    def fold(total):
-        if s.pack == 1:
-            return total
-        low = lax.broadcasted_iota(jnp.int32, total.shape, 1) < s.height
-        up = pltpu.roll(total, s.height, 1)
-        down = pltpu.roll(total, s.lanes - s.height, 1)
-        return total + jnp.where(low, down, up)
-
-    average = fold(jnp.sum(values, 0)) * (1.0 / s.hidden)
-    centered = values - average[None]
-    variance = fold(jnp.sum(centered * centered, 0)) * (1.0 / s.hidden)
-    settled = centered * lax.rsqrt(variance + EPS)[None]
-    settled = settled.reshape(count * s.slots, s.lanes)
-    for tile in range(s.lanes // LANES):
-        wide[tile] = settled[:, tile * LANES : (tile + 1) * LANES]
+    tiles = s.lanes // LANES
+    for peer in range(s.peers):
+        rows = received[peer].astype(F32)
+        for tile in range(tiles):
+            wide[tile, peer * rows.shape[0] : (peer + 1) * rows.shape[0]] = (
+                rows[:, tile * LANES : (tile + 1) * LANES]
+            )
+
+    def average(values):
+        total = jnp.sum(values, 0, keepdims=True)
+        if s.pack > 1:
+            low = lax.broadcasted_iota(jnp.int32, total.shape, 1) < s.height
+            up = pltpu.roll(total, s.height, 1)
+            down = pltpu.roll(total, s.lanes - s.height, 1)
+            total = total + jnp.where(low, down, up)
+        return total * (1.0 / s.hidden)
+
     for at in range(s.width):
-        rows = [
-            wide[tile, pl.ds(at, count, stride=s.slots), :] for tile in range(s.lanes // LANES)
-        ]
-        rows = (jnp.concatenate(rows, 1) * scale[...]).astype(BF16)
-        out = jnp.dot(rows.T, weight[...], preferred_element_type=F32)
+        rows = [wide[tile, pl.ds(at, count, stride=s.width), :] for tile in range(tiles)]
+        rows = jnp.concatenate(rows, 1)
+        rows = rows - average(rows)
+        rows = rows * lax.rsqrt(average(rows * rows) + EPS) * scale[...]
+        out = jnp.dot(rows.astype(BF16).T, weight[...], preferred_element_type=F32)
         total = out[: s.height, : s.channels]
         for block in range(1, s.pack):
             total += out[
@@ -186,9 +199,9 @@
         update[at] = (gating[at] * total).astype(BF16)
 
 
-def call(body, s, out_shape, scratch, flops, *operands):
+def call(body, s, out_shape, scratch, flops, *operands, memory=pltpu.VMEM):
     def space(operand):
-        return pl.BlockSpec(memory_space=pltpu.SMEM if operand.dtype == jnp.int32 else pltpu.VMEM)
+        return pl.BlockSpec(memory_space=pltpu.SMEM if operand.dtype == jnp.int32 else memory)
 
     sent = sum(o.size * o.dtype.itemsize for o in operands)
     return pl.pallas_call(
@@ -197,7 +210,7 @@
         in_specs=[space(o) for o in operands],
         out_specs=jax.tree.map(lambda _: pl.BlockSpec(memory_space=pltpu.VMEM), out_shape),
         scratch_shapes=scratch,
-        compiler_params=pltpu.CompilerParams(vmem_limit_bytes=56 * 1024 * 1024),
+        compiler_params=pltpu.CompilerParams(vmem_limit_bytes=24 * 1024 * 1024),
         cost_estimate=pl.CostEstimate(flops=flops, bytes_accessed=sent, transcendentals=0),
         name=body.__name__,
     )(*operands)
@@ -229,19 +242,17 @@
     cells = height * width
 
     sent = (s.peers, s.steps, 2 * s.each, s.lanes)
+    operands = (pair, gain, left_gate, left_value, right_gate, right_value)
     message = call(
         produce,
         s,
         shape(sent if s.direct else (s.steps, 2 * hidden, s.lanes), BF16),
-        [],
+        [pltpu.VMEM(o.shape, o.dtype) for o in operands]
+        + [pltpu.SemaphoreType.DMA((len(operands),))],
         8 * cells * channels * hidden,
-        pair,
         valid_length,
-        gain,
-        left_gate,
-        left_value,
-        right_gate,
-        right_value,
+        *operands,
+        memory=pltpu.HBM,
     )
     if not s.direct:
         message = message.reshape(s.steps, 2, s.peers, s.each, s.lanes)
@@ -272,8 +283,12 @@
     sums = call(
         multiply,
         s,
-        shape((s.peers, s.groups, s.slots, s.lanes), BF16),
-        [pltpu.VMEM(scratch, F32), pltpu.VMEM((s.rows, side, s.lanes), F32)],
+        shape((s.peers, s.groups * s.width, s.lanes), BF16),
+        [
+            pltpu.VMEM(scratch, F32),
+            pltpu.VMEM((s.groups, s.rows, side, s.lanes), F32),
+            pltpu.VMEM((s.peers, s.groups * s.width, s.lanes), F32),
+        ],
         2 * s.each * (s.rows * height) ** 2 * s.cols * width,
         received,
     )
@@ -281,7 +296,7 @@
         finish,
         s,
         shape((width, height, channels), BF16),
-        [pltpu.VMEM((s.lanes // LANES, hidden // s.pack * s.slots, LANES), F32)],
+        [pltpu.VMEM((s.lanes // LANES, hidden // s.pack * width, LANES), F32)],
         2 * cells * channels * hidden,
         exchange(sums),
         gating,

time: 45.3 us -> 45 us (level)
  Pallas kernels: 9.98 us -> 4.77 us
  local copies, waits for them, and re-layouts: 0.71 us -> 5.24 us
    pallas_call x4, Pallas kernels: 9.98 us -> 4.77 us  [call(): pl.pallas_call(functools.partial(body, s), out_shape=out_shape, in_specs=...]
    unnamed x2 -> x20, local copies, waits for them, and re-layouts: 0.71 us -> 5.24 us
  transfers between devices with their start and end apart: 1 -> 1, of which waited for: 1 -> 1; matrix products, arithmetic and copies ran while one was open for 0% -> 0% of each run, Pallas kernels for 5% -> 1%
where the time goes in v3:
time: 45 us; the launch traced here: 44.5 us
  blocking collectives  21.6 us (48%)
  waiting for transfers between devices  8.45 us (19%)
  local copies, waits for them, and re-layouts  5.24 us (12%)
  Pallas kernels  4.77 us (11%)
  starting transfers between devices  3.66 us (8%)
  between operations  0.72 us (2%)
    all_to_all x1, blocking collectives, exchange(): lax.all_to_all(blocks, ('row', 'col'), split_axis=0, concat_axis=0, tiled...  21.6 us
    all_to_all x1, waiting for transfers between devices, exchange(): lax.all_to_all(blocks, ('row', 'col'), split_axis=0, concat_axis=0, tiled...  8.45 us
    unnamed x20, local copies, waits for them, and re-layouts  5.24 us
    pallas_call x4, Pallas kernels, call(): pl.pallas_call(functools.partial(body, s), out_shape=out_shape, in_specs=...  4.77 us
    all_to_all x1, starting transfers between devices, exchange(): lax.all_to_all(blocks, ('row', 'col'), split_axis=0, concat_axis=0, tiled...  3.66 us
  transfers between devices with their start and end apart: 1, of which 1 were waited for; matrix products, arithmetic and copies ran while one was open for 0% of the time, Pallas kernels for 1%

profile of v3, /device:TPU:0, one launch (start us, length us, event | category | flops | bytes accessed | tf_op | source)
XLA Modules:
  0.0 44.5 jit_solution(14988035664271149031)
XLA Ops:
  0.7 0.0 copy-start.8
  0.7 0.6 %copy-done.8 = f32[128]{0:T(128)S(1)} copy-done((f32[128]{0:T(128)S(1)}, f32[128]{0:T(128)}, u32[]{:S(2)}) %copy-start.8) | copy-done | bytes 536
  1.3 0.0 copy-start
  1.3 0.9 %copy-done = bf16[56,14,128]{2,0,1:T(8,128)(2,1)S(1)} copy-done((bf16[56,14,128]{2,0,1:T(8,128)(2,1)S(1)}, bf16[56,14,128]{2,0,1:T(8,128)(2,1)}, u32[]{:S(2)}) %copy-start) | copy-done | bytes 200728
  2.2 0.0 copy-start.2
  2.2 0.8 %copy-done.2 = bf16[128,128]{1,0:T(8,128)(2,1)S(1)} copy-done((bf16[128,128]{1,0:T(8,128)(2,1)S(1)}, bf16[128,128]{1,0:T(8,128)(2,1)}, u32[]{:S(2)}) %copy-start.2) | copy-done | bytes 32792
  3.0 0.0 copy-start.3
  3.0 0.8 %copy-done.3 = bf16[128,128]{1,0:T(8,128)(2,1)S(1)} copy-done((bf16[128,128]{1,0:T(8,128)(2,1)S(1)}, bf16[128,128]{1,0:T(8,128)(2,1)}, u32[]{:S(2)}) %copy-start.3) | copy-done | bytes 32792
  3.8 0.0 copy-start.4
  3.8 0.8 %copy-done.4 = bf16[128,128]{1,0:T(8,128)(2,1)S(1)} copy-done((bf16[128,128]{1,0:T(8,128)(2,1)S(1)}, bf16[128,128]{1,0:T(8,128)(2,1)}, u32[]{:S(2)}) %copy-start.4) | copy-done | bytes 32792
  4.5 0.0 copy-start.5
  4.5 0.8 %copy-done.5 = bf16[128,128]{1,0:T(8,128)(2,1)S(1)} copy-done((bf16[128,128]{1,0:T(8,128)(2,1)S(1)}, bf16[128,128]{1,0:T(8,128)(2,1)}, u32[]{:S(2)}) %copy-start.5) | copy-done | bytes 32792
  5.3 1.2 %produce.1 = bf16[16,7,16,128]{3,2,1,0:T(8,128)(2,1)S(1)} custom-call(s32[1]{0:T(128)S(6)} %copy.11.length, bf16[14,56,128]{2,1,0:T(8,128)(2,1)S(1)} %bitcast.4, f32[1,128]{1,0:T(1,128)S(1)} %bitcast.6, bf16[128,128]{1,0:T(8,128)(2,1)S(1)} %copy-done.2, bf16[128,128]{1,0:T(8,128)(2,1)S(1)} %copy-done.3, bf16[128,128]{1,0:T(8,128)(2,1)S(1)} %copy-done.4, ...), custom_call_target="tpu_custom_call" | custom-call | flops 102760448 | bytes 332292 | tf_op jit(solution)/shard_map/produce/pallas_call | solution.py:207
  6.5 21.6 %all_to_all.10.received = bf16[16,7,16,128]{3,2,1,0:T(8,128)(2,1)S(1)} all-to-all(bf16[16,7,16,128]{3,2,1,0:T(8,128)(2,1)S(1)} %produce.1), channel_id=1, replica_groups=mesh['parts'=2,'row'=2,'col'=8] {'row','col'}, dimensions={0} | all-to-all | bytes 917504 | tf_op jit(solution)/shard_map/all_to_all | solution.py:220
  28.1 1.7 %multiply.1 = bf16[16,56,128]{2,1,0:T(8,128)(2,1)} custom-call(bf16[16,7,16,128]{3,2,1,0:T(8,128)(2,1)S(1)} %all_to_all.10.received), custom_call_target="tpu_custom_call" | custom-call | flops 22478848 | bytes 458752 | tf_op jit(solution)/shard_map/multiply/pallas_call | solution.py:207
  29.8 0.0 copy-start.1
  29.8 0.0 copy-start.6
  29.8 0.0 copy-start.7
  29.8 3.7 %all-to-all-start.1 = ((bf16[16,56,128]{2,1,0:T(8,128)(2,1)}), bf16[16,56,128]{2,1,0:T(8,128)(2,1)S(1)}, u32[]{:S(2)}, u32[]{:S(2)}) async-start(bf16[16,56,128]{2,1,0:T(8,128)(2,1)} %multiply.1), calls=%async_computation.1 | async-start | bytes 458752 | tf_op jit(solution)/shard_map/all_to_all | solution.py:220
  33.5 0.0 copy-start.9
  33.5 0.0 copy-done.1
  33.5 0.0 copy-done.6
  33.5 0.0 copy-done.7
  33.5 0.6 %copy-done.9 = f32[128]{0:T(128)S(1)} copy-done((f32[128]{0:T(128)S(1)}, f32[128]{0:T(128)}, u32[]{:S(2)}) %copy-start.9) | copy-done | bytes 536
  34.1 0.5 %gate.1 = (f32[14,56,128]{2,1,0:T(8,128)S(1)}, bf16[64,256]{1,0:T(8,128)(2,1)S(1)}, f32[64,128]{1,0:T(8,128)S(1)}) custom-call(bf16[14,56,128]{2,1,0:T(8,128)(2,1)S(1)} %bitcast.5, f32[1,128]{1,0:T(1,128)S(1)} %bitcast.7, bf16[128,128]{1,0:T(8,128)(2,1)S(1)} %copy-done.6, bf16[128,128]{1,0:T(8,128)(2,1)S(1)} %copy-done.7, f32[1,128]{1,0:T(1,128)S(1)} %bitcast.8), custom_call_target="tpu_custom_call" | custom-call | flops 25690112 | bytes 267264 | tf_op jit(solution)/shard_map/gate/pallas_call | solution.py:207
  34.6 8.4 %all-to-all-done.1.received = bf16[16,56,128]{2,1,0:T(8,128)(2,1)S(1)} async-done(((bf16[16,56,128]{2,1,0:T(8,128)(2,1)}), bf16[16,56,128]{2,1,0:T(8,128)(2,1)S(1)}, u32[]{:S(2)}, u32[]{:S(2)}) %all-to-all-start.1) | async-done | bytes 229408 | tf_op jit(solution)/shard_map/all_to_all | solution.py:220
  43.1 1.4 %finish.1 = bf16[14,56,128]{2,1,0:T(8,128)(2,1)} custom-call(bf16[16,56,128]{2,1,0:T(8,128)(2,1)S(1)} %all-to-all-done.1.received, f32[14,56,128]{2,1,0:T(8,128)S(1)} %get-tuple-element.8.gating, bf16[64,256]{1,0:T(8,128)(2,1)S(1)} %get-tuple-element.9.weight, f32[64,128]{1,0:T(8,128)S(1)} %get-tuple-element.10.scale), custom_call_target="tpu_custom_call" | custom-call | flops 25690112 | bytes 696320 | tf_op jit(solution)/shard_map/finish/pallas_call | solution.py:207
Async XLA Ops:
  0.7 0.7 %copy-start.8 = (f32[128]{0:T(128)S(1)}, f32[128]{0:T(128)}, u32[]{:S(2)}) copy-start(f32[128]{0:T(128)} %param.12) | copy-start | bytes 1540
  1.3 0.9 %copy-start = (bf16[56,14,128]{2,0,1:T(8,128)(2,1)S(1)}, bf16[56,14,128]{2,0,1:T(8,128)(2,1)}, u32[]{:S(2)}) copy-start(bf16[56,14,128]{2,0,1:T(8,128)(2,1)} %param.10) | copy-start | bytes 602116
  2.2 0.8 %copy-start.2 = (bf16[128,128]{1,0:T(8,128)(2,1)S(1)}, bf16[128,128]{1,0:T(8,128)(2,1)}, u32[]{:S(2)}) copy-start(bf16[128,128]{1,0:T(8,128)(2,1)} %refs_2_.1) | copy-start | bytes 98308
  3.0 0.8 %copy-start.3 = (bf16[128,128]{1,0:T(8,128)(2,1)S(1)}, bf16[128,128]{1,0:T(8,128)(2,1)}, u32[]{:S(2)}) copy-start(bf16[128,128]{1,0:T(8,128)(2,1)} %refs_3_.1) | copy-start | bytes 98308
  3.8 0.8 %copy-start.4 = (bf16[128,128]{1,0:T(8,128)(2,1)S(1)}, bf16[128,128]{1,0:T(8,128)(2,1)}, u32[]{:S(2)}) copy-start(bf16[128,128]{1,0:T(8,128)(2,1)} %refs_4_.1) | copy-start | bytes 98308
  4.5 0.8 %copy-start.5 = (bf16[128,128]{1,0:T(8,128)(2,1)S(1)}, bf16[128,128]{1,0:T(8,128)(2,1)}, u32[]{:S(2)}) copy-start(bf16[128,128]{1,0:T(8,128)(2,1)} %refs_5_.1) | copy-start | bytes 98308
  29.8 3.7 %copy-start.1 = (bf16[56,14,128]{2,0,1:T(8,128)(2,1)S(1)}, bf16[56,14,128]{2,0,1:T(8,128)(2,1)}, u32[]{:S(2)}) copy-start(bf16[56,14,128]{2,0,1:T(8,128)(2,1)} %param.10) | copy-start | bytes 602116
  29.8 3.7 %copy-start.6 = (bf16[128,128]{1,0:T(8,128)(2,1)S(1)}, bf16[128,128]{1,0:T(8,128)(2,1)}, u32[]{:S(2)}) copy-start(bf16[128,128]{1,0:T(8,128)(2,1)} %out_gate.1) | copy-start | bytes 98308
  29.8 3.7 %copy-start.7 = (bf16[128,128]{1,0:T(8,128)(2,1)S(1)}, bf16[128,128]{1,0:T(8,128)(2,1)}, u32[]{:S(2)}) copy-start(bf16[128,128]{1,0:T(8,128)(2,1)} %out_weight.1) | copy-start | bytes 98308
  29.8 13.3 %all-to-all-start.1 = ((bf16[16,56,128]{2,1,0:T(8,128)(2,1)}), bf16[16,56,128]{2,1,0:T(8,128)(2,1)S(1)}, u32[]{:S(2)}, u32[]{:S(2)}) async-start(bf16[16,56,128]{2,1,0:T(8,128)(2,1)} %multiply.1), calls=%async_computation.1 | async-start | bytes 458752 | tf_op jit(solution)/shard_map/all_to_all | solution.py:220
  33.5 0.7 %copy-start.9 = (f32[128]{0:T(128)S(1)}, f32[128]{0:T(128)}, u32[]{:S(2)}) copy-start(f32[128]{0:T(128)} %param.18) | copy-start | bytes 1540

commit v4 on v3

--- a/solution.py
+++ b/solution.py
@@ -25,12 +25,13 @@
         self.height, self.width = height, width
         self.channels, self.hidden = channels, hidden
         self.each = hidden // self.peers
-        fits = self.rows * height <= LANES
-        self.pack = self.rows if fits and width % self.rows == 0 and self.each % self.rows == 0 else 1
-        self.steps = width // self.pack
+        self.tokens = self.rows * height
+        self.wide = round_up(self.tokens, LANES)
+        fits = self.tokens <= LANES and self.each % self.rows == 0
+        self.pack = self.rows if fits else 1
         self.groups = self.each // self.pack
         self.lanes = round_up(self.pack * height, LANES)
-        self.direct = self.each % 8 == 0 and self.lanes == LANES
+        self.direct = self.each % 8 == 0 and self.wide == LANES
 
 
 def normalise(values):
@@ -53,42 +54,28 @@
     )
 
 
-def produce(s, length, *refs):
-    sources, message, held, arrived = refs[:6], refs[6], refs[7:13], refs[13]
-    copies = [
-        pltpu.make_async_copy(source, target, arrived.at[at])
-        for at, (source, target) in enumerate(zip(sources, held))
-    ]
-    for copy in copies:
-        copy.start()
-    pair, gain, left_gate, left_value, right_gate, right_value = held
-    for copy in copies:
-        copy.wait()
-    first = lax.axis_index("row") * s.height
+def produce(s, pair, length, gain, left_gate, left_value, right_gate, right_value, message, turned):
+    mine = lax.axis_index("row")
     second = lax.axis_index("col") * s.width
     limit = length[0]
-    weights = jnp.concatenate(
-        [w[...].T for w in (left_gate, left_value, right_gate, right_value)], 0
-    )
-    scale = gain[...]
-    lane = lax.broadcasted_iota(jnp.int32, (1, s.lanes), 1)
-    block = lane // s.height
-    token = first + lane - block * s.height
-    for step in range(s.steps):
-        normed = [
-            normalise(pair[at * s.steps + step].astype(F32)) * scale for at in range(s.pack)
-        ]
-        if s.lanes > s.pack * s.height:
-            normed.append(jnp.zeros((s.lanes - s.pack * s.height, s.channels), F32))
-        normed = jnp.concatenate(normed, 0).astype(BF16)
+    split = (s.rows, s.cols, s.each, s.channels)
+    half = s.hidden // s.rows
+    for at, weight in enumerate((left_gate, left_value, right_gate, right_value)):
+        turned[at] = weight[...].astype(F32).T.reshape(split)
+    weights = turned[:, mine].reshape(4 * half, s.channels).astype(BF16)
+    token = lax.broadcasted_iota(jnp.int32, (1, s.wide), 1)
+    for step in range(s.width):
+        normed = normalise(pair[step].astype(F32)) * gain[...]
+        if s.wide > s.tokens:
+            empty = jnp.zeros((s.wide - s.tokens, s.channels), F32)
+            normed = jnp.concatenate([normed, empty], 0)
+        normed = normed.astype(BF16)
         out = lax.dot_general(weights, normed, (((1,), (1,)), ((), ())), preferred_element_type=F32)
-        inner = second + block * s.steps + step
-        mask = ((token < limit) & (inner < limit)).astype(F32)
-        h = s.hidden
-        left = sigmoid(out[:h]) * out[h : 2 * h] * mask
-        right = sigmoid(out[2 * h : 3 * h]) * out[3 * h :] * mask
+        mask = ((token < limit) & (second + step < limit)).astype(F32)
+        left = sigmoid(out[:half]) * out[half : 2 * half] * mask
+        right = sigmoid(out[2 * half : 3 * half]) * out[3 * half :] * mask
         if s.direct:
-            split = (s.peers, s.each, s.lanes)
+            split = (s.cols, s.each, s.wide)
             both = jnp.concatenate([left.reshape(split), right.reshape(split)], 1)
             message[:, step] = both.astype(BF16)
         else:
@@ -114,40 +101,28 @@
 
 
 def multiply(s, received, message, wide, square, stage):
-    span = s.steps * 2 * s.each
+    depth = s.cols * s.width
     if s.direct:
-        for peer in range(s.peers):
+        span = s.width * 2 * s.each
+        for peer in range(s.cols):
             wide[peer * span : (peer + 1) * span] = (
-                received[peer].reshape(span, s.lanes).astype(F32)
+                received[peer].reshape(span, s.wide).astype(F32)
             )
-    depth = s.cols * s.steps
-
-    def operand(side, channel):
-        at = side * s.each + channel
+
+    def operand(at):
         if s.direct:
-            blocks = [
-                wide[pl.ds(row * s.cols * span + at, depth, stride=2 * s.each), :]
-                for row in range(s.rows)
-            ]
-        else:
-            blocks = [received[at, row].astype(F32) for row in range(s.rows)]
-        if s.pack == 1:
-            return jnp.concatenate(blocks, 1).astype(BF16)
-        pad = round_up(depth, 64) - depth
-        blocks = swap_blocks(*blocks, s.height)
-        if pad:
-            empty = jnp.zeros((pad, s.lanes), F32)
-            blocks = [part for block in blocks for part in (block, empty)]
-        return jnp.concatenate(blocks, 0).astype(BF16)
+            return wide[pl.ds(at, depth, stride=2 * s.each), :].astype(BF16)
+        return received[at]
 
     for group in range(s.groups):
         sums = []
         for at in range(s.pack):
             channel = group * s.pack + at
-            left, right = operand(0, channel), operand(1, channel)
+            left, right = operand(channel), operand(s.each + channel)
             sums.append(jnp.dot(right.T, left, preferred_element_type=F32))
         if s.pack == 1:
-            sums = [sums[0][:, row * s.lanes : (row + 1) * s.lanes] for row in range(s.rows)]
+            shifts = [(s.wide - row * s.height) % s.wide for row in range(s.rows)]
+            sums = [(pltpu.roll(sums[0], at, 1) if at else sums[0])[:, : s.lanes] for at in shifts]
         else:
             sums = swap_blocks(*sums, s.height)
         for row in range(s.rows):
@@ -156,8 +131,6 @@
         for col in range(s.cols):
             peer = row * s.cols + col
             start = col * s.width
-            if s.pack == 1:
-                start = start // s.height * s.lanes + start % s.height
             for group in range(s.groups):
                 stage[peer, group * s.width : (group + 1) * s.width] = (
                     square[group, row, start : start + s.width]
@@ -199,9 +172,9 @@
         update[at] = (gating[at] * total).astype(BF16)
 
 
-def call(body, s, out_shape, scratch, flops, *operands, memory=pltpu.VMEM):
+def call(body, s, out_shape, scratch, flops, *operands):
     def space(operand):
-        return pl.BlockSpec(memory_space=pltpu.SMEM if operand.dtype == jnp.int32 else memory)
+        return pl.BlockSpec(memory_space=pltpu.SMEM if operand.dtype == jnp.int32 else pltpu.VMEM)
 
     sent = sum(o.size * o.dtype.itemsize for o in operands)
     return pl.pallas_call(
@@ -216,8 +189,8 @@
     )(*operands)
 
 
-def exchange(blocks):
-    return lax.all_to_all(blocks, ("row", "col"), split_axis=0, concat_axis=0, tiled=True)
+def exchange(blocks, axes):
+    return lax.all_to_all(blocks, axes, split_axis=0, concat_axis=0, tiled=True)
 
 
 def local(
@@ -241,23 +214,26 @@
     gain = input_gain.reshape(1, channels)
     cells = height * width
 
-    sent = (s.peers, s.steps, 2 * s.each, s.lanes)
-    operands = (pair, gain, left_gate, left_value, right_gate, right_value)
+    sent = (s.cols, s.width, 2 * s.each, s.wide)
+    whole = lax.all_gather(pair, "row", axis=1, tiled=True)
     message = call(
         produce,
         s,
-        shape(sent if s.direct else (s.steps, 2 * hidden, s.lanes), BF16),
-        [pltpu.VMEM(o.shape, o.dtype) for o in operands]
-        + [pltpu.SemaphoreType.DMA((len(operands),))],
+        shape(sent if s.direct else (s.width, 2 * s.cols * s.each, s.wide), BF16),
+        [pltpu.VMEM((4, s.rows, s.cols, s.each, channels), F32)],
         8 * cells * channels * hidden,
+        whole,
         valid_length,
-        *operands,
-        memory=pltpu.HBM,
+        gain,
+        left_gate,
+        left_value,
+        right_gate,
+        right_value,
     )
     if not s.direct:
-        message = message.reshape(s.steps, 2, s.peers, s.each, s.lanes)
+        message = message.reshape(s.width, 2, s.cols, s.each, s.wide)
         message = message.transpose(2, 0, 1, 3, 4).reshape(sent)
-    received = exchange(message)
+    received = exchange(message, "col")
     gating, weight, scale = call(
         gate,
         s,
@@ -274,19 +250,17 @@
         out_weight,
         output_gain.reshape(1, hidden),
     )
-    scratch = (s.peers * s.steps * 2 * s.each, s.lanes)
+    scratch = (s.cols * s.width * 2 * s.each, s.wide)
     if not s.direct:
-        received = received.reshape(s.rows, s.cols * s.steps, 2 * s.each, s.lanes)
-        received = received.transpose(2, 0, 1, 3)
-        scratch = (8, s.lanes)
-    side = s.lanes if s.pack > 1 else s.rows * s.lanes
+        received = received.reshape(s.cols * s.width, 2 * s.each, s.wide).transpose(1, 0, 2)
+        scratch = (8, s.wide)
     sums = call(
         multiply,
         s,
         shape((s.peers, s.groups * s.width, s.lanes), BF16),
         [
             pltpu.VMEM(scratch, F32),
-            pltpu.VMEM((s.groups, s.rows, side, s.lanes), F32),
+            pltpu.VMEM((s.groups, s.rows, s.wide, s.lanes), F32),
             pltpu.VMEM((s.peers, s.groups * s.width, s.lanes), F32),
         ],
         2 * s.each * (s.rows * height) ** 2 * s.cols * width,
@@ -298,7 +272,7 @@
         shape((width, height, channels), BF16),
         [pltpu.VMEM((s.lanes // LANES, hidden // s.pack * width, LANES), F32)],
         2 * cells * channels * hidden,
-        exchange(sums),
+        exchange(sums, ("row", "col")),
         gating,
         weight,
         scale,

time: 45 us -> 41.9 us (0.931)
  local copies, waits for them, and re-layouts: 5.24 us -> 1.28 us
  blocking collectives: 21.6 us -> 23 us
  Pallas kernels: 4.77 us -> 4.19 us
    unnamed x20 -> x18, local copies, waits for them, and re-layouts: 5.24 us -> 1.28 us
    all_gather x0 -> x1, blocking collectives: none -> 2.55 us  [local(): whole = lax.all_gather(pair, 'row', axis=1, tiled=True)]
    all_to_all x1, blocking collectives: 21.6 us -> 20.5 us  [exchange(): return lax.all_to_all(blocks, axes, split_axis=0, concat_axis=0, tiled=True)]
    pallas_call x4, Pallas kernels: 4.77 us -> 4.19 us  [call(): pl.pallas_call(functools.partial(body, s), out_shape=out_shape, in_specs=...]
where the time goes in v4:
time: 41.9 us; the launch traced here: 41.5 us
  blocking collectives  23 us (55%)
  waiting for transfers between devices  8.52 us (20%)
  Pallas kernels  4.19 us (10%)
  starting transfers between devices  3.76 us (9%)
  local copies, waits for them, and re-layouts  1.28 us (3%)
  between operations  0.76 us (2%)
    all_to_all x1, blocking collectives, exchange(): return lax.all_to_all(blocks, axes, split_axis=0, concat_axis=0, tiled=True)  20.5 us
    all_to_all x1, waiting for transfers between devices, exchange(): return lax.all_to_all(blocks, axes, split_axis=0, concat_axis=0, tiled=True)  8.52 us
    pallas_call x4, Pallas kernels, call(): pl.pallas_call(functools.partial(body, s), out_shape=out_shape, in_specs=...  4.19 us
    all_to_all x1, starting transfers between devices, exchange(): return lax.all_to_all(blocks, axes, split_axis=0, concat_axis=0, tiled=True)  3.76 us
    all_gather x1, blocking collectives, local(): whole = lax.all_gather(pair, 'row', axis=1, tiled=True)  2.55 us
    unnamed x18, local copies, waits for them, and re-layouts  1.28 us
  transfers between devices with their start and end apart: 1, of which 1 were waited for; matrix products, arithmetic and copies ran while one was open for 0% of the time, Pallas kernels for 1%

profile of v4, /device:TPU:0, one launch (start us, length us, event | category | flops | bytes accessed | tf_op | source)
XLA Modules:
  0.0 41.5 jit_solution(9717108981655202039)
XLA Ops:
  0.7 0.0 copy-start.1
  0.7 0.0 copy-start.2
  0.7 0.0 copy-start.3
  0.7 0.0 copy-start.4
  0.7 2.5 %all_gather.3.pair = bf16[14,112,128]{2,1,0:T(8,128)(2,1)S(1)} all-gather(bf16[14,56,128]{2,1,0:T(8,128)(2,1)} %bitcast.4), channel_id=1, replica_groups=mesh['parts'=2,'row'=2,'col'=8] {'row'}, dimensions={1}, use_global_device_ids=true | all-gather | bytes 602112 | tf_op jit(solution)/shard_map/all_gather | solution.py:218
  3.2 0.0 copy-start.7
  3.2 0.0 copy-done.1
  3.2 0.0 copy-done.2
  3.2 0.0 copy-done.3
  3.3 0.0 copy-done.4
  3.3 0.6 %copy-done.7 = f32[128]{0:T(128)S(1)} copy-done((f32[128]{0:T(128)S(1)}, f32[128]{0:T(128)}, u32[]{:S(2)}) %copy-start.7) | copy-done | bytes 536
  3.9 1.0 %produce.1 = bf16[8,14,16,128]{3,2,1,0:T(8,128)(2,1)S(1)} custom-call(bf16[14,112,128]{2,1,0:T(8,128)(2,1)S(1)} %all_gather.3.pair, s32[1]{0:T(128)S(6)} %copy.11.length, f32[1,128]{1,0:T(1,128)S(1)} %bitcast.6, bf16[128,128]{1,0:T(8,128)(2,1)S(1)} %copy-done.1, bf16[128,128]{1,0:T(8,128)(2,1)S(1)} %copy-done.2, bf16[128,128]{1,0:T(8,128)(2,1)S(1)} %copy-done.3, ...), custom_call_target="tpu_custom_call" | custom-call | flops 102760448 | bytes 532996 | tf_op jit(solution)/shard_map/produce/pallas_call | solution.py:180
  4.9 20.5 %all_to_all.10.received = bf16[8,14,16,128]{3,2,1,0:T(8,128)(2,1)S(1)} all-to-all(bf16[8,14,16,128]{3,2,1,0:T(8,128)(2,1)S(1)} %produce.1), channel_id=1, replica_groups=mesh['parts'=2,'row'=2,'col'=8] {'col'}, dimensions={0} | all-to-all | bytes 917504 | tf_op jit(solution)/shard_map/all_to_all | solution.py:193
  25.4 1.3 %multiply.1 = bf16[16,56,128]{2,1,0:T(8,128)(2,1)} custom-call(bf16[8,14,16,128]{3,2,1,0:T(8,128)(2,1)S(1)} %all_to_all.10.received), custom_call_target="tpu_custom_call" | custom-call | flops 22478848 | bytes 458752 | tf_op jit(solution)/shard_map/multiply/pallas_call | solution.py:180
  26.7 0.0 copy-start
  26.7 0.0 copy-start.5
  26.7 0.0 copy-start.6
  26.7 3.8 %all-to-all-start.1 = ((bf16[16,56,128]{2,1,0:T(8,128)(2,1)}), bf16[16,56,128]{2,1,0:T(8,128)(2,1)S(1)}, u32[]{:S(2)}, u32[]{:S(2)}) async-start(bf16[16,56,128]{2,1,0:T(8,128)(2,1)} %multiply.1), calls=%async_computation.1 | async-start | bytes 458752 | tf_op jit(solution)/shard_map/all_to_all | solution.py:193
  30.5 0.0 copy-start.8
  30.5 0.0 copy-done
  30.5 0.0 copy-done.5
  30.5 0.0 copy-done.6
  30.5 0.6 %copy-done.8 = f32[128]{0:T(128)S(1)} copy-done((f32[128]{0:T(128)S(1)}, f32[128]{0:T(128)}, u32[]{:S(2)}) %copy-start.8) | copy-done | bytes 536
  31.1 0.5 %gate.1 = (f32[14,56,128]{2,1,0:T(8,128)S(1)}, bf16[64,256]{1,0:T(8,128)(2,1)S(1)}, f32[64,128]{1,0:T(8,128)S(1)}) custom-call(bf16[14,56,128]{2,1,0:T(8,128)(2,1)S(1)} %bitcast.5, f32[1,128]{1,0:T(1,128)S(1)} %bitcast.7, bf16[128,128]{1,0:T(8,128)(2,1)S(1)} %copy-done.5, bf16[128,128]{1,0:T(8,128)(2,1)S(1)} %copy-done.6, f32[1,128]{1,0:T(1,128)S(1)} %bitcast.8), custom_call_target="tpu_custom_call" | custom-call | flops 25690112 | bytes 267264 | tf_op jit(solution)/shard_map/gate/pallas_call | solution.py:180
  31.6 8.5 %all-to-all-done.1.received = bf16[16,56,128]{2,1,0:T(8,128)(2,1)S(1)} async-done(((bf16[16,56,128]{2,1,0:T(8,128)(2,1)}), bf16[16,56,128]{2,1,0:T(8,128)(2,1)S(1)}, u32[]{:S(2)}, u32[]{:S(2)}) %all-to-all-start.1) | async-done | bytes 229408 | tf_op jit(solution)/shard_map/all_to_all | solution.py:193
  40.2 1.4 %finish.1 = bf16[14,56,128]{2,1,0:T(8,128)(2,1)} custom-call(bf16[16,56,128]{2,1,0:T(8,128)(2,1)S(1)} %all-to-all-done.1.received, f32[14,56,128]{2,1,0:T(8,128)S(1)} %get-tuple-element.8.gating, bf16[64,256]{1,0:T(8,128)(2,1)S(1)} %get-tuple-element.9.weight, f32[64,128]{1,0:T(8,128)S(1)} %get-tuple-element.10.scale), custom_call_target="tpu_custom_call" | custom-call | flops 25690112 | bytes 696320 | tf_op jit(solution)/shard_map/finish/pallas_call | solution.py:180
Async XLA Ops:
  0.7 2.6 %copy-start.1 = (bf16[128,128]{1,0:T(8,128)(2,1)S(1)}, bf16[128,128]{1,0:T(8,128)(2,1)}, u32[]{:S(2)}) copy-start(bf16[128,128]{1,0:T(8,128)(2,1)} %left_gate.1) | copy-start | bytes 98308
  0.7 2.6 %copy-start.2 = (bf16[128,128]{1,0:T(8,128)(2,1)S(1)}, bf16[128,128]{1,0:T(8,128)(2,1)}, u32[]{:S(2)}) copy-start(bf16[128,128]{1,0:T(8,128)(2,1)} %left_value.1) | copy-start | bytes 98308
  0.7 2.6 %copy-start.3 = (bf16[128,128]{1,0:T(8,128)(2,1)S(1)}, bf16[128,128]{1,0:T(8,128)(2,1)}, u32[]{:S(2)}) copy-start(bf16[128,128]{1,0:T(8,128)(2,1)} %right_gate.1) | copy-start | bytes 98308
  0.7 2.6 %copy-start.4 = (bf16[128,128]{1,0:T(8,128)(2,1)S(1)}, bf16[128,128]{1,0:T(8,128)(2,1)}, u32[]{:S(2)}) copy-start(bf16[128,128]{1,0:T(8,128)(2,1)} %right_value.1) | copy-start | bytes 98308
  3.2 0.7 %copy-start.7 = (f32[128]{0:T(128)S(1)}, f32[128]{0:T(128)}, u32[]{:S(2)}) copy-start(f32[128]{0:T(128)} %param.12) | copy-start | bytes 1540
  26.7 3.8 %copy-start = (bf16[56,14,128]{2,0,1:T(8,128)(2,1)S(1)}, bf16[56,14,128]{2,0,1:T(8,128)(2,1)}, u32[]{:S(2)}) copy-start(bf16[56,14,128]{2,0,1:T(8,128)(2,1)} %param.10) | copy-start | bytes 602116
  26.7 3.8 %copy-start.5 = (bf16[128,128]{1,0:T(8,128)(2,1)S(1)}, bf16[128,128]{1,0:T(8,128)(2,1)}, u32[]{:S(2)}) copy-start(bf16[128,128]{1,0:T(8,128)(2,1)} %out_gate.1) | copy-start | bytes 98308
  26.7 3.8 %copy-start.6 = (bf16[128,128]{1,0:T(8,128)(2,1)S(1)}, bf16[128,128]{1,0:T(8,128)(2,1)}, u32[]{:S(2)}) copy-start(bf16[128,128]{1,0:T(8,128)(2,1)} %out_weight.1) | copy-start | bytes 98308
  26.7 13.5 %all-to-all-start.1 = ((bf16[16,56,128]{2,1,0:T(8,128)(2,1)}), bf16[16,56,128]{2,1,0:T(8,128)(2,1)S(1)}, u32[]{:S(2)}, u32[]{:S(2)}) async-start(bf16[16,56,128]{2,1,0:T(8,128)(2,1)} %multiply.1), calls=%async_computation.1 | async-start | bytes 458752 | tf_op jit(solution)/shard_map/all_to_all | solution.py:193
  30.5 0.7 %copy-start.8 = (f32[128]{0:T(128)S(1)}, f32[128]{0:T(128)}, u32[]{:S(2)}) copy-start(f32[128]{0:T(128)} %param.18) | copy-start | bytes 1540

commit v5 on v0

v5 whole, which is shorter than its diff:
```python
import functools

import jax
import jax.numpy as jnp
from jax import lax
from jax.experimental import pallas as pl
from jax.experimental.pallas import tpu as pltpu
from jax.sharding import PartitionSpec as P

F32 = jnp.float32
BF16 = jnp.bfloat16
EPS = 1e-05
TILE = 16
CHUNK = 56
GROUP = 7


class Sizes:
    def __init__(self, mesh, height, width, channels, hidden):
        self.rows = mesh.shape["row"]
        self.cols = mesh.shape["col"]
        self.height, self.width = height, width
        self.channels, self.hidden = channels, hidden
        self.half = width // 2
        self.slots = -(-width // TILE) * TILE


def column_at(place, cols):
    return jnp.where(place < cols // 2, 2 * place, 2 * (cols - place) - 1)


def place_of(column, cols):
    return jnp.where(column % 2 == 0, column // 2, cols - 1 - column // 2)


def ring(cols):
    return [2 * at if at < cols // 2 else 2 * (cols - at) - 1 for at in range(cols)]


def normalise(values):
    average = jnp.mean(values, -1, keepdims=True)
    centered = values - average
    variance = jnp.mean(centered * centered, -1, keepdims=True)
    return centered * lax.rsqrt(variance + EPS)


def sigmoid(values):
    return 0.5 * jnp.tanh(0.5 * values) + 0.5


def dot(left, right):
    return jnp.dot(left, right, preferred_element_type=F32)


def project(s, sources, gated, length, gain, *refs):
    count = len(sources)
    halves, refs = refs[:count], refs[count:]
    left_gate, left_value, right_gate, right_value, *refs = refs
    if gated:
        out_gate, left, right, gating, rows, picked = refs
    else:
        left, right, rows, picked = refs
    row, col = lax.axis_index("row"), lax.axis_index("col")
    limit = length[0]
    first = row * s.height
    offset = (col % (s.height // s.width)) * s.width
    below = lax.broadcasted_iota(jnp.int32, (s.height, 1), 0) + first < limit
    mine = lax.broadcasted_iota(jnp.int32, (s.slots, 1), 0) + col * s.width < limit
    for index, (distance, start) in enumerate(sources):
        place = (place_of(col, s.cols) + distance + s.cols) % s.cols
        token = column_at(place, s.cols) * s.width + start
        for step in range(s.half):
            at = step * s.height
            rows[at : at + s.height] = normalise(halves[index][step].astype(F32)) * gain[...]
            picked[step * s.slots : (step + 1) * s.slots] = rows[pl.ds(at + offset, s.slots), :]
        span = s.half * s.height
        normed = rows[:span].astype(BF16)
        value = sigmoid(dot(normed, left_gate[...])) * dot(normed, left_value[...])
        for step in range(s.half):
            mask = (below & (token + step < limit)).astype(F32)
            part = value[step * s.height : (step + 1) * s.height] * mask
            left[index * s.half + step] = part.astype(BF16)
        if gated:
            gate = sigmoid(dot(normed, out_gate[...]))
            for step in range(s.half):
                gating[index * s.half + step] = gate[step * s.height : (step + 1) * s.height]
        normed = picked[...].astype(BF16)
        value = sigmoid(dot(normed, right_gate[...])) * dot(normed, right_value[...])
        for step in range(s.half):
            mask = (mine & (token + step < limit)).astype(F32)
            part = value[step * s.slots : (step + 1) * s.slots] * mask
            right[index * s.half + step] = part.astype(BF16)


def accumulate(s, left, right, other, total, partner, fresh):
    row, col = lax.axis_index("row"), lax.axis_index("col")
    owner = col // (s.height // s.width)
    depth = left.shape[0]

    @pl.when(row == owner)
    def _():
        partner[:depth] = right[...].astype(F32)

    @pl.when(row != owner)
    def _():
        partner[:depth] = other[...].astype(F32)

    size = CHUNK if s.height % CHUNK == 0 else s.height
    group = GROUP if s.width % GROUP == 0 else 1

    def chunk(index, carry):
        at = pl.ds(pl.multiple_of(index * size, 8), size)
        for first in range(0, s.width, group):
            members = range(first, first + group)
            if fresh:
                sums = tuple(jnp.zeros((size, s.hidden), F32) for _ in members)
            else:
                sums = tuple(total[j, at] for j in members)

            def step(k, sums):
                value = left[k, at].astype(F32)
                return tuple(
                    so_far + value * partner[k, j : j + 1] for so_far, j in zip(sums, members)
                )

            sums = lax.fori_loop(0, depth, step, sums)
            for so_far, j in zip(sums, members):
                total[j, at] = so_far
        return carry

    lax.fori_loop(0, s.height // size, chunk, 0)


def add_first(s, left, right, other, total, partner):
    accumulate(s, left, right, other, total, partner, True)


def add_more(s, left, right, other, before, total, partner):
    total[...] = before[...]
    accumulate(s, left, right, other, total, partner, False)


def finish(s, left, right, other, before, gating, gain, weight, update, total, partner):
    total[...] = before[...]
    accumulate(s, left, right, other, total, partner, False)
    for at in range(s.width):
        settled = (normalise(total[at]) * gain[...]).astype(BF16)
        update[at] = (gating[at] * dot(settled, weight[...])).astype(BF16)


def call(body, out_shape, scratch, flops, *operands, aliases=None):
    def space(operand):
        return pl.BlockSpec(memory_space=pltpu.SMEM if operand.dtype == jnp.int32 else pltpu.VMEM)

    sent = sum(o.size * o.dtype.itemsize for o in operands)
    return pl.pallas_call(
        body,
        out_shape=out_shape,
        in_specs=[space(o) for o in operands],
        out_specs=jax.tree.map(lambda _: pl.BlockSpec(memory_space=pltpu.VMEM), out_shape),
        scratch_shapes=scratch,
        compiler_params=pltpu.CompilerParams(vmem_limit_bytes=24 * 1024 * 1024),
        cost_estimate=pl.CostEstimate(flops=flops, bytes_accessed=sent, transcendentals=0),
        name=body.func.__name__,
    )(*operands)


def local(
    mesh,
    pair_state,
    valid_length,
    input_gain,
    left_gate,
    left_value,
    right_gate,
    right_value,
    out_gate,
    output_gain,
    out_weight,
):
    height, width, channels = pair_state.shape
    hidden = left_gate.shape[1]
    s = Sizes(mesh, height, width, channels, hidden)
    shape = jax.ShapeDtypeStruct
    pair = jnp.transpose(pair_state, (1, 0, 2))
    gain = input_gain.reshape(1, channels)
    weights = (left_gate, left_value, right_gate, right_value)
    order = ring(s.cols)

    def shift(block, by):
        pairs = [(order[at], order[(at + by) % s.cols]) for at in range(s.cols)]
        return lax.ppermute(block, "col", pairs)

    def swap(block):
        return lax.ppermute(block, "row", [(at, (at + 1) % s.rows) for at in range(s.rows)])

    def run(halves, sources, gated=False):
        depth = len(halves) * s.half
        out = [
            shape((depth, height, hidden), BF16),
            shape((depth, s.slots, hidden), BF16),
        ]
        if gated:
            out.append(shape((width, height, channels), F32))
        left, right, *more = call(
            functools.partial(project, s, sources, gated),
            out,
            [
                pltpu.VMEM((s.half * height + TILE, channels), F32),
                pltpu.VMEM((s.half * s.slots, channels), F32),
            ],
            4 * depth * height * channels * hidden,
            valid_length,
            gain,
            *halves,
            *weights,
            *((out_gate,) if gated else ()),
        )
        return (left, right), more

    low, high = pair[: s.half], pair[s.half :]
    starts = (0, s.half)
    sums = shape((width, height, hidden), F32)

    def add(total, terms):
        left, right = terms
        depth = left.shape[0]
        body, before = (add_first, ()) if total is None else (add_more, (total,))
        return call(
            functools.partial(body, s),
            sums,
            [pltpu.VMEM((depth, s.slots, hidden), F32)],
            16 * depth * height * width * hidden,
            left,
            right,
            swap(right),
            *before,
        )

    blocks, sources, gating = [low, high], [(0, at) for at in starts], None
    travel = [low, high, low, high]
    total = terms = None
    for distance in range(1, s.cols // 2 + 1):
        if distance < s.cols // 2:
            arrived = [shift(block, by) for block, by in zip(travel, (1, 1, -1, -1))]
            after = [(by, at) for by in (-distance, distance) for at in starts]
        else:
            arrived = [shift(travel[0], 1), shift(travel[3], -1)]
            after = [(-distance, 0), (distance, s.half)]
        pending, more = run(blocks, sources, gated=gating is None)
        gating = more[0] if more else gating
        if terms is not None:
            total = add(total, terms)
        terms = pending
        arrived, terms, total = lax.optimization_barrier((arrived, terms, total))
        blocks, sources, travel = arrived, after, arrived
    pending, _ = run(blocks, sources)
    left, right = pending
    other = swap(right)
    total = add(total, terms)
    update = call(
        functools.partial(finish, s),
        shape((width, height, channels), BF16),
        [pltpu.VMEM(sums.shape, F32), pltpu.VMEM((left.shape[0], s.slots, hidden), F32)],
        16 * width * height * width * hidden,
        left,
        right,
        other,
        total,
        gating,
        output_gain.reshape(1, hidden),
        out_weight,
    )
    return jnp.transpose(update, (1, 0, 2))


def solution(mesh):
    return jax.shard_map(
        functools.partial(local, mesh),
        mesh=mesh,
        in_specs=(P(("parts", "row"), "col", None), P("parts")) + (P(),) * 8,
        out_specs=P(("parts", "row"), "col", None),
        check_vma=False,
    )
```

time: 93.2 us -> 40.3 us (0.43)
  waiting for transfers between devices: 40.9 us -> 7.29 us
  local copies, waits for them, and re-layouts: 16.3 us -> 2.25 us
  Pallas kernels: 0 us -> 13.8 us
  between operations: 14.3 us -> 0.87 us
  starting transfers between devices: 7.23 us -> 15.9 us
  matrix products: 8.26 us -> 0 us
  other arithmetic: 3.02 us -> 0 us
  blocking collectives: 2.17 us -> 0 us
    all_gather x1 -> x0, waiting for transfers between devices: 21.2 us -> none  [local(): piece = lax.all_gather(left, 'col', axis=1, tiled=True)]
    all_to_all x1 -> x0, waiting for transfers between devices: 19.7 us -> none  [local(): lax.all_to_all(right_full, 'col', split_axis=0, concat_axis=1, tiled=True)]
    ppermute x0 -> x19, starting transfers between devices: none -> 15.9 us  [the longest x14 15.3 us: shift(): return lax.ppermute(block, 'col', pairs)]
    dynamic_slice x32 -> x0, local copies, waits for them, and re-layouts: 14.9 us -> none  [the longest x16 11.1 us: add_block(): left_part = lax.dynamic_slice_in_dim(piece, offset, width, 1)]
    pallas_call x0 -> x10, Pallas kernels: none -> 13.8 us  [call(): pl.pallas_call(body, out_shape=out_shape, in_specs=[space(o) for o in ope...]
    dot_general x14 -> x0, matrix products: 8.26 us -> none  [the longest x5 4.41 us: project(): jnp.einsum('rjc,ch->rjh', normed, weight, preferred_element_type=jnp.floa...]
    ppermute x0 -> x19, waiting for transfers between devices: none -> 7.29 us  [the longest x14 7.28 us: shift(): return lax.ppermute(block, 'col', pairs)]
    all_to_all x1 -> x0, starting transfers between devices: 7.2 us -> none  [local(): lax.all_to_all(right_full, 'col', split_axis=0, concat_axis=1, tiled=True)]
  transfers between devices with their start and end apart: 2 -> 19, of which waited for: 2 -> 8; matrix products, arithmetic and copies ran while one was open for 2% -> 0% of each run, Pallas kernels for 0% -> 29%
where the time goes in v5:
time: 40.3 us; the launch traced here: 40.1 us
  starting transfers between devices  15.9 us (39%)
  Pallas kernels  13.8 us (34%)
  waiting for transfers between devices  7.29 us (18%)
  local copies, waits for them, and re-layouts  2.25 us (6%)
  between operations  0.87 us (2%)
    ppermute x14, starting transfers between devices, shift(): return lax.ppermute(block, 'col', pairs)  15.3 us
    pallas_call x10, Pallas kernels, call(): pl.pallas_call(body, out_shape=out_shape, in_specs=[space(o) for o in ope...  13.8 us
    ppermute x14, waiting for transfers between devices, shift(): return lax.ppermute(block, 'col', pairs)  7.28 us
    unnamed x16, local copies, waits for them, and re-layouts  1.27 us
    slice x1, local copies, waits for them, and re-layouts, local(): low, high = (pair[:s.half], pair[s.half:])  0.98 us
  transfers between devices with their start and end apart: 19, of which 8 were waited for; matrix products, arithmetic and copies ran while one was open for 0% of the time, Pallas kernels for 29%

profile of v5, /device:TPU:0, one launch (start us, length us, event | category | flops | bytes accessed | tf_op | source)
XLA Modules:
  0.0 40.1 jit_solution(10985018917114786386)
XLA Ops:
  0.0 1.0 %fusion = (bf16[7,56,128]{2,1,0:T(8,128)(2,1)S(1)}, bf16[7,56,128]{2,1,0:T(8,128)(2,1)S(1)}) fusion(bf16[14,56,128]{2,1,0:T(8,128)(2,1)} %bitcast.10), kind=kLoop, calls=%fused_computation | loop fusion | bytes 401408 | tf_op jit(solution)/shard_map/slice | solution.py:221
  1.0 3.1 %collective-permute-start = (bf16[7,56,128]{2,1,0:T(8,128)(2,1)S(1)}, bf16[7,56,128]{2,1,0:T(8,128)(2,1)S(1)}, u32[]{:S(2)}, u32[]{:S(2)}) collective-permute-start(bf16[7,56,128]{2,1,0:T(8,128)(2,1)S(1)} %get-tuple-element.78.refs_0_), channel_id=1, source_target_pairs={{0,2},{2,4},{4,6},{6,7},{7,5},{5,3},{3,1},{1,0},{8,10},{10,12},{12... | collective-permute-start | bytes 301064 | tf_op jit(solution)/shard_map/ppermute | solution.py:192
  4.1 1.6 %collective-permute-start.1 = (bf16[7,56,128]{2,1,0:T(8,128)(2,1)S(1)}, bf16[7,56,128]{2,1,0:T(8,128)(2,1)S(1)}, u32[]{:S(2)}, u32[]{:S(2)}) collective-permute-start(bf16[7,56,128]{2,1,0:T(8,128)(2,1)S(1)} %get-tuple-element.77.refs_1_), channel_id=1, source_target_pairs={{0,2},{2,4},{4,6},{6,7},{7,5},{5,3},{3,1},{1,0},{8,10},{10,12},{12... | collective-permute-start | bytes 301064 | tf_op jit(solution)/shard_map/ppermute | solution.py:192
  6.9 0.6 %copy-done.6 = f32[128]{0:T(128)S(1)} copy-done((f32[128]{0:T(128)S(1)}, f32[128]{0:T(128)}, u32[]{:S(2)}) %copy-start.6) | copy-done | bytes 536
  7.5 0.9 %project.5 = (bf16[14,56,128]{2,1,0:T(8,128)(2,1)S(1)}, bf16[14,16,128]{2,1,0:T(8,128)(2,1)S(1)}, f32[14,56,128]{2,1,0:T(8,128)S(1)}) custom-call(s32[1]{0:T(128)S(6)} %copy.11.length, f32[1,128]{1,0:T(1,128)S(1)} %bitcast.4, bf16[7,56,128]{2,1,0:T(8,128)(2,1)S(1)} %get-tuple-element.78.refs_0_, bf16[7,56,128]{2,1,0:T(8,128)(2,1)S(1)} %get-tuple-element.77.refs_1_, ...), custom_call_target="tpu_custom_call" | custom-call | flops 51380224 | bytes 365060 | tf_op jit(solution)/shard_map/project/pallas_call | solution.py:156
  8.4 0.6 %collective-permute-done.1.refs_1_ = bf16[7,56,128]{2,1,0:T(8,128)(2,1)S(1)} collective-permute-done((bf16[7,56,128]{2,1,0:T(8,128)(2,1)S(1)}, bf16[7,56,128]{2,1,0:T(8,128)(2,1)S(1)}, u32[]{:S(2)}, u32[]{:S(2)}) %collective-permute-start.1) | collective-permute-done | bytes 100384 | tf_op jit(solution)/shard_map/ppermute | solution.py:192
  9.0 1.7 %collective-permute-done.2.refs_2_ = bf16[7,56,128]{2,1,0:T(8,128)(2,1)S(1)} collective-permute-done((bf16[7,56,128]{2,1,0:T(8,128)(2,1)S(1)}, bf16[7,56,128]{2,1,0:T(8,128)(2,1)S(1)}, u32[]{:S(2)}, u32[]{:S(2)}) %collective-permute-start.2) | collective-permute-done | bytes 100384 | tf_op jit(solution)/shard_map/ppermute | solution.py:192
  10.8 1.1 %collective-permute-done.3.refs_3_ = bf16[7,56,128]{2,1,0:T(8,128)(2,1)S(1)} collective-permute-done((bf16[7,56,128]{2,1,0:T(8,128)(2,1)S(1)}, bf16[7,56,128]{2,1,0:T(8,128)(2,1)S(1)}, u32[]{:S(2)}, u32[]{:S(2)}) %collective-permute-start.3) | collective-permute-done | bytes 100384 | tf_op jit(solution)/shard_map/ppermute | solution.py:192
  11.9 1.6 %collective-permute-start.4 = (bf16[7,56,128]{2,1,0:T(8,128)(2,1)S(1)}, bf16[7,56,128]{2,1,0:T(8,128)(2,1)S(1)}, u32[]{:S(2)}, u32[]{:S(2)}) collective-permute-start(bf16[7,56,128]{2,1,0:T(8,128)(2,1)S(1)} %collective-permute-done.refs_0_), channel_id=1, source_target_pairs={{0,2},{2,4},{4,6},{6,7},{7,5},{5,3},{3,1},{1,0},{8,10},{10,12},{12... | collective-permute-start | bytes 301064 | tf_op jit(solution)/shard_map/ppermute | solution.py:192
  13.4 1.5 %collective-permute-start.5 = (bf16[7,56,128]{2,1,0:T(8,128)(2,1)S(1)}, bf16[7,56,128]{2,1,0:T(8,128)(2,1)S(1)}, u32[]{:S(2)}, u32[]{:S(2)}) collective-permute-start(bf16[7,56,128]{2,1,0:T(8,128)(2,1)S(1)} %collective-permute-done.1.refs_1_), channel_id=1, source_target_pairs={{0,2},{2,4},{4,6},{6,7},{7,5},{5,3},{3,1},{1,0},{8,10},{10,12},{12... | collective-permute-start | bytes 301064 | tf_op jit(solution)/shard_map/ppermute | solution.py:192
  15.0 0.5 %collective-permute-start.6 = (bf16[7,56,128]{2,1,0:T(8,128)(2,1)S(1)}, bf16[7,56,128]{2,1,0:T(8,128)(2,1)S(1)}, u32[]{:S(2)}, u32[]{:S(2)}) collective-permute-start(bf16[7,56,128]{2,1,0:T(8,128)(2,1)S(1)} %collective-permute-done.2.refs_2_), channel_id=1, source_target_pairs={{0,1},{2,0},{4,2},{6,4},{7,6},{5,7},{3,5},{1,3},{8,9},{10,8},{12,1... | collective-permute-start | bytes 301064 | tf_op jit(solution)/shard_map/ppermute | solution.py:192
  15.5 0.4 %collective-permute-start.7 = (bf16[7,56,128]{2,1,0:T(8,128)(2,1)S(1)}, bf16[7,56,128]{2,1,0:T(8,128)(2,1)S(1)}, u32[]{:S(2)}, u32[]{:S(2)}) collective-permute-start(bf16[7,56,128]{2,1,0:T(8,128)(2,1)S(1)} %collective-permute-done.3.refs_3_), channel_id=1, source_target_pairs={{0,1},{2,0},{4,2},{6,4},{7,6},{5,7},{3,5},{1,3},{8,9},{10,8},{12,1... | collective-permute-start | bytes 301064 | tf_op jit(solution)/shard_map/ppermute | solution.py:192
  15.9 1.5 %project.6 = (bf16[28,56,128]{2,1,0:T(8,128)(2,1)S(1)}, bf16[28,16,128]{2,1,0:T(8,128)(2,1)S(1)}) custom-call(s32[1]{0:T(128)S(6)} %copy.11.length, f32[1,128]{1,0:T(1,128)S(1)} %bitcast.5, bf16[7,56,128]{2,1,0:T(8,128)(2,1)S(1)} %collective-permute-done.refs_0_, bf16[7,56,128]{2,1,0:T(8,128)(2,1)S(1)} %collective-permute-done.1.refs_1_, ...), custom_call_target="tpu_custom_call" | custom-call | flops 102760448 | bytes 532996 | tf_op jit(solution)/shard_map/project/pallas_call | solution.py:156
  17.4 0.8 %add_first.1.before = f32[14,56,128]{2,1,0:T(8,128)S(1)} custom-call(bf16[14,56,128]{2,1,0:T(8,128)(2,1)S(1)} %get-tuple-element.49.left, bf16[14,16,128]{2,1,0:T(8,128)(2,1)S(1)} %get-tuple-element.50.right, bf16[14,16,128]{2,1,0:T(8,128)(2,1)S(1)} %collective-permute-done.8.other), custom_call_target="tpu_custom_call" | custom-call | flops 22478848 | bytes 315392 | tf_op jit(solution)/shard_map/add_first/pallas_call | solution.py:156
  18.3 1.3 %collective-permute-done.6.refs_2_ = bf16[7,56,128]{2,1,0:T(8,128)(2,1)S(1)} collective-permute-done((bf16[7,56,128]{2,1,0:T(8,128)(2,1)S(1)}, bf16[7,56,128]{2,1,0:T(8,128)(2,1)S(1)}, u32[]{:S(2)}, u32[]{:S(2)}) %collective-permute-start.6) | collective-permute-done | bytes 100384 | tf_op jit(solution)/shard_map/ppermute | solution.py:192
  19.6 1.1 %collective-permute-done.7.refs_3_ = bf16[7,56,128]{2,1,0:T(8,128)(2,1)S(1)} collective-permute-done((bf16[7,56,128]{2,1,0:T(8,128)(2,1)S(1)}, bf16[7,56,128]{2,1,0:T(8,128)(2,1)S(1)}, u32[]{:S(2)}, u32[]{:S(2)}) %collective-permute-start.7) | collective-permute-done | bytes 100384 | tf_op jit(solution)/shard_map/ppermute | solution.py:192
  20.7 1.0 %collective-permute-start.10 = (bf16[7,56,128]{2,1,0:T(8,128)(2,1)S(1)}, bf16[7,56,128]{2,1,0:T(8,128)(2,1)S(1)}, u32[]{:S(2)}, u32[]{:S(2)}) collective-permute-start(bf16[7,56,128]{2,1,0:T(8,128)(2,1)S(1)} %collective-permute-done.5.refs_1_), channel_id=1, source_target_pairs={{0,2},{2,4},{4,6},{6,7},{7,5},{5,3},{3,1},{1,0},{8,10},{10,12},{12... | collective-permute-start | bytes 301064 | tf_op jit(solution)/shard_map/ppermute | solution.py:192
  21.6 1.1 %collective-permute-start.11 = (bf16[7,56,128]{2,1,0:T(8,128)(2,1)S(1)}, bf16[7,56,128]{2,1,0:T(8,128)(2,1)S(1)}, u32[]{:S(2)}, u32[]{:S(2)}) collective-permute-start(bf16[7,56,128]{2,1,0:T(8,128)(2,1)S(1)} %collective-permute-done.6.refs_2_), channel_id=1, source_target_pairs={{0,1},{2,0},{4,2},{6,4},{7,6},{5,7},{3,5},{1,3},{8,9},{10,8},{12,1... | collective-permute-start | bytes 301064 | tf_op jit(solution)/shard_map/ppermute | solution.py:192
  22.7 0.5 %collective-permute-start.12 = (bf16[7,56,128]{2,1,0:T(8,128)(2,1)S(1)}, bf16[7,56,128]{2,1,0:T(8,128)(2,1)S(1)}, u32[]{:S(2)}, u32[]{:S(2)}) collective-permute-start(bf16[7,56,128]{2,1,0:T(8,128)(2,1)S(1)} %collective-permute-done.7.refs_3_), channel_id=1, source_target_pairs={{0,1},{2,0},{4,2},{6,4},{7,6},{5,7},{3,5},{1,3},{8,9},{10,8},{12,1... | collective-permute-start | bytes 301064 | tf_op jit(solution)/shard_map/ppermute | solution.py:192
  23.2 1.5 %collective-permute-start.9 = (bf16[7,56,128]{2,1,0:T(8,128)(2,1)S(1)}, bf16[7,56,128]{2,1,0:T(8,128)(2,1)S(1)}, u32[]{:S(2)}, u32[]{:S(2)}) collective-permute-start(bf16[7,56,128]{2,1,0:T(8,128)(2,1)S(1)} %collective-permute-done.4.refs_0_), channel_id=1, source_target_pairs={{0,2},{2,4},{4,6},{6,7},{7,5},{5,3},{3,1},{1,0},{8,10},{10,12},{12... | collective-permute-start | bytes 301064 | tf_op jit(solution)/shard_map/ppermute | solution.py:192
  24.7 1.5 %project.7 = (bf16[28,56,128]{2,1,0:T(8,128)(2,1)S(1)}, bf16[28,16,128]{2,1,0:T(8,128)(2,1)S(1)}) custom-call(s32[1]{0:T(128)S(6)} %copy.11.length, f32[1,128]{1,0:T(1,128)S(1)} %bitcast.6, bf16[7,56,128]{2,1,0:T(8,128)(2,1)S(1)} %collective-permute-done.4.refs_0_, bf16[7,56,128]{2,1,0:T(8,128)(2,1)S(1)} %collective-permute-done.5.refs_1_, ...), custom_call_target="tpu_custom_call" | custom-call | flops 102760448 | bytes 532996 | tf_op jit(solution)/shard_map/project/pallas_call | solution.py:156
  26.2 1.6 %add_more.3.before = f32[14,56,128]{2,1,0:T(8,128)S(1)} custom-call(bf16[28,56,128]{2,1,0:T(8,128)(2,1)S(1)} %get-tuple-element.57.left, bf16[28,16,128]{2,1,0:T(8,128)(2,1)S(1)} %get-tuple-element.58.right, bf16[28,16,128]{2,1,0:T(8,128)(2,1)S(1)} %collective-permute-done.13.other, f32[14,56,128]{2,1,0:T(8,128)S(1)} %add_first.1.before), custom_call_target="tpu_custom_call" | custom-call | flops 44957696 | bytes 1032192 | tf_op jit(solution)/shard_map/add_more/pallas_call | solution.py:156
  27.8 0.9 %collective-permute-done.12.refs_3_ = bf16[7,56,128]{2,1,0:T(8,128)(2,1)S(1)} collective-permute-done((bf16[7,56,128]{2,1,0:T(8,128)(2,1)S(1)}, bf16[7,56,128]{2,1,0:T(8,128)(2,1)S(1)}, u32[]{:S(2)}, u32[]{:S(2)}) %collective-permute-start.12) | collective-permute-done | bytes 100384 | tf_op jit(solution)/shard_map/ppermute | solution.py:192
  28.8 0.7 %collective-permute-start.14 = (bf16[7,56,128]{2,1,0:T(8,128)(2,1)S(1)}, bf16[7,56,128]{2,1,0:T(8,128)(2,1)S(1)}, u32[]{:S(2)}, u32[]{:S(2)}) collective-permute-start(bf16[7,56,128]{2,1,0:T(8,128)(2,1)S(1)} %collective-permute-done.9.refs_0_), channel_id=1, source_target_pairs={{0,2},{2,4},{4,6},{6,7},{7,5},{5,3},{3,1},{1,0},{8,10},{10,12},{12... | collective-permute-start | bytes 301064 | tf_op jit(solution)/shard_map/ppermute | solution.py:192
  29.4 1.4 %collective-permute-start.15 = (bf16[7,56,128]{2,1,0:T(8,128)(2,1)S(1)}, bf16[7,56,128]{2,1,0:T(8,128)(2,1)S(1)}, u32[]{:S(2)}, u32[]{:S(2)}) collective-permute-start(bf16[7,56,128]{2,1,0:T(8,128)(2,1)S(1)} %collective-permute-done.12.refs_3_), channel_id=1, source_target_pairs={{0,1},{2,0},{4,2},{6,4},{7,6},{5,7},{3,5},{1,3},{8,9},{10,8},{12,1... | collective-permute-start | bytes 301064 | tf_op jit(solution)/shard_map/ppermute | solution.py:192
  30.8 1.5 %project.8 = (bf16[28,56,128]{2,1,0:T(8,128)(2,1)S(1)}, bf16[28,16,128]{2,1,0:T(8,128)(2,1)S(1)}) custom-call(s32[1]{0:T(128)S(6)} %copy.11.length, f32[1,128]{1,0:T(1,128)S(1)} %bitcast.7, bf16[7,56,128]{2,1,0:T(8,128)(2,1)S(1)} %collective-permute-done.9.refs_0_, bf16[7,56,128]{2,1,0:T(8,128)(2,1)S(1)} %collective-permute-done.10.refs_1_, ...), custom_call_target="tpu_custom_call" | custom-call | flops 102760448 | bytes 532996 | tf_op jit(solution)/shard_map/project/pallas_call | solution.py:156
  32.3 1.6 %add_more.4.before = f32[14,56,128]{2,1,0:T(8,128)S(1)} custom-call(bf16[28,56,128]{2,1,0:T(8,128)(2,1)S(1)} %get-tuple-element.66.left, bf16[28,16,128]{2,1,0:T(8,128)(2,1)S(1)} %get-tuple-element.67.right, bf16[28,16,128]{2,1,0:T(8,128)(2,1)S(1)} %collective-permute-done.16.other, f32[14,56,128]{2,1,0:T(8,128)S(1)} %add_more.3.before), custom_call_target="tpu_custom_call" | custom-call | flops 44957696 | bytes 1032192 | tf_op jit(solution)/shard_map/add_more/pallas_call | solution.py:156
  34.4 0.9 %project.9 = (bf16[14,56,128]{2,1,0:T(8,128)(2,1)S(1)}, bf16[14,16,128]{2,1,0:T(8,128)(2,1)S(1)}) custom-call(s32[1]{0:T(128)S(6)} %copy.11.length, f32[1,128]{1,0:T(1,128)S(1)} %bitcast.8, bf16[7,56,128]{2,1,0:T(8,128)(2,1)S(1)} %collective-permute-done.14.refs_0_, bf16[7,56,128]{2,1,0:T(8,128)(2,1)S(1)} %collective-permute-done.15.refs_1_, ...), custom_call_target="tpu_custom_call" | custom-call | flops 51380224 | bytes 332292 | tf_op jit(solution)/shard_map/project/pallas_call | solution.py:156
  35.3 0.6 %collective-permute-start.17 = (bf16[14,16,128]{2,1,0:T(8,128)(2,1)S(1)}, bf16[14,16,128]{2,1,0:T(8,128)(2,1)S(1)}, u32[]{:S(2)}, u32[]{:S(2)}) collective-permute-start(bf16[14,16,128]{2,1,0:T(8,128)(2,1)S(1)} %get-tuple-element.72.right), channel_id=1, source_target_pairs={{0,8},{8,0},{1,9},{9,1},{2,10},{10,2},{3,11},{11,3},{4,12},{12,4},... | collective-permute-start | bytes 172040 | tf_op jit(solution)/shard_map/ppermute | solution.py:195
  35.9 1.6 %add_more.5.before = f32[14,56,128]{2,1,0:T(8,128)S(1)} custom-call(bf16[28,56,128]{2,1,0:T(8,128)(2,1)S(1)} %get-tuple-element.73.left, bf16[28,16,128]{2,1,0:T(8,128)(2,1)S(1)} %get-tuple-element.74.right, bf16[28,16,128]{2,1,0:T(8,128)(2,1)S(1)} %collective-permute-done.18.other, f32[14,56,128]{2,1,0:T(8,128)S(1)} %add_more.4.before), custom_call_target="tpu_custom_call" | custom-call | flops 44957696 | bytes 1032192 | tf_op jit(solution)/shard_map/add_more/pallas_call | solution.py:156
  37.5 0.6 %copy-done.7 = f32[128]{0:T(128)S(1)} copy-done((f32[128]{0:T(128)S(1)}, f32[128]{0:T(128)}, u32[]{:S(2)}) %copy-start.7) | copy-done | bytes 536
  38.1 2.0 %finish.1 = bf16[14,56,128]{2,1,0:T(8,128)(2,1)} custom-call(bf16[14,56,128]{2,1,0:T(8,128)(2,1)S(1)} %get-tuple-element.71.left, bf16[14,16,128]{2,1,0:T(8,128)(2,1)S(1)} %get-tuple-element.72.right, bf16[14,16,128]{2,1,0:T(8,128)(2,1)S(1)} %collective-permute-done.17.other, f32[14,56,128]{2,1,0:T(8,128)S(1)} %add_more.5.before, ...), custom_call_target="tpu_custom_call" | custom-call | flops 22478848 | bytes 1151488 | tf_op jit(solution)/shard_map/finish/pallas_call | solution.py:156
  (33 shorter events, 1.1 us)
Async XLA Ops:
  0.0 6.8 %copy-start = (bf16[128,128]{1,0:T(8,128)(2,1)S(1)}, bf16[128,128]{1,0:T(8,128)(2,1)}, u32[]{:S(2)}) copy-start(bf16[128,128]{1,0:T(8,128)(2,1)} %refs_2_.3) | copy-start | bytes 98308
  0.0 6.8 %copy-start.1 = (bf16[128,128]{1,0:T(8,128)(2,1)S(1)}, bf16[128,128]{1,0:T(8,128)(2,1)}, u32[]{:S(2)}) copy-start(bf16[128,128]{1,0:T(8,128)(2,1)} %refs_3_.3) | copy-start | bytes 98308
  0.0 6.9 %copy-start.2 = (bf16[128,128]{1,0:T(8,128)(2,1)S(1)}, bf16[128,128]{1,0:T(8,128)(2,1)}, u32[]{:S(2)}) copy-start(bf16[128,128]{1,0:T(8,128)(2,1)} %refs_4_.9) | copy-start | bytes 98308
  0.0 6.9 %copy-start.3 = (bf16[128,128]{1,0:T(8,128)(2,1)S(1)}, bf16[128,128]{1,0:T(8,128)(2,1)}, u32[]{:S(2)}) copy-start(bf16[128,128]{1,0:T(8,128)(2,1)} %refs_5_.9) | copy-start | bytes 98308
  0.0 6.9 %copy-start.4 = (bf16[128,128]{1,0:T(8,128)(2,1)S(1)}, bf16[128,128]{1,0:T(8,128)(2,1)}, u32[]{:S(2)}) copy-start(bf16[128,128]{1,0:T(8,128)(2,1)} %refs_6_.4) | copy-start | bytes 98308
  1.0 7.4 %collective-permute-start = (bf16[7,56,128]{2,1,0:T(8,128)(2,1)S(1)}, bf16[7,56,128]{2,1,0:T(8,128)(2,1)S(1)}, u32[]{:S(2)}, u32[]{:S(2)}) collective-permute-start(bf16[7,56,128]{2,1,0:T(8,128)(2,1)S(1)} %get-tuple-element.78.refs_0_), channel_id=1, source_target_pairs={{0,2},{2,4},{4,6},{6,7},{7,5},{5,3},{3,1},{1,0},{8,10},{10,12},{12... | collective-permute-start | bytes 301064 | tf_op jit(solution)/shard_map/ppermute | solution.py:192
  4.1 4.9 %collective-permute-start.1 = (bf16[7,56,128]{2,1,0:T(8,128)(2,1)S(1)}, bf16[7,56,128]{2,1,0:T(8,128)(2,1)S(1)}, u32[]{:S(2)}, u32[]{:S(2)}) collective-permute-start(bf16[7,56,128]{2,1,0:T(8,128)(2,1)S(1)} %get-tuple-element.77.refs_1_), channel_id=1, source_target_pairs={{0,2},{2,4},{4,6},{6,7},{7,5},{5,3},{3,1},{1,0},{8,10},{10,12},{12... | collective-permute-start | bytes 301064 | tf_op jit(solution)/shard_map/ppermute | solution.py:192
  5.7 5.1 %collective-permute-start.2 = (bf16[7,56,128]{2,1,0:T(8,128)(2,1)S(1)}, bf16[7,56,128]{2,1,0:T(8,128)(2,1)S(1)}, u32[]{:S(2)}, u32[]{:S(2)}) collective-permute-start(bf16[7,56,128]{2,1,0:T(8,128)(2,1)S(1)} %get-tuple-element.78.refs_0_), channel_id=1, source_target_pairs={{0,1},{2,0},{4,2},{6,4},{7,6},{5,7},{3,5},{1,3},{8,9},{10,8},{12,1... | collective-permute-start | bytes 301064 | tf_op jit(solution)/shard_map/ppermute | solution.py:192
  6.1 5.7 %collective-permute-start.3 = (bf16[7,56,128]{2,1,0:T(8,128)(2,1)S(1)}, bf16[7,56,128]{2,1,0:T(8,128)(2,1)S(1)}, u32[]{:S(2)}, u32[]{:S(2)}) collective-permute-start(bf16[7,56,128]{2,1,0:T(8,128)(2,1)S(1)} %get-tuple-element.77.refs_1_), channel_id=1, source_target_pairs={{0,1},{2,0},{4,2},{6,4},{7,6},{5,7},{3,5},{1,3},{8,9},{10,8},{12,1... | collective-permute-start | bytes 301064 | tf_op jit(solution)/shard_map/ppermute | solution.py:192
  6.8 0.7 %copy-start.6 = (f32[128]{0:T(128)S(1)}, f32[128]{0:T(128)}, u32[]{:S(2)}) copy-start(f32[128]{0:T(128)} %param.12) | copy-start | bytes 1540
  11.9 6.4 %collective-permute-start.4 = (bf16[7,56,128]{2,1,0:T(8,128)(2,1)S(1)}, bf16[7,56,128]{2,1,0:T(8,128)(2,1)S(1)}, u32[]{:S(2)}, u32[]{:S(2)}) collective-permute-start(bf16[7,56,128]{2,1,0:T(8,128)(2,1)S(1)} %collective-permute-done.refs_0_), channel_id=1, source_target_pairs={{0,2},{2,4},{4,6},{6,7},{7,5},{5,3},{3,1},{1,0},{8,10},{10,12},{12... | collective-permute-start | bytes 301064 | tf_op jit(solution)/shard_map/ppermute | solution.py:192
  13.4 4.8 %collective-permute-start.5 = (bf16[7,56,128]{2,1,0:T(8,128)(2,1)S(1)}, bf16[7,56,128]{2,1,0:T(8,128)(2,1)S(1)}, u32[]{:S(2)}, u32[]{:S(2)}) collective-permute-start(bf16[7,56,128]{2,1,0:T(8,128)(2,1)S(1)} %collective-permute-done.1.refs_1_), channel_id=1, source_target_pairs={{0,2},{2,4},{4,6},{6,7},{7,5},{5,3},{3,1},{1,0},{8,10},{10,12},{12... | collective-permute-start | bytes 301064 | tf_op jit(solution)/shard_map/ppermute | solution.py:192
  15.0 4.6 %collective-permute-start.6 = (bf16[7,56,128]{2,1,0:T(8,128)(2,1)S(1)}, bf16[7,56,128]{2,1,0:T(8,128)(2,1)S(1)}, u32[]{:S(2)}, u32[]{:S(2)}) collective-permute-start(bf16[7,56,128]{2,1,0:T(8,128)(2,1)S(1)} %collective-permute-done.2.refs_2_), channel_id=1, source_target_pairs={{0,1},{2,0},{4,2},{6,4},{7,6},{5,7},{3,5},{1,3},{8,9},{10,8},{12,1... | collective-permute-start | bytes 301064 | tf_op jit(solution)/shard_map/ppermute | solution.py:192
  15.5 5.2 %collective-permute-start.7 = (bf16[7,56,128]{2,1,0:T(8,128)(2,1)S(1)}, bf16[7,56,128]{2,1,0:T(8,128)(2,1)S(1)}, u32[]{:S(2)}, u32[]{:S(2)}) collective-permute-start(bf16[7,56,128]{2,1,0:T(8,128)(2,1)S(1)} %collective-permute-done.3.refs_3_), channel_id=1, source_target_pairs={{0,1},{2,0},{4,2},{6,4},{7,6},{5,7},{3,5},{1,3},{8,9},{10,8},{12,1... | collective-permute-start | bytes 301064 | tf_op jit(solution)/shard_map/ppermute | solution.py:192
  15.9 1.5 %collective-permute-start.8 = (bf16[14,16,128]{2,1,0:T(8,128)(2,1)S(1)}, bf16[14,16,128]{2,1,0:T(8,128)(2,1)S(1)}, u32[]{:S(2)}, u32[]{:S(2)}) collective-permute-start(bf16[14,16,128]{2,1,0:T(8,128)(2,1)S(1)} %get-tuple-element.50.right), channel_id=1, source_target_pairs={{0,8},{8,0},{1,9},{9,1},{2,10},{10,2},{3,11},{11,3},{4,12},{12,4},... | collective-permute-start | bytes 172040 | tf_op jit(solution)/shard_map/ppermute | solution.py:195
  20.7 5.5 %collective-permute-start.13 = (bf16[28,16,128]{2,1,0:T(8,128)(2,1)S(1)}, bf16[28,16,128]{2,1,0:T(8,128)(2,1)S(1)}, u32[]{:S(2)}, u32[]{:S(2)}) collective-permute-start(bf16[28,16,128]{2,1,0:T(8,128)(2,1)S(1)} %get-tuple-element.58.right), channel_id=1, source_target_pairs={{0,8},{8,0},{1,9},{9,1},{2,10},{10,2},{3,11},{11,3},{4,12},{12,4},... | collective-permute-start | bytes 344072 | tf_op jit(solution)/shard_map/ppermute | solution.py:195
  20.7 7.1 %collective-permute-start.10 = (bf16[7,56,128]{2,1,0:T(8,128)(2,1)S(1)}, bf16[7,56,128]{2,1,0:T(8,128)(2,1)S(1)}, u32[]{:S(2)}, u32[]{:S(2)}) collective-permute-start(bf16[7,56,128]{2,1,0:T(8,128)(2,1)S(1)} %collective-permute-done.5.refs_1_), channel_id=1, source_target_pairs={{0,2},{2,4},{4,6},{6,7},{7,5},{5,3},{3,1},{1,0},{8,10},{10,12},{12... | collective-permute-start | bytes 301064 | tf_op jit(solution)/shard_map/ppermute | solution.py:192
  21.6 6.2 %collective-permute-start.11 = (bf16[7,56,128]{2,1,0:T(8,128)(2,1)S(1)}, bf16[7,56,128]{2,1,0:T(8,128)(2,1)S(1)}, u32[]{:S(2)}, u32[]{:S(2)}) collective-permute-start(bf16[7,56,128]{2,1,0:T(8,128)(2,1)S(1)} %collective-permute-done.6.refs_2_), channel_id=1, source_target_pairs={{0,1},{2,0},{4,2},{6,4},{7,6},{5,7},{3,5},{1,3},{8,9},{10,8},{12,1... | collective-permute-start | bytes 301064 | tf_op jit(solution)/shard_map/ppermute | solution.py:192
  22.7 6.0 %collective-permute-start.12 = (bf16[7,56,128]{2,1,0:T(8,128)(2,1)S(1)}, bf16[7,56,128]{2,1,0:T(8,128)(2,1)S(1)}, u32[]{:S(2)}, u32[]{:S(2)}) collective-permute-start(bf16[7,56,128]{2,1,0:T(8,128)(2,1)S(1)} %collective-permute-done.7.refs_3_), channel_id=1, source_target_pairs={{0,1},{2,0},{4,2},{6,4},{7,6},{5,7},{3,5},{1,3},{8,9},{10,8},{12,1... | collective-permute-start | bytes 301064 | tf_op jit(solution)/shard_map/ppermute | solution.py:192
  23.2 5.5 %collective-permute-start.9 = (bf16[7,56,128]{2,1,0:T(8,128)(2,1)S(1)}, bf16[7,56,128]{2,1,0:T(8,128)(2,1)S(1)}, u32[]{:S(2)}, u32[]{:S(2)}) collective-permute-start(bf16[7,56,128]{2,1,0:T(8,128)(2,1)S(1)} %collective-permute-done.4.refs_0_), channel_id=1, source_target_pairs={{0,2},{2,4},{4,6},{6,7},{7,5},{5,3},{3,1},{1,0},{8,10},{10,12},{12... | collective-permute-start | bytes 301064 | tf_op jit(solution)/shard_map/ppermute | solution.py:192
  28.8 3.5 %collective-permute-start.16 = (bf16[28,16,128]{2,1,0:T(8,128)(2,1)S(1)}, bf16[28,16,128]{2,1,0:T(8,128)(2,1)S(1)}, u32[]{:S(2)}, u32[]{:S(2)}) collective-permute-start(bf16[28,16,128]{2,1,0:T(8,128)(2,1)S(1)} %get-tuple-element.67.right), channel_id=1, source_target_pairs={{0,8},{8,0},{1,9},{9,1},{2,10},{10,2},{3,11},{11,3},{4,12},{12,4},... | collective-permute-start | bytes 344072 | tf_op jit(solution)/shard_map/ppermute | solution.py:195
  28.8 5.3 %collective-permute-start.14 = (bf16[7,56,128]{2,1,0:T(8,128)(2,1)S(1)}, bf16[7,56,128]{2,1,0:T(8,128)(2,1)S(1)}, u32[]{:S(2)}, u32[]{:S(2)}) collective-permute-start(bf16[7,56,128]{2,1,0:T(8,128)(2,1)S(1)} %collective-permute-done.9.refs_0_), channel_id=1, source_target_pairs={{0,2},{2,4},{4,6},{6,7},{7,5},{5,3},{3,1},{1,0},{8,10},{10,12},{12... | collective-permute-start | bytes 301064 | tf_op jit(solution)/shard_map/ppermute | solution.py:192
  29.4 5.0 %collective-permute-start.15 = (bf16[7,56,128]{2,1,0:T(8,128)(2,1)S(1)}, bf16[7,56,128]{2,1,0:T(8,128)(2,1)S(1)}, u32[]{:S(2)}, u32[]{:S(2)}) collective-permute-start(bf16[7,56,128]{2,1,0:T(8,128)(2,1)S(1)} %collective-permute-done.12.refs_3_), channel_id=1, source_target_pairs={{0,1},{2,0},{4,2},{6,4},{7,6},{5,7},{3,5},{1,3},{8,9},{10,8},{12,1... | collective-permute-start | bytes 301064 | tf_op jit(solution)/shard_map/ppermute | solution.py:192
  34.4 1.5 %collective-permute-start.18 = (bf16[28,16,128]{2,1,0:T(8,128)(2,1)S(1)}, bf16[28,16,128]{2,1,0:T(8,128)(2,1)S(1)}, u32[]{:S(2)}, u32[]{:S(2)}) collective-permute-start(bf16[28,16,128]{2,1,0:T(8,128)(2,1)S(1)} %get-tuple-element.74.right), channel_id=1, source_target_pairs={{0,8},{8,0},{1,9},{9,1},{2,10},{10,2},{3,11},{11,3},{4,12},{12,4},... | collective-permute-start | bytes 344072 | tf_op jit(solution)/shard_map/ppermute | solution.py:195
  35.3 2.2 %copy-start.5 = (bf16[128,128]{1,0:T(8,128)(2,1)S(1)}, bf16[128,128]{1,0:T(8,128)(2,1)}, u32[]{:S(2)}) copy-start(bf16[128,128]{1,0:T(8,128)(2,1)} %weight.1) | copy-start | bytes 98308
  35.3 2.2 %collective-permute-start.17 = (bf16[14,16,128]{2,1,0:T(8,128)(2,1)S(1)}, bf16[14,16,128]{2,1,0:T(8,128)(2,1)S(1)}, u32[]{:S(2)}, u32[]{:S(2)}) collective-permute-start(bf16[14,16,128]{2,1,0:T(8,128)(2,1)S(1)} %get-tuple-element.72.right), channel_id=1, source_target_pairs={{0,8},{8,0},{1,9},{9,1},{2,10},{10,2},{3,11},{11,3},{4,12},{12,4},... | collective-permute-start | bytes 172040 | tf_op jit(solution)/shard_map/ppermute | solution.py:195
  37.5 0.7 %copy-start.7 = (f32[128]{0:T(128)S(1)}, f32[128]{0:T(128)}, u32[]{:S(2)}) copy-start(f32[128]{0:T(128)} %param.18) | copy-start | bytes 1540

commit v6 on v5

--- a/solution.py
+++ b/solution.py
@@ -53,25 +53,28 @@
 
 
 def project(s, sources, gated, length, gain, *refs):
-    count = len(sources)
-    halves, refs = refs[:count], refs[count:]
+    count = 1 + max(source[0] for source in sources)
+    blocks, refs = refs[:count], refs[count:]
     left_gate, left_value, right_gate, right_value, *refs = refs
     if gated:
-        out_gate, left, right, gating, rows, picked = refs
+        out_gate, *later, left, right, gating = refs[:-4]
+        for source, target in zip(later, refs[-4:-2]):
+            target[...] = source[...]
     else:
-        left, right, rows, picked = refs
+        left, right = refs[:-2]
+    rows, picked = refs[-2:]
     row, col = lax.axis_index("row"), lax.axis_index("col")
     limit = length[0]
     first = row * s.height
     offset = (col % (s.height // s.width)) * s.width
     below = lax.broadcasted_iota(jnp.int32, (s.height, 1), 0) + first < limit
     mine = lax.broadcasted_iota(jnp.int32, (s.slots, 1), 0) + col * s.width < limit
-    for index, (distance, start) in enumerate(sources):
+    for index, (block, inside, distance, start) in enumerate(sources):
         place = (place_of(col, s.cols) + distance + s.cols) % s.cols
         token = column_at(place, s.cols) * s.width + start
         for step in range(s.half):
             at = step * s.height
-            rows[at : at + s.height] = normalise(halves[index][step].astype(F32)) * gain[...]
+            rows[at : at + s.height] = normalise(blocks[block][inside + step].astype(F32)) * gain[...]
             picked[step * s.slots : (step + 1) * s.slots] = rows[pl.ds(at + offset, s.slots), :]
         span = s.half * s.height
         normed = rows[:span].astype(BF16)
@@ -79,7 +82,7 @@
         for step in range(s.half):
             mask = (below & (token + step < limit)).astype(F32)
             part = value[step * s.height : (step + 1) * s.height] * mask
-            left[index * s.half + step] = part.astype(BF16)
+            left[index * s.half + step] = part
         if gated:
             gate = sigmoid(dot(normed, out_gate[...]))
             for step in range(s.half):
@@ -118,7 +121,7 @@
                 sums = tuple(total[j, at] for j in members)
 
             def step(k, sums):
-                value = left[k, at].astype(F32)
+                value = left[k, at]
                 return tuple(
                     so_far + value * partner[k, j : j + 1] for so_far, j in zip(sums, members)
                 )
@@ -148,7 +151,7 @@
         update[at] = (gating[at] * dot(settled, weight[...])).astype(BF16)
 
 
-def call(body, out_shape, scratch, flops, *operands, aliases=None):
+def call(body, out_shape, scratch, flops, *operands, grant=24):
     def space(operand):
         return pl.BlockSpec(memory_space=pltpu.SMEM if operand.dtype == jnp.int32 else pltpu.VMEM)
 
@@ -159,7 +162,7 @@
         in_specs=[space(o) for o in operands],
         out_specs=jax.tree.map(lambda _: pl.BlockSpec(memory_space=pltpu.VMEM), out_shape),
         scratch_shapes=scratch,
-        compiler_params=pltpu.CompilerParams(vmem_limit_bytes=24 * 1024 * 1024),
+        compiler_params=pltpu.CompilerParams(vmem_limit_bytes=grant * 1024 * 1024),
         cost_estimate=pl.CostEstimate(flops=flops, bytes_accessed=sent, transcendentals=0),
         name=body.func.__name__,
     )(*operands)
@@ -194,14 +197,13 @@
     def swap(block):
         return lax.ppermute(block, "row", [(at, (at + 1) % s.rows) for at in range(s.rows)])
 
-    def run(halves, sources, gated=False):
-        depth = len(halves) * s.half
-        out = [
-            shape((depth, height, hidden), BF16),
-            shape((depth, s.slots, hidden), BF16),
-        ]
+    def run(blocks, sources, gated=False):
+        depth = len(sources) * s.half
+        later = (output_gain.reshape(1, hidden), out_weight) if gated else ()
+        out = [shape((depth, height, hidden), F32), shape((depth, s.slots, hidden), BF16)]
         if gated:
-            out.append(shape((width, height, channels), F32))
+            out += [shape((width, height, channels), F32)]
+            out += [shape(o.shape, o.dtype) for o in later]
         left, right, *more = call(
             functools.partial(project, s, sources, gated),
             out,
@@ -212,13 +214,13 @@
             4 * depth * height * channels * hidden,
             valid_length,
             gain,
-            *halves,
+            *blocks,
             *weights,
-            *((out_gate,) if gated else ()),
+            *((out_gate, *later) if gated else ()),
+            grant=56 if gated else 24,
         )
         return (left, right), more
 
-    low, high = pair[: s.half], pair[s.half :]
     starts = (0, s.half)
     sums = shape((width, height, hidden), F32)
 
@@ -237,27 +239,30 @@
             *before,
         )
 
-    blocks, sources, gating = [low, high], [(0, at) for at in starts], None
-    travel = [low, high, low, high]
-    total = terms = None
-    for distance in range(1, s.cols // 2 + 1):
-        if distance < s.cols // 2:
-            arrived = [shift(block, by) for block, by in zip(travel, (1, 1, -1, -1))]
-            after = [(by, at) for by in (-distance, distance) for at in starts]
-        else:
-            arrived = [shift(travel[0], 1), shift(travel[3], -1)]
-            after = [(-distance, 0), (distance, s.half)]
-        pending, more = run(blocks, sources, gated=gating is None)
-        gating = more[0] if more else gating
+    def whole(distances):
+        return [
+            (block, at, distance, at) for block, distance in enumerate(distances) for at in starts
+        ]
+
+    far = s.cols // 2
+    blocks, sources, travel = [pair], whole([0]), [pair, pair]
+    total = terms = kept = None
+    for distance in range(1, far + 1):
+        if distance == far:
+            travel = [travel[0][: s.half], travel[1][s.half :]]
+        arrived = [shift(block, by) for block, by in zip(travel, (1, -1))]
+        pending, more = run(blocks, sources, gated=kept is None)
+        kept = more or kept
         if terms is not None:
             total = add(total, terms)
         terms = pending
-        arrived, terms, total = lax.optimization_barrier((arrived, terms, total))
-        blocks, sources, travel = arrived, after, arrived
-    pending, _ = run(blocks, sources)
-    left, right = pending
+        done = (terms, total)
+        travel = [lax.optimization_barrier((block, done))[0] for block in arrived]
+        blocks, sources = arrived, whole([-distance, distance])
+    left, right = run(travel, [(0, 0, -far, 0), (1, 0, far, s.half)])[0]
     other = swap(right)
     total = add(total, terms)
+    gating, last_gain, last_weight = kept
     update = call(
         functools.partial(finish, s),
         shape((width, height, channels), BF16),
@@ -268,8 +273,8 @@
         other,
         total,
         gating,
-        output_gain.reshape(1, hidden),
-        out_weight,
+        last_gain,
+        last_weight,
     )
     return jnp.transpose(update, (1, 0, 2))
 

time: 40.3 us -> 35.1 us (0.87)
  starting transfers between devices: 15.9 us -> 10 us
  Pallas kernels: 13.8 us -> 15.6 us
  waiting for transfers between devices: 7.29 us -> 5.81 us
    ppermute x14 -> x8, starting transfers between devices: 15.3 us -> 9.31 us  [shift(): return lax.ppermute(block, 'col', pairs)]
    ppermute x14 -> x8, waiting for transfers between devices: 7.28 us -> 4.35 us  [shift(): return lax.ppermute(block, 'col', pairs)]
    pallas_call x10, Pallas kernels: 13.8 us -> 15.6 us  [call(): pl.pallas_call(body, out_shape=out_shape, in_specs=[space(o) for o in ope...]
    ppermute x5, waiting for transfers between devices: 0.01 us -> 1.46 us  [swap(): lax.ppermute(block, 'row', [(at, (at + 1) % s.rows) for at in range(s.row...]
    unnamed x16 -> x20, local copies, waits for them, and re-layouts: 1.27 us -> 2.46 us
    slice x1 -> x2, local copies, waits for them, and re-layouts: 0.98 us -> 0.02 us  [local(): travel = [travel[0][:s.half], travel[1][s.half:]]]
  transfers between devices with their start and end apart: 19 -> 13, of which waited for: 8 -> 4; matrix products, arithmetic and copies ran while one was open for 0% -> 0% of each run, Pallas kernels for 29% -> 39%
where the time goes in v6:
time: 35.1 us; the launch traced here: 34.8 us
  Pallas kernels  15.6 us (44%)
  starting transfers between devices  10 us (28%)
  waiting for transfers between devices  5.81 us (17%)
  local copies, waits for them, and re-layouts  2.47 us (7%)
  between operations  0.87 us (2%)
    pallas_call x10, Pallas kernels, call(): pl.pallas_call(body, out_shape=out_shape, in_specs=[space(o) for o in ope...  15.6 us
    ppermute x8, starting transfers between devices, shift(): return lax.ppermute(block, 'col', pairs)  9.31 us
    ppermute x8, waiting for transfers between devices, shift(): return lax.ppermute(block, 'col', pairs)  4.35 us
    unnamed x20, local copies, waits for them, and re-layouts  2.46 us
    ppermute x5, waiting for transfers between devices, swap(): lax.ppermute(block, 'row', [(at, (at + 1) % s.rows) for at in range(s.row...  1.46 us
    ppermute x5, starting transfers between devices, swap(): lax.ppermute(block, 'row', [(at, (at + 1) % s.rows) for at in range(s.row...  0.72 us
  transfers between devices with their start and end apart: 13, of which 4 were waited for; matrix products, arithmetic and copies ran while one was open for 0% of the time, Pallas kernels for 39%

profile of v6, /device:TPU:0, one launch (start us, length us, event | category | flops | bytes accessed | tf_op | source)
XLA Modules:
  0.0 34.8 jit_solution(3820605782150234334)
XLA Ops:
  0.0 3.0 %collective-permute-start = (bf16[14,56,128]{2,1,0:T(8,128)(2,1)}, bf16[14,56,128]{2,1,0:T(8,128)(2,1)S(1)}, u32[]{:S(2)}, u32[]{:S(2)}) collective-permute-start(bf16[14,56,128]{2,1,0:T(8,128)(2,1)} %bitcast.9), channel_id=1, source_target_pairs={{0,2},{2,4},{4,6},{6,7},{7,5},{5,3},{3,1},{1,0},{8,10},{10,12},{12... | collective-permute-start | bytes 602120 | tf_op jit(solution)/shard_map/ppermute | solution.py:195
  3.7 2.8 %project.5 = (f32[14,56,128]{2,1,0:T(8,128)}, bf16[14,16,128]{2,1,0:T(8,128)(2,1)}, f32[14,56,128]{2,1,0:T(8,128)}, f32[1,128]{1,0:T(1,128)}, bf16[128,128]{1,0:T(8,128)(2,1)}) custom-call(s32[1]{0:T(128)S(6)} %copy.11.length, f32[1,128]{1,0:T(1,128)} %bitcast.4, bf16[14,56,128]{2,1,0:T(8,128)(2,1)} %bitcast.11, bf16[128,128]{1,0:T(8,128)(2,1)} %refs_2_.9, ...), custom_call_target="tpu_custom_call" | custom-call | flops 51380224 | bytes 398340 | tf_op jit(solution)/shard_map/project/pallas_call | solution.py:159
  6.5 1.7 %collective-permute-done.refs_0_ = bf16[14,56,128]{2,1,0:T(8,128)(2,1)S(1)} collective-permute-done((bf16[14,56,128]{2,1,0:T(8,128)(2,1)}, bf16[14,56,128]{2,1,0:T(8,128)(2,1)S(1)}, u32[]{:S(2)}, u32[]{:S(2)}) %collective-permute-start) | collective-permute-done | bytes 200736 | tf_op jit(solution)/shard_map/ppermute | solution.py:195
  8.2 0.0 copy-start.3
  8.2 1.9 %collective-permute-start.1 = (bf16[14,56,128]{2,1,0:T(8,128)(2,1)S(1)}, bf16[14,56,128]{2,1,0:T(8,128)(2,1)S(1)}, u32[]{:S(2)}, u32[]{:S(2)}) collective-permute-start(bf16[14,56,128]{2,1,0:T(8,128)(2,1)S(1)} %collective-permute-done.refs_0_), channel_id=1, source_target_pairs={{0,2},{2,4},{4,6},{6,7},{7,5},{5,3},{3,1},{1,0},{8,10},{10,12},{12... | collective-permute-start | bytes 602120 | tf_op jit(solution)/shard_map/ppermute | solution.py:195
  10.0 0.2 collective-permute-start.5
  10.3 1.4 %collective-permute-done.3.other = bf16[14,16,128]{2,1,0:T(8,128)(2,1)S(1)} collective-permute-done((bf16[14,16,128]{2,1,0:T(8,128)(2,1)}, bf16[14,16,128]{2,1,0:T(8,128)(2,1)S(1)}, u32[]{:S(2)}, u32[]{:S(2)}) %collective-permute-start.3) | collective-permute-done | bytes 57376 | tf_op jit(solution)/shard_map/ppermute | solution.py:198
  11.7 1.0 %copy-done.4 = f32[14,56,128]{2,1,0:T(8,128)S(1)} copy-done((f32[14,56,128]{2,1,0:T(8,128)S(1)}, f32[14,56,128]{2,1,0:T(8,128)}, u32[]{:S(2)}) %copy-start.4) | copy-done | bytes 401432
  12.7 0.8 %copy-done.6 = bf16[14,16,128]{2,1,0:T(8,128)(2,1)S(1)} copy-done((bf16[14,16,128]{2,1,0:T(8,128)(2,1)S(1)}, bf16[14,16,128]{2,1,0:T(8,128)(2,1)}, u32[]{:S(2)}) %copy-start.6) | copy-done | bytes 57368
  13.5 0.8 %add_first.1.before = f32[14,56,128]{2,1,0:T(8,128)S(1)} custom-call(f32[14,56,128]{2,1,0:T(8,128)S(1)} %copy-done.4, bf16[14,16,128]{2,1,0:T(8,128)(2,1)S(1)} %copy-done.6, bf16[14,16,128]{2,1,0:T(8,128)(2,1)S(1)} %collective-permute-done.3.other), custom_call_target="tpu_custom_call" | custom-call | flops 22478848 | bytes 516096 | tf_op jit(solution)/shard_map/add_first/pallas_call | solution.py:159
  14.4 1.5 %project.6 = (f32[28,56,128]{2,1,0:T(8,128)S(1)}, bf16[28,16,128]{2,1,0:T(8,128)(2,1)S(1)}) custom-call(s32[1]{0:T(128)S(6)} %copy.11.length, f32[1,128]{1,0:T(1,128)S(1)} %bitcast.5, bf16[14,56,128]{2,1,0:T(8,128)(2,1)S(1)} %collective-permute-done.refs_0_, bf16[14,56,128]{2,1,0:T(8,128)(2,1)S(1)} %collective-permute-done.2.refs_1_, ...), custom_call_target="tpu_custom_call" | custom-call | flops 102760448 | bytes 532996 | tf_op jit(solution)/shard_map/project/pallas_call | solution.py:159
  15.9 0.0 collective-permute-done.1.refs_0_
  15.9 1.9 %collective-permute-start.4 = (bf16[14,56,128]{2,1,0:T(8,128)(2,1)S(1)}, bf16[14,56,128]{2,1,0:T(8,128)(2,1)S(1)}, u32[]{:S(2)}, u32[]{:S(2)}) collective-permute-start(bf16[14,56,128]{2,1,0:T(8,128)(2,1)S(1)} %collective-permute-done.1.refs_0_), channel_id=1, source_target_pairs={{0,2},{2,4},{4,6},{6,7},{7,5},{5,3},{3,1},{1,0},{8,10},{10,12},{12... | collective-permute-start | bytes 602120 | tf_op jit(solution)/shard_map/ppermute | solution.py:195
  17.8 0.2 collective-permute-start.8
  18.0 0.0 collective-permute-start.6
  18.0 1.5 %project.7 = (f32[28,56,128]{2,1,0:T(8,128)S(1)}, bf16[28,16,128]{2,1,0:T(8,128)(2,1)S(1)}) custom-call(s32[1]{0:T(128)S(6)} %copy.11.length, f32[1,128]{1,0:T(1,128)S(1)} %bitcast.6, bf16[14,56,128]{2,1,0:T(8,128)(2,1)S(1)} %collective-permute-done.1.refs_0_, bf16[14,56,128]{2,1,0:T(8,128)(2,1)S(1)} %collective-permute-done.5.refs_1_, ...), custom_call_target="tpu_custom_call" | custom-call | flops 102760448 | bytes 532996 | tf_op jit(solution)/shard_map/project/pallas_call | solution.py:159
  19.5 0.6 %collective-permute-start.9 = (bf16[28,16,128]{2,1,0:T(8,128)(2,1)S(1)}, bf16[28,16,128]{2,1,0:T(8,128)(2,1)S(1)}, u32[]{:S(2)}, u32[]{:S(2)}) collective-permute-start(bf16[28,16,128]{2,1,0:T(8,128)(2,1)S(1)} %get-tuple-element.34.right), channel_id=1, source_target_pairs={{0,8},{8,0},{1,9},{9,1},{2,10},{10,2},{3,11},{11,3},{4,12},{12,4},... | collective-permute-start | bytes 344072 | tf_op jit(solution)/shard_map/ppermute | solution.py:198
  20.1 1.6 %add_more.3.before = f32[14,56,128]{2,1,0:T(8,128)S(1)} custom-call(f32[28,56,128]{2,1,0:T(8,128)S(1)} %get-tuple-element.29.left, bf16[28,16,128]{2,1,0:T(8,128)(2,1)S(1)} %get-tuple-element.30.right, bf16[28,16,128]{2,1,0:T(8,128)(2,1)S(1)} %collective-permute-done.6.other, f32[14,56,128]{2,1,0:T(8,128)S(1)} %add_first.1.before), custom_call_target="tpu_custom_call" | custom-call | flops 44957696 | bytes 1433600 | tf_op jit(solution)/shard_map/add_more/pallas_call | solution.py:159
  21.7 1.4 %collective-permute-done.4.refs_0_ = bf16[14,56,128]{2,1,0:T(8,128)(2,1)S(1)} collective-permute-done((bf16[14,56,128]{2,1,0:T(8,128)(2,1)S(1)}, bf16[14,56,128]{2,1,0:T(8,128)(2,1)S(1)}, u32[]{:S(2)}, u32[]{:S(2)}) %collective-permute-start.4) | collective-permute-done | bytes 200736 | tf_op jit(solution)/shard_map/ppermute | solution.py:195
  23.0 1.9 %collective-permute-start.7 = (bf16[7,56,128]{2,1,0:T(8,128)(2,1)S(1)}, bf16[7,56,128]{2,1,0:T(8,128)(2,1)S(1)}, u32[]{:S(2)}, u32[]{:S(2)}) collective-permute-start(bf16[7,56,128]{2,1,0:T(8,128)(2,1)S(1)} %slice.6), channel_id=1, source_target_pairs={{0,2},{2,4},{4,6},{6,7},{7,5},{5,3},{3,1},{1,0},{8,10},{10,12},{12... | collective-permute-start | bytes 301064 | tf_op jit(solution)/shard_map/ppermute | solution.py:195
  24.9 0.0 collective-permute-done.8.refs_1_
  24.9 0.3 collective-permute-start.10
  25.2 1.5 %project.8 = (f32[28,56,128]{2,1,0:T(8,128)S(1)}, bf16[28,16,128]{2,1,0:T(8,128)(2,1)S(1)}) custom-call(s32[1]{0:T(128)S(6)} %copy.11.length, f32[1,128]{1,0:T(1,128)S(1)} %bitcast.7, bf16[14,56,128]{2,1,0:T(8,128)(2,1)S(1)} %collective-permute-done.4.refs_0_, bf16[14,56,128]{2,1,0:T(8,128)(2,1)S(1)} %collective-permute-done.8.refs_1_, ...), custom_call_target="tpu_custom_call" | custom-call | flops 102760448 | bytes 532996 | tf_op jit(solution)/shard_map/project/pallas_call | solution.py:159
  26.7 0.1 collective-permute-start.12
  26.8 0.0 collective-permute-done.9.other
  26.8 1.6 %add_more.4.before = f32[14,56,128]{2,1,0:T(8,128)S(1)} custom-call(f32[28,56,128]{2,1,0:T(8,128)S(1)} %get-tuple-element.33.left, bf16[28,16,128]{2,1,0:T(8,128)(2,1)S(1)} %get-tuple-element.34.right, bf16[28,16,128]{2,1,0:T(8,128)(2,1)S(1)} %collective-permute-done.9.other, f32[14,56,128]{2,1,0:T(8,128)S(1)} %add_more.3.before), custom_call_target="tpu_custom_call" | custom-call | flops 44957696 | bytes 1433600 | tf_op jit(solution)/shard_map/add_more/pallas_call | solution.py:159
  28.4 1.2 %collective-permute-done.10.refs_1_ = bf16[7,56,128]{2,1,0:T(8,128)(2,1)S(1)} collective-permute-done((bf16[7,56,128]{2,1,0:T(8,128)(2,1)S(1)}, bf16[7,56,128]{2,1,0:T(8,128)(2,1)S(1)}, u32[]{:S(2)}, u32[]{:S(2)}) %collective-permute-start.10) | collective-permute-done | bytes 100384 | tf_op jit(solution)/shard_map/ppermute | solution.py:195
  29.6 0.9 %project.9 = (f32[14,56,128]{2,1,0:T(8,128)S(1)}, bf16[14,16,128]{2,1,0:T(8,128)(2,1)S(1)}) custom-call(s32[1]{0:T(128)S(6)} %copy.11.length, f32[1,128]{1,0:T(1,128)S(1)} %bitcast.8, bf16[7,56,128]{2,1,0:T(8,128)(2,1)S(1)} %collective-permute-done.7.refs_0_, bf16[7,56,128]{2,1,0:T(8,128)(2,1)S(1)} %collective-permute-done.10.refs_1_, ...), custom_call_target="tpu_custom_call" | custom-call | flops 51380224 | bytes 332292 | tf_op jit(solution)/shard_map/project/pallas_call | solution.py:159
  30.5 0.1 collective-permute-start.11
  30.6 1.6 %add_more.5.before = f32[14,56,128]{2,1,0:T(8,128)S(1)} custom-call(f32[28,56,128]{2,1,0:T(8,128)S(1)} %get-tuple-element.37.left, bf16[28,16,128]{2,1,0:T(8,128)(2,1)S(1)} %get-tuple-element.38.right, bf16[28,16,128]{2,1,0:T(8,128)(2,1)S(1)} %collective-permute-done.12.other, f32[14,56,128]{2,1,0:T(8,128)S(1)} %add_more.4.before), custom_call_target="tpu_custom_call" | custom-call | flops 44957696 | bytes 1433600 | tf_op jit(solution)/shard_map/add_more/pallas_call | solution.py:159
  32.2 0.6 %copy-done.9 = f32[1,128]{1,0:T(1,128)S(1)} copy-done((f32[1,128]{1,0:T(1,128)S(1)}, f32[1,128]{1,0:T(1,128)}, u32[]{:S(2)}) %copy-start.9) | copy-done | bytes 536
  32.8 2.0 %finish.1 = bf16[14,56,128]{2,1,0:T(8,128)(2,1)} custom-call(f32[14,56,128]{2,1,0:T(8,128)S(1)} %get-tuple-element.42.left, bf16[14,16,128]{2,1,0:T(8,128)(2,1)S(1)} %get-tuple-element.43.right, bf16[14,16,128]{2,1,0:T(8,128)(2,1)S(1)} %collective-permute-done.11.other, f32[14,56,128]{2,1,0:T(8,128)S(1)} %add_more.5.before, f32[14,56,128]{2,1,0:T(8,128)S(1)} %copy-done.5, ...), custom_call_target="tpu_custom_call" | custom-call | flops 22478848 | bytes 1352192 | tf_op jit(solution)/shard_map/finish/pallas_call | solution.py:159
  (26 shorter events, 0.1 us)
Async XLA Ops:
  0.0 8.2 %collective-permute-start = (bf16[14,56,128]{2,1,0:T(8,128)(2,1)}, bf16[14,56,128]{2,1,0:T(8,128)(2,1)S(1)}, u32[]{:S(2)}, u32[]{:S(2)}) collective-permute-start(bf16[14,56,128]{2,1,0:T(8,128)(2,1)} %bitcast.9), channel_id=1, source_target_pairs={{0,2},{2,4},{4,6},{6,7},{7,5},{5,3},{3,1},{1,0},{8,10},{10,12},{12... | collective-permute-start | bytes 602120 | tf_op jit(solution)/shard_map/ppermute | solution.py:195
  3.0 7.0 %collective-permute-start.2 = (bf16[14,56,128]{2,1,0:T(8,128)(2,1)}, bf16[14,56,128]{2,1,0:T(8,128)(2,1)S(1)}, u32[]{:S(2)}, u32[]{:S(2)}) collective-permute-start(bf16[14,56,128]{2,1,0:T(8,128)(2,1)} %bitcast.10), channel_id=1, source_target_pairs={{0,1},{2,0},{4,2},{6,4},{7,6},{5,7},{3,5},{1,3},{8,9},{10,8},{12,1... | collective-permute-start | bytes 602120 | tf_op jit(solution)/shard_map/ppermute | solution.py:195
  8.2 6.2 %copy-start.8 = (f32[128]{0:T(128)S(1)}, f32[128]{0:T(128)}, u32[]{:S(2)}) copy-start(f32[128]{0:T(128)} %param.12) | copy-start | bytes 1540
  8.2 6.2 %copy-start = (bf16[128,128]{1,0:T(8,128)(2,1)S(1)}, bf16[128,128]{1,0:T(8,128)(2,1)}, u32[]{:S(2)}) copy-start(bf16[128,128]{1,0:T(8,128)(2,1)} %refs_2_.9) | copy-start | bytes 98308
  8.2 6.2 %copy-start.1 = (bf16[128,128]{1,0:T(8,128)(2,1)S(1)}, bf16[128,128]{1,0:T(8,128)(2,1)}, u32[]{:S(2)}) copy-start(bf16[128,128]{1,0:T(8,128)(2,1)} %refs_3_.9) | copy-start | bytes 98308
  8.2 6.2 %copy-start.2 = (bf16[128,128]{1,0:T(8,128)(2,1)S(1)}, bf16[128,128]{1,0:T(8,128)(2,1)}, u32[]{:S(2)}) copy-start(bf16[128,128]{1,0:T(8,128)(2,1)} %refs_4_.9) | copy-start | bytes 98308
  8.2 6.2 %copy-start.3 = (bf16[128,128]{1,0:T(8,128)(2,1)S(1)}, bf16[128,128]{1,0:T(8,128)(2,1)}, u32[]{:S(2)}) copy-start(bf16[128,128]{1,0:T(8,128)(2,1)} %refs_5_.9) | copy-start | bytes 98308
  8.2 7.7 %collective-permute-start.1 = (bf16[14,56,128]{2,1,0:T(8,128)(2,1)S(1)}, bf16[14,56,128]{2,1,0:T(8,128)(2,1)S(1)}, u32[]{:S(2)}, u32[]{:S(2)}) collective-permute-start(bf16[14,56,128]{2,1,0:T(8,128)(2,1)S(1)} %collective-permute-done.refs_0_), channel_id=1, source_target_pairs={{0,2},{2,4},{4,6},{6,7},{7,5},{5,3},{3,1},{1,0},{8,10},{10,12},{12... | collective-permute-start | bytes 602120 | tf_op jit(solution)/shard_map/ppermute | solution.py:195
  10.0 7.7 %collective-permute-start.5 = (bf16[14,56,128]{2,1,0:T(8,128)(2,1)S(1)}, bf16[14,56,128]{2,1,0:T(8,128)(2,1)S(1)}, u32[]{:S(2)}, u32[]{:S(2)}) collective-permute-start(bf16[14,56,128]{2,1,0:T(8,128)(2,1)S(1)} %collective-permute-done.2.refs_1_), channel_id=1, source_target_pairs={{0,1},{2,0},{4,2},{6,4},{7,6},{5,7},{3,5},{1,3},{8,9},{10,8},{12,1... | collective-permute-start | bytes 602120 | tf_op jit(solution)/shard_map/ppermute | solution.py:195
  10.3 1.5 %collective-permute-start.3 = (bf16[14,16,128]{2,1,0:T(8,128)(2,1)}, bf16[14,16,128]{2,1,0:T(8,128)(2,1)S(1)}, u32[]{:S(2)}, u32[]{:S(2)}) collective-permute-start(bf16[14,16,128]{2,1,0:T(8,128)(2,1)} %get-tuple-element.27.right), channel_id=1, source_target_pairs={{0,8},{8,0},{1,9},{9,1},{2,10},{10,2},{3,11},{11,3},{4,12},{12,4},... | collective-permute-start | bytes 172040 | tf_op jit(solution)/shard_map/ppermute | solution.py:198
  11.7 1.0 %copy-start.4 = (f32[14,56,128]{2,1,0:T(8,128)S(1)}, f32[14,56,128]{2,1,0:T(8,128)}, u32[]{:S(2)}) copy-start(f32[14,56,128]{2,1,0:T(8,128)} %get-tuple-element.26.left) | copy-start | bytes 1204228
  12.7 0.8 %copy-start.6 = (bf16[14,16,128]{2,1,0:T(8,128)(2,1)S(1)}, bf16[14,16,128]{2,1,0:T(8,128)(2,1)}, u32[]{:S(2)}) copy-start(bf16[14,16,128]{2,1,0:T(8,128)(2,1)} %get-tuple-element.27.right) | copy-start | bytes 172036
  15.9 7.1 %collective-permute-start.4 = (bf16[14,56,128]{2,1,0:T(8,128)(2,1)S(1)}, bf16[14,56,128]{2,1,0:T(8,128)(2,1)S(1)}, u32[]{:S(2)}, u32[]{:S(2)}) collective-permute-start(bf16[14,56,128]{2,1,0:T(8,128)(2,1)S(1)} %collective-permute-done.1.refs_0_), channel_id=1, source_target_pairs={{0,2},{2,4},{4,6},{6,7},{7,5},{5,3},{3,1},{1,0},{8,10},{10,12},{12... | collective-permute-start | bytes 602120 | tf_op jit(solution)/shard_map/ppermute | solution.py:195
  17.8 7.1 %collective-permute-start.8 = (bf16[14,56,128]{2,1,0:T(8,128)(2,1)S(1)}, bf16[14,56,128]{2,1,0:T(8,128)(2,1)S(1)}, u32[]{:S(2)}, u32[]{:S(2)}) collective-permute-start(bf16[14,56,128]{2,1,0:T(8,128)(2,1)S(1)} %collective-permute-done.5.refs_1_), channel_id=1, source_target_pairs={{0,1},{2,0},{4,2},{6,4},{7,6},{5,7},{3,5},{1,3},{8,9},{10,8},{12,1... | collective-permute-start | bytes 602120 | tf_op jit(solution)/shard_map/ppermute | solution.py:195
  18.0 2.1 %collective-permute-start.6 = (bf16[28,16,128]{2,1,0:T(8,128)(2,1)S(1)}, bf16[28,16,128]{2,1,0:T(8,128)(2,1)S(1)}, u32[]{:S(2)}, u32[]{:S(2)}) collective-permute-start(bf16[28,16,128]{2,1,0:T(8,128)(2,1)S(1)} %get-tuple-element.30.right), channel_id=1, source_target_pairs={{0,8},{8,0},{1,9},{9,1},{2,10},{10,2},{3,11},{11,3},{4,12},{12,4},... | collective-permute-start | bytes 344072 | tf_op jit(solution)/shard_map/ppermute | solution.py:198
  19.5 7.3 %collective-permute-start.9 = (bf16[28,16,128]{2,1,0:T(8,128)(2,1)S(1)}, bf16[28,16,128]{2,1,0:T(8,128)(2,1)S(1)}, u32[]{:S(2)}, u32[]{:S(2)}) collective-permute-start(bf16[28,16,128]{2,1,0:T(8,128)(2,1)S(1)} %get-tuple-element.34.right), channel_id=1, source_target_pairs={{0,8},{8,0},{1,9},{9,1},{2,10},{10,2},{3,11},{11,3},{4,12},{12,4},... | collective-permute-start | bytes 344072 | tf_op jit(solution)/shard_map/ppermute | solution.py:198
  23.0 5.3 %collective-permute-start.7 = (bf16[7,56,128]{2,1,0:T(8,128)(2,1)S(1)}, bf16[7,56,128]{2,1,0:T(8,128)(2,1)S(1)}, u32[]{:S(2)}, u32[]{:S(2)}) collective-permute-start(bf16[7,56,128]{2,1,0:T(8,128)(2,1)S(1)} %slice.6), channel_id=1, source_target_pairs={{0,2},{2,4},{4,6},{6,7},{7,5},{5,3},{3,1},{1,0},{8,10},{10,12},{12... | collective-permute-start | bytes 301064 | tf_op jit(solution)/shard_map/ppermute | solution.py:195
  24.9 4.7 %collective-permute-start.10 = (bf16[7,56,128]{2,1,0:T(8,128)(2,1)S(1)}, bf16[7,56,128]{2,1,0:T(8,128)(2,1)S(1)}, u32[]{:S(2)}, u32[]{:S(2)}) collective-permute-start(bf16[7,56,128]{2,1,0:T(8,128)(2,1)S(1)} %slice.7), channel_id=1, source_target_pairs={{0,1},{2,0},{4,2},{6,4},{7,6},{5,7},{3,5},{1,3},{8,9},{10,8},{12,1... | collective-permute-start | bytes 301064 | tf_op jit(solution)/shard_map/ppermute | solution.py:195
  26.7 3.9 %collective-permute-start.12 = (bf16[28,16,128]{2,1,0:T(8,128)(2,1)S(1)}, bf16[28,16,128]{2,1,0:T(8,128)(2,1)S(1)}, u32[]{:S(2)}, u32[]{:S(2)}) collective-permute-start(bf16[28,16,128]{2,1,0:T(8,128)(2,1)S(1)} %get-tuple-element.38.right), channel_id=1, source_target_pairs={{0,8},{8,0},{1,9},{9,1},{2,10},{10,2},{3,11},{11,3},{4,12},{12,4},... | collective-permute-start | bytes 344072 | tf_op jit(solution)/shard_map/ppermute | solution.py:198
  30.5 1.7 %copy-start.5 = (f32[14,56,128]{2,1,0:T(8,128)S(1)}, f32[14,56,128]{2,1,0:T(8,128)}, u32[]{:S(2)}) copy-start(f32[14,56,128]{2,1,0:T(8,128)} %get-tuple-element.44.gating) | copy-start | bytes 1204228
  30.5 1.7 %copy-start.7 = (bf16[128,128]{1,0:T(8,128)(2,1)S(1)}, bf16[128,128]{1,0:T(8,128)(2,1)}, u32[]{:S(2)}) copy-start(bf16[128,128]{1,0:T(8,128)(2,1)} %get-tuple-element.46.weight) | copy-start | bytes 98308
  30.5 1.7 %collective-permute-start.11 = (bf16[14,16,128]{2,1,0:T(8,128)(2,1)S(1)}, bf16[14,16,128]{2,1,0:T(8,128)(2,1)S(1)}, u32[]{:S(2)}, u32[]{:S(2)}) collective-permute-start(bf16[14,16,128]{2,1,0:T(8,128)(2,1)S(1)} %get-tuple-element.43.right), channel_id=1, source_target_pairs={{0,8},{8,0},{1,9},{9,1},{2,10},{10,2},{3,11},{11,3},{4,12},{12,4},... | collective-permute-start | bytes 172040 | tf_op jit(solution)/shard_map/ppermute | solution.py:198
  32.2 0.6 %copy-start.9 = (f32[1,128]{1,0:T(1,128)S(1)}, f32[1,128]{1,0:T(1,128)}, u32[]{:S(2)}) copy-start(f32[1,128]{1,0:T(1,128)} %get-tuple-element.45.gain) | copy-start | bytes 1540

commit v7 on v6

--- a/solution.py
+++ b/solution.py
@@ -52,50 +52,48 @@
     return jnp.dot(left, right, preferred_element_type=F32)
 
 
-def project(s, sources, gated, length, gain, *refs):
-    count = 1 + max(source[0] for source in sources)
-    blocks, refs = refs[:count], refs[count:]
-    left_gate, left_value, right_gate, right_value, *refs = refs
-    if gated:
-        out_gate, *later, left, right, gating = refs[:-4]
-        for source, target in zip(later, refs[-4:-2]):
-            target[...] = source[...]
-    else:
-        left, right = refs[:-2]
-    rows, picked = refs[-2:]
+def project(s, sources, length, gain, weight, *refs):
+    *blocks, left, right, rows = refs
     row, col = lax.axis_index("row"), lax.axis_index("col")
     limit = length[0]
-    first = row * s.height
     offset = (col % (s.height // s.width)) * s.width
-    below = lax.broadcasted_iota(jnp.int32, (s.height, 1), 0) + first < limit
+    below = lax.broadcasted_iota(jnp.int32, (s.height, 1), 0) + row * s.height < limit
     mine = lax.broadcasted_iota(jnp.int32, (s.slots, 1), 0) + col * s.width < limit
+    h = s.hidden
     for index, (block, inside, distance, start) in enumerate(sources):
         place = (place_of(col, s.cols) + distance + s.cols) % s.cols
         token = column_at(place, s.cols) * s.width + start
-        for step in range(s.half):
-            at = step * s.height
-            rows[at : at + s.height] = normalise(blocks[block][inside + step].astype(F32)) * gain[...]
-            picked[step * s.slots : (step + 1) * s.slots] = rows[pl.ds(at + offset, s.slots), :]
-        span = s.half * s.height
-        normed = rows[:span].astype(BF16)
-        value = sigmoid(dot(normed, left_gate[...])) * dot(normed, left_value[...])
+        normed = []
+        for step in range(s.half):
+            normed.append(normalise(blocks[block][inside + step].astype(F32)) * gain[...])
+            rows[index, step, : s.height] = normed[-1]
+        out = dot(jnp.concatenate(normed, 0).astype(BF16), weight[:, : 2 * h])
+        value = sigmoid(out[:, :h]) * out[:, h:]
         for step in range(s.half):
             mask = (below & (token + step < limit)).astype(F32)
-            part = value[step * s.height : (step + 1) * s.height] * mask
-            left[index * s.half + step] = part
-        if gated:
-            gate = sigmoid(dot(normed, out_gate[...]))
-            for step in range(s.half):
-                gating[index * s.half + step] = gate[step * s.height : (step + 1) * s.height]
-        normed = picked[...].astype(BF16)
-        value = sigmoid(dot(normed, right_gate[...])) * dot(normed, right_value[...])
+            left[index * s.half + step] = value[step * s.height : (step + 1) * s.height] * mask
+        picked = [rows[index, step, pl.ds(offset, s.slots), :] for step in range(s.half)]
+        out = dot(jnp.concatenate(picked, 0).astype(BF16), weight[:, 2 * h :])
+        value = sigmoid(out[:, :h]) * out[:, h:]
         for step in range(s.half):
             mask = (mine & (token + step < limit)).astype(F32)
             part = value[step * s.slots : (step + 1) * s.slots] * mask
             right[index * s.half + step] = part.astype(BF16)
 
 
-def accumulate(s, left, right, other, total, partner, fresh):
+def gate(s, pair, gain, out_gate, last_gain, last_weight, gating, kept_gain, kept_weight):
+    kept_gain[...] = last_gain[...]
+    kept_weight[...] = last_weight[...]
+    for start in range(0, s.width, s.half):
+        normed = [
+            normalise(pair[start + step].astype(F32)) * gain[...] for step in range(s.half)
+        ]
+        value = sigmoid(dot(jnp.concatenate(normed, 0).astype(BF16), out_gate[...]))
+        for step in range(s.half):
+            gating[start + step] = value[step * s.height : (step + 1) * s.height]
+
+
+def accumulate(s, left, right, other, before, total, partner):
     row, col = lax.axis_index("row"), lax.axis_index("col")
     owner = col // (s.height // s.width)
     depth = left.shape[0]
@@ -115,10 +113,10 @@
         at = pl.ds(pl.multiple_of(index * size, 8), size)
         for first in range(0, s.width, group):
             members = range(first, first + group)
-            if fresh:
+            if before is None:
                 sums = tuple(jnp.zeros((size, s.hidden), F32) for _ in members)
             else:
-                sums = tuple(total[j, at] for j in members)
+                sums = tuple(before[j, at] for j in members)
 
             def step(k, sums):
                 value = left[k, at]
@@ -126,7 +124,7 @@
                     so_far + value * partner[k, j : j + 1] for so_far, j in zip(sums, members)
                 )
 
-            sums = lax.fori_loop(0, depth, step, sums)
+            sums = lax.fori_loop(0, depth, step, sums, unroll=s.half)
             for so_far, j in zip(sums, members):
                 total[j, at] = so_far
         return carry
@@ -135,23 +133,24 @@
 
 
 def add_first(s, left, right, other, total, partner):
-    accumulate(s, left, right, other, total, partner, True)
+    accumulate(s, left, right, other, None, total, partner)
 
 
 def add_more(s, left, right, other, before, total, partner):
-    total[...] = before[...]
-    accumulate(s, left, right, other, total, partner, False)
+    accumulate(s, left, right, other, before, total, partner)
 
 
 def finish(s, left, right, other, before, gating, gain, weight, update, total, partner):
-    total[...] = before[...]
-    accumulate(s, left, right, other, total, partner, False)
-    for at in range(s.width):
-        settled = (normalise(total[at]) * gain[...]).astype(BF16)
-        update[at] = (gating[at] * dot(settled, weight[...])).astype(BF16)
-
-
-def call(body, out_shape, scratch, flops, *operands, grant=24):
+    accumulate(s, left, right, other, before, total, partner)
+    for start in range(0, s.width, s.half):
+        settled = [normalise(total[start + step]) * gain[...] for step in range(s.half)]
+        value = dot(jnp.concatenate(settled, 0).astype(BF16), weight[...])
+        for step in range(s.half):
+            part = gating[start + step] * value[step * s.height : (step + 1) * s.height]
+            update[start + step] = part.astype(BF16)
+
+
+def call(body, out_shape, scratch, flops, *operands):
     def space(operand):
         return pl.BlockSpec(memory_space=pltpu.SMEM if operand.dtype == jnp.int32 else pltpu.VMEM)
 
@@ -162,7 +161,7 @@
         in_specs=[space(o) for o in operands],
         out_specs=jax.tree.map(lambda _: pl.BlockSpec(memory_space=pltpu.VMEM), out_shape),
         scratch_shapes=scratch,
-        compiler_params=pltpu.CompilerParams(vmem_limit_bytes=grant * 1024 * 1024),
+        compiler_params=pltpu.CompilerParams(vmem_limit_bytes=24 * 1024 * 1024),
         cost_estimate=pl.CostEstimate(flops=flops, bytes_accessed=sent, transcendentals=0),
         name=body.func.__name__,
     )(*operands)
@@ -187,7 +186,7 @@
     shape = jax.ShapeDtypeStruct
     pair = jnp.transpose(pair_state, (1, 0, 2))
     gain = input_gain.reshape(1, channels)
-    weights = (left_gate, left_value, right_gate, right_value)
+    weights = jnp.concatenate([left_gate, left_value, right_gate, right_value], 1)
     order = ring(s.cols)
 
     def shift(block, by):
@@ -197,29 +196,18 @@
     def swap(block):
         return lax.ppermute(block, "row", [(at, (at + 1) % s.rows) for at in range(s.rows)])
 
-    def run(blocks, sources, gated=False):
+    def run(blocks, sources):
         depth = len(sources) * s.half
-        later = (output_gain.reshape(1, hidden), out_weight) if gated else ()
-        out = [shape((depth, height, hidden), F32), shape((depth, s.slots, hidden), BF16)]
-        if gated:
-            out += [shape((width, height, channels), F32)]
-            out += [shape(o.shape, o.dtype) for o in later]
-        left, right, *more = call(
-            functools.partial(project, s, sources, gated),
-            out,
-            [
-                pltpu.VMEM((s.half * height + TILE, channels), F32),
-                pltpu.VMEM((s.half * s.slots, channels), F32),
-            ],
+        return call(
+            functools.partial(project, s, sources),
+            [shape((depth, height, hidden), F32), shape((depth, s.slots, hidden), BF16)],
+            [pltpu.VMEM((len(sources), s.half, height + TILE, channels), F32)],
             4 * depth * height * channels * hidden,
             valid_length,
             gain,
+            weights,
             *blocks,
-            *weights,
-            *((out_gate, *later) if gated else ()),
-            grant=56 if gated else 24,
         )
-        return (left, right), more
 
     starts = (0, s.half)
     sums = shape((width, height, hidden), F32)
@@ -251,15 +239,30 @@
         if distance == far:
             travel = [travel[0][: s.half], travel[1][s.half :]]
         arrived = [shift(block, by) for block, by in zip(travel, (1, -1))]
-        pending, more = run(blocks, sources, gated=kept is None)
-        kept = more or kept
+        pending = run(blocks, sources)
+        if distance == 2:
+            kept = call(
+                functools.partial(gate, s),
+                [
+                    shape((width, height, channels), F32),
+                    shape((1, hidden), F32),
+                    shape(out_weight.shape, BF16),
+                ],
+                [],
+                2 * height * width * channels * channels,
+                pair,
+                gain,
+                out_gate,
+                output_gain.reshape(1, hidden),
+                out_weight,
+            )
         if terms is not None:
             total = add(total, terms)
         terms = pending
-        done = (terms, total)
+        done = (terms, total, kept)
         travel = [lax.optimization_barrier((block, done))[0] for block in arrived]
         blocks, sources = arrived, whole([-distance, distance])
-    left, right = run(travel, [(0, 0, -far, 0), (1, 0, far, s.half)])[0]
+    left, right = run(travel, [(0, 0, -far, 0), (1, 0, far, s.half)])
     other = swap(right)
     total = add(total, terms)
     gating, last_gain, last_weight = kept

time: 35.1 us -> 30.7 us (0.87)
  Pallas kernels: 15.6 us -> 9.3 us
  local copies, waits for them, and re-layouts: 2.47 us -> 3.75 us
  waiting for transfers between devices: 5.81 us -> 6.53 us
    pallas_call x10 -> x11, Pallas kernels: 15.6 us -> 9.3 us  [call(): pl.pallas_call(body, out_shape=out_shape, in_specs=[space(o) for o in ope...]
    ppermute x8, waiting for transfers between devices: 4.35 us -> 5.51 us  [shift(): return lax.ppermute(block, 'col', pairs)]
    concatenate x0 -> x1, local copies, waits for them, and re-layouts: none -> 0.77 us  [local(): jnp.concatenate([left_gate, left_value, right_gate, right_value], 1)]
    unnamed x20 -> x13, local copies, waits for them, and re-layouts: 2.46 us -> 2.96 us
    ppermute x5, waiting for transfers between devices: 1.46 us -> 1.01 us  [swap(): lax.ppermute(block, 'row', [(at, (at + 1) % s.rows) for at in range(s.row...]
  transfers between devices with their start and end apart: 13 -> 13, of which waited for: 4 -> 7; matrix products, arithmetic and copies ran while one was open for 0% -> 10% of each run, Pallas kernels for 39% -> 25%
where the time goes in v7:
time: 30.7 us; the launch traced here: 30.3 us
  starting transfers between devices  9.92 us (32%)
  Pallas kernels  9.3 us (30%)
  waiting for transfers between devices  6.53 us (21%)
  local copies, waits for them, and re-layouts  3.75 us (12%)
  between operations  0.79 us (3%)
    pallas_call x11, Pallas kernels, call(): pl.pallas_call(body, out_shape=out_shape, in_specs=[space(o) for o in ope...  9.3 us
    ppermute x8, starting transfers between devices, shift(): return lax.ppermute(block, 'col', pairs)  9.21 us
    ppermute x8, waiting for transfers between devices, shift(): return lax.ppermute(block, 'col', pairs)  5.51 us
    unnamed x13, local copies, waits for them, and re-layouts  2.96 us
    ppermute x5, waiting for transfers between devices, swap(): lax.ppermute(block, 'row', [(at, (at + 1) % s.rows) for at in range(s.row...  1.01 us
    concatenate x1, local copies, waits for them, and re-layouts, local(): jnp.concatenate([left_gate, left_value, right_gate, right_value], 1)  0.77 us
    ppermute x5, starting transfers between devices, swap(): lax.ppermute(block, 'row', [(at, (at + 1) % s.rows) for at in range(s.row...  0.71 us
  transfers between devices with their start and end apart: 13, of which 7 were waited for; matrix products, arithmetic and copies ran while one was open for 10% of the time, Pallas kernels for 25%

profile of v7, /device:TPU:0, one launch (start us, length us, event | category | flops | bytes accessed | tf_op | source)
XLA Modules:
  0.0 30.3 jit_solution(15485334830273414436)
XLA Ops:
  0.0 3.0 %collective-permute-start = (bf16[14,56,128]{2,1,0:T(8,128)(2,1)}, bf16[14,56,128]{2,1,0:T(8,128)(2,1)S(1)}, u32[]{:S(2)}, u32[]{:S(2)}) collective-permute-start(bf16[14,56,128]{2,1,0:T(8,128)(2,1)} %bitcast.4), channel_id=1, source_target_pairs={{0,2},{2,4},{4,6},{6,7},{7,5},{5,3},{3,1},{1,0},{8,10},{10,12},{12... | collective-permute-start | bytes 602120 | tf_op jit(solution)/shard_map/ppermute | solution.py:194
  3.7 0.8 %constant_dynamic-update-slice_fusion.3 = bf16[128,512]{1,0:T(8,128)(2,1)S(1)} fusion(bf16[128,128]{1,0:T(8,128)(2,1)} %param.13), kind=kLoop, calls=%fused_computation.3 | loop fusion | bytes 65536
  4.4 0.8 %constant_dynamic-update-slice_fusion.2 = bf16[128,512]{1,0:T(8,128)(2,1)S(1)} fusion(bf16[128,512]{1,0:T(8,128)(2,1)S(1)} %constant_dynamic-update-slice_fusion.3, bf16[128,128]{1,0:T(8,128)(2,1)} %param.14), kind=kLoop, calls=%fused_computation.2 | loop fusion | bytes 65536
  5.2 0.8 %constant_dynamic-update-slice_fusion.1 = bf16[128,512]{1,0:T(8,128)(2,1)S(1)} fusion(bf16[128,512]{1,0:T(8,128)(2,1)S(1)} %constant_dynamic-update-slice_fusion.2, bf16[128,128]{1,0:T(8,128)(2,1)} %param.15), kind=kLoop, calls=%fused_computation.1 | loop fusion | bytes 65536
  6.0 0.8 %constant_dynamic-update-slice_fusion.weight = bf16[128,512]{1,0:T(8,128)(2,1)S(1)} fusion(bf16[128,512]{1,0:T(8,128)(2,1)S(1)} %constant_dynamic-update-slice_fusion.1, bf16[128,128]{1,0:T(8,128)(2,1)} %param.16), kind=kLoop, calls=%fused_computation | loop fusion | bytes 65536 | tf_op jit(solution)/shard_map/concatenate | solution.py:189
  6.8 0.6 %copy-done.3 = f32[128]{0:T(128)S(1)} copy-done((f32[128]{0:T(128)S(1)}, f32[128]{0:T(128)}, u32[]{:S(2)}) %copy-start.3) | copy-done | bytes 536
  7.4 0.6 %project.5 = (f32[14,56,128]{2,1,0:T(8,128)S(1)}, bf16[14,16,128]{2,1,0:T(8,128)(2,1)S(1)}) custom-call(s32[1]{0:T(128)S(6)} %copy.14.length, f32[1,128]{1,0:T(1,128)S(1)} %bitcast.8, bf16[128,512]{1,0:T(8,128)(2,1)S(1)} %constant_dynamic-update-slice_fusion.weight, bf16[14,56,128]{2,1,0:T(8,128)(2,1)S(1)} %bitcast.6), custom_call_target="tpu_custom_call" | custom-call | flops 51380224 | bytes 332292 | tf_op jit(solution)/shard_map/project/pallas_call | solution.py:158
  8.0 0.2 collective-permute-done.refs_0_
  8.2 1.9 %collective-permute-start.1 = (bf16[14,56,128]{2,1,0:T(8,128)(2,1)S(1)}, bf16[14,56,128]{2,1,0:T(8,128)(2,1)S(1)}, u32[]{:S(2)}, u32[]{:S(2)}) collective-permute-start(bf16[14,56,128]{2,1,0:T(8,128)(2,1)S(1)} %collective-permute-done.refs_0_), channel_id=1, source_target_pairs={{0,2},{2,4},{4,6},{6,7},{7,5},{5,3},{3,1},{1,0},{8,10},{10,12},{12... | collective-permute-start | bytes 602120 | tf_op jit(solution)/shard_map/ppermute | solution.py:194
  10.1 0.2 collective-permute-start.5
  10.3 0.5 %gate.1 = (f32[14,56,128]{2,1,0:T(8,128)S(1)}, f32[1,128]{1,0:T(1,128)S(1)}, bf16[128,128]{1,0:T(8,128)(2,1)S(1)}) custom-call(bf16[14,56,128]{2,1,0:T(8,128)(2,1)S(1)} %bitcast.7, f32[1,128]{1,0:T(1,128)S(1)} %bitcast.9, bf16[128,128]{1,0:T(8,128)(2,1)S(1)} %copy-done.1, f32[1,128]{1,0:T(1,128)S(1)} %bitcast.14, bf16[128,128]{1,0:T(8,128)(2,1)S(1)} %copy-done.2), custom_call_target="tpu_custom_call" | custom-call | flops 25690112 | bytes 267264 | tf_op jit(solution)/shard_map/gate/pallas_call | solution.py:158
  10.8 0.7 %collective-permute-done.3.other = bf16[14,16,128]{2,1,0:T(8,128)(2,1)S(1)} collective-permute-done((bf16[14,16,128]{2,1,0:T(8,128)(2,1)S(1)}, bf16[14,16,128]{2,1,0:T(8,128)(2,1)S(1)}, u32[]{:S(2)}, u32[]{:S(2)}) %collective-permute-start.3) | collective-permute-done | bytes 57376 | tf_op jit(solution)/shard_map/ppermute | solution.py:197
  11.5 0.5 %add_first.1.before = f32[14,56,128]{2,1,0:T(8,128)S(1)} custom-call(f32[14,56,128]{2,1,0:T(8,128)S(1)} %get-tuple-element.26.left, bf16[14,16,128]{2,1,0:T(8,128)(2,1)S(1)} %get-tuple-element.27.right, bf16[14,16,128]{2,1,0:T(8,128)(2,1)S(1)} %collective-permute-done.3.other), custom_call_target="tpu_custom_call" | custom-call | flops 22478848 | bytes 516096 | tf_op jit(solution)/shard_map/add_first/pallas_call | solution.py:158
  12.0 0.9 %project.6 = (f32[28,56,128]{2,1,0:T(8,128)S(1)}, bf16[28,16,128]{2,1,0:T(8,128)(2,1)S(1)}) custom-call(s32[1]{0:T(128)S(6)} %copy.14.length, f32[1,128]{1,0:T(1,128)S(1)} %bitcast.10, bf16[128,512]{1,0:T(8,128)(2,1)S(1)} %constant_dynamic-update-slice_fusion.weight, bf16[14,56,128]{2,1,0:T(8,128)(2,1)S(1)} %collective-permute-done.refs_0_, ...), custom_call_target="tpu_custom_call" | custom-call | flops 102760448 | bytes 532996 | tf_op jit(solution)/shard_map/project/pallas_call | solution.py:158
  12.9 1.6 %collective-permute-done.1.refs_0_ = bf16[14,56,128]{2,1,0:T(8,128)(2,1)S(1)} collective-permute-done((bf16[14,56,128]{2,1,0:T(8,128)(2,1)S(1)}, bf16[14,56,128]{2,1,0:T(8,128)(2,1)S(1)}, u32[]{:S(2)}, u32[]{:S(2)}) %collective-permute-start.1) | collective-permute-done | bytes 200736 | tf_op jit(solution)/shard_map/ppermute | solution.py:194
  14.5 1.7 %collective-permute-start.4 = (bf16[14,56,128]{2,1,0:T(8,128)(2,1)S(1)}, bf16[14,56,128]{2,1,0:T(8,128)(2,1)S(1)}, u32[]{:S(2)}, u32[]{:S(2)}) collective-permute-start(bf16[14,56,128]{2,1,0:T(8,128)(2,1)S(1)} %collective-permute-done.1.refs_0_), channel_id=1, source_target_pairs={{0,2},{2,4},{4,6},{6,7},{7,5},{5,3},{3,1},{1,0},{8,10},{10,12},{12... | collective-permute-start | bytes 602120 | tf_op jit(solution)/shard_map/ppermute | solution.py:194
  16.3 0.3 collective-permute-start.8
  16.6 0.9 %project.7 = (f32[28,56,128]{2,1,0:T(8,128)S(1)}, bf16[28,16,128]{2,1,0:T(8,128)(2,1)S(1)}) custom-call(s32[1]{0:T(128)S(6)} %copy.14.length, f32[1,128]{1,0:T(1,128)S(1)} %bitcast.11, bf16[128,512]{1,0:T(8,128)(2,1)S(1)} %constant_dynamic-update-slice_fusion.weight, bf16[14,56,128]{2,1,0:T(8,128)(2,1)S(1)} %collective-permute-done.1.refs_0_, ...), custom_call_target="tpu_custom_call" | custom-call | flops 102760448 | bytes 532996 | tf_op jit(solution)/shard_map/project/pallas_call | solution.py:158
  17.5 0.6 %collective-permute-start.9 = (bf16[28,16,128]{2,1,0:T(8,128)(2,1)S(1)}, bf16[28,16,128]{2,1,0:T(8,128)(2,1)S(1)}, u32[]{:S(2)}, u32[]{:S(2)}) collective-permute-start(bf16[28,16,128]{2,1,0:T(8,128)(2,1)S(1)} %get-tuple-element.37.right), channel_id=1, source_target_pairs={{0,8},{8,0},{1,9},{9,1},{2,10},{10,2},{3,11},{11,3},{4,12},{12,4},... | collective-permute-start | bytes 344072 | tf_op jit(solution)/shard_map/ppermute | solution.py:197
  18.1 0.9 %add_more.3.before = f32[14,56,128]{2,1,0:T(8,128)S(1)} custom-call(f32[28,56,128]{2,1,0:T(8,128)S(1)} %get-tuple-element.29.left, bf16[28,16,128]{2,1,0:T(8,128)(2,1)S(1)} %get-tuple-element.30.right, bf16[28,16,128]{2,1,0:T(8,128)(2,1)S(1)} %collective-permute-done.6.other, f32[14,56,128]{2,1,0:T(8,128)S(1)} %add_first.1.before), custom_call_target="tpu_custom_call" | custom-call | flops 44957696 | bytes 1433600 | tf_op jit(solution)/shard_map/add_more/pallas_call | solution.py:158
  19.0 1.3 %collective-permute-done.4.refs_0_ = bf16[14,56,128]{2,1,0:T(8,128)(2,1)S(1)} collective-permute-done((bf16[14,56,128]{2,1,0:T(8,128)(2,1)S(1)}, bf16[14,56,128]{2,1,0:T(8,128)(2,1)S(1)}, u32[]{:S(2)}, u32[]{:S(2)}) %collective-permute-start.4) | collective-permute-done | bytes 200736 | tf_op jit(solution)/shard_map/ppermute | solution.py:194
  20.3 1.8 %collective-permute-start.7 = (bf16[7,56,128]{2,1,0:T(8,128)(2,1)S(1)}, bf16[7,56,128]{2,1,0:T(8,128)(2,1)S(1)}, u32[]{:S(2)}, u32[]{:S(2)}) collective-permute-start(bf16[7,56,128]{2,1,0:T(8,128)(2,1)S(1)} %slice.6), channel_id=1, source_target_pairs={{0,2},{2,4},{4,6},{6,7},{7,5},{5,3},{3,1},{1,0},{8,10},{10,12},{12... | collective-permute-start | bytes 301064 | tf_op jit(solution)/shard_map/ppermute | solution.py:194
  22.1 0.3 %collective-permute-start.10 = (bf16[7,56,128]{2,1,0:T(8,128)(2,1)S(1)}, bf16[7,56,128]{2,1,0:T(8,128)(2,1)S(1)}, u32[]{:S(2)}, u32[]{:S(2)}) collective-permute-start(bf16[7,56,128]{2,1,0:T(8,128)(2,1)S(1)} %slice.7), channel_id=1, source_target_pairs={{0,1},{2,0},{4,2},{6,4},{7,6},{5,7},{3,5},{1,3},{8,9},{10,8},{12,1... | collective-permute-start | bytes 301064 | tf_op jit(solution)/shard_map/ppermute | solution.py:194
  22.4 0.9 %project.8 = (f32[28,56,128]{2,1,0:T(8,128)S(1)}, bf16[28,16,128]{2,1,0:T(8,128)(2,1)S(1)}) custom-call(s32[1]{0:T(128)S(6)} %copy.14.length, f32[1,128]{1,0:T(1,128)S(1)} %bitcast.12, bf16[128,512]{1,0:T(8,128)(2,1)S(1)} %constant_dynamic-update-slice_fusion.weight, bf16[14,56,128]{2,1,0:T(8,128)(2,1)S(1)} %collective-permute-done.4.refs_0_, ...), custom_call_target="tpu_custom_call" | custom-call | flops 102760448 | bytes 532996 | tf_op jit(solution)/shard_map/project/pallas_call | solution.py:158
  23.3 0.1 collective-permute-start.12
  23.4 0.9 %add_more.4.before = f32[14,56,128]{2,1,0:T(8,128)S(1)} custom-call(f32[28,56,128]{2,1,0:T(8,128)S(1)} %get-tuple-element.36.left, bf16[28,16,128]{2,1,0:T(8,128)(2,1)S(1)} %get-tuple-element.37.right, bf16[28,16,128]{2,1,0:T(8,128)(2,1)S(1)} %collective-permute-done.9.other, f32[14,56,128]{2,1,0:T(8,128)S(1)} %add_more.3.before), custom_call_target="tpu_custom_call" | custom-call | flops 44957696 | bytes 1433600 | tf_op jit(solution)/shard_map/add_more/pallas_call | solution.py:158
  24.4 0.6 %collective-permute-done.7.refs_0_ = bf16[7,56,128]{2,1,0:T(8,128)(2,1)S(1)} collective-permute-done((bf16[7,56,128]{2,1,0:T(8,128)(2,1)S(1)}, bf16[7,56,128]{2,1,0:T(8,128)(2,1)S(1)}, u32[]{:S(2)}, u32[]{:S(2)}) %collective-permute-start.7) | collective-permute-done | bytes 100384 | tf_op jit(solution)/shard_map/ppermute | solution.py:194
  25.0 1.8 %collective-permute-done.10.refs_1_ = bf16[7,56,128]{2,1,0:T(8,128)(2,1)S(1)} collective-permute-done((bf16[7,56,128]{2,1,0:T(8,128)(2,1)S(1)}, bf16[7,56,128]{2,1,0:T(8,128)(2,1)S(1)}, u32[]{:S(2)}, u32[]{:S(2)}) %collective-permute-start.10) | collective-permute-done | bytes 100384 | tf_op jit(solution)/shard_map/ppermute | solution.py:194
  26.8 0.6 %project.9 = (f32[14,56,128]{2,1,0:T(8,128)S(1)}, bf16[14,16,128]{2,1,0:T(8,128)(2,1)S(1)}) custom-call(s32[1]{0:T(128)S(6)} %copy.14.length, f32[1,128]{1,0:T(1,128)S(1)} %bitcast.13, bf16[128,512]{1,0:T(8,128)(2,1)S(1)} %constant_dynamic-update-slice_fusion.weight, bf16[7,56,128]{2,1,0:T(8,128)(2,1)S(1)} %collective-permute-done.7.refs_0_, ...), custom_call_target="tpu_custom_call" | custom-call | flops 51380224 | bytes 332292 | tf_op jit(solution)/shard_map/project/pallas_call | solution.py:158
  27.4 0.9 %add_more.5.before = f32[14,56,128]{2,1,0:T(8,128)S(1)} custom-call(f32[28,56,128]{2,1,0:T(8,128)S(1)} %get-tuple-element.40.left, bf16[28,16,128]{2,1,0:T(8,128)(2,1)S(1)} %get-tuple-element.41.right, bf16[28,16,128]{2,1,0:T(8,128)(2,1)S(1)} %collective-permute-done.12.other, f32[14,56,128]{2,1,0:T(8,128)S(1)} %add_more.4.before), custom_call_target="tpu_custom_call" | custom-call | flops 44957696 | bytes 1433600 | tf_op jit(solution)/shard_map/add_more/pallas_call | solution.py:158
  28.4 0.3 collective-permute-done.11.other
  28.7 1.6 %finish.1 = bf16[14,56,128]{2,1,0:T(8,128)(2,1)} custom-call(f32[14,56,128]{2,1,0:T(8,128)S(1)} %get-tuple-element.45.left, bf16[14,16,128]{2,1,0:T(8,128)(2,1)S(1)} %get-tuple-element.46.right, bf16[14,16,128]{2,1,0:T(8,128)(2,1)S(1)} %collective-permute-done.11.other, f32[14,56,128]{2,1,0:T(8,128)S(1)} %add_more.5.before, ...), custom_call_target="tpu_custom_call" | custom-call | flops 22478848 | bytes 1352192 | tf_op jit(solution)/shard_map/finish/pallas_call | solution.py:158
  (21 shorter events, 0.1 us)
Async XLA Ops:
  0.0 6.8 %copy-start = (bf16[56,14,128]{2,0,1:T(8,128)(2,1)S(1)}, bf16[56,14,128]{2,0,1:T(8,128)(2,1)}, u32[]{:S(2)}) copy-start(bf16[56,14,128]{2,0,1:T(8,128)(2,1)} %param.10) | copy-start | bytes 602116
  0.0 8.2 %collective-permute-start = (bf16[14,56,128]{2,1,0:T(8,128)(2,1)}, bf16[14,56,128]{2,1,0:T(8,128)(2,1)S(1)}, u32[]{:S(2)}, u32[]{:S(2)}) collective-permute-start(bf16[14,56,128]{2,1,0:T(8,128)(2,1)} %bitcast.4), channel_id=1, source_target_pairs={{0,2},{2,4},{4,6},{6,7},{7,5},{5,3},{3,1},{1,0},{8,10},{10,12},{12... | collective-permute-start | bytes 602120 | tf_op jit(solution)/shard_map/ppermute | solution.py:194
  3.0 7.1 %collective-permute-start.2 = (bf16[14,56,128]{2,1,0:T(8,128)(2,1)}, bf16[14,56,128]{2,1,0:T(8,128)(2,1)S(1)}, u32[]{:S(2)}, u32[]{:S(2)}) collective-permute-start(bf16[14,56,128]{2,1,0:T(8,128)(2,1)} %bitcast.5), channel_id=1, source_target_pairs={{0,1},{2,0},{4,2},{6,4},{7,6},{5,7},{3,5},{1,3},{8,9},{10,8},{12,1... | collective-permute-start | bytes 602120 | tf_op jit(solution)/shard_map/ppermute | solution.py:194
  6.8 0.7 %copy-start.3 = (f32[128]{0:T(128)S(1)}, f32[128]{0:T(128)}, u32[]{:S(2)}) copy-start(f32[128]{0:T(128)} %param.12) | copy-start | bytes 1540
  7.4 2.9 %copy-start.1 = (bf16[128,128]{1,0:T(8,128)(2,1)S(1)}, bf16[128,128]{1,0:T(8,128)(2,1)}, u32[]{:S(2)}) copy-start(bf16[128,128]{1,0:T(8,128)(2,1)} %out_gate.1) | copy-start | bytes 98308
  7.4 2.9 %copy-start.2 = (bf16[128,128]{1,0:T(8,128)(2,1)S(1)}, bf16[128,128]{1,0:T(8,128)(2,1)}, u32[]{:S(2)}) copy-start(bf16[128,128]{1,0:T(8,128)(2,1)} %last_weight.1) | copy-start | bytes 98308
  8.2 2.0 %copy-start.4 = (f32[128]{0:T(128)S(1)}, f32[128]{0:T(128)}, u32[]{:S(2)}) copy-start(f32[128]{0:T(128)} %param.18) | copy-start | bytes 1540
  8.2 6.3 %collective-permute-start.1 = (bf16[14,56,128]{2,1,0:T(8,128)(2,1)S(1)}, bf16[14,56,128]{2,1,0:T(8,128)(2,1)S(1)}, u32[]{:S(2)}, u32[]{:S(2)}) collective-permute-start(bf16[14,56,128]{2,1,0:T(8,128)(2,1)S(1)} %collective-permute-done.refs_0_), channel_id=1, source_target_pairs={{0,2},{2,4},{4,6},{6,7},{7,5},{5,3},{3,1},{1,0},{8,10},{10,12},{12... | collective-permute-start | bytes 602120 | tf_op jit(solution)/shard_map/ppermute | solution.py:194
  10.1 6.2 %collective-permute-start.5 = (bf16[14,56,128]{2,1,0:T(8,128)(2,1)S(1)}, bf16[14,56,128]{2,1,0:T(8,128)(2,1)S(1)}, u32[]{:S(2)}, u32[]{:S(2)}) collective-permute-start(bf16[14,56,128]{2,1,0:T(8,128)(2,1)S(1)} %collective-permute-done.2.refs_1_), channel_id=1, source_target_pairs={{0,1},{2,0},{4,2},{6,4},{7,6},{5,7},{3,5},{1,3},{8,9},{10,8},{12,1... | collective-permute-start | bytes 602120 | tf_op jit(solution)/shard_map/ppermute | solution.py:194
  10.3 1.2 %collective-permute-start.3 = (bf16[14,16,128]{2,1,0:T(8,128)(2,1)S(1)}, bf16[14,16,128]{2,1,0:T(8,128)(2,1)S(1)}, u32[]{:S(2)}, u32[]{:S(2)}) collective-permute-start(bf16[14,16,128]{2,1,0:T(8,128)(2,1)S(1)} %get-tuple-element.27.right), channel_id=1, source_target_pairs={{0,8},{8,0},{1,9},{9,1},{2,10},{10,2},{3,11},{11,3},{4,12},{12,4},... | collective-permute-start | bytes 172040 | tf_op jit(solution)/shard_map/ppermute | solution.py:197
  14.5 5.7 %collective-permute-start.4 = (bf16[14,56,128]{2,1,0:T(8,128)(2,1)S(1)}, bf16[14,56,128]{2,1,0:T(8,128)(2,1)S(1)}, u32[]{:S(2)}, u32[]{:S(2)}) collective-permute-start(bf16[14,56,128]{2,1,0:T(8,128)(2,1)S(1)} %collective-permute-done.1.refs_0_), channel_id=1, source_target_pairs={{0,2},{2,4},{4,6},{6,7},{7,5},{5,3},{3,1},{1,0},{8,10},{10,12},{12... | collective-permute-start | bytes 602120 | tf_op jit(solution)/shard_map/ppermute | solution.py:194
  16.3 5.8 %collective-permute-start.8 = (bf16[14,56,128]{2,1,0:T(8,128)(2,1)S(1)}, bf16[14,56,128]{2,1,0:T(8,128)(2,1)S(1)}, u32[]{:S(2)}, u32[]{:S(2)}) collective-permute-start(bf16[14,56,128]{2,1,0:T(8,128)(2,1)S(1)} %collective-permute-done.5.refs_1_), channel_id=1, source_target_pairs={{0,1},{2,0},{4,2},{6,4},{7,6},{5,7},{3,5},{1,3},{8,9},{10,8},{12,1... | collective-permute-start | bytes 602120 | tf_op jit(solution)/shard_map/ppermute | solution.py:194
  16.6 1.5 %collective-permute-start.6 = (bf16[28,16,128]{2,1,0:T(8,128)(2,1)S(1)}, bf16[28,16,128]{2,1,0:T(8,128)(2,1)S(1)}, u32[]{:S(2)}, u32[]{:S(2)}) collective-permute-start(bf16[28,16,128]{2,1,0:T(8,128)(2,1)S(1)} %get-tuple-element.30.right), channel_id=1, source_target_pairs={{0,8},{8,0},{1,9},{9,1},{2,10},{10,2},{3,11},{11,3},{4,12},{12,4},... | collective-permute-start | bytes 344072 | tf_op jit(solution)/shard_map/ppermute | solution.py:197
  17.5 5.9 %collective-permute-start.9 = (bf16[28,16,128]{2,1,0:T(8,128)(2,1)S(1)}, bf16[28,16,128]{2,1,0:T(8,128)(2,1)S(1)}, u32[]{:S(2)}, u32[]{:S(2)}) collective-permute-start(bf16[28,16,128]{2,1,0:T(8,128)(2,1)S(1)} %get-tuple-element.37.right), channel_id=1, source_target_pairs={{0,8},{8,0},{1,9},{9,1},{2,10},{10,2},{3,11},{11,3},{4,12},{12,4},... | collective-permute-start | bytes 344072 | tf_op jit(solution)/shard_map/ppermute | solution.py:197
  20.3 4.7 %collective-permute-start.7 = (bf16[7,56,128]{2,1,0:T(8,128)(2,1)S(1)}, bf16[7,56,128]{2,1,0:T(8,128)(2,1)S(1)}, u32[]{:S(2)}, u32[]{:S(2)}) collective-permute-start(bf16[7,56,128]{2,1,0:T(8,128)(2,1)S(1)} %slice.6), channel_id=1, source_target_pairs={{0,2},{2,4},{4,6},{6,7},{7,5},{5,3},{3,1},{1,0},{8,10},{10,12},{12... | collective-permute-start | bytes 301064 | tf_op jit(solution)/shard_map/ppermute | solution.py:194
  22.1 4.7 %collective-permute-start.10 = (bf16[7,56,128]{2,1,0:T(8,128)(2,1)S(1)}, bf16[7,56,128]{2,1,0:T(8,128)(2,1)S(1)}, u32[]{:S(2)}, u32[]{:S(2)}) collective-permute-start(bf16[7,56,128]{2,1,0:T(8,128)(2,1)S(1)} %slice.7), channel_id=1, source_target_pairs={{0,1},{2,0},{4,2},{6,4},{7,6},{5,7},{3,5},{1,3},{8,9},{10,8},{12,1... | collective-permute-start | bytes 301064 | tf_op jit(solution)/shard_map/ppermute | solution.py:194
  23.3 4.1 %collective-permute-start.12 = (bf16[28,16,128]{2,1,0:T(8,128)(2,1)S(1)}, bf16[28,16,128]{2,1,0:T(8,128)(2,1)S(1)}, u32[]{:S(2)}, u32[]{:S(2)}) collective-permute-start(bf16[28,16,128]{2,1,0:T(8,128)(2,1)S(1)} %get-tuple-element.41.right), channel_id=1, source_target_pairs={{0,8},{8,0},{1,9},{9,1},{2,10},{10,2},{3,11},{11,3},{4,12},{12,4},... | collective-permute-start | bytes 344072 | tf_op jit(solution)/shard_map/ppermute | solution.py:197
  27.4 1.3 %collective-permute-start.11 = (bf16[14,16,128]{2,1,0:T(8,128)(2,1)S(1)}, bf16[14,16,128]{2,1,0:T(8,128)(2,1)S(1)}, u32[]{:S(2)}, u32[]{:S(2)}) collective-permute-start(bf16[14,16,128]{2,1,0:T(8,128)(2,1)S(1)} %get-tuple-element.46.right), channel_id=1, source_target_pairs={{0,8},{8,0},{1,9},{9,1},{2,10},{10,2},{3,11},{11,3},{4,12},{12,4},... | collective-permute-start | bytes 172040 | tf_op jit(solution)/shard_map/ppermute | solution.py:197

commit v8 on v7

--- a/solution.py
+++ b/solution.py
@@ -81,6 +81,11 @@
             right[index * s.half + step] = part.astype(BF16)
 
 
+def join(left_gate, left_value, right_gate, right_value, weight):
+    for at, part in enumerate((left_gate, left_value, right_gate, right_value)):
+        weight[:, at * part.shape[1] : (at + 1) * part.shape[1]] = part[...]
+
+
 def gate(s, pair, gain, out_gate, last_gain, last_weight, gating, kept_gain, kept_weight):
     kept_gain[...] = last_gain[...]
     kept_weight[...] = last_weight[...]
@@ -150,7 +155,7 @@
             update[start + step] = part.astype(BF16)
 
 
-def call(body, out_shape, scratch, flops, *operands):
+def call(body, out_shape, scratch, flops, *operands, grant=24):
     def space(operand):
         return pl.BlockSpec(memory_space=pltpu.SMEM if operand.dtype == jnp.int32 else pltpu.VMEM)
 
@@ -161,9 +166,9 @@
         in_specs=[space(o) for o in operands],
         out_specs=jax.tree.map(lambda _: pl.BlockSpec(memory_space=pltpu.VMEM), out_shape),
         scratch_shapes=scratch,
-        compiler_params=pltpu.CompilerParams(vmem_limit_bytes=24 * 1024 * 1024),
+        compiler_params=pltpu.CompilerParams(vmem_limit_bytes=grant * 1024 * 1024),
         cost_estimate=pl.CostEstimate(flops=flops, bytes_accessed=sent, transcendentals=0),
-        name=body.func.__name__,
+        name=getattr(body, "func", body).__name__,
     )(*operands)
 
 
@@ -186,7 +191,17 @@
     shape = jax.ShapeDtypeStruct
     pair = jnp.transpose(pair_state, (1, 0, 2))
     gain = input_gain.reshape(1, channels)
-    weights = jnp.concatenate([left_gate, left_value, right_gate, right_value], 1)
+    weights = call(
+        join,
+        shape((channels, 4 * hidden), BF16),
+        [],
+        0,
+        left_gate,
+        left_value,
+        right_gate,
+        right_value,
+        grant=56,
+    )
     order = ring(s.cols)
 
     def shift(block, by):
@@ -234,37 +249,42 @@
 
     far = s.cols // 2
     blocks, sources, travel = [pair], whole([0]), [pair, pair]
-    total = terms = kept = None
-    for distance in range(1, far + 1):
-        if distance == far:
-            travel = [travel[0][: s.half], travel[1][s.half :]]
+    total = kept = last = None
+    waiting = []
+    for distance in range(1, far):
         arrived = [shift(block, by) for block, by in zip(travel, (1, -1))]
-        pending = run(blocks, sources)
-        if distance == 2:
-            kept = call(
-                functools.partial(gate, s),
-                [
-                    shape((width, height, channels), F32),
-                    shape((1, hidden), F32),
-                    shape(out_weight.shape, BF16),
-                ],
-                [],
-                2 * height * width * channels * channels,
-                pair,
-                gain,
-                out_gate,
-                output_gain.reshape(1, hidden),
-                out_weight,
-            )
-        if terms is not None:
-            total = add(total, terms)
-        terms = pending
-        done = (terms, total, kept)
+        if distance == far - 1:
+            blocks, sources = blocks + [last], sources + [(2, at, far, at) for at in starts]
+        waiting.append(run(blocks, sources))
+        if distance == 1:
+            last = shift(lax.optimization_barrier((pair, waiting[0]))[0], far)
+        else:
+            if kept is None:
+                kept = call(
+                    functools.partial(gate, s),
+                    [
+                        shape((width, height, channels), F32),
+                        shape((1, hidden), F32),
+                        shape(out_weight.shape, BF16),
+                    ],
+                    [],
+                    2 * height * width * channels * channels,
+                    pair,
+                    gain,
+                    out_gate,
+                    output_gain.reshape(1, hidden),
+                    out_weight,
+                )
+            for terms in waiting:
+                total = add(total, terms)
+            waiting = []
+        done = (waiting, total, kept)
         travel = [lax.optimization_barrier((block, done))[0] for block in arrived]
-        blocks, sources = arrived, whole([-distance, distance])
-    left, right = run(travel, [(0, 0, -far, 0), (1, 0, far, s.half)])
-    other = swap(right)
-    total = add(total, terms)
+        blocks, sources = travel, whole([-distance, distance])
+    for block, way in zip(travel, (1 - far, far - 1)):
+        waiting.append(run([block], whole([way])))
+    total = add(total, waiting[0])
+    left, right = waiting[1]
     gating, last_gain, last_weight = kept
     update = call(
         functools.partial(finish, s),
@@ -273,7 +293,7 @@
         16 * width * height * width * hidden,
         left,
         right,
-        other,
+        swap(right),
         total,
         gating,
         last_gain,

time: 30.7 us -> 34.4 us (1.12)
  waiting for transfers between devices: 6.53 us -> 2.66 us
  starting transfers between devices: 9.92 us -> 13.4 us
  Pallas kernels: 9.3 us -> 12.6 us
  local copies, waits for them, and re-layouts: 3.75 us -> 4.39 us
    ppermute x8 -> x7, waiting for transfers between devices: 5.51 us -> 0.85 us  [shift(): return lax.ppermute(block, 'col', pairs)]
    pallas_call x11 -> x12, Pallas kernels: 9.3 us -> 12.6 us  [call(): pl.pallas_call(body, out_shape=out_shape, in_specs=[space(o) for o in ope...]
    ppermute x8 -> x7, starting transfers between devices: 9.21 us -> 12.2 us  [shift(): return lax.ppermute(block, 'col', pairs)]
    unnamed x13 -> x16, local copies, waits for them, and re-layouts: 2.96 us -> 4.39 us
    ppermute x5, waiting for transfers between devices: 1.01 us -> 1.81 us  [swap(): lax.ppermute(block, 'row', [(at, (at + 1) % s.rows) for at in range(s.row...]
    concatenate x1 -> x0, local copies, waits for them, and re-layouts: 0.77 us -> none  [local(): jnp.concatenate([left_gate, left_value, right_gate, right_value], 1)]
    ppermute x5, starting transfers between devices: 0.71 us -> 1.26 us  [swap(): lax.ppermute(block, 'row', [(at, (at + 1) % s.rows) for at in range(s.row...]
  transfers between devices with their start and end apart: 13 -> 12, of which waited for: 7 -> 4; matrix products, arithmetic and copies ran while one was open for 10% -> 0% of each run, Pallas kernels for 25% -> 33%
where the time goes in v8:
time: 34.4 us; the launch traced here: 33.9 us
  starting transfers between devices  13.4 us (39%)
  Pallas kernels  12.6 us (37%)
  local copies, waits for them, and re-layouts  4.39 us (13%)
  waiting for transfers between devices  2.66 us (8%)
  between operations  0.82 us (2%)
    pallas_call x12, Pallas kernels, call(): pl.pallas_call(body, out_shape=out_shape, in_specs=[space(o) for o in ope...  12.6 us
    ppermute x7, starting transfers between devices, shift(): return lax.ppermute(block, 'col', pairs)  12.2 us
    unnamed x16, local copies, waits for them, and re-layouts  4.39 us
    ppermute x5, waiting for transfers between devices, swap(): lax.ppermute(block, 'row', [(at, (at + 1) % s.rows) for at in range(s.row...  1.81 us
    ppermute x5, starting transfers between devices, swap(): lax.ppermute(block, 'row', [(at, (at + 1) % s.rows) for at in range(s.row...  1.26 us
    ppermute x7, waiting for transfers between devices, shift(): return lax.ppermute(block, 'col', pairs)  0.85 us
  transfers between devices with their start and end apart: 12, of which 4 were waited for; matrix products, arithmetic and copies ran while one was open for 0% of the time, Pallas kernels for 33%

profile of v8, /device:TPU:0, one launch (start us, length us, event | category | flops | bytes accessed | tf_op | source)
XLA Modules:
  0.0 33.9 jit_solution(3001525128290230404)
XLA Ops:
  0.0 3.0 %collective-permute-start.2 = (bf16[14,56,128]{2,1,0:T(8,128)(2,1)}, bf16[14,56,128]{2,1,0:T(8,128)(2,1)S(1)}, u32[]{:S(2)}, u32[]{:S(2)}) collective-permute-start(bf16[14,56,128]{2,1,0:T(8,128)(2,1)} %bitcast.1.refs_0_.pair), channel_id=1, source_target_pairs={{0,2},{2,4},{4,6},{6,7},{7,5},{5,3},{3,1},{1,0},{8,10},{10,12},{12... | collective-permute-start | bytes 602120 | tf_op jit(solution)/shard_map/ppermute | solution.py:209
  3.7 1.5 %join.1.weight = bf16[128,512]{1,0:T(8,128)(2,1)} custom-call(bf16[128,128]{1,0:T(8,128)(2,1)} %left_gate.1, bf16[128,128]{1,0:T(8,128)(2,1)} %left_value.1, bf16[128,128]{1,0:T(8,128)(2,1)} %right_gate.1, bf16[128,128]{1,0:T(8,128)(2,1)} %right_value.1), custom_call_target="tpu_custom_call" | custom-call | bytes 131072 | tf_op jit(solution)/shard_map/join/pallas_call | solution.py:163
  5.2 0.9 %copy-done = bf16[128,512]{1,0:T(8,128)(2,1)S(1)} copy-done((bf16[128,512]{1,0:T(8,128)(2,1)S(1)}, bf16[128,512]{1,0:T(8,128)(2,1)}, u32[]{:S(2)}) %copy-start) | copy-done | bytes 131096
  6.1 0.7 %copy-done.4 = f32[128]{0:T(128)S(1)} copy-done((f32[128]{0:T(128)S(1)}, f32[128]{0:T(128)}, u32[]{:S(2)}) %copy-start.4) | copy-done | bytes 536
  6.7 1.5 %project.5 = (f32[14,56,128]{2,1,0:T(8,128)S(1)}, bf16[14,16,128]{2,1,0:T(8,128)(2,1)S(1)}) custom-call(s32[1]{0:T(128)S(6)} %copy.11.length, f32[1,128]{1,0:T(1,128)S(1)} %bitcast.4, bf16[128,512]{1,0:T(8,128)(2,1)S(1)} %copy-done, bf16[14,56,128]{2,1,0:T(8,128)(2,1)} %bitcast.1.refs_0_.pair), custom_call_target="tpu_custom_call" | custom-call | flops 51380224 | bytes 332292 | tf_op jit(solution)/shard_map/project/pallas_call | solution.py:163
  8.3 2.1 %collective-permute-start.6 = (bf16[14,56,128]{2,1,0:T(8,128)(2,1)S(1)}, bf16[14,56,128]{2,1,0:T(8,128)(2,1)S(1)}, u32[]{:S(2)}, u32[]{:S(2)}) collective-permute-start(bf16[14,56,128]{2,1,0:T(8,128)(2,1)S(1)} %collective-permute-done.2.refs_0_), channel_id=1, source_target_pairs={{0,2},{2,4},{4,6},{6,7},{7,5},{5,3},{3,1},{1,0},{8,10},{10,12},{12... | collective-permute-start | bytes 602120 | tf_op jit(solution)/shard_map/ppermute | solution.py:209
  10.4 5.0 %collective-permute-start.7 = (bf16[14,56,128]{2,1,0:T(8,128)(2,1)}, bf16[14,56,128]{2,1,0:T(8,128)(2,1)S(1)}, u32[]{:S(2)}, u32[]{:S(2)}) collective-permute-start(bf16[14,56,128]{2,1,0:T(8,128)(2,1)} %bitcast.1.refs_0_.pair), channel_id=1, source_target_pairs={{0,7},{2,5},{4,3},{6,1},{7,0},{5,2},{3,4},{1,6},{8,15},{10,13},{12... | collective-permute-start | bytes 602120 | tf_op jit(solution)/shard_map/ppermute | solution.py:209
  15.3 0.9 %project.6 = (f32[28,56,128]{2,1,0:T(8,128)S(1)}, bf16[28,16,128]{2,1,0:T(8,128)(2,1)S(1)}) custom-call(s32[1]{0:T(128)S(6)} %copy.11.length, f32[1,128]{1,0:T(1,128)S(1)} %bitcast.5, bf16[128,512]{1,0:T(8,128)(2,1)S(1)} %copy-done, bf16[14,56,128]{2,1,0:T(8,128)(2,1)S(1)} %collective-permute-done.2.refs_0_, ...), custom_call_target="tpu_custom_call" | custom-call | flops 102760448 | bytes 532996 | tf_op jit(solution)/shard_map/project/pallas_call | solution.py:163
  16.3 0.1 collective-permute-start.3
  16.3 0.5 %collective-permute-start.4 = (bf16[14,16,128]{2,1,0:T(8,128)(2,1)S(1)}, bf16[14,16,128]{2,1,0:T(8,128)(2,1)S(1)}, u32[]{:S(2)}, u32[]{:S(2)}) collective-permute-start(bf16[14,16,128]{2,1,0:T(8,128)(2,1)S(1)} %get-tuple-element.26.right), channel_id=1, source_target_pairs={{0,8},{8,0},{1,9},{9,1},{2,10},{10,2},{3,11},{11,3},{4,12},{12,4},... | collective-permute-start | bytes 172040 | tf_op jit(solution)/shard_map/ppermute | solution.py:212
  16.8 0.8 %copy-done.2 = bf16[128,128]{1,0:T(8,128)(2,1)S(1)} copy-done((bf16[128,128]{1,0:T(8,128)(2,1)S(1)}, bf16[128,128]{1,0:T(8,128)(2,1)}, u32[]{:S(2)}) %copy-start.2) | copy-done | bytes 32792
  17.6 0.8 %copy-done.3 = bf16[128,128]{1,0:T(8,128)(2,1)S(1)} copy-done((bf16[128,128]{1,0:T(8,128)(2,1)S(1)}, bf16[128,128]{1,0:T(8,128)(2,1)}, u32[]{:S(2)}) %copy-start.3) | copy-done | bytes 32792
  18.4 0.7 %copy-done.5 = f32[128]{0:T(128)S(1)} copy-done((f32[128]{0:T(128)S(1)}, f32[128]{0:T(128)}, u32[]{:S(2)}) %copy-start.5) | copy-done | bytes 536
  19.0 0.7 %copy-done.7 = f32[128]{0:T(128)S(1)} copy-done((f32[128]{0:T(128)S(1)}, f32[128]{0:T(128)}, u32[]{:S(2)}) %copy-start.7) | copy-done | bytes 536
  19.7 1.4 %gate.1 = (f32[14,56,128]{2,1,0:T(8,128)S(1)}, f32[1,128]{1,0:T(1,128)S(1)}, bf16[128,128]{1,0:T(8,128)(2,1)S(1)}) custom-call(bf16[14,56,128]{2,1,0:T(8,128)(2,1)} %bitcast.1.refs_0_.pair, f32[1,128]{1,0:T(1,128)S(1)} %bitcast.6, bf16[128,128]{1,0:T(8,128)(2,1)S(1)} %copy-done.2, f32[1,128]{1,0:T(1,128)S(1)} %bitcast.10, bf16[128,128]{1,0:T(8,128)(2,1)S(1)} %copy-done.3), custom_call_target="tpu_custom_call" | custom-call | flops 25690112 | bytes 267264 | tf_op jit(solution)/shard_map/gate/pallas_call | solution.py:163
  21.1 0.5 %add_first.1.before = f32[14,56,128]{2,1,0:T(8,128)S(1)} custom-call(f32[14,56,128]{2,1,0:T(8,128)S(1)} %get-tuple-element.25.left, bf16[14,16,128]{2,1,0:T(8,128)(2,1)S(1)} %get-tuple-element.26.right, bf16[14,16,128]{2,1,0:T(8,128)(2,1)S(1)} %collective-permute-done.4.other), custom_call_target="tpu_custom_call" | custom-call | flops 22478848 | bytes 516096 | tf_op jit(solution)/shard_map/add_first/pallas_call | solution.py:163
  21.6 0.9 %add_more.3.before = f32[14,56,128]{2,1,0:T(8,128)S(1)} custom-call(f32[28,56,128]{2,1,0:T(8,128)S(1)} %get-tuple-element.29.left, bf16[28,16,128]{2,1,0:T(8,128)(2,1)S(1)} %get-tuple-element.30.right, bf16[28,16,128]{2,1,0:T(8,128)(2,1)S(1)} %collective-permute-done.3.other, f32[14,56,128]{2,1,0:T(8,128)S(1)} %add_first.1.before), custom_call_target="tpu_custom_call" | custom-call | flops 44957696 | bytes 1433600 | tf_op jit(solution)/shard_map/add_more/pallas_call | solution.py:163
  22.6 0.1 collective-permute-start.10
  22.7 2.0 %collective-permute-start.5 = (bf16[14,56,128]{2,1,0:T(8,128)(2,1)S(1)}, bf16[14,56,128]{2,1,0:T(8,128)(2,1)S(1)}, u32[]{:S(2)}, u32[]{:S(2)}) collective-permute-start(bf16[14,56,128]{2,1,0:T(8,128)(2,1)S(1)} %collective-permute-done.1.refs_1_), channel_id=1, source_target_pairs={{0,1},{2,0},{4,2},{6,4},{7,6},{5,7},{3,5},{1,3},{8,9},{10,8},{12,1... | collective-permute-start | bytes 602120 | tf_op jit(solution)/shard_map/ppermute | solution.py:209
  24.7 1.3 %project.7 = (f32[42,56,128]{2,1,0:T(8,128)S(1)}, bf16[42,16,128]{2,1,0:T(8,128)(2,1)S(1)}) custom-call(s32[1]{0:T(128)S(6)} %copy.11.length, f32[1,128]{1,0:T(1,128)S(1)} %bitcast.7, bf16[128,512]{1,0:T(8,128)(2,1)S(1)} %copy-done.1, bf16[14,56,128]{2,1,0:T(8,128)(2,1)S(1)} %collective-permute-done.6.refs_0_, ...), custom_call_target="tpu_custom_call" | custom-call | flops 154140672 | bytes 733700 | tf_op jit(solution)/shard_map/project/pallas_call | solution.py:163
  25.9 0.1 collective-permute-start.8
  26.0 1.4 %collective-permute-done.8.other = bf16[42,16,128]{2,1,0:T(8,128)(2,1)S(1)} collective-permute-done((bf16[42,16,128]{2,1,0:T(8,128)(2,1)S(1)}, bf16[42,16,128]{2,1,0:T(8,128)(2,1)S(1)}, u32[]{:S(2)}, u32[]{:S(2)}) %collective-permute-start.8) | collective-permute-done | bytes 172064 | tf_op jit(solution)/shard_map/ppermute | solution.py:212
  27.4 1.4 %add_more.4.before = f32[14,56,128]{2,1,0:T(8,128)S(1)} custom-call(f32[42,56,128]{2,1,0:T(8,128)S(1)} %get-tuple-element.37.left, bf16[42,16,128]{2,1,0:T(8,128)(2,1)S(1)} %get-tuple-element.38.right, bf16[42,16,128]{2,1,0:T(8,128)(2,1)S(1)} %collective-permute-done.8.other, f32[14,56,128]{2,1,0:T(8,128)S(1)} %add_more.3.before), custom_call_target="tpu_custom_call" | custom-call | flops 67436544 | bytes 1949696 | tf_op jit(solution)/shard_map/add_more/pallas_call | solution.py:163
  28.8 0.8 %collective-permute-done.10.refs_0_ = bf16[14,56,128]{2,1,0:T(8,128)(2,1)S(1)} collective-permute-done((bf16[14,56,128]{2,1,0:T(8,128)(2,1)S(1)}, bf16[14,56,128]{2,1,0:T(8,128)(2,1)S(1)}, u32[]{:S(2)}, u32[]{:S(2)}) %collective-permute-start.10) | collective-permute-done | bytes 200736 | tf_op jit(solution)/shard_map/ppermute | solution.py:209
  29.6 0.6 %project.9 = (f32[14,56,128]{2,1,0:T(8,128)S(1)}, bf16[14,16,128]{2,1,0:T(8,128)(2,1)S(1)}) custom-call(s32[1]{0:T(128)S(6)} %copy.11.length, f32[1,128]{1,0:T(1,128)S(1)} %bitcast.8, bf16[128,512]{1,0:T(8,128)(2,1)S(1)} %copy-done.1, bf16[14,56,128]{2,1,0:T(8,128)(2,1)S(1)} %collective-permute-done.10.refs_0_), custom_call_target="tpu_custom_call" | custom-call | flops 51380224 | bytes 332292 | tf_op jit(solution)/shard_map/project/pallas_call | solution.py:163
  30.2 0.1 collective-permute-start.11
  30.3 0.6 %project.8 = (f32[14,56,128]{2,1,0:T(8,128)S(1)}, bf16[14,16,128]{2,1,0:T(8,128)(2,1)S(1)}) custom-call(s32[1]{0:T(128)S(6)} %copy.11.length, f32[1,128]{1,0:T(1,128)S(1)} %bitcast.9, bf16[128,512]{1,0:T(8,128)(2,1)S(1)} %copy-done.1, bf16[14,56,128]{2,1,0:T(8,128)(2,1)S(1)} %collective-permute-done.5.refs_0_), custom_call_target="tpu_custom_call" | custom-call | flops 51380224 | bytes 332292 | tf_op jit(solution)/shard_map/project/pallas_call | solution.py:163
  30.9 0.5 %collective-permute-start.9 = (bf16[14,16,128]{2,1,0:T(8,128)(2,1)S(1)}, bf16[14,16,128]{2,1,0:T(8,128)(2,1)S(1)}, u32[]{:S(2)}, u32[]{:S(2)}) collective-permute-start(bf16[14,16,128]{2,1,0:T(8,128)(2,1)S(1)} %get-tuple-element.41.right), channel_id=1, source_target_pairs={{0,8},{8,0},{1,9},{9,1},{2,10},{10,2},{3,11},{11,3},{4,12},{12,4},... | collective-permute-start | bytes 172040 | tf_op jit(solution)/shard_map/ppermute | solution.py:212
  31.4 0.1 collective-permute-done.11.other
  31.5 0.5 %add_more.5.before = f32[14,56,128]{2,1,0:T(8,128)S(1)} custom-call(f32[14,56,128]{2,1,0:T(8,128)S(1)} %get-tuple-element.43.left, bf16[14,16,128]{2,1,0:T(8,128)(2,1)S(1)} %get-tuple-element.44.right, bf16[14,16,128]{2,1,0:T(8,128)(2,1)S(1)} %collective-permute-done.11.other, f32[14,56,128]{2,1,0:T(8,128)S(1)} %add_more.4.before), custom_call_target="tpu_custom_call" | custom-call | flops 22478848 | bytes 917504 | tf_op jit(solution)/shard_map/add_more/pallas_call | solution.py:163
  32.0 0.3 %collective-permute-done.9.other = bf16[14,16,128]{2,1,0:T(8,128)(2,1)S(1)} collective-permute-done((bf16[14,16,128]{2,1,0:T(8,128)(2,1)S(1)}, bf16[14,16,128]{2,1,0:T(8,128)(2,1)S(1)}, u32[]{:S(2)}, u32[]{:S(2)}) %collective-permute-start.9) | collective-permute-done | bytes 57376 | tf_op jit(solution)/shard_map/ppermute | solution.py:212
  32.3 1.6 %finish.1 = bf16[14,56,128]{2,1,0:T(8,128)(2,1)} custom-call(f32[14,56,128]{2,1,0:T(8,128)S(1)} %get-tuple-element.40.left, bf16[14,16,128]{2,1,0:T(8,128)(2,1)S(1)} %get-tuple-element.41.right, bf16[14,16,128]{2,1,0:T(8,128)(2,1)S(1)} %collective-permute-done.9.other, f32[14,56,128]{2,1,0:T(8,128)S(1)} %add_more.5.before, ...), custom_call_target="tpu_custom_call" | custom-call | flops 22478848 | bytes 1352192 | tf_op jit(solution)/shard_map/finish/pallas_call | solution.py:163
  (20 shorter events, 0.1 us)
Async XLA Ops:
  0.0 8.2 %collective-permute-start.2 = (bf16[14,56,128]{2,1,0:T(8,128)(2,1)}, bf16[14,56,128]{2,1,0:T(8,128)(2,1)S(1)}, u32[]{:S(2)}, u32[]{:S(2)}) collective-permute-start(bf16[14,56,128]{2,1,0:T(8,128)(2,1)} %bitcast.1.refs_0_.pair), channel_id=1, source_target_pairs={{0,2},{2,4},{4,6},{6,7},{7,5},{5,3},{3,1},{1,0},{8,10},{10,12},{12... | collective-permute-start | bytes 602120 | tf_op jit(solution)/shard_map/ppermute | solution.py:209
  3.0 7.3 %collective-permute-start = (bf16[14,56,128]{2,1,0:T(8,128)(2,1)}, bf16[14,56,128]{2,1,0:T(8,128)(2,1)S(1)}, u32[]{:S(2)}, u32[]{:S(2)}) collective-permute-start(bf16[14,56,128]{2,1,0:T(8,128)(2,1)} %bitcast.1.refs_0_.pair), channel_id=1, source_target_pairs={{0,1},{2,0},{4,2},{6,4},{7,6},{5,7},{3,5},{1,3},{8,9},{10,8},{12,1... | collective-permute-start | bytes 602120 | tf_op jit(solution)/shard_map/ppermute | solution.py:209
  5.2 0.9 %copy-start = (bf16[128,512]{1,0:T(8,128)(2,1)S(1)}, bf16[128,512]{1,0:T(8,128)(2,1)}, u32[]{:S(2)}) copy-start(bf16[128,512]{1,0:T(8,128)(2,1)} %join.1.weight) | copy-start | bytes 393220
  6.1 0.7 %copy-start.4 = (f32[128]{0:T(128)S(1)}, f32[128]{0:T(128)}, u32[]{:S(2)}) copy-start(f32[128]{0:T(128)} %param.12) | copy-start | bytes 1540
  8.3 14.3 %collective-permute-start.6 = (bf16[14,56,128]{2,1,0:T(8,128)(2,1)S(1)}, bf16[14,56,128]{2,1,0:T(8,128)(2,1)S(1)}, u32[]{:S(2)}, u32[]{:S(2)}) collective-permute-start(bf16[14,56,128]{2,1,0:T(8,128)(2,1)S(1)} %collective-permute-done.2.refs_0_), channel_id=1, source_target_pairs={{0,2},{2,4},{4,6},{6,7},{7,5},{5,3},{3,1},{1,0},{8,10},{10,12},{12... | collective-permute-start | bytes 602120 | tf_op jit(solution)/shard_map/ppermute | solution.py:209
  10.3 12.3 %collective-permute-start.1 = (bf16[14,56,128]{2,1,0:T(8,128)(2,1)S(1)}, bf16[14,56,128]{2,1,0:T(8,128)(2,1)S(1)}, u32[]{:S(2)}, u32[]{:S(2)}) collective-permute-start(bf16[14,56,128]{2,1,0:T(8,128)(2,1)S(1)} %collective-permute-done.refs_1_), channel_id=1, source_target_pairs={{0,1},{2,0},{4,2},{6,4},{7,6},{5,7},{3,5},{1,3},{8,9},{10,8},{12,1... | collective-permute-start | bytes 602120 | tf_op jit(solution)/shard_map/ppermute | solution.py:209
  10.4 14.3 %collective-permute-start.7 = (bf16[14,56,128]{2,1,0:T(8,128)(2,1)}, bf16[14,56,128]{2,1,0:T(8,128)(2,1)S(1)}, u32[]{:S(2)}, u32[]{:S(2)}) collective-permute-start(bf16[14,56,128]{2,1,0:T(8,128)(2,1)} %bitcast.1.refs_0_.pair), channel_id=1, source_target_pairs={{0,7},{2,5},{4,3},{6,1},{7,0},{5,2},{3,4},{1,6},{8,15},{10,13},{12... | collective-permute-start | bytes 602120 | tf_op jit(solution)/shard_map/ppermute | solution.py:209
  16.3 5.3 %collective-permute-start.3 = (bf16[28,16,128]{2,1,0:T(8,128)(2,1)S(1)}, bf16[28,16,128]{2,1,0:T(8,128)(2,1)S(1)}, u32[]{:S(2)}, u32[]{:S(2)}) collective-permute-start(bf16[28,16,128]{2,1,0:T(8,128)(2,1)S(1)} %get-tuple-element.30.right), channel_id=1, source_target_pairs={{0,8},{8,0},{1,9},{9,1},{2,10},{10,2},{3,11},{11,3},{4,12},{12,4},... | collective-permute-start | bytes 344072 | tf_op jit(solution)/shard_map/ppermute | solution.py:212
  16.3 4.8 %collective-permute-start.4 = (bf16[14,16,128]{2,1,0:T(8,128)(2,1)S(1)}, bf16[14,16,128]{2,1,0:T(8,128)(2,1)S(1)}, u32[]{:S(2)}, u32[]{:S(2)}) collective-permute-start(bf16[14,16,128]{2,1,0:T(8,128)(2,1)S(1)} %get-tuple-element.26.right), channel_id=1, source_target_pairs={{0,8},{8,0},{1,9},{9,1},{2,10},{10,2},{3,11},{11,3},{4,12},{12,4},... | collective-permute-start | bytes 172040 | tf_op jit(solution)/shard_map/ppermute | solution.py:212
  16.8 0.8 %copy-start.2 = (bf16[128,128]{1,0:T(8,128)(2,1)S(1)}, bf16[128,128]{1,0:T(8,128)(2,1)}, u32[]{:S(2)}) copy-start(bf16[128,128]{1,0:T(8,128)(2,1)} %out_gate.1) | copy-start | bytes 98308
  17.6 0.8 %copy-start.3 = (bf16[128,128]{1,0:T(8,128)(2,1)S(1)}, bf16[128,128]{1,0:T(8,128)(2,1)}, u32[]{:S(2)}) copy-start(bf16[128,128]{1,0:T(8,128)(2,1)} %last_weight.1) | copy-start | bytes 98308
  18.4 0.7 %copy-start.5 = (f32[128]{0:T(128)S(1)}, f32[128]{0:T(128)}, u32[]{:S(2)}) copy-start(f32[128]{0:T(128)} %param.12) | copy-start | bytes 1540
  19.0 0.7 %copy-start.7 = (f32[128]{0:T(128)S(1)}, f32[128]{0:T(128)}, u32[]{:S(2)}) copy-start(f32[128]{0:T(128)} %param.18) | copy-start | bytes 1540
  21.1 3.6 %copy-start.1 = (bf16[128,512]{1,0:T(8,128)(2,1)S(1)}, bf16[128,512]{1,0:T(8,128)(2,1)}, u32[]{:S(2)}) copy-start(bf16[128,512]{1,0:T(8,128)(2,1)} %join.1.weight) | copy-start | bytes 393220
  22.6 7.0 %collective-permute-start.10 = (bf16[14,56,128]{2,1,0:T(8,128)(2,1)S(1)}, bf16[14,56,128]{2,1,0:T(8,128)(2,1)S(1)}, u32[]{:S(2)}, u32[]{:S(2)}) collective-permute-start(bf16[14,56,128]{2,1,0:T(8,128)(2,1)S(1)} %collective-permute-done.6.refs_0_), channel_id=1, source_target_pairs={{0,2},{2,4},{4,6},{6,7},{7,5},{5,3},{3,1},{1,0},{8,10},{10,12},{12... | collective-permute-start | bytes 602120 | tf_op jit(solution)/shard_map/ppermute | solution.py:209
  22.7 7.6 %collective-permute-start.5 = (bf16[14,56,128]{2,1,0:T(8,128)(2,1)S(1)}, bf16[14,56,128]{2,1,0:T(8,128)(2,1)S(1)}, u32[]{:S(2)}, u32[]{:S(2)}) collective-permute-start(bf16[14,56,128]{2,1,0:T(8,128)(2,1)S(1)} %collective-permute-done.1.refs_1_), channel_id=1, source_target_pairs={{0,1},{2,0},{4,2},{6,4},{7,6},{5,7},{3,5},{1,3},{8,9},{10,8},{12,1... | collective-permute-start | bytes 602120 | tf_op jit(solution)/shard_map/ppermute | solution.py:209
  25.9 1.5 %collective-permute-start.8 = (bf16[42,16,128]{2,1,0:T(8,128)(2,1)S(1)}, bf16[42,16,128]{2,1,0:T(8,128)(2,1)S(1)}, u32[]{:S(2)}, u32[]{:S(2)}) collective-permute-start(bf16[42,16,128]{2,1,0:T(8,128)(2,1)S(1)} %get-tuple-element.38.right), channel_id=1, source_target_pairs={{0,8},{8,0},{1,9},{9,1},{2,10},{10,2},{3,11},{11,3},{4,12},{12,4},... | collective-permute-start | bytes 516104 | tf_op jit(solution)/shard_map/ppermute | solution.py:212
  27.4 2.9 %copy-start.6 = (f32[128]{0:T(128)S(1)}, f32[128]{0:T(128)}, u32[]{:S(2)}) copy-start(f32[128]{0:T(128)} %param.12) | copy-start | bytes 1540
  30.2 1.3 %collective-permute-start.11 = (bf16[14,16,128]{2,1,0:T(8,128)(2,1)S(1)}, bf16[14,16,128]{2,1,0:T(8,128)(2,1)S(1)}, u32[]{:S(2)}, u32[]{:S(2)}) collective-permute-start(bf16[14,16,128]{2,1,0:T(8,128)(2,1)S(1)} %get-tuple-element.44.right), channel_id=1, source_target_pairs={{0,8},{8,0},{1,9},{9,1},{2,10},{10,2},{3,11},{11,3},{4,12},{12,4},... | collective-permute-start | bytes 172040 | tf_op jit(solution)/shard_map/ppermute | solution.py:212
  30.9 1.4 %collective-permute-start.9 = (bf16[14,16,128]{2,1,0:T(8,128)(2,1)S(1)}, bf16[14,16,128]{2,1,0:T(8,128)(2,1)S(1)}, u32[]{:S(2)}, u32[]{:S(2)}) collective-permute-start(bf16[14,16,128]{2,1,0:T(8,128)(2,1)S(1)} %get-tuple-element.41.right), channel_id=1, source_target_pairs={{0,8},{8,0},{1,9},{9,1},{2,10},{10,2},{3,11},{11,3},{4,12},{12,4},... | collective-permute-start | bytes 172040 | tf_op jit(solution)/shard_map/ppermute | solution.py:212

commit v9 on v7

--- a/solution.py
+++ b/solution.py
@@ -235,10 +235,10 @@
     far = s.cols // 2
     blocks, sources, travel = [pair], whole([0]), [pair, pair]
     total = terms = kept = None
-    for distance in range(1, far + 1):
-        if distance == far:
-            travel = [travel[0][: s.half], travel[1][s.half :]]
+    for distance in range(1, far):
         arrived = [shift(block, by) for block, by in zip(travel, (1, -1))]
+        if distance == far - 1:
+            last = [shift(travel[0][: s.half], 2), shift(travel[1][s.half :], -2)]
         pending = run(blocks, sources)
         if distance == 2:
             kept = call(
@@ -261,8 +261,11 @@
         terms = pending
         done = (terms, total, kept)
         travel = [lax.optimization_barrier((block, done))[0] for block in arrived]
-        blocks, sources = arrived, whole([-distance, distance])
-    left, right = run(travel, [(0, 0, -far, 0), (1, 0, far, s.half)])
+        blocks, sources = travel, whole([-distance, distance])
+    pending = run(blocks, sources)
+    total = add(total, terms)
+    last, terms, total = lax.optimization_barrier((last, pending, total))
+    left, right = run(last, [(0, 0, -far, 0), (1, 0, far, s.half)])
     other = swap(right)
     total = add(total, terms)
     gating, last_gain, last_weight = kept

time: 30.7 us -> 32.6 us (1.062)
  starting transfers between devices: 9.92 us -> 11.3 us
  waiting for transfers between devices: 6.53 us -> 6.96 us
    ppermute x8, waiting for transfers between devices: 5.51 us -> 6.79 us  [shift(): return lax.ppermute(block, 'col', pairs)]
    ppermute x8, starting transfers between devices: 9.21 us -> 10.1 us  [shift(): return lax.ppermute(block, 'col', pairs)]
    ppermute x5, waiting for transfers between devices: 1.01 us -> 0.17 us  [swap(): lax.ppermute(block, 'row', [(at, (at + 1) % s.rows) for at in range(s.row...]
    ppermute x5, starting transfers between devices: 0.71 us -> 1.22 us  [swap(): lax.ppermute(block, 'row', [(at, (at + 1) % s.rows) for at in range(s.row...]
  transfers between devices with their start and end apart: 13 -> 13, of which waited for: 7 -> 5; matrix products, arithmetic and copies ran while one was open for 10% -> 10% of each run, Pallas kernels for 25% -> 24%
where the time goes in v9:
time: 32.6 us; the launch traced here: 32.2 us
  starting transfers between devices  11.3 us (35%)
  Pallas kernels  9.32 us (29%)
  waiting for transfers between devices  6.96 us (21%)
  local copies, waits for them, and re-layouts  3.82 us (12%)
  between operations  0.81 us (2%)
    ppermute x8, starting transfers between devices, shift(): return lax.ppermute(block, 'col', pairs)  10.1 us
    pallas_call x11, Pallas kernels, call(): pl.pallas_call(body, out_shape=out_shape, in_specs=[space(o) for o in ope...  9.32 us
    ppermute x8, waiting for transfers between devices, shift(): return lax.ppermute(block, 'col', pairs)  6.79 us
    unnamed x13, local copies, waits for them, and re-layouts  3.03 us
    ppermute x5, starting transfers between devices, swap(): lax.ppermute(block, 'row', [(at, (at + 1) % s.rows) for at in range(s.row...  1.22 us
    concatenate x1, local copies, waits for them, and re-layouts, local(): jnp.concatenate([left_gate, left_value, right_gate, right_value], 1)  0.77 us
  transfers between devices with their start and end apart: 13, of which 5 were waited for; matrix products, arithmetic and copies ran while one was open for 10% of the time, Pallas kernels for 24%

profile of v9, /device:TPU:0, one launch (start us, length us, event | category | flops | bytes accessed | tf_op | source)
XLA Modules:
  0.0 32.2 jit_solution(2048409785226495929)
XLA Ops:
  0.0 3.0 %collective-permute-start.2 = (bf16[14,56,128]{2,1,0:T(8,128)(2,1)}, bf16[14,56,128]{2,1,0:T(8,128)(2,1)S(1)}, u32[]{:S(2)}, u32[]{:S(2)}) collective-permute-start(bf16[14,56,128]{2,1,0:T(8,128)(2,1)} %bitcast.4), channel_id=1, source_target_pairs={{0,1},{2,0},{4,2},{6,4},{7,6},{5,7},{3,5},{1,3},{8,9},{10,8},{12,1... | collective-permute-start | bytes 602120 | tf_op jit(solution)/shard_map/ppermute | solution.py:194
  3.0 0.1 collective-permute-start
  3.7 0.8 %constant_dynamic-update-slice_fusion.3 = bf16[128,512]{1,0:T(8,128)(2,1)S(1)} fusion(bf16[128,128]{1,0:T(8,128)(2,1)} %param.13), kind=kLoop, calls=%fused_computation.3 | loop fusion | bytes 65536
  4.5 0.8 %constant_dynamic-update-slice_fusion.2 = bf16[128,512]{1,0:T(8,128)(2,1)S(1)} fusion(bf16[128,512]{1,0:T(8,128)(2,1)S(1)} %constant_dynamic-update-slice_fusion.3, bf16[128,128]{1,0:T(8,128)(2,1)} %param.14), kind=kLoop, calls=%fused_computation.2 | loop fusion | bytes 65536
  5.3 0.8 %constant_dynamic-update-slice_fusion.1 = bf16[128,512]{1,0:T(8,128)(2,1)S(1)} fusion(bf16[128,512]{1,0:T(8,128)(2,1)S(1)} %constant_dynamic-update-slice_fusion.2, bf16[128,128]{1,0:T(8,128)(2,1)} %param.15), kind=kLoop, calls=%fused_computation.1 | loop fusion | bytes 65536
  6.0 0.8 %constant_dynamic-update-slice_fusion.weight = bf16[128,512]{1,0:T(8,128)(2,1)S(1)} fusion(bf16[128,512]{1,0:T(8,128)(2,1)S(1)} %constant_dynamic-update-slice_fusion.1, bf16[128,128]{1,0:T(8,128)(2,1)} %param.16), kind=kLoop, calls=%fused_computation | loop fusion | bytes 65536 | tf_op jit(solution)/shard_map/concatenate | solution.py:189
  6.8 0.6 %copy-done.3 = f32[128]{0:T(128)S(1)} copy-done((f32[128]{0:T(128)S(1)}, f32[128]{0:T(128)}, u32[]{:S(2)}) %copy-start.3) | copy-done | bytes 536
  7.5 0.6 %project.5 = (f32[14,56,128]{2,1,0:T(8,128)S(1)}, bf16[14,16,128]{2,1,0:T(8,128)(2,1)S(1)}) custom-call(s32[1]{0:T(128)S(6)} %copy.14.length, f32[1,128]{1,0:T(1,128)S(1)} %bitcast.8, bf16[128,512]{1,0:T(8,128)(2,1)S(1)} %constant_dynamic-update-slice_fusion.weight, bf16[14,56,128]{2,1,0:T(8,128)(2,1)S(1)} %bitcast.6), custom_call_target="tpu_custom_call" | custom-call | flops 51380224 | bytes 332292 | tf_op jit(solution)/shard_map/project/pallas_call | solution.py:158
  8.0 0.2 collective-permute-done.2.refs_1_
  8.3 1.8 %collective-permute-start.5 = (bf16[14,56,128]{2,1,0:T(8,128)(2,1)S(1)}, bf16[14,56,128]{2,1,0:T(8,128)(2,1)S(1)}, u32[]{:S(2)}, u32[]{:S(2)}) collective-permute-start(bf16[14,56,128]{2,1,0:T(8,128)(2,1)S(1)} %collective-permute-done.2.refs_1_), channel_id=1, source_target_pairs={{0,1},{2,0},{4,2},{6,4},{7,6},{5,7},{3,5},{1,3},{8,9},{10,8},{12,1... | collective-permute-start | bytes 602120 | tf_op jit(solution)/shard_map/ppermute | solution.py:194
  10.1 0.3 collective-permute-start.1
  10.3 0.9 %project.6 = (f32[28,56,128]{2,1,0:T(8,128)S(1)}, bf16[28,16,128]{2,1,0:T(8,128)(2,1)S(1)}) custom-call(s32[1]{0:T(128)S(6)} %copy.14.length, f32[1,128]{1,0:T(1,128)S(1)} %bitcast.9, bf16[128,512]{1,0:T(8,128)(2,1)S(1)} %constant_dynamic-update-slice_fusion.weight, bf16[14,56,128]{2,1,0:T(8,128)(2,1)S(1)} %collective-permute-done.refs_0_, ...), custom_call_target="tpu_custom_call" | custom-call | flops 102760448 | bytes 532996 | tf_op jit(solution)/shard_map/project/pallas_call | solution.py:158
  11.3 0.6 %collective-permute-start.8 = (bf16[28,16,128]{2,1,0:T(8,128)(2,1)S(1)}, bf16[28,16,128]{2,1,0:T(8,128)(2,1)S(1)}, u32[]{:S(2)}, u32[]{:S(2)}) collective-permute-start(bf16[28,16,128]{2,1,0:T(8,128)(2,1)S(1)} %get-tuple-element.34.right), channel_id=1, source_target_pairs={{0,8},{8,0},{1,9},{9,1},{2,10},{10,2},{3,11},{11,3},{4,12},{12,4},... | collective-permute-start | bytes 344072 | tf_op jit(solution)/shard_map/ppermute | solution.py:197
  11.9 0.5 %gate.1 = (f32[14,56,128]{2,1,0:T(8,128)S(1)}, f32[1,128]{1,0:T(1,128)S(1)}, bf16[128,128]{1,0:T(8,128)(2,1)S(1)}) custom-call(bf16[14,56,128]{2,1,0:T(8,128)(2,1)S(1)} %bitcast.7, f32[1,128]{1,0:T(1,128)S(1)} %bitcast.10, bf16[128,128]{1,0:T(8,128)(2,1)S(1)} %copy-done.1, f32[1,128]{1,0:T(1,128)S(1)} %bitcast.14, bf16[128,128]{1,0:T(8,128)(2,1)S(1)} %copy-done.2), custom_call_target="tpu_custom_call" | custom-call | flops 25690112 | bytes 267264 | tf_op jit(solution)/shard_map/gate/pallas_call | solution.py:158
  12.4 0.5 %add_first.1.before = f32[14,56,128]{2,1,0:T(8,128)S(1)} custom-call(f32[14,56,128]{2,1,0:T(8,128)S(1)} %get-tuple-element.29.left, bf16[14,16,128]{2,1,0:T(8,128)(2,1)S(1)} %get-tuple-element.30.right, bf16[14,16,128]{2,1,0:T(8,128)(2,1)S(1)} %collective-permute-done.3.other), custom_call_target="tpu_custom_call" | custom-call | flops 22478848 | bytes 516096 | tf_op jit(solution)/shard_map/add_first/pallas_call | solution.py:158
  12.9 1.7 %collective-permute-done.5.refs_1_ = bf16[14,56,128]{2,1,0:T(8,128)(2,1)S(1)} collective-permute-done((bf16[14,56,128]{2,1,0:T(8,128)(2,1)S(1)}, bf16[14,56,128]{2,1,0:T(8,128)(2,1)S(1)}, u32[]{:S(2)}, u32[]{:S(2)}) %collective-permute-start.5) | collective-permute-done | bytes 200736 | tf_op jit(solution)/shard_map/ppermute | solution.py:194
  14.6 1.6 %collective-permute-start.9 = (bf16[14,56,128]{2,1,0:T(8,128)(2,1)S(1)}, bf16[14,56,128]{2,1,0:T(8,128)(2,1)S(1)}, u32[]{:S(2)}, u32[]{:S(2)}) collective-permute-start(bf16[14,56,128]{2,1,0:T(8,128)(2,1)S(1)} %collective-permute-done.5.refs_1_), channel_id=1, source_target_pairs={{0,1},{2,0},{4,2},{6,4},{7,6},{5,7},{3,5},{1,3},{8,9},{10,8},{12,1... | collective-permute-start | bytes 602120 | tf_op jit(solution)/shard_map/ppermute | solution.py:194
  16.2 0.4 %collective-permute-start.7 = (bf16[14,56,128]{2,1,0:T(8,128)(2,1)S(1)}, bf16[14,56,128]{2,1,0:T(8,128)(2,1)S(1)}, u32[]{:S(2)}, u32[]{:S(2)}) collective-permute-start(bf16[14,56,128]{2,1,0:T(8,128)(2,1)S(1)} %collective-permute-done.1.refs_0_), channel_id=1, source_target_pairs={{0,2},{2,4},{4,6},{6,7},{7,5},{5,3},{3,1},{1,0},{8,10},{10,12},{12... | collective-permute-start | bytes 602120 | tf_op jit(solution)/shard_map/ppermute | solution.py:194
  16.6 0.9 %project.7 = (f32[28,56,128]{2,1,0:T(8,128)S(1)}, bf16[28,16,128]{2,1,0:T(8,128)(2,1)S(1)}) custom-call(s32[1]{0:T(128)S(6)} %copy.14.length, f32[1,128]{1,0:T(1,128)S(1)} %bitcast.11, bf16[128,512]{1,0:T(8,128)(2,1)S(1)} %constant_dynamic-update-slice_fusion.weight, bf16[14,56,128]{2,1,0:T(8,128)(2,1)S(1)} %collective-permute-done.1.refs_0_, ...), custom_call_target="tpu_custom_call" | custom-call | flops 102760448 | bytes 532996 | tf_op jit(solution)/shard_map/project/pallas_call | solution.py:158
  17.5 0.1 collective-permute-start.10
  17.7 2.7 %collective-permute-start.6 = (bf16[7,56,128]{2,1,0:T(8,128)(2,1)S(1)}, bf16[7,56,128]{2,1,0:T(8,128)(2,1)S(1)}, u32[]{:S(2)}, u32[]{:S(2)}) collective-permute-start(bf16[7,56,128]{2,1,0:T(8,128)(2,1)S(1)} %slice.7), channel_id=1, source_target_pairs={{0,3},{2,1},{4,0},{6,2},{7,4},{5,6},{3,7},{1,5},{8,11},{10,9},{12,... | collective-permute-start | bytes 301064 | tf_op jit(solution)/shard_map/ppermute | solution.py:194
  20.4 0.3 collective-permute-start.4
  20.6 0.9 %add_more.3.before = f32[14,56,128]{2,1,0:T(8,128)S(1)} custom-call(f32[28,56,128]{2,1,0:T(8,128)S(1)} %get-tuple-element.33.left, bf16[28,16,128]{2,1,0:T(8,128)(2,1)S(1)} %get-tuple-element.34.right, bf16[28,16,128]{2,1,0:T(8,128)(2,1)S(1)} %collective-permute-done.8.other, f32[14,56,128]{2,1,0:T(8,128)S(1)} %add_first.1.before), custom_call_target="tpu_custom_call" | custom-call | flops 44957696 | bytes 1433600 | tf_op jit(solution)/shard_map/add_more/pallas_call | solution.py:158
  21.6 0.9 %add_more.4.before = f32[14,56,128]{2,1,0:T(8,128)S(1)} custom-call(f32[28,56,128]{2,1,0:T(8,128)S(1)} %get-tuple-element.40.left, bf16[28,16,128]{2,1,0:T(8,128)(2,1)S(1)} %get-tuple-element.41.right, bf16[28,16,128]{2,1,0:T(8,128)(2,1)S(1)} %collective-permute-done.10.other, f32[14,56,128]{2,1,0:T(8,128)S(1)} %add_more.3.before), custom_call_target="tpu_custom_call" | custom-call | flops 44957696 | bytes 1433600 | tf_op jit(solution)/shard_map/add_more/pallas_call | solution.py:158
  22.5 0.9 %project.8 = (f32[28,56,128]{2,1,0:T(8,128)S(1)}, bf16[28,16,128]{2,1,0:T(8,128)(2,1)S(1)}) custom-call(s32[1]{0:T(128)S(6)} %copy.14.length, f32[1,128]{1,0:T(1,128)S(1)} %bitcast.12, bf16[128,512]{1,0:T(8,128)(2,1)S(1)} %constant_dynamic-update-slice_fusion.weight, bf16[14,56,128]{2,1,0:T(8,128)(2,1)S(1)} %collective-permute-done.7.refs_0_, ...), custom_call_target="tpu_custom_call" | custom-call | flops 102760448 | bytes 532996 | tf_op jit(solution)/shard_map/project/pallas_call | solution.py:158
  23.5 2.6 %collective-permute-done.6.refs_1_ = bf16[7,56,128]{2,1,0:T(8,128)(2,1)S(1)} collective-permute-done((bf16[7,56,128]{2,1,0:T(8,128)(2,1)S(1)}, bf16[7,56,128]{2,1,0:T(8,128)(2,1)S(1)}, u32[]{:S(2)}, u32[]{:S(2)}) %collective-permute-start.6) | collective-permute-done | bytes 100384 | tf_op jit(solution)/shard_map/ppermute | solution.py:194
  26.1 2.3 %collective-permute-done.4.refs_0_ = bf16[7,56,128]{2,1,0:T(8,128)(2,1)S(1)} collective-permute-done((bf16[7,56,128]{2,1,0:T(8,128)(2,1)S(1)}, bf16[7,56,128]{2,1,0:T(8,128)(2,1)S(1)}, u32[]{:S(2)}, u32[]{:S(2)}) %collective-permute-start.4) | collective-permute-done | bytes 100384 | tf_op jit(solution)/shard_map/ppermute | solution.py:194
  28.3 0.6 %project.9 = (f32[14,56,128]{2,1,0:T(8,128)S(1)}, bf16[14,16,128]{2,1,0:T(8,128)(2,1)S(1)}) custom-call(s32[1]{0:T(128)S(6)} %copy.14.length, f32[1,128]{1,0:T(1,128)S(1)} %bitcast.13, bf16[128,512]{1,0:T(8,128)(2,1)S(1)} %constant_dynamic-update-slice_fusion.weight, bf16[7,56,128]{2,1,0:T(8,128)(2,1)S(1)} %collective-permute-done.4.refs_0_, ...), custom_call_target="tpu_custom_call" | custom-call | flops 51380224 | bytes 332292 | tf_op jit(solution)/shard_map/project/pallas_call | solution.py:158
  28.9 0.6 %collective-permute-start.11 = (bf16[14,16,128]{2,1,0:T(8,128)(2,1)S(1)}, bf16[14,16,128]{2,1,0:T(8,128)(2,1)S(1)}, u32[]{:S(2)}, u32[]{:S(2)}) collective-permute-start(bf16[14,16,128]{2,1,0:T(8,128)(2,1)S(1)} %get-tuple-element.49.right), channel_id=1, source_target_pairs={{0,8},{8,0},{1,9},{9,1},{2,10},{10,2},{3,11},{11,3},{4,12},{12,4},... | collective-permute-start | bytes 172040 | tf_op jit(solution)/shard_map/ppermute | solution.py:197
  29.5 0.2 collective-permute-done.12.other
  29.7 0.9 %add_more.5.before = f32[14,56,128]{2,1,0:T(8,128)S(1)} custom-call(f32[28,56,128]{2,1,0:T(8,128)S(1)} %get-tuple-element.50.left, bf16[28,16,128]{2,1,0:T(8,128)(2,1)S(1)} %get-tuple-element.51.right, bf16[28,16,128]{2,1,0:T(8,128)(2,1)S(1)} %collective-permute-done.12.other, f32[14,56,128]{2,1,0:T(8,128)S(1)} %add_more.4.before), custom_call_target="tpu_custom_call" | custom-call | flops 44957696 | bytes 1433600 | tf_op jit(solution)/shard_map/add_more/pallas_call | solution.py:158
  30.6 1.6 %finish.1 = bf16[14,56,128]{2,1,0:T(8,128)(2,1)} custom-call(f32[14,56,128]{2,1,0:T(8,128)S(1)} %get-tuple-element.48.left, bf16[14,16,128]{2,1,0:T(8,128)(2,1)S(1)} %get-tuple-element.49.right, bf16[14,16,128]{2,1,0:T(8,128)(2,1)S(1)} %collective-permute-done.11.other, f32[14,56,128]{2,1,0:T(8,128)S(1)} %add_more.5.before, ...), custom_call_target="tpu_custom_call" | custom-call | flops 22478848 | bytes 1352192 | tf_op jit(solution)/shard_map/finish/pallas_call | solution.py:158
  (21 shorter events, 0.1 us)
Async XLA Ops:
  0.0 6.8 %copy-start = (bf16[56,14,128]{2,0,1:T(8,128)(2,1)S(1)}, bf16[56,14,128]{2,0,1:T(8,128)(2,1)}, u32[]{:S(2)}) copy-start(bf16[56,14,128]{2,0,1:T(8,128)(2,1)} %param.10) | copy-start | bytes 602116
  0.0 8.3 %collective-permute-start.2 = (bf16[14,56,128]{2,1,0:T(8,128)(2,1)}, bf16[14,56,128]{2,1,0:T(8,128)(2,1)S(1)}, u32[]{:S(2)}, u32[]{:S(2)}) collective-permute-start(bf16[14,56,128]{2,1,0:T(8,128)(2,1)} %bitcast.4), channel_id=1, source_target_pairs={{0,1},{2,0},{4,2},{6,4},{7,6},{5,7},{3,5},{1,3},{8,9},{10,8},{12,1... | collective-permute-start | bytes 602120 | tf_op jit(solution)/shard_map/ppermute | solution.py:194
  3.0 7.1 %collective-permute-start = (bf16[14,56,128]{2,1,0:T(8,128)(2,1)}, bf16[14,56,128]{2,1,0:T(8,128)(2,1)S(1)}, u32[]{:S(2)}, u32[]{:S(2)}) collective-permute-start(bf16[14,56,128]{2,1,0:T(8,128)(2,1)} %bitcast.5), channel_id=1, source_target_pairs={{0,2},{2,4},{4,6},{6,7},{7,5},{5,3},{3,1},{1,0},{8,10},{10,12},{12... | collective-permute-start | bytes 602120 | tf_op jit(solution)/shard_map/ppermute | solution.py:194
  6.8 0.7 %copy-start.3 = (f32[128]{0:T(128)S(1)}, f32[128]{0:T(128)}, u32[]{:S(2)}) copy-start(f32[128]{0:T(128)} %param.12) | copy-start | bytes 1540
  8.3 3.6 %copy-start.1 = (bf16[128,128]{1,0:T(8,128)(2,1)S(1)}, bf16[128,128]{1,0:T(8,128)(2,1)}, u32[]{:S(2)}) copy-start(bf16[128,128]{1,0:T(8,128)(2,1)} %out_gate.1) | copy-start | bytes 98308
  8.3 3.6 %copy-start.2 = (bf16[128,128]{1,0:T(8,128)(2,1)S(1)}, bf16[128,128]{1,0:T(8,128)(2,1)}, u32[]{:S(2)}) copy-start(bf16[128,128]{1,0:T(8,128)(2,1)} %last_weight.1) | copy-start | bytes 98308
  8.3 6.3 %collective-permute-start.5 = (bf16[14,56,128]{2,1,0:T(8,128)(2,1)S(1)}, bf16[14,56,128]{2,1,0:T(8,128)(2,1)S(1)}, u32[]{:S(2)}, u32[]{:S(2)}) collective-permute-start(bf16[14,56,128]{2,1,0:T(8,128)(2,1)S(1)} %collective-permute-done.2.refs_1_), channel_id=1, source_target_pairs={{0,1},{2,0},{4,2},{6,4},{7,6},{5,7},{3,5},{1,3},{8,9},{10,8},{12,1... | collective-permute-start | bytes 602120 | tf_op jit(solution)/shard_map/ppermute | solution.py:194
  10.1 6.2 %collective-permute-start.1 = (bf16[14,56,128]{2,1,0:T(8,128)(2,1)S(1)}, bf16[14,56,128]{2,1,0:T(8,128)(2,1)S(1)}, u32[]{:S(2)}, u32[]{:S(2)}) collective-permute-start(bf16[14,56,128]{2,1,0:T(8,128)(2,1)S(1)} %collective-permute-done.refs_0_), channel_id=1, source_target_pairs={{0,2},{2,4},{4,6},{6,7},{7,5},{5,3},{3,1},{1,0},{8,10},{10,12},{12... | collective-permute-start | bytes 602120 | tf_op jit(solution)/shard_map/ppermute | solution.py:194
  10.3 2.1 %collective-permute-start.3 = (bf16[14,16,128]{2,1,0:T(8,128)(2,1)S(1)}, bf16[14,16,128]{2,1,0:T(8,128)(2,1)S(1)}, u32[]{:S(2)}, u32[]{:S(2)}) collective-permute-start(bf16[14,16,128]{2,1,0:T(8,128)(2,1)S(1)} %get-tuple-element.30.right), channel_id=1, source_target_pairs={{0,8},{8,0},{1,9},{9,1},{2,10},{10,2},{3,11},{11,3},{4,12},{12,4},... | collective-permute-start | bytes 172040 | tf_op jit(solution)/shard_map/ppermute | solution.py:197
  11.3 0.7 %copy-start.4 = (f32[128]{0:T(128)S(1)}, f32[128]{0:T(128)}, u32[]{:S(2)}) copy-start(f32[128]{0:T(128)} %param.18) | copy-start | bytes 1540
  11.3 9.1 %collective-permute-start.8 = (bf16[28,16,128]{2,1,0:T(8,128)(2,1)S(1)}, bf16[28,16,128]{2,1,0:T(8,128)(2,1)S(1)}, u32[]{:S(2)}, u32[]{:S(2)}) collective-permute-start(bf16[28,16,128]{2,1,0:T(8,128)(2,1)S(1)} %get-tuple-element.34.right), channel_id=1, source_target_pairs={{0,8},{8,0},{1,9},{9,1},{2,10},{10,2},{3,11},{11,3},{4,12},{12,4},... | collective-permute-start | bytes 344072 | tf_op jit(solution)/shard_map/ppermute | solution.py:197
  14.6 7.9 %collective-permute-start.9 = (bf16[14,56,128]{2,1,0:T(8,128)(2,1)S(1)}, bf16[14,56,128]{2,1,0:T(8,128)(2,1)S(1)}, u32[]{:S(2)}, u32[]{:S(2)}) collective-permute-start(bf16[14,56,128]{2,1,0:T(8,128)(2,1)S(1)} %collective-permute-done.5.refs_1_), channel_id=1, source_target_pairs={{0,1},{2,0},{4,2},{6,4},{7,6},{5,7},{3,5},{1,3},{8,9},{10,8},{12,1... | collective-permute-start | bytes 602120 | tf_op jit(solution)/shard_map/ppermute | solution.py:194
  16.2 6.3 %collective-permute-start.7 = (bf16[14,56,128]{2,1,0:T(8,128)(2,1)S(1)}, bf16[14,56,128]{2,1,0:T(8,128)(2,1)S(1)}, u32[]{:S(2)}, u32[]{:S(2)}) collective-permute-start(bf16[14,56,128]{2,1,0:T(8,128)(2,1)S(1)} %collective-permute-done.1.refs_0_), channel_id=1, source_target_pairs={{0,2},{2,4},{4,6},{6,7},{7,5},{5,3},{3,1},{1,0},{8,10},{10,12},{12... | collective-permute-start | bytes 602120 | tf_op jit(solution)/shard_map/ppermute | solution.py:194
  17.5 4.0 %collective-permute-start.10 = (bf16[28,16,128]{2,1,0:T(8,128)(2,1)S(1)}, bf16[28,16,128]{2,1,0:T(8,128)(2,1)S(1)}, u32[]{:S(2)}, u32[]{:S(2)}) collective-permute-start(bf16[28,16,128]{2,1,0:T(8,128)(2,1)S(1)} %get-tuple-element.41.right), channel_id=1, source_target_pairs={{0,8},{8,0},{1,9},{9,1},{2,10},{10,2},{3,11},{11,3},{4,12},{12,4},... | collective-permute-start | bytes 344072 | tf_op jit(solution)/shard_map/ppermute | solution.py:197
  17.7 8.4 %collective-permute-start.6 = (bf16[7,56,128]{2,1,0:T(8,128)(2,1)S(1)}, bf16[7,56,128]{2,1,0:T(8,128)(2,1)S(1)}, u32[]{:S(2)}, u32[]{:S(2)}) collective-permute-start(bf16[7,56,128]{2,1,0:T(8,128)(2,1)S(1)} %slice.7), channel_id=1, source_target_pairs={{0,3},{2,1},{4,0},{6,2},{7,4},{5,6},{3,7},{1,5},{8,11},{10,9},{12,... | collective-permute-start | bytes 301064 | tf_op jit(solution)/shard_map/ppermute | solution.py:194
  20.4 8.0 %collective-permute-start.4 = (bf16[7,56,128]{2,1,0:T(8,128)(2,1)S(1)}, bf16[7,56,128]{2,1,0:T(8,128)(2,1)S(1)}, u32[]{:S(2)}, u32[]{:S(2)}) collective-permute-start(bf16[7,56,128]{2,1,0:T(8,128)(2,1)S(1)} %slice.6), channel_id=1, source_target_pairs={{0,4},{2,6},{4,7},{6,5},{7,3},{5,1},{3,0},{1,2},{8,12},{10,14},{12... | collective-permute-start | bytes 301064 | tf_op jit(solution)/shard_map/ppermute | solution.py:194
  28.3 1.3 %collective-permute-start.12 = (bf16[28,16,128]{2,1,0:T(8,128)(2,1)S(1)}, bf16[28,16,128]{2,1,0:T(8,128)(2,1)S(1)}, u32[]{:S(2)}, u32[]{:S(2)}) collective-permute-start(bf16[28,16,128]{2,1,0:T(8,128)(2,1)S(1)} %get-tuple-element.51.right), channel_id=1, source_target_pairs={{0,8},{8,0},{1,9},{9,1},{2,10},{10,2},{3,11},{11,3},{4,12},{12,4},... | collective-permute-start | bytes 344072 | tf_op jit(solution)/shard_map/ppermute | solution.py:197
  28.9 1.7 %collective-permute-start.11 = (bf16[14,16,128]{2,1,0:T(8,128)(2,1)S(1)}, bf16[14,16,128]{2,1,0:T(8,128)(2,1)S(1)}, u32[]{:S(2)}, u32[]{:S(2)}) collective-permute-start(bf16[14,16,128]{2,1,0:T(8,128)(2,1)S(1)} %get-tuple-element.49.right), channel_id=1, source_target_pairs={{0,8},{8,0},{1,9},{9,1},{2,10},{10,2},{3,11},{11,3},{4,12},{12,4},... | collective-permute-start | bytes 172040 | tf_op jit(solution)/shard_map/ppermute | solution.py:197

commit v10 on v7

--- a/solution.py
+++ b/solution.py
@@ -93,19 +93,8 @@
             gating[start + step] = value[step * s.height : (step + 1) * s.height]
 
 
-def accumulate(s, left, right, other, before, total, partner):
-    row, col = lax.axis_index("row"), lax.axis_index("col")
-    owner = col // (s.height // s.width)
+def accumulate(s, left, partner, before, total):
     depth = left.shape[0]
-
-    @pl.when(row == owner)
-    def _():
-        partner[:depth] = right[...].astype(F32)
-
-    @pl.when(row != owner)
-    def _():
-        partner[:depth] = other[...].astype(F32)
-
     size = CHUNK if s.height % CHUNK == 0 else s.height
     group = GROUP if s.width % GROUP == 0 else 1
 
@@ -133,17 +122,96 @@
 
 
 def add_first(s, left, right, other, total, partner):
-    accumulate(s, left, right, other, None, total, partner)
-
-
-def add_more(s, left, right, other, before, total, partner):
-    accumulate(s, left, right, other, before, total, partner)
-
-
-def finish(s, left, right, other, before, gating, gain, weight, update, total, partner):
-    accumulate(s, left, right, other, before, total, partner)
+    row, col = lax.axis_index("row"), lax.axis_index("col")
+    choose(row == owner_of(s, col), right, other, partner)
+    accumulate(s, left, partner, None, total)
+
+
+def owner_of(s, col):
+    return col // (s.height // s.width)
+
+
+def choose(first, one, other, target):
+    @pl.when(first)
+    def _():
+        target[...] = one[...].astype(F32)
+
+    @pl.when(jnp.logical_not(first))
+    def _():
+        target[...] = other[...].astype(F32)
+
+
+def first_token(s, distance, halved):
+    row, col = lax.axis_index("row"), lax.axis_index("col")
+    step = distance * (2 * row - 1)
+    token = column_at((place_of(col, s.cols) + step + s.cols) % s.cols, s.cols) * s.width
+    return token + row * s.half if halved else token
+
+
+def project_right(s, own, other, token, limit, gain, weight, picked, partner):
+    row, col = lax.axis_index("row"), lax.axis_index("col")
+    h, depth = s.hidden, own.shape[0]
+    choose(row == owner_of(s, col), own, other, picked.at[:, : s.height])
+    offset = (col % (s.height // s.width)) * s.width
+    mine = lax.broadcasted_iota(jnp.int32, (s.slots, 1), 0) + col * s.width < limit
+    for start in range(0, depth, s.half):
+        rows = [
+            normalise(picked[start + step, pl.ds(offset, s.slots), :]) * gain[...]
+            for step in range(s.half)
+        ]
+        out = dot(jnp.concatenate(rows, 0).astype(BF16), weight[:, 2 * h :])
+        value = sigmoid(out[:, :h]) * out[:, h:]
+        for step in range(s.half):
+            mask = (mine & (token + start + step < limit)).astype(F32)
+            partner[start + step] = value[step * s.slots : (step + 1) * s.slots] * mask
+
+
+def project_left(s, block, row, token, limit, gain, weight, left):
+    h = s.hidden
+    below = lax.broadcasted_iota(jnp.int32, (s.height, 1), 0) + row * s.height < limit
+    for start in range(0, block.shape[0], s.half):
+        rows = [
+            normalise(block[start + step].astype(F32)) * gain[...] for step in range(s.half)
+        ]
+        out = dot(jnp.concatenate(rows, 0).astype(BF16), weight[:, : 2 * h])
+        value = sigmoid(out[:, :h]) * out[:, h:]
+        for step in range(s.half):
+            mask = (below & (token + start + step < limit)).astype(F32)
+            left[start + step] = value[step * s.height : (step + 1) * s.height] * mask
+
+
+def add_both(s, distance, length, gain, weight, own, other, *refs):
+    before, (mine, theirs, left, right, picked, partner) = refs[:-6], refs[-6:]
+    row, limit = lax.axis_index("row"), length[0]
+    token = first_token(s, distance, False)
+    project_right(s, own, other, token, limit, gain, weight, picked, partner)
+    project_left(s, own, row, token, limit, gain, weight, left)
+    project_left(s, other, 1 - row, token, limit, gain, weight, right)
+    accumulate(s, left, partner, before[0], mine)
+    accumulate(s, right, partner, before[1] if len(before) > 1 else None, theirs)
+
+
+def add_theirs(s, distance, length, gain, weight, own, other, before, theirs, partner, left, picked, total):
+    row, limit = lax.axis_index("row"), length[0]
+    token = first_token(s, distance, True)
+    project_right(s, own, other, token, limit, gain, weight, picked, partner)
+    project_left(s, other, 1 - row, token, limit, gain, weight, left)
+    accumulate(s, left, partner, before, total)
+    theirs[...] = total[...].astype(BF16)
+
+
+def add_mine(s, distance, length, gain, weight, own, before, partner, mine, left):
+    token = first_token(s, distance, True)
+    project_left(s, own, lax.axis_index("row"), token, length[0], gain, weight, left)
+    accumulate(s, left, partner, before, mine)
+
+
+def finish(s, mine, given, gating, gain, weight, update):
     for start in range(0, s.width, s.half):
-        settled = [normalise(total[start + step]) * gain[...] for step in range(s.half)]
+        settled = [
+            normalise(mine[start + step] + given[start + step].astype(F32)) * gain[...]
+            for step in range(s.half)
+        ]
         value = dot(jnp.concatenate(settled, 0).astype(BF16), weight[...])
         for step in range(s.half):
             part = gating[start + step] * value[step * s.height : (step + 1) * s.height]
@@ -189,9 +257,14 @@
     weights = jnp.concatenate([left_gate, left_value, right_gate, right_value], 1)
     order = ring(s.cols)
 
-    def shift(block, by):
-        pairs = [(order[at], order[(at + by) % s.cols]) for at in range(s.cols)]
-        return lax.ppermute(block, "col", pairs)
+    def shift(block, crossed=False):
+        pairs = []
+        for row in range(s.rows):
+            target = s.rows - 1 - row if crossed else row
+            for at in range(s.cols):
+                to = (at + 1 - 2 * target) % s.cols
+                pairs.append((row * s.cols + order[at], target * s.cols + order[to]))
+        return lax.ppermute(block, ("row", "col"), pairs)
 
     def swap(block):
         return lax.ppermute(block, "row", [(at, (at + 1) % s.rows) for at in range(s.rows)])
@@ -211,70 +284,107 @@
 
     starts = (0, s.half)
     sums = shape((width, height, hidden), F32)
-
-    def add(total, terms):
-        left, right = terms
-        depth = left.shape[0]
-        body, before = (add_first, ()) if total is None else (add_more, (total,))
-        return call(
-            functools.partial(body, s),
-            sums,
-            [pltpu.VMEM((depth, s.slots, hidden), F32)],
-            16 * depth * height * width * hidden,
-            left,
-            right,
-            swap(right),
-            *before,
-        )
-
-    def whole(distances):
-        return [
-            (block, at, distance, at) for block, distance in enumerate(distances) for at in starts
-        ]
+    last_row = output_gain.reshape(1, hidden)
+    product = 16 * height * width * hidden
+
+    def tokens(depth):
+        return pltpu.VMEM((depth, height, hidden), F32)
+
+    def picked(depth):
+        return pltpu.VMEM((depth, height + TILE, channels), F32)
+
+    def right(depth):
+        return shape((depth, s.slots, hidden), F32)
+
+    def held(depth):
+        return pltpu.VMEM(right(depth).shape, F32)
 
     far = s.cols // 2
-    blocks, sources, travel = [pair], whole([0]), [pair, pair]
-    total = terms = kept = None
-    for distance in range(1, far + 1):
-        if distance == far:
-            travel = [travel[0][: s.half], travel[1][s.half :]]
-        arrived = [shift(block, by) for block, by in zip(travel, (1, -1))]
-        pending = run(blocks, sources)
-        if distance == 2:
+    left, partner = run([pair], [(0, at, 0, at) for at in starts])
+    own, other = shift(pair), shift(pair, crossed=True)
+    given = swap(partner)
+    done = (left, partner)
+    total = kept = None
+    for distance in range(1, far):
+        own, other = [lax.optimization_barrier((block, done))[0] for block in (own, other)]
+        if distance < far - 1:
+            ahead = [shift(own), shift(other)]
+        else:
+            start = lax.axis_index("row") * s.half
+            ahead = [
+                shift(lax.dynamic_slice_in_dim(block, start, s.half, 0)) for block in (own, other)
+            ]
             kept = call(
                 functools.partial(gate, s),
-                [
-                    shape((width, height, channels), F32),
-                    shape((1, hidden), F32),
-                    shape(out_weight.shape, BF16),
-                ],
+                [shape(sums.shape, F32), shape((1, hidden), F32), shape(out_weight.shape, BF16)],
                 [],
                 2 * height * width * channels * channels,
                 pair,
                 gain,
                 out_gate,
-                output_gain.reshape(1, hidden),
+                last_row,
                 out_weight,
             )
-        if terms is not None:
-            total = add(total, terms)
-        terms = pending
-        done = (terms, total, kept)
-        travel = [lax.optimization_barrier((block, done))[0] for block in arrived]
-        blocks, sources = arrived, whole([-distance, distance])
-    left, right = run(travel, [(0, 0, -far, 0), (1, 0, far, s.half)])
-    other = swap(right)
-    total = add(total, terms)
-    gating, last_gain, last_weight = kept
+        if total is None:
+            total = [
+                call(
+                    functools.partial(add_first, s),
+                    sums,
+                    [held(width)],
+                    width * product,
+                    left,
+                    partner,
+                    given,
+                )
+            ]
+        total = call(
+            functools.partial(add_both, s, distance),
+            [sums, sums],
+            [tokens(width), tokens(width), picked(width), held(width)],
+            2 * width * product,
+            valid_length,
+            gain,
+            weights,
+            own,
+            other,
+            *total,
+        )
+        done = (total, kept)
+        own, other = ahead
+    own, other, done = lax.optimization_barrier((own, other, done))
+    (mine, theirs), (gating, last_gain, last_weight) = done
+    theirs, partner = call(
+        functools.partial(add_theirs, s, far),
+        [shape(sums.shape, BF16), right(s.half)],
+        [tokens(s.half), picked(s.half), pltpu.VMEM(sums.shape, F32)],
+        s.half * product,
+        valid_length,
+        gain,
+        weights,
+        own,
+        other,
+        theirs,
+    )
+    given = swap(theirs)
+    mine = call(
+        functools.partial(add_mine, s, far),
+        sums,
+        [tokens(s.half)],
+        s.half * product,
+        valid_length,
+        gain,
+        weights,
+        own,
+        mine,
+        partner,
+    )
     update = call(
         functools.partial(finish, s),
         shape((width, height, channels), BF16),
-        [pltpu.VMEM(sums.shape, F32), pltpu.VMEM((left.shape[0], s.slots, hidden), F32)],
-        16 * width * height * width * hidden,
-        left,
-        right,
-        other,
-        total,
+        [],
+        2 * height * width * channels * hidden,
+        mine,
+        given,
         gating,
         last_gain,
         last_weight,

time: 30.7 us -> 33.1 us (1.078)
  starting transfers between devices: 9.92 us -> 13 us
  waiting for transfers between devices: 6.53 us -> 5.92 us
    ppermute x8, starting transfers between devices: 9.21 us -> 12.9 us  [shift(): return lax.ppermute(block, ('row', 'col'), pairs)]
    ppermute x8, waiting for transfers between devices: 5.51 us -> 3.85 us  [shift(): return lax.ppermute(block, ('row', 'col'), pairs)]
    ppermute x5 -> x2, waiting for transfers between devices: 1.01 us -> 2.08 us  [swap(): lax.ppermute(block, 'row', [(at, (at + 1) % s.rows) for at in range(s.row...]
    ppermute x5 -> x2, starting transfers between devices: 0.71 us -> 0.07 us  [swap(): lax.ppermute(block, 'row', [(at, (at + 1) % s.rows) for at in range(s.row...]
    pallas_call x11 -> x9, Pallas kernels: 9.3 us -> 9.23 us  [call(): pl.pallas_call(body, out_shape=out_shape, in_specs=[space(o) for o in ope...]
  transfers between devices with their start and end apart: 13 -> 10, of which waited for: 7 -> 5; matrix products, arithmetic and copies ran while one was open for 10% -> 9% of each run, Pallas kernels for 25% -> 23%
where the time goes in v10:
time: 33.1 us; the launch traced here: 32.7 us
  starting transfers between devices  13 us (39%)
  Pallas kernels  9.23 us (28%)
  waiting for transfers between devices  5.92 us (18%)
  local copies, waits for them, and re-layouts  3.76 us (11%)
  between operations  0.79 us (2%)
    ppermute x8, starting transfers between devices, shift(): return lax.ppermute(block, ('row', 'col'), pairs)  12.9 us
    pallas_call x9, Pallas kernels, call(): pl.pallas_call(body, out_shape=out_shape, in_specs=[space(o) for o in ope...  9.23 us
    ppermute x8, waiting for transfers between devices, shift(): return lax.ppermute(block, ('row', 'col'), pairs)  3.85 us
    unnamed x13, local copies, waits for them, and re-layouts  2.97 us
    ppermute x2, waiting for transfers between devices, swap(): lax.ppermute(block, 'row', [(at, (at + 1) % s.rows) for at in range(s.row...  2.08 us
    concatenate x1, local copies, waits for them, and re-layouts, local(): jnp.concatenate([left_gate, left_value, right_gate, right_value], 1)  0.77 us
  transfers between devices with their start and end apart: 10, of which 5 were waited for; matrix products, arithmetic and copies ran while one was open for 9% of the time, Pallas kernels for 23%

profile of v10, /device:TPU:0, one launch (start us, length us, event | category | flops | bytes accessed | tf_op | source)
XLA Modules:
  0.0 32.7 jit_solution(182609588228160900)
XLA Ops:
  0.0 2.4 %collective-permute-start.2 = (bf16[14,56,128]{2,1,0:T(8,128)(2,1)}, bf16[14,56,128]{2,1,0:T(8,128)(2,1)S(1)}, u32[]{:S(2)}, u32[]{:S(2)}) collective-permute-start(bf16[14,56,128]{2,1,0:T(8,128)(2,1)} %bitcast.4), channel_id=1, source_target_pairs={{0,9},{2,8},{4,10},{6,12},{7,14},{5,15},{3,13},{1,11},{8,2},{10,4}... | collective-permute-start | bytes 602120 | tf_op jit(solution)/shard_map/ppermute | solution.py:267
  2.4 0.7 %collective-permute-start = (bf16[14,56,128]{2,1,0:T(8,128)(2,1)}, bf16[14,56,128]{2,1,0:T(8,128)(2,1)S(1)}, u32[]{:S(2)}, u32[]{:S(2)}) collective-permute-start(bf16[14,56,128]{2,1,0:T(8,128)(2,1)} %bitcast.5), channel_id=1, source_target_pairs={{0,2},{2,4},{4,6},{6,7},{7,5},{5,3},{3,1},{1,0},{8,9},{10,8},{12,1... | collective-permute-start | bytes 602120 | tf_op jit(solution)/shard_map/ppermute | solution.py:267
  3.1 0.8 %constant_dynamic-update-slice_fusion.3 = bf16[128,512]{1,0:T(8,128)(2,1)S(1)} fusion(bf16[128,128]{1,0:T(8,128)(2,1)} %param.13), kind=kLoop, calls=%fused_computation.3 | loop fusion | bytes 65536
  4.5 0.8 %constant_dynamic-update-slice_fusion.2 = bf16[128,512]{1,0:T(8,128)(2,1)S(1)} fusion(bf16[128,512]{1,0:T(8,128)(2,1)S(1)} %constant_dynamic-update-slice_fusion.3, bf16[128,128]{1,0:T(8,128)(2,1)} %param.14), kind=kLoop, calls=%fused_computation.2 | loop fusion | bytes 65536
  5.3 0.8 %constant_dynamic-update-slice_fusion.1 = bf16[128,512]{1,0:T(8,128)(2,1)S(1)} fusion(bf16[128,512]{1,0:T(8,128)(2,1)S(1)} %constant_dynamic-update-slice_fusion.2, bf16[128,128]{1,0:T(8,128)(2,1)} %param.15), kind=kLoop, calls=%fused_computation.1 | loop fusion | bytes 65536
  6.0 0.8 %constant_dynamic-update-slice_fusion.weight = bf16[128,512]{1,0:T(8,128)(2,1)S(1)} fusion(bf16[128,512]{1,0:T(8,128)(2,1)S(1)} %constant_dynamic-update-slice_fusion.1, bf16[128,128]{1,0:T(8,128)(2,1)} %param.16), kind=kLoop, calls=%fused_computation | loop fusion | bytes 65536 | tf_op jit(solution)/shard_map/concatenate | solution.py:257
  6.8 0.6 %copy-done.3 = f32[128]{0:T(128)S(1)} copy-done((f32[128]{0:T(128)S(1)}, f32[128]{0:T(128)}, u32[]{:S(2)}) %copy-start.3) | copy-done | bytes 536
  7.5 0.6 %project.1 = (f32[14,56,128]{2,1,0:T(8,128)S(1)}, bf16[14,16,128]{2,1,0:T(8,128)(2,1)S(1)}) custom-call(s32[1]{0:T(128)S(6)} %copy.14.length, f32[1,128]{1,0:T(1,128)S(1)} %bitcast.8, bf16[128,512]{1,0:T(8,128)(2,1)S(1)} %constant_dynamic-update-slice_fusion.weight, bf16[14,56,128]{2,1,0:T(8,128)(2,1)S(1)} %bitcast.6), custom_call_target="tpu_custom_call" | custom-call | flops 51380224 | bytes 332292 | tf_op jit(solution)/shard_map/project/pallas_call | solution.py:226
  8.1 0.0 collective-permute-done.2.other
  8.1 1.9 %collective-permute-start.5 = (bf16[14,56,128]{2,1,0:T(8,128)(2,1)S(1)}, bf16[14,56,128]{2,1,0:T(8,128)(2,1)S(1)}, u32[]{:S(2)}, u32[]{:S(2)}) collective-permute-start(bf16[14,56,128]{2,1,0:T(8,128)(2,1)S(1)} %collective-permute-done.2.other), channel_id=1, source_target_pairs={{0,2},{2,4},{4,6},{6,7},{7,5},{5,3},{3,1},{1,0},{8,9},{10,8},{12,1... | collective-permute-start | bytes 602120 | tf_op jit(solution)/shard_map/ppermute | solution.py:267
  10.0 1.6 %collective-permute-start.1 = (bf16[14,56,128]{2,1,0:T(8,128)(2,1)S(1)}, bf16[14,56,128]{2,1,0:T(8,128)(2,1)S(1)}, u32[]{:S(2)}, u32[]{:S(2)}) collective-permute-start(bf16[14,56,128]{2,1,0:T(8,128)(2,1)S(1)} %collective-permute-done.own), channel_id=1, source_target_pairs={{0,2},{2,4},{4,6},{6,7},{7,5},{5,3},{3,1},{1,0},{8,9},{10,8},{12,1... | collective-permute-start | bytes 602120 | tf_op jit(solution)/shard_map/ppermute | solution.py:267
  11.5 1.2 %collective-permute-done.3.other = bf16[14,16,128]{2,1,0:T(8,128)(2,1)S(1)} collective-permute-done((bf16[14,16,128]{2,1,0:T(8,128)(2,1)S(1)}, bf16[14,16,128]{2,1,0:T(8,128)(2,1)S(1)}, u32[]{:S(2)}, u32[]{:S(2)}) %collective-permute-start.3) | collective-permute-done | bytes 57376 | tf_op jit(solution)/shard_map/ppermute | solution.py:270
  12.8 0.5 %add_first.1.refs_0_ = f32[14,56,128]{2,1,0:T(8,128)S(1)} custom-call(f32[14,56,128]{2,1,0:T(8,128)S(1)} %get-tuple-element.31.left, bf16[14,16,128]{2,1,0:T(8,128)(2,1)S(1)} %get-tuple-element.32.right, bf16[14,16,128]{2,1,0:T(8,128)(2,1)S(1)} %collective-permute-done.3.other), custom_call_target="tpu_custom_call" | custom-call | flops 22478848 | bytes 516096 | tf_op jit(solution)/shard_map/add_first/pallas_call | solution.py:226
  13.3 1.8 %add_both.3 = (f32[14,56,128]{2,1,0:T(8,128)S(1)}, f32[14,56,128]{2,1,0:T(8,128)S(1)}) custom-call(s32[1]{0:T(128)S(6)} %copy.14.length, f32[1,128]{1,0:T(1,128)S(1)} %bitcast.9, bf16[128,512]{1,0:T(8,128)(2,1)S(1)} %constant_dynamic-update-slice_fusion.weight, bf16[14,56,128]{2,1,0:T(8,128)(2,1)S(1)} %collective-permute-done.own, ...), custom_call_target="tpu_custom_call" | custom-call | flops 44957696 | bytes 934404 | tf_op jit(solution)/shard_map/add_both/pallas_call | solution.py:226
  15.0 1.6 %collective-permute-start.7 = (bf16[14,56,128]{2,1,0:T(8,128)(2,1)S(1)}, bf16[14,56,128]{2,1,0:T(8,128)(2,1)S(1)}, u32[]{:S(2)}, u32[]{:S(2)}) collective-permute-start(bf16[14,56,128]{2,1,0:T(8,128)(2,1)S(1)} %collective-permute-done.5.other), channel_id=1, source_target_pairs={{0,2},{2,4},{4,6},{6,7},{7,5},{5,3},{3,1},{1,0},{8,9},{10,8},{12,1... | collective-permute-start | bytes 602120 | tf_op jit(solution)/shard_map/ppermute | solution.py:267
  16.7 1.5 %collective-permute-start.4 = (bf16[14,56,128]{2,1,0:T(8,128)(2,1)S(1)}, bf16[14,56,128]{2,1,0:T(8,128)(2,1)S(1)}, u32[]{:S(2)}, u32[]{:S(2)}) collective-permute-start(bf16[14,56,128]{2,1,0:T(8,128)(2,1)S(1)} %collective-permute-done.1.own), channel_id=1, source_target_pairs={{0,2},{2,4},{4,6},{6,7},{7,5},{5,3},{3,1},{1,0},{8,9},{10,8},{12,1... | collective-permute-start | bytes 602120 | tf_op jit(solution)/shard_map/ppermute | solution.py:267
  18.2 1.7 %add_both.4 = (f32[14,56,128]{2,1,0:T(8,128)S(1)}, f32[14,56,128]{2,1,0:T(8,128)S(1)}) custom-call(s32[1]{0:T(128)S(6)} %copy.14.length, f32[1,128]{1,0:T(1,128)S(1)} %bitcast.10, bf16[128,512]{1,0:T(8,128)(2,1)S(1)} %constant_dynamic-update-slice_fusion.weight, bf16[14,56,128]{2,1,0:T(8,128)(2,1)S(1)} %collective-permute-done.1.own, ...), custom_call_target="tpu_custom_call" | custom-call | flops 44957696 | bytes 1335812 | tf_op jit(solution)/shard_map/add_both/pallas_call | solution.py:226
  19.9 0.9 %collective-permute-done.7.other = bf16[14,56,128]{2,1,0:T(8,128)(2,1)S(1)} collective-permute-done((bf16[14,56,128]{2,1,0:T(8,128)(2,1)S(1)}, bf16[14,56,128]{2,1,0:T(8,128)(2,1)S(1)}, u32[]{:S(2)}, u32[]{:S(2)}) %collective-permute-start.7) | collective-permute-done | bytes 200736 | tf_op jit(solution)/shard_map/ppermute | solution.py:267
  20.8 2.1 %collective-permute-done.4.own = bf16[14,56,128]{2,1,0:T(8,128)(2,1)S(1)} collective-permute-done((bf16[14,56,128]{2,1,0:T(8,128)(2,1)S(1)}, bf16[14,56,128]{2,1,0:T(8,128)(2,1)S(1)}, u32[]{:S(2)}, u32[]{:S(2)}) %collective-permute-start.4) | collective-permute-done | bytes 200736 | tf_op jit(solution)/shard_map/ppermute | solution.py:267
  23.0 0.0 copy-start.1
  23.0 0.0 copy-start.2
  23.0 1.6 %collective-permute-start.8 = (bf16[7,56,128]{2,1,0:T(8,128)(2,1)S(1)}, bf16[7,56,128]{2,1,0:T(8,128)(2,1)S(1)}, u32[]{:S(2)}, u32[]{:S(2)}) collective-permute-start(bf16[7,56,128]{2,1,0:T(8,128)(2,1)S(1)} %constant_dynamic-slice_fusion), channel_id=1, source_target_pairs={{0,2},{2,4},{4,6},{6,7},{7,5},{5,3},{3,1},{1,0},{8,9},{10,8},{12,1... | collective-permute-start | bytes 301064 | tf_op jit(solution)/shard_map/ppermute | solution.py:267
  24.6 0.0 copy-start.4
  24.6 1.6 %collective-permute-start.6 = (bf16[7,56,128]{2,1,0:T(8,128)(2,1)S(1)}, bf16[7,56,128]{2,1,0:T(8,128)(2,1)S(1)}, u32[]{:S(2)}, u32[]{:S(2)}) collective-permute-start(bf16[7,56,128]{2,1,0:T(8,128)(2,1)S(1)} %constant_dynamic-slice_fusion.1), channel_id=1, source_target_pairs={{0,2},{2,4},{4,6},{6,7},{7,5},{5,3},{3,1},{1,0},{8,9},{10,8},{12,1... | collective-permute-start | bytes 301064 | tf_op jit(solution)/shard_map/ppermute | solution.py:267
  26.2 0.5 %gate.1 = (f32[14,56,128]{2,1,0:T(8,128)S(1)}, f32[1,128]{1,0:T(1,128)S(1)}, bf16[128,128]{1,0:T(8,128)(2,1)S(1)}) custom-call(bf16[14,56,128]{2,1,0:T(8,128)(2,1)S(1)} %bitcast.7, f32[1,128]{1,0:T(1,128)S(1)} %bitcast.11, bf16[128,128]{1,0:T(8,128)(2,1)S(1)} %copy-done.1, f32[1,128]{1,0:T(1,128)S(1)} %bitcast.15, bf16[128,128]{1,0:T(8,128)(2,1)S(1)} %copy-done.2), custom_call_target="tpu_custom_call" | custom-call | flops 25690112 | bytes 267264 | tf_op jit(solution)/shard_map/gate/pallas_call | solution.py:226
  26.7 1.8 %add_both.5 = (f32[14,56,128]{2,1,0:T(8,128)S(1)}, f32[14,56,128]{2,1,0:T(8,128)S(1)}) custom-call(s32[1]{0:T(128)S(6)} %copy.14.length, f32[1,128]{1,0:T(1,128)S(1)} %bitcast.12, bf16[128,512]{1,0:T(8,128)(2,1)S(1)} %constant_dynamic-update-slice_fusion.weight, bf16[14,56,128]{2,1,0:T(8,128)(2,1)S(1)} %collective-permute-done.4.own, ...), custom_call_target="tpu_custom_call" | custom-call | flops 44957696 | bytes 1335812 | tf_op jit(solution)/shard_map/add_both/pallas_call | solution.py:226
  28.5 0.8 %collective-permute-done.6.own = bf16[7,56,128]{2,1,0:T(8,128)(2,1)S(1)} collective-permute-done((bf16[7,56,128]{2,1,0:T(8,128)(2,1)S(1)}, bf16[7,56,128]{2,1,0:T(8,128)(2,1)S(1)}, u32[]{:S(2)}, u32[]{:S(2)}) %collective-permute-start.6) | collective-permute-done | bytes 100384 | tf_op jit(solution)/shard_map/ppermute | solution.py:267
  29.3 0.7 %add_theirs.1 = (bf16[14,56,128]{2,1,0:T(8,128)(2,1)S(1)}, f32[7,16,128]{2,1,0:T(8,128)S(1)}) custom-call(s32[1]{0:T(128)S(6)} %copy.14.length, f32[1,128]{1,0:T(1,128)S(1)} %bitcast.13, bf16[128,512]{1,0:T(8,128)(2,1)S(1)} %constant_dynamic-update-slice_fusion.weight, bf16[7,56,128]{2,1,0:T(8,128)(2,1)S(1)} %collective-permute-done.6.own, ...), custom_call_target="tpu_custom_call" | custom-call | flops 11239424 | bytes 733700 | tf_op jit(solution)/shard_map/add_theirs/pallas_call | solution.py:226
  30.0 0.1 collective-permute-start.9
  30.1 0.6 %add_mine.1.mine = f32[14,56,128]{2,1,0:T(8,128)S(1)} custom-call(s32[1]{0:T(128)S(6)} %copy.14.length, f32[1,128]{1,0:T(1,128)S(1)} %bitcast.14, bf16[128,512]{1,0:T(8,128)(2,1)S(1)} %constant_dynamic-update-slice_fusion.weight, bf16[7,56,128]{2,1,0:T(8,128)(2,1)S(1)} %collective-permute-done.6.own, f32[14,56,128]{2,1,0:T(8,128)S(1)} %get-tuple-element.49.before, ...), custom_call_target="tpu_custom_call" | custom-call | flops 11239424 | bytes 690692 | tf_op jit(solution)/shard_map/add_mine/pallas_call | solution.py:226
  30.7 0.8 %collective-permute-done.9.given = bf16[14,56,128]{2,1,0:T(8,128)(2,1)S(1)} collective-permute-done((bf16[14,56,128]{2,1,0:T(8,128)(2,1)S(1)}, bf16[14,56,128]{2,1,0:T(8,128)(2,1)S(1)}, u32[]{:S(2)}, u32[]{:S(2)}) %collective-permute-start.9) | collective-permute-done | bytes 200736 | tf_op jit(solution)/shard_map/ppermute | solution.py:270
  31.5 1.2 %finish.1 = bf16[14,56,128]{2,1,0:T(8,128)(2,1)} custom-call(f32[14,56,128]{2,1,0:T(8,128)S(1)} %add_mine.1.mine, bf16[14,56,128]{2,1,0:T(8,128)(2,1)S(1)} %collective-permute-done.9.given, f32[14,56,128]{2,1,0:T(8,128)S(1)} %get-tuple-element.54.gating, f32[1,128]{1,0:T(1,128)S(1)} %get-tuple-element.55.gain, bf16[128,128]{1,0:T(8,128)(2,1)S(1)} %get-tuple-element.56.weight), custom_call_target="tpu_custom_call" | custom-call | flops 25690112 | bytes 1036800 | tf_op jit(solution)/shard_map/finish/pallas_call | solution.py:226
  (13 shorter events, 0.0 us)
Async XLA Ops:
  0.0 6.8 %copy-start = (bf16[56,14,128]{2,0,1:T(8,128)(2,1)S(1)}, bf16[56,14,128]{2,0,1:T(8,128)(2,1)}, u32[]{:S(2)}) copy-start(bf16[56,14,128]{2,0,1:T(8,128)(2,1)} %param.10) | copy-start | bytes 602116
  0.0 8.1 %collective-permute-start.2 = (bf16[14,56,128]{2,1,0:T(8,128)(2,1)}, bf16[14,56,128]{2,1,0:T(8,128)(2,1)S(1)}, u32[]{:S(2)}, u32[]{:S(2)}) collective-permute-start(bf16[14,56,128]{2,1,0:T(8,128)(2,1)} %bitcast.4), channel_id=1, source_target_pairs={{0,9},{2,8},{4,10},{6,12},{7,14},{5,15},{3,13},{1,11},{8,2},{10,4}... | collective-permute-start | bytes 602120 | tf_op jit(solution)/shard_map/ppermute | solution.py:267
  2.4 7.5 %collective-permute-start = (bf16[14,56,128]{2,1,0:T(8,128)(2,1)}, bf16[14,56,128]{2,1,0:T(8,128)(2,1)S(1)}, u32[]{:S(2)}, u32[]{:S(2)}) collective-permute-start(bf16[14,56,128]{2,1,0:T(8,128)(2,1)} %bitcast.5), channel_id=1, source_target_pairs={{0,2},{2,4},{4,6},{6,7},{7,5},{5,3},{3,1},{1,0},{8,9},{10,8},{12,1... | collective-permute-start | bytes 602120 | tf_op jit(solution)/shard_map/ppermute | solution.py:267
  6.8 0.7 %copy-start.3 = (f32[128]{0:T(128)S(1)}, f32[128]{0:T(128)}, u32[]{:S(2)}) copy-start(f32[128]{0:T(128)} %param.12) | copy-start | bytes 1540
  8.1 7.0 %collective-permute-start.5 = (bf16[14,56,128]{2,1,0:T(8,128)(2,1)S(1)}, bf16[14,56,128]{2,1,0:T(8,128)(2,1)S(1)}, u32[]{:S(2)}, u32[]{:S(2)}) collective-permute-start(bf16[14,56,128]{2,1,0:T(8,128)(2,1)S(1)} %collective-permute-done.2.other), channel_id=1, source_target_pairs={{0,2},{2,4},{4,6},{6,7},{7,5},{5,3},{3,1},{1,0},{8,9},{10,8},{12,1... | collective-permute-start | bytes 602120 | tf_op jit(solution)/shard_map/ppermute | solution.py:267
  10.0 6.7 %collective-permute-start.1 = (bf16[14,56,128]{2,1,0:T(8,128)(2,1)S(1)}, bf16[14,56,128]{2,1,0:T(8,128)(2,1)S(1)}, u32[]{:S(2)}, u32[]{:S(2)}) collective-permute-start(bf16[14,56,128]{2,1,0:T(8,128)(2,1)S(1)} %collective-permute-done.own), channel_id=1, source_target_pairs={{0,2},{2,4},{4,6},{6,7},{7,5},{5,3},{3,1},{1,0},{8,9},{10,8},{12,1... | collective-permute-start | bytes 602120 | tf_op jit(solution)/shard_map/ppermute | solution.py:267
  11.5 1.2 %collective-permute-start.3 = (bf16[14,16,128]{2,1,0:T(8,128)(2,1)S(1)}, bf16[14,16,128]{2,1,0:T(8,128)(2,1)S(1)}, u32[]{:S(2)}, u32[]{:S(2)}) collective-permute-start(bf16[14,16,128]{2,1,0:T(8,128)(2,1)S(1)} %get-tuple-element.32.right), channel_id=1, source_target_pairs={{0,8},{8,0},{1,9},{9,1},{2,10},{10,2},{3,11},{11,3},{4,12},{12,4},... | collective-permute-start | bytes 172040 | tf_op jit(solution)/shard_map/ppermute | solution.py:270
  15.0 5.8 %collective-permute-start.7 = (bf16[14,56,128]{2,1,0:T(8,128)(2,1)S(1)}, bf16[14,56,128]{2,1,0:T(8,128)(2,1)S(1)}, u32[]{:S(2)}, u32[]{:S(2)}) collective-permute-start(bf16[14,56,128]{2,1,0:T(8,128)(2,1)S(1)} %collective-permute-done.5.other), channel_id=1, source_target_pairs={{0,2},{2,4},{4,6},{6,7},{7,5},{5,3},{3,1},{1,0},{8,9},{10,8},{12,1... | collective-permute-start | bytes 602120 | tf_op jit(solution)/shard_map/ppermute | solution.py:267
  16.7 6.3 %collective-permute-start.4 = (bf16[14,56,128]{2,1,0:T(8,128)(2,1)S(1)}, bf16[14,56,128]{2,1,0:T(8,128)(2,1)S(1)}, u32[]{:S(2)}, u32[]{:S(2)}) collective-permute-start(bf16[14,56,128]{2,1,0:T(8,128)(2,1)S(1)} %collective-permute-done.1.own), channel_id=1, source_target_pairs={{0,2},{2,4},{4,6},{6,7},{7,5},{5,3},{3,1},{1,0},{8,9},{10,8},{12,1... | collective-permute-start | bytes 602120 | tf_op jit(solution)/shard_map/ppermute | solution.py:267
  23.0 3.3 %copy-start.1 = (bf16[128,128]{1,0:T(8,128)(2,1)S(1)}, bf16[128,128]{1,0:T(8,128)(2,1)}, u32[]{:S(2)}) copy-start(bf16[128,128]{1,0:T(8,128)(2,1)} %out_gate.1) | copy-start | bytes 98308
  23.0 3.2 %copy-start.2 = (bf16[128,128]{1,0:T(8,128)(2,1)S(1)}, bf16[128,128]{1,0:T(8,128)(2,1)}, u32[]{:S(2)}) copy-start(bf16[128,128]{1,0:T(8,128)(2,1)} %last_weight.1) | copy-start | bytes 98308
  23.0 5.5 %collective-permute-start.8 = (bf16[7,56,128]{2,1,0:T(8,128)(2,1)S(1)}, bf16[7,56,128]{2,1,0:T(8,128)(2,1)S(1)}, u32[]{:S(2)}, u32[]{:S(2)}) collective-permute-start(bf16[7,56,128]{2,1,0:T(8,128)(2,1)S(1)} %constant_dynamic-slice_fusion), channel_id=1, source_target_pairs={{0,2},{2,4},{4,6},{6,7},{7,5},{5,3},{3,1},{1,0},{8,9},{10,8},{12,1... | collective-permute-start | bytes 301064 | tf_op jit(solution)/shard_map/ppermute | solution.py:267
  24.6 1.6 %copy-start.4 = (f32[128]{0:T(128)S(1)}, f32[128]{0:T(128)}, u32[]{:S(2)}) copy-start(f32[128]{0:T(128)} %param.18) | copy-start | bytes 1540
  24.6 4.7 %collective-permute-start.6 = (bf16[7,56,128]{2,1,0:T(8,128)(2,1)S(1)}, bf16[7,56,128]{2,1,0:T(8,128)(2,1)S(1)}, u32[]{:S(2)}, u32[]{:S(2)}) collective-permute-start(bf16[7,56,128]{2,1,0:T(8,128)(2,1)S(1)} %constant_dynamic-slice_fusion.1), channel_id=1, source_target_pairs={{0,2},{2,4},{4,6},{6,7},{7,5},{5,3},{3,1},{1,0},{8,9},{10,8},{12,1... | collective-permute-start | bytes 301064 | tf_op jit(solution)/shard_map/ppermute | solution.py:267
  30.0 1.5 %collective-permute-start.9 = (bf16[14,56,128]{2,1,0:T(8,128)(2,1)S(1)}, bf16[14,56,128]{2,1,0:T(8,128)(2,1)S(1)}, u32[]{:S(2)}, u32[]{:S(2)}) collective-permute-start(bf16[14,56,128]{2,1,0:T(8,128)(2,1)S(1)} %get-tuple-element.53), channel_id=1, source_target_pairs={{0,8},{8,0},{1,9},{9,1},{2,10},{10,2},{3,11},{11,3},{4,12},{12,4},... | collective-permute-start | bytes 602120 | tf_op jit(solution)/shard_map/ppermute | solution.py:270

commit v11 on v7

--- a/solution.py
+++ b/solution.py
@@ -61,7 +61,7 @@
     mine = lax.broadcasted_iota(jnp.int32, (s.slots, 1), 0) + col * s.width < limit
     h = s.hidden
     for index, (block, inside, distance, start) in enumerate(sources):
-        place = (place_of(col, s.cols) + distance + s.cols) % s.cols
+        place = (place_of(col, s.cols) + distance * (2 * row - 1) + s.cols) % s.cols
         token = column_at(place, s.cols) * s.width + start
         normed = []
         for step in range(s.half):
@@ -104,7 +104,9 @@
 
     @pl.when(row != owner)
     def _():
-        partner[:depth] = other[...].astype(F32)
+        for start in range(0, depth, s.width):
+            there = depth - s.width - start
+            partner[start : start + s.width] = other[there : there + s.width].astype(F32)
 
     size = CHUNK if s.height % CHUNK == 0 else s.height
     group = GROUP if s.width % GROUP == 0 else 1
@@ -189,9 +191,14 @@
     weights = jnp.concatenate([left_gate, left_value, right_gate, right_value], 1)
     order = ring(s.cols)
 
-    def shift(block, by):
-        pairs = [(order[at], order[(at + by) % s.cols]) for at in range(s.cols)]
-        return lax.ppermute(block, "col", pairs)
+    def shift(block, way):
+        pairs = []
+        for row in range(s.rows):
+            by = way if row == 0 else -way
+            for at in range(s.cols):
+                to = order[(at + by) % s.cols]
+                pairs.append((row * s.cols + order[at], row * s.cols + to))
+        return lax.ppermute(block, ("row", "col"), pairs)
 
     def swap(block):
         return lax.ppermute(block, "row", [(at, (at + 1) % s.rows) for at in range(s.rows)])
@@ -236,9 +243,8 @@
     blocks, sources, travel = [pair], whole([0]), [pair, pair]
     total = terms = kept = None
     for distance in range(1, far + 1):
-        if distance == far:
-            travel = [travel[0][: s.half], travel[1][s.half :]]
-        arrived = [shift(block, by) for block, by in zip(travel, (1, -1))]
+        ways = (1, -1) if distance < far else (1,)
+        arrived = [shift(block, way) for block, way in zip(travel, ways)]
         pending = run(blocks, sources)
         if distance == 2:
             kept = call(
@@ -261,8 +267,8 @@
         terms = pending
         done = (terms, total, kept)
         travel = [lax.optimization_barrier((block, done))[0] for block in arrived]
-        blocks, sources = arrived, whole([-distance, distance])
-    left, right = run(travel, [(0, 0, -far, 0), (1, 0, far, s.half)])
+        blocks, sources = travel, whole([distance, -distance])
+    left, right = run(travel, whole([far]))
     other = swap(right)
     total = add(total, terms)
     gating, last_gain, last_weight = kept

time: 30.7 us -> 33.7 us (1.098)
  waiting for transfers between devices: 6.53 us -> 11.5 us
  starting transfers between devices: 9.92 us -> 8.1 us
    ppermute x8 -> x7, waiting for transfers between devices: 5.51 us -> 11.2 us  [shift(): return lax.ppermute(block, ('row', 'col'), pairs)]
    ppermute x8 -> x7, starting transfers between devices: 9.21 us -> 7.45 us  [shift(): return lax.ppermute(block, ('row', 'col'), pairs)]
    ppermute x5, waiting for transfers between devices: 1.01 us -> 0.28 us  [swap(): lax.ppermute(block, 'row', [(at, (at + 1) % s.rows) for at in range(s.row...]
  transfers between devices with their start and end apart: 13 -> 12, of which waited for: 7 -> 5; matrix products, arithmetic and copies ran while one was open for 10% -> 9% of each run, Pallas kernels for 25% -> 23%
where the time goes in v11:
time: 33.7 us; the launch traced here: 33.4 us
  waiting for transfers between devices  11.5 us (34%)
  Pallas kernels  9.31 us (28%)
  starting transfers between devices  8.1 us (24%)
  local copies, waits for them, and re-layouts  3.73 us (11%)
  between operations  0.77 us (2%)
    ppermute x7, waiting for transfers between devices, shift(): return lax.ppermute(block, ('row', 'col'), pairs)  11.2 us
    pallas_call x11, Pallas kernels, call(): pl.pallas_call(body, out_shape=out_shape, in_specs=[space(o) for o in ope...  9.31 us
    ppermute x7, starting transfers between devices, shift(): return lax.ppermute(block, ('row', 'col'), pairs)  7.45 us
    unnamed x13, local copies, waits for them, and re-layouts  2.96 us
    concatenate x1, local copies, waits for them, and re-layouts, local(): jnp.concatenate([left_gate, left_value, right_gate, right_value], 1)  0.77 us
  transfers between devices with their start and end apart: 12, of which 5 were waited for; matrix products, arithmetic and copies ran while one was open for 9% of the time, Pallas kernels for 23%

profile of v11, /device:TPU:0, one launch (start us, length us, event | category | flops | bytes accessed | tf_op | source)
XLA Modules:
  0.0 33.4 jit_solution(9061482583861595635)
XLA Ops:
  0.0 3.0 %collective-permute-start.2 = (bf16[14,56,128]{2,1,0:T(8,128)(2,1)}, bf16[14,56,128]{2,1,0:T(8,128)(2,1)S(1)}, u32[]{:S(2)}, u32[]{:S(2)}) collective-permute-start(bf16[14,56,128]{2,1,0:T(8,128)(2,1)} %bitcast.4), channel_id=1, source_target_pairs={{0,1},{2,0},{4,2},{6,4},{7,6},{5,7},{3,5},{1,3},{8,10},{10,12},{12... | collective-permute-start | bytes 602120 | tf_op jit(solution)/shard_map/ppermute | solution.py:201
  3.0 0.1 collective-permute-start
  3.7 0.8 %constant_dynamic-update-slice_fusion.3 = bf16[128,512]{1,0:T(8,128)(2,1)S(1)} fusion(bf16[128,128]{1,0:T(8,128)(2,1)} %param.13), kind=kLoop, calls=%fused_computation.3 | loop fusion | bytes 65536
  4.5 0.8 %constant_dynamic-update-slice_fusion.2 = bf16[128,512]{1,0:T(8,128)(2,1)S(1)} fusion(bf16[128,512]{1,0:T(8,128)(2,1)S(1)} %constant_dynamic-update-slice_fusion.3, bf16[128,128]{1,0:T(8,128)(2,1)} %param.14), kind=kLoop, calls=%fused_computation.2 | loop fusion | bytes 65536
  5.3 0.8 %constant_dynamic-update-slice_fusion.1 = bf16[128,512]{1,0:T(8,128)(2,1)S(1)} fusion(bf16[128,512]{1,0:T(8,128)(2,1)S(1)} %constant_dynamic-update-slice_fusion.2, bf16[128,128]{1,0:T(8,128)(2,1)} %param.15), kind=kLoop, calls=%fused_computation.1 | loop fusion | bytes 65536
  6.0 0.8 %constant_dynamic-update-slice_fusion.weight = bf16[128,512]{1,0:T(8,128)(2,1)S(1)} fusion(bf16[128,512]{1,0:T(8,128)(2,1)S(1)} %constant_dynamic-update-slice_fusion.1, bf16[128,128]{1,0:T(8,128)(2,1)} %param.16), kind=kLoop, calls=%fused_computation | loop fusion | bytes 65536 | tf_op jit(solution)/shard_map/concatenate | solution.py:191
  6.8 0.6 %copy-done.3 = f32[128]{0:T(128)S(1)} copy-done((f32[128]{0:T(128)S(1)}, f32[128]{0:T(128)}, u32[]{:S(2)}) %copy-start.3) | copy-done | bytes 536
  7.5 0.6 %project.5 = (f32[14,56,128]{2,1,0:T(8,128)S(1)}, bf16[14,16,128]{2,1,0:T(8,128)(2,1)S(1)}) custom-call(s32[1]{0:T(128)S(6)} %copy.14.length, f32[1,128]{1,0:T(1,128)S(1)} %bitcast.8, bf16[128,512]{1,0:T(8,128)(2,1)S(1)} %constant_dynamic-update-slice_fusion.weight, bf16[14,56,128]{2,1,0:T(8,128)(2,1)S(1)} %bitcast.6), custom_call_target="tpu_custom_call" | custom-call | flops 51380224 | bytes 332292 | tf_op jit(solution)/shard_map/project/pallas_call | solution.py:160
  8.1 0.8 %collective-permute-done.refs_0_ = bf16[14,56,128]{2,1,0:T(8,128)(2,1)S(1)} collective-permute-done((bf16[14,56,128]{2,1,0:T(8,128)(2,1)}, bf16[14,56,128]{2,1,0:T(8,128)(2,1)S(1)}, u32[]{:S(2)}, u32[]{:S(2)}) %collective-permute-start) | collective-permute-done | bytes 200736 | tf_op jit(solution)/shard_map/ppermute | solution.py:201
  8.9 1.2 %collective-permute-start.1 = (bf16[14,56,128]{2,1,0:T(8,128)(2,1)S(1)}, bf16[14,56,128]{2,1,0:T(8,128)(2,1)S(1)}, u32[]{:S(2)}, u32[]{:S(2)}) collective-permute-start(bf16[14,56,128]{2,1,0:T(8,128)(2,1)S(1)} %collective-permute-done.refs_0_), channel_id=1, source_target_pairs={{0,2},{2,4},{4,6},{6,7},{7,5},{5,3},{3,1},{1,0},{8,9},{10,8},{12,1... | collective-permute-start | bytes 602120 | tf_op jit(solution)/shard_map/ppermute | solution.py:201
  10.1 0.0 collective-permute-start.3
  10.1 0.8 %collective-permute-start.5 = (bf16[14,56,128]{2,1,0:T(8,128)(2,1)S(1)}, bf16[14,56,128]{2,1,0:T(8,128)(2,1)S(1)}, u32[]{:S(2)}, u32[]{:S(2)}) collective-permute-start(bf16[14,56,128]{2,1,0:T(8,128)(2,1)S(1)} %collective-permute-done.2.refs_1_), channel_id=1, source_target_pairs={{0,1},{2,0},{4,2},{6,4},{7,6},{5,7},{3,5},{1,3},{8,10},{10,12},{12... | collective-permute-start | bytes 602120 | tf_op jit(solution)/shard_map/ppermute | solution.py:201
  10.9 0.5 %gate.1 = (f32[14,56,128]{2,1,0:T(8,128)S(1)}, f32[1,128]{1,0:T(1,128)S(1)}, bf16[128,128]{1,0:T(8,128)(2,1)S(1)}) custom-call(bf16[14,56,128]{2,1,0:T(8,128)(2,1)S(1)} %bitcast.7, f32[1,128]{1,0:T(1,128)S(1)} %bitcast.9, bf16[128,128]{1,0:T(8,128)(2,1)S(1)} %copy-done.1, f32[1,128]{1,0:T(1,128)S(1)} %bitcast.14, bf16[128,128]{1,0:T(8,128)(2,1)S(1)} %copy-done.2), custom_call_target="tpu_custom_call" | custom-call | flops 25690112 | bytes 267264 | tf_op jit(solution)/shard_map/gate/pallas_call | solution.py:160
  11.4 0.0 collective-permute-done.3.other
  11.4 0.5 %add_first.1.before = f32[14,56,128]{2,1,0:T(8,128)S(1)} custom-call(f32[14,56,128]{2,1,0:T(8,128)S(1)} %get-tuple-element.25.left, bf16[14,16,128]{2,1,0:T(8,128)(2,1)S(1)} %get-tuple-element.26.right, bf16[14,16,128]{2,1,0:T(8,128)(2,1)S(1)} %collective-permute-done.3.other), custom_call_target="tpu_custom_call" | custom-call | flops 22478848 | bytes 516096 | tf_op jit(solution)/shard_map/add_first/pallas_call | solution.py:160
  11.9 0.9 %project.6 = (f32[28,56,128]{2,1,0:T(8,128)S(1)}, bf16[28,16,128]{2,1,0:T(8,128)(2,1)S(1)}) custom-call(s32[1]{0:T(128)S(6)} %copy.14.length, f32[1,128]{1,0:T(1,128)S(1)} %bitcast.10, bf16[128,512]{1,0:T(8,128)(2,1)S(1)} %constant_dynamic-update-slice_fusion.weight, bf16[14,56,128]{2,1,0:T(8,128)(2,1)S(1)} %collective-permute-done.refs_0_, ...), custom_call_target="tpu_custom_call" | custom-call | flops 102760448 | bytes 532996 | tf_op jit(solution)/shard_map/project/pallas_call | solution.py:160
  12.9 3.2 %collective-permute-done.1.refs_0_ = bf16[14,56,128]{2,1,0:T(8,128)(2,1)S(1)} collective-permute-done((bf16[14,56,128]{2,1,0:T(8,128)(2,1)S(1)}, bf16[14,56,128]{2,1,0:T(8,128)(2,1)S(1)}, u32[]{:S(2)}, u32[]{:S(2)}) %collective-permute-start.1) | collective-permute-done | bytes 200736 | tf_op jit(solution)/shard_map/ppermute | solution.py:201
  16.0 0.8 %collective-permute-start.4 = (bf16[14,56,128]{2,1,0:T(8,128)(2,1)S(1)}, bf16[14,56,128]{2,1,0:T(8,128)(2,1)S(1)}, u32[]{:S(2)}, u32[]{:S(2)}) collective-permute-start(bf16[14,56,128]{2,1,0:T(8,128)(2,1)S(1)} %collective-permute-done.1.refs_0_), channel_id=1, source_target_pairs={{0,2},{2,4},{4,6},{6,7},{7,5},{5,3},{3,1},{1,0},{8,9},{10,8},{12,1... | collective-permute-start | bytes 602120 | tf_op jit(solution)/shard_map/ppermute | solution.py:201
  16.8 1.6 %collective-permute-start.8 = (bf16[14,56,128]{2,1,0:T(8,128)(2,1)S(1)}, bf16[14,56,128]{2,1,0:T(8,128)(2,1)S(1)}, u32[]{:S(2)}, u32[]{:S(2)}) collective-permute-start(bf16[14,56,128]{2,1,0:T(8,128)(2,1)S(1)} %collective-permute-done.5.refs_1_), channel_id=1, source_target_pairs={{0,1},{2,0},{4,2},{6,4},{7,6},{5,7},{3,5},{1,3},{8,10},{10,12},{12... | collective-permute-start | bytes 602120 | tf_op jit(solution)/shard_map/ppermute | solution.py:201
  18.4 0.0 collective-permute-done.6.other
  18.4 0.9 %add_more.3.before = f32[14,56,128]{2,1,0:T(8,128)S(1)} custom-call(f32[28,56,128]{2,1,0:T(8,128)S(1)} %get-tuple-element.29.left, bf16[28,16,128]{2,1,0:T(8,128)(2,1)S(1)} %get-tuple-element.30.right, bf16[28,16,128]{2,1,0:T(8,128)(2,1)S(1)} %collective-permute-done.6.other, f32[14,56,128]{2,1,0:T(8,128)S(1)} %add_first.1.before), custom_call_target="tpu_custom_call" | custom-call | flops 44957696 | bytes 1433600 | tf_op jit(solution)/shard_map/add_more/pallas_call | solution.py:160
  19.3 0.9 %project.7 = (f32[28,56,128]{2,1,0:T(8,128)S(1)}, bf16[28,16,128]{2,1,0:T(8,128)(2,1)S(1)}) custom-call(s32[1]{0:T(128)S(6)} %copy.14.length, f32[1,128]{1,0:T(1,128)S(1)} %bitcast.11, bf16[128,512]{1,0:T(8,128)(2,1)S(1)} %constant_dynamic-update-slice_fusion.weight, bf16[14,56,128]{2,1,0:T(8,128)(2,1)S(1)} %collective-permute-done.1.refs_0_, ...), custom_call_target="tpu_custom_call" | custom-call | flops 102760448 | bytes 532996 | tf_op jit(solution)/shard_map/project/pallas_call | solution.py:160
  20.3 3.9 %collective-permute-done.4.refs_0_ = bf16[14,56,128]{2,1,0:T(8,128)(2,1)S(1)} collective-permute-done((bf16[14,56,128]{2,1,0:T(8,128)(2,1)S(1)}, bf16[14,56,128]{2,1,0:T(8,128)(2,1)S(1)}, u32[]{:S(2)}, u32[]{:S(2)}) %collective-permute-start.4) | collective-permute-done | bytes 200736 | tf_op jit(solution)/shard_map/ppermute | solution.py:201
  24.1 0.9 %project.8 = (f32[28,56,128]{2,1,0:T(8,128)S(1)}, bf16[28,16,128]{2,1,0:T(8,128)(2,1)S(1)}) custom-call(s32[1]{0:T(128)S(6)} %copy.14.length, f32[1,128]{1,0:T(1,128)S(1)} %bitcast.12, bf16[128,512]{1,0:T(8,128)(2,1)S(1)} %constant_dynamic-update-slice_fusion.weight, bf16[14,56,128]{2,1,0:T(8,128)(2,1)S(1)} %collective-permute-done.4.refs_0_, ...), custom_call_target="tpu_custom_call" | custom-call | flops 102760448 | bytes 532996 | tf_op jit(solution)/shard_map/project/pallas_call | solution.py:160
  25.1 0.6 %collective-permute-start.11 = (bf16[28,16,128]{2,1,0:T(8,128)(2,1)S(1)}, bf16[28,16,128]{2,1,0:T(8,128)(2,1)S(1)}, u32[]{:S(2)}, u32[]{:S(2)}) collective-permute-start(bf16[28,16,128]{2,1,0:T(8,128)(2,1)S(1)} %get-tuple-element.41.right), channel_id=1, source_target_pairs={{0,8},{8,0},{1,9},{9,1},{2,10},{10,2},{3,11},{11,3},{4,12},{12,4},... | collective-permute-start | bytes 344072 | tf_op jit(solution)/shard_map/ppermute | solution.py:204
  25.6 0.9 %add_more.4.before = f32[14,56,128]{2,1,0:T(8,128)S(1)} custom-call(f32[28,56,128]{2,1,0:T(8,128)S(1)} %get-tuple-element.36.left, bf16[28,16,128]{2,1,0:T(8,128)(2,1)S(1)} %get-tuple-element.37.right, bf16[28,16,128]{2,1,0:T(8,128)(2,1)S(1)} %collective-permute-done.9.other, f32[14,56,128]{2,1,0:T(8,128)S(1)} %add_more.3.before), custom_call_target="tpu_custom_call" | custom-call | flops 44957696 | bytes 1433600 | tf_op jit(solution)/shard_map/add_more/pallas_call | solution.py:160
  26.5 3.3 %collective-permute-done.7.refs_0_ = bf16[14,56,128]{2,1,0:T(8,128)(2,1)S(1)} collective-permute-done((bf16[14,56,128]{2,1,0:T(8,128)(2,1)S(1)}, bf16[14,56,128]{2,1,0:T(8,128)(2,1)S(1)}, u32[]{:S(2)}, u32[]{:S(2)}) %collective-permute-start.7) | collective-permute-done | bytes 200736 | tf_op jit(solution)/shard_map/ppermute | solution.py:201
  29.8 0.6 %project.9 = (f32[14,56,128]{2,1,0:T(8,128)S(1)}, bf16[14,16,128]{2,1,0:T(8,128)(2,1)S(1)}) custom-call(s32[1]{0:T(128)S(6)} %copy.14.length, f32[1,128]{1,0:T(1,128)S(1)} %bitcast.13, bf16[128,512]{1,0:T(8,128)(2,1)S(1)} %constant_dynamic-update-slice_fusion.weight, bf16[14,56,128]{2,1,0:T(8,128)(2,1)S(1)} %collective-permute-done.7.refs_0_), custom_call_target="tpu_custom_call" | custom-call | flops 51380224 | bytes 332292 | tf_op jit(solution)/shard_map/project/pallas_call | solution.py:160
  30.4 0.1 collective-permute-start.10
  30.5 0.9 %add_more.5.before = f32[14,56,128]{2,1,0:T(8,128)S(1)} custom-call(f32[28,56,128]{2,1,0:T(8,128)S(1)} %get-tuple-element.40.left, bf16[28,16,128]{2,1,0:T(8,128)(2,1)S(1)} %get-tuple-element.41.right, bf16[28,16,128]{2,1,0:T(8,128)(2,1)S(1)} %collective-permute-done.11.other, f32[14,56,128]{2,1,0:T(8,128)S(1)} %add_more.4.before), custom_call_target="tpu_custom_call" | custom-call | flops 44957696 | bytes 1433600 | tf_op jit(solution)/shard_map/add_more/pallas_call | solution.py:160
  31.4 0.3 collective-permute-done.10.other
  31.7 1.6 %finish.1 = bf16[14,56,128]{2,1,0:T(8,128)(2,1)} custom-call(f32[14,56,128]{2,1,0:T(8,128)S(1)} %get-tuple-element.43.left, bf16[14,16,128]{2,1,0:T(8,128)(2,1)S(1)} %get-tuple-element.44.right, bf16[14,16,128]{2,1,0:T(8,128)(2,1)S(1)} %collective-permute-done.10.other, f32[14,56,128]{2,1,0:T(8,128)S(1)} %add_more.5.before, ...), custom_call_target="tpu_custom_call" | custom-call | flops 22478848 | bytes 1352192 | tf_op jit(solution)/shard_map/finish/pallas_call | solution.py:160
  (17 shorter events, 0.0 us)
Async XLA Ops:
  0.0 6.8 %copy-start = (bf16[56,14,128]{2,0,1:T(8,128)(2,1)S(1)}, bf16[56,14,128]{2,0,1:T(8,128)(2,1)}, u32[]{:S(2)}) copy-start(bf16[56,14,128]{2,0,1:T(8,128)(2,1)} %param.10) | copy-start | bytes 602116
  0.0 10.1 %collective-permute-start.2 = (bf16[14,56,128]{2,1,0:T(8,128)(2,1)}, bf16[14,56,128]{2,1,0:T(8,128)(2,1)S(1)}, u32[]{:S(2)}, u32[]{:S(2)}) collective-permute-start(bf16[14,56,128]{2,1,0:T(8,128)(2,1)} %bitcast.4), channel_id=1, source_target_pairs={{0,1},{2,0},{4,2},{6,4},{7,6},{5,7},{3,5},{1,3},{8,10},{10,12},{12... | collective-permute-start | bytes 602120 | tf_op jit(solution)/shard_map/ppermute | solution.py:201
  3.0 5.9 %collective-permute-start = (bf16[14,56,128]{2,1,0:T(8,128)(2,1)}, bf16[14,56,128]{2,1,0:T(8,128)(2,1)S(1)}, u32[]{:S(2)}, u32[]{:S(2)}) collective-permute-start(bf16[14,56,128]{2,1,0:T(8,128)(2,1)} %bitcast.5), channel_id=1, source_target_pairs={{0,2},{2,4},{4,6},{6,7},{7,5},{5,3},{3,1},{1,0},{8,9},{10,8},{12,1... | collective-permute-start | bytes 602120 | tf_op jit(solution)/shard_map/ppermute | solution.py:201
  6.8 0.7 %copy-start.3 = (f32[128]{0:T(128)S(1)}, f32[128]{0:T(128)}, u32[]{:S(2)}) copy-start(f32[128]{0:T(128)} %param.12) | copy-start | bytes 1540
  7.5 3.5 %copy-start.1 = (bf16[128,128]{1,0:T(8,128)(2,1)S(1)}, bf16[128,128]{1,0:T(8,128)(2,1)}, u32[]{:S(2)}) copy-start(bf16[128,128]{1,0:T(8,128)(2,1)} %out_gate.1) | copy-start | bytes 98308
  7.5 3.5 %copy-start.2 = (bf16[128,128]{1,0:T(8,128)(2,1)S(1)}, bf16[128,128]{1,0:T(8,128)(2,1)}, u32[]{:S(2)}) copy-start(bf16[128,128]{1,0:T(8,128)(2,1)} %last_weight.1) | copy-start | bytes 98308
  8.9 2.0 %copy-start.4 = (f32[128]{0:T(128)S(1)}, f32[128]{0:T(128)}, u32[]{:S(2)}) copy-start(f32[128]{0:T(128)} %param.18) | copy-start | bytes 1540
  8.9 7.1 %collective-permute-start.1 = (bf16[14,56,128]{2,1,0:T(8,128)(2,1)S(1)}, bf16[14,56,128]{2,1,0:T(8,128)(2,1)S(1)}, u32[]{:S(2)}, u32[]{:S(2)}) collective-permute-start(bf16[14,56,128]{2,1,0:T(8,128)(2,1)S(1)} %collective-permute-done.refs_0_), channel_id=1, source_target_pairs={{0,2},{2,4},{4,6},{6,7},{7,5},{5,3},{3,1},{1,0},{8,9},{10,8},{12,1... | collective-permute-start | bytes 602120 | tf_op jit(solution)/shard_map/ppermute | solution.py:201
  10.1 1.3 %collective-permute-start.3 = (bf16[14,16,128]{2,1,0:T(8,128)(2,1)S(1)}, bf16[14,16,128]{2,1,0:T(8,128)(2,1)S(1)}, u32[]{:S(2)}, u32[]{:S(2)}) collective-permute-start(bf16[14,16,128]{2,1,0:T(8,128)(2,1)S(1)} %get-tuple-element.26.right), channel_id=1, source_target_pairs={{0,8},{8,0},{1,9},{9,1},{2,10},{10,2},{3,11},{11,3},{4,12},{12,4},... | collective-permute-start | bytes 172040 | tf_op jit(solution)/shard_map/ppermute | solution.py:204
  10.1 6.7 %collective-permute-start.5 = (bf16[14,56,128]{2,1,0:T(8,128)(2,1)S(1)}, bf16[14,56,128]{2,1,0:T(8,128)(2,1)S(1)}, u32[]{:S(2)}, u32[]{:S(2)}) collective-permute-start(bf16[14,56,128]{2,1,0:T(8,128)(2,1)S(1)} %collective-permute-done.2.refs_1_), channel_id=1, source_target_pairs={{0,1},{2,0},{4,2},{6,4},{7,6},{5,7},{3,5},{1,3},{8,10},{10,12},{12... | collective-permute-start | bytes 602120 | tf_op jit(solution)/shard_map/ppermute | solution.py:201
  16.0 8.1 %collective-permute-start.4 = (bf16[14,56,128]{2,1,0:T(8,128)(2,1)S(1)}, bf16[14,56,128]{2,1,0:T(8,128)(2,1)S(1)}, u32[]{:S(2)}, u32[]{:S(2)}) collective-permute-start(bf16[14,56,128]{2,1,0:T(8,128)(2,1)S(1)} %collective-permute-done.1.refs_0_), channel_id=1, source_target_pairs={{0,2},{2,4},{4,6},{6,7},{7,5},{5,3},{3,1},{1,0},{8,9},{10,8},{12,1... | collective-permute-start | bytes 602120 | tf_op jit(solution)/shard_map/ppermute | solution.py:201
  16.8 1.6 %collective-permute-start.6 = (bf16[28,16,128]{2,1,0:T(8,128)(2,1)S(1)}, bf16[28,16,128]{2,1,0:T(8,128)(2,1)S(1)}, u32[]{:S(2)}, u32[]{:S(2)}) collective-permute-start(bf16[28,16,128]{2,1,0:T(8,128)(2,1)S(1)} %get-tuple-element.30.right), channel_id=1, source_target_pairs={{0,8},{8,0},{1,9},{9,1},{2,10},{10,2},{3,11},{11,3},{4,12},{12,4},... | collective-permute-start | bytes 344072 | tf_op jit(solution)/shard_map/ppermute | solution.py:204
  16.8 7.3 %collective-permute-start.8 = (bf16[14,56,128]{2,1,0:T(8,128)(2,1)S(1)}, bf16[14,56,128]{2,1,0:T(8,128)(2,1)S(1)}, u32[]{:S(2)}, u32[]{:S(2)}) collective-permute-start(bf16[14,56,128]{2,1,0:T(8,128)(2,1)S(1)} %collective-permute-done.5.refs_1_), channel_id=1, source_target_pairs={{0,1},{2,0},{4,2},{6,4},{7,6},{5,7},{3,5},{1,3},{8,10},{10,12},{12... | collective-permute-start | bytes 602120 | tf_op jit(solution)/shard_map/ppermute | solution.py:201
  24.1 5.7 %collective-permute-start.7 = (bf16[14,56,128]{2,1,0:T(8,128)(2,1)S(1)}, bf16[14,56,128]{2,1,0:T(8,128)(2,1)S(1)}, u32[]{:S(2)}, u32[]{:S(2)}) collective-permute-start(bf16[14,56,128]{2,1,0:T(8,128)(2,1)S(1)} %collective-permute-done.4.refs_0_), channel_id=1, source_target_pairs={{0,2},{2,4},{4,6},{6,7},{7,5},{5,3},{3,1},{1,0},{8,9},{10,8},{12,1... | collective-permute-start | bytes 602120 | tf_op jit(solution)/shard_map/ppermute | solution.py:201
  24.1 1.5 %collective-permute-start.9 = (bf16[28,16,128]{2,1,0:T(8,128)(2,1)S(1)}, bf16[28,16,128]{2,1,0:T(8,128)(2,1)S(1)}, u32[]{:S(2)}, u32[]{:S(2)}) collective-permute-start(bf16[28,16,128]{2,1,0:T(8,128)(2,1)S(1)} %get-tuple-element.37.right), channel_id=1, source_target_pairs={{0,8},{8,0},{1,9},{9,1},{2,10},{10,2},{3,11},{11,3},{4,12},{12,4},... | collective-permute-start | bytes 344072 | tf_op jit(solution)/shard_map/ppermute | solution.py:204
  25.1 5.4 %collective-permute-start.11 = (bf16[28,16,128]{2,1,0:T(8,128)(2,1)S(1)}, bf16[28,16,128]{2,1,0:T(8,128)(2,1)S(1)}, u32[]{:S(2)}, u32[]{:S(2)}) collective-permute-start(bf16[28,16,128]{2,1,0:T(8,128)(2,1)S(1)} %get-tuple-element.41.right), channel_id=1, source_target_pairs={{0,8},{8,0},{1,9},{9,1},{2,10},{10,2},{3,11},{11,3},{4,12},{12,4},... | collective-permute-start | bytes 344072 | tf_op jit(solution)/shard_map/ppermute | solution.py:204
  30.4 1.3 %collective-permute-start.10 = (bf16[14,16,128]{2,1,0:T(8,128)(2,1)S(1)}, bf16[14,16,128]{2,1,0:T(8,128)(2,1)S(1)}, u32[]{:S(2)}, u32[]{:S(2)}) collective-permute-start(bf16[14,16,128]{2,1,0:T(8,128)(2,1)S(1)} %get-tuple-element.44.right), channel_id=1, source_target_pairs={{0,8},{8,0},{1,9},{9,1},{2,10},{10,2},{3,11},{11,3},{4,12},{12,4},... | collective-permute-start | bytes 172040 | tf_op jit(solution)/shard_map/ppermute | solution.py:204

commit v12 on v11

v12 whole, which is shorter than its diff:
```python
import functools

import jax
import jax.numpy as jnp
from jax import lax
from jax.experimental import pallas as pl
from jax.experimental.pallas import tpu as pltpu
from jax.sharding import PartitionSpec as P

F32 = jnp.float32
BF16 = jnp.bfloat16
EPS = 1e-05
TILE = 16
CHUNK = 56
GROUP = 7


class Sizes:
    def __init__(self, mesh, height, width, channels, hidden):
        self.rows = mesh.shape["row"]
        self.cols = mesh.shape["col"]
        self.height, self.width = height, width
        self.channels, self.hidden = channels, hidden
        self.half = width // 2
        self.slots = -(-width // TILE) * TILE


def column_at(place, cols):
    return jnp.where(place < cols // 2, 2 * place, 2 * (cols - place) - 1)


def place_of(column, cols):
    return jnp.where(column % 2 == 0, column // 2, cols - 1 - column // 2)


def ring(cols):
    return [2 * at if at < cols // 2 else 2 * (cols - at) - 1 for at in range(cols)]


def normalise(values):
    average = jnp.mean(values, -1, keepdims=True)
    centered = values - average
    variance = jnp.mean(centered * centered, -1, keepdims=True)
    return centered * lax.rsqrt(variance + EPS)


def sigmoid(values):
    return 0.5 * jnp.tanh(0.5 * values) + 0.5


def dot(left, right):
    return jnp.dot(left, right, preferred_element_type=F32)


def gate(s, pair, gain, out_gate, last_gain, last_weight, gating, kept_gain, kept_weight):
    kept_gain[...] = last_gain[...]
    kept_weight[...] = last_weight[...]
    for start in range(0, s.width, s.half):
        normed = [
            normalise(pair[start + step].astype(F32)) * gain[...] for step in range(s.half)
        ]
        value = sigmoid(dot(jnp.concatenate(normed, 0).astype(BF16), out_gate[...]))
        for step in range(s.half):
            gating[start + step] = value[step * s.height : (step + 1) * s.height]


def accumulate(s, left, partner, before, total):
    depth = left.shape[0]
    size = CHUNK if s.height % CHUNK == 0 else s.height
    group = GROUP if s.width % GROUP == 0 else 1

    def chunk(index, carry):
        at = pl.ds(pl.multiple_of(index * size, 8), size)
        for first in range(0, s.width, group):
            members = range(first, first + group)
            if before is None:
                sums = tuple(jnp.zeros((size, s.hidden), F32) for _ in members)
            else:
                sums = tuple(before[j, at] for j in members)

            def step(k, sums):
                value = left[k, at]
                return tuple(
                    so_far + value * partner[k, j : j + 1] for so_far, j in zip(sums, members)
                )

            sums = lax.fori_loop(0, depth, step, sums, unroll=s.half)
            for so_far, j in zip(sums, members):
                total[j, at] = so_far
        return carry

    lax.fori_loop(0, s.height // size, chunk, 0)


def owner_of(s, col):
    return col // (s.height // s.width)


def choose(first, one, other, target):
    @pl.when(first)
    def _():
        target[...] = one[...].astype(F32)

    @pl.when(jnp.logical_not(first))
    def _():
        target[...] = other[...].astype(F32)


def offset_in(s, col):
    return (col % (s.height // s.width)) * s.width


def column_from(s, distance):
    row, col = lax.axis_index("row"), lax.axis_index("col")
    step = distance * (2 * row - 1)
    return column_at((place_of(col, s.cols) + step + s.cols) % s.cols, s.cols)


def gated(s, rows, gain, weight, masks):
    h, size = s.hidden, rows[0].shape[0]
    rows = [normalise(row) * gain[...] for row in rows]
    out = dot(jnp.concatenate(rows, 0).astype(BF16), weight)
    value = sigmoid(out[:, :h]) * out[:, h:]
    return [value[at * size : (at + 1) * size] * mask for at, mask in enumerate(masks)]


def project_right(s, rows_of, base, depth, token, limit, gain, weight, partner):
    first = lax.axis_index("col") * s.width
    mine = lax.broadcasted_iota(jnp.int32, (s.slots, 1), 0) + first < limit
    for start in range(0, depth, s.half):
        steps = range(start, start + s.half)
        masks = [(mine & (token + step < limit)).astype(F32) for step in steps]
        rows = [rows_of(base + step) for step in steps]
        for step, part in zip(steps, gated(s, rows, gain, weight[:, 2 * s.hidden :], masks)):
            partner[step] = part


def project_left(s, block, row, base, depth, token, limit, gain, weight, left):
    below = lax.broadcasted_iota(jnp.int32, (s.height, 1), 0) + row * s.height < limit
    for start in range(0, depth, s.half):
        steps = range(start, start + s.half)
        masks = [(below & (token + step < limit)).astype(F32) for step in steps]
        rows = [block[base + step].astype(F32) for step in steps]
        for step, part in zip(steps, gated(s, rows, gain, weight[:, : 2 * s.hidden], masks)):
            left[step] = part


def add_both(s, distance, narrow, length, gain, weight, own, other, *refs):
    before, (mine, theirs, left, right, picked, partner) = refs[:-6], refs[-6:]
    row, col, limit = lax.axis_index("row"), lax.axis_index("col"), length[0]
    depth = left.shape[0]
    base = row * s.half if distance == 0 else 0
    token = column_from(s, distance) * s.width + base
    choose(row == owner_of(s, col), own, other, picked.at[:, : s.height])

    def rows_of(at):
        return picked[at, pl.ds(offset_in(s, col), s.slots), :]

    project_right(s, rows_of, base, depth, token, limit, gain, weight, partner)
    project_left(s, own, row, base, depth, token, limit, gain, weight, left)
    project_left(s, other, 1 - row, base, depth, token, limit, gain, weight, right)
    old_mine, old_theirs = before if before else (None, None)
    accumulate(s, left, partner, old_mine, mine)
    if not narrow:
        accumulate(s, right, partner, old_theirs, theirs)
    else:
        accumulate(s, right, partner, old_theirs, picked)
        theirs[...] = picked[:, : s.height].astype(BF16)


def pick(s, own, other, rows, picked):
    col = column_from(s, -2)
    choose(lax.axis_index("row") == owner_of(s, col), own, other, picked.at[:, : s.height])
    for step in range(s.width):
        rows[step] = picked[step, pl.ds(offset_in(s, col), s.slots), :].astype(BF16)


def finish(s, length, gain, weight, own, rows, mine, given, gating, last_gain, last_weight, *refs):
    update, left, partner, total = refs
    token = column_from(s, s.cols // 2) * s.width
    limit, row = length[0], lax.axis_index("row")
    project_right(
        s, lambda at: rows[at].astype(F32), 0, s.width, token, limit, gain, weight, partner
    )
    project_left(s, own, row, 0, s.width, token, limit, gain, weight, left)
    accumulate(s, left, partner, mine, total)
    for start in range(0, s.width, s.half):
        settled = [
            normalise(total[start + step] + given[start + step].astype(F32)) * last_gain[...]
            for step in range(s.half)
        ]
        value = dot(jnp.concatenate(settled, 0).astype(BF16), last_weight[...])
        for step in range(s.half):
            part = gating[start + step] * value[step * s.height : (step + 1) * s.height]
            update[start + step] = part.astype(BF16)


def call(body, out_shape, scratch, flops, *operands):
    def space(operand):
        return pl.BlockSpec(memory_space=pltpu.SMEM if operand.dtype == jnp.int32 else pltpu.VMEM)

    sent = sum(o.size * o.dtype.itemsize for o in operands)
    return pl.pallas_call(
        body,
        out_shape=out_shape,
        in_specs=[space(o) for o in operands],
        out_specs=jax.tree.map(lambda _: pl.BlockSpec(memory_space=pltpu.VMEM), out_shape),
        scratch_shapes=scratch,
        compiler_params=pltpu.CompilerParams(vmem_limit_bytes=24 * 1024 * 1024),
        cost_estimate=pl.CostEstimate(flops=flops, bytes_accessed=sent, transcendentals=0),
        name=body.func.__name__,
    )(*operands)


def local(
    mesh,
    pair_state,
    valid_length,
    input_gain,
    left_gate,
    left_value,
    right_gate,
    right_value,
    out_gate,
    output_gain,
    out_weight,
):
    height, width, channels = pair_state.shape
    hidden = left_gate.shape[1]
    s = Sizes(mesh, height, width, channels, hidden)
    shape = jax.ShapeDtypeStruct
    pair = jnp.transpose(pair_state, (1, 0, 2))
    gain = input_gain.reshape(1, channels)
    weights = jnp.concatenate([left_gate, left_value, right_gate, right_value], 1)
    order = ring(s.cols)

    def shift(block, crossed=False, by=1):
        pairs = []
        for row in range(s.rows):
            target = s.rows - 1 - row if crossed else row
            for at in range(s.cols):
                to = (at + by * (1 - 2 * target)) % s.cols
                pairs.append((row * s.cols + order[at], target * s.cols + order[to]))
        return lax.ppermute(block, ("row", "col"), pairs)

    def swap(block):
        return lax.ppermute(block, "row", [(at, (at + 1) % s.rows) for at in range(s.rows)])

    sums = shape((width, height, hidden), F32)
    common = (valid_length, gain, weights)
    product = 16 * height * width * hidden
    tokens = pltpu.VMEM((width, height, hidden), F32)
    halved = pltpu.VMEM((s.half, height, hidden), F32)
    padded = pltpu.VMEM((width, height + TILE, channels), F32)
    partner = pltpu.VMEM((width, s.slots, hidden), F32)
    few = pltpu.VMEM((s.half, s.slots, hidden), F32)

    def add(distance, own, other, before, narrow=False):
        left, right = (halved, few) if distance == 0 else (tokens, partner)
        return call(
            functools.partial(add_both, s, distance, narrow),
            [sums, shape(sums.shape, BF16) if narrow else sums],
            [left, left, padded, right],
            2 * left.shape[0] * product,
            *common,
            own,
            other,
            *before,
        )

    def in_turn(other, own, done):
        own = lax.optimization_barrier((own, done))[0]
        return lax.optimization_barrier((other, own))[0], own

    far = s.cols // 2
    other = shift(pair, crossed=True)
    own = shift(pair)
    total = add(0, pair, swap(pair), ())
    other, own = in_turn(other, own, weights)
    rows = ()
    for distance in range(1, far - 1):
        ahead = [shift(other), shift(own)]
        if distance == far - 2:
            rows = call(
                functools.partial(pick, s),
                shape((width, s.slots, channels), BF16),
                [padded],
                0,
                own,
                other,
            )
            rows = shift(rows, by=2)
        total = add(distance, own, other, total)
        done = (total, rows)
        other, own = in_turn(*ahead, done)
    last = shift(own)
    gating = call(
        functools.partial(gate, s),
        [sums, shape((1, hidden), F32), shape(out_weight.shape, BF16)],
        [],
        2 * height * width * channels * channels,
        pair,
        gain,
        out_gate,
        output_gain.reshape(1, hidden),
        out_weight,
    )
    mine, theirs = add(far - 1, own, other, total, narrow=True)
    given = swap(theirs)
    last, mine, gating = lax.optimization_barrier((last, mine, gating))
    update = call(
        functools.partial(finish, s),
        shape((width, height, channels), BF16),
        [tokens, partner, pltpu.VMEM(sums.shape, F32)],
        width * product,
        *common,
        last,
        rows,
        mine,
        given,
        *gating,
    )
    return jnp.transpose(update, (1, 0, 2))


def solution(mesh):
    return jax.shard_map(
        functools.partial(local, mesh),
        mesh=mesh,
        in_specs=(P(("parts", "row"), "col", None), P("parts")) + (P(),) * 8,
        out_specs=P(("parts", "row"), "col", None),
        check_vma=False,
    )
```

time: 33.7 us -> 34 us (level)
  waiting for transfers between devices: 11.5 us -> 5.28 us
  starting transfers between devices: 8.1 us -> 14.3 us
  local copies, waits for them, and re-layouts: 3.73 us -> 4.26 us
    ppermute x7 -> x8, starting transfers between devices: 7.45 us -> 13.8 us  [shift(): return lax.ppermute(block, ('row', 'col'), pairs)]
    ppermute x7 -> x8, waiting for transfers between devices: 11.2 us -> 5.28 us  [shift(): return lax.ppermute(block, ('row', 'col'), pairs)]
    unnamed x13, local copies, waits for them, and re-layouts: 2.96 us -> 3.49 us
    pallas_call x11 -> x7, Pallas kernels: 9.31 us -> 8.97 us  [call(): pl.pallas_call(body, out_shape=out_shape, in_specs=[space(o) for o in ope...]
  transfers between devices with their start and end apart: 12 -> 10, of which waited for: 5 -> 3; matrix products, arithmetic and copies ran while one was open for 9% -> 9% of each run, Pallas kernels for 23% -> 20%
where the time goes in v12:
time: 34 us; the launch traced here: 33.6 us
  starting transfers between devices  14.3 us (42%)
  Pallas kernels  8.97 us (26%)
  waiting for transfers between devices  5.28 us (16%)
  local copies, waits for them, and re-layouts  4.26 us (13%)
  between operations  0.77 us (2%)
    ppermute x8, starting transfers between devices, shift(): return lax.ppermute(block, ('row', 'col'), pairs)  13.8 us
    pallas_call x7, Pallas kernels, call(): pl.pallas_call(body, out_shape=out_shape, in_specs=[space(o) for o in ope...  8.97 us
    ppermute x8, waiting for transfers between devices, shift(): return lax.ppermute(block, ('row', 'col'), pairs)  5.28 us
    unnamed x13, local copies, waits for them, and re-layouts  3.49 us
    concatenate x1, local copies, waits for them, and re-layouts, local(): jnp.concatenate([left_gate, left_value, right_gate, right_value], 1)  0.77 us
  transfers between devices with their start and end apart: 10, of which 3 were waited for; matrix products, arithmetic and copies ran while one was open for 9% of the time, Pallas kernels for 20%

profile of v12, /device:TPU:0, one launch (start us, length us, event | category | flops | bytes accessed | tf_op | source)
XLA Modules:
  0.0 33.6 jit_solution(3241429593709653205)
XLA Ops:
  0.0 0.5 %collective-permute-start.3 = (bf16[14,56,128]{2,1,0:T(8,128)(2,1)}, bf16[14,56,128]{2,1,0:T(8,128)(2,1)S(1)}, u32[]{:S(2)}, u32[]{:S(2)}) collective-permute-start(bf16[14,56,128]{2,1,0:T(8,128)(2,1)} %bitcast.4), channel_id=1, source_target_pairs={{0,8},{8,0},{1,9},{9,1},{2,10},{10,2},{3,11},{11,3},{4,12},{12,4},... | collective-permute-start | bytes 602120 | tf_op jit(solution)/shard_map/ppermute | solution.py:247
  0.5 2.6 %collective-permute-start = (bf16[14,56,128]{2,1,0:T(8,128)(2,1)}, bf16[14,56,128]{2,1,0:T(8,128)(2,1)S(1)}, u32[]{:S(2)}, u32[]{:S(2)}) collective-permute-start(bf16[14,56,128]{2,1,0:T(8,128)(2,1)} %bitcast.5), channel_id=1, source_target_pairs={{0,2},{2,4},{4,6},{6,7},{7,5},{5,3},{3,1},{1,0},{8,9},{10,8},{12,1... | collective-permute-start | bytes 602120 | tf_op jit(solution)/shard_map/ppermute | solution.py:244
  3.1 1.3 %collective-permute-start.2 = (bf16[14,56,128]{2,1,0:T(8,128)(2,1)}, bf16[14,56,128]{2,1,0:T(8,128)(2,1)S(1)}, u32[]{:S(2)}, u32[]{:S(2)}) collective-permute-start(bf16[14,56,128]{2,1,0:T(8,128)(2,1)} %bitcast.6), channel_id=1, source_target_pairs={{0,9},{2,8},{4,10},{6,12},{7,14},{5,15},{3,13},{1,11},{8,2},{10,4}... | collective-permute-start | bytes 602120 | tf_op jit(solution)/shard_map/ppermute | solution.py:244
  4.4 0.8 %constant_dynamic-update-slice_fusion.3 = bf16[128,512]{1,0:T(8,128)(2,1)S(1)} fusion(bf16[128,128]{1,0:T(8,128)(2,1)} %param.13), kind=kLoop, calls=%fused_computation.3 | loop fusion | bytes 65536
  5.1 0.8 %constant_dynamic-update-slice_fusion.2 = bf16[128,512]{1,0:T(8,128)(2,1)S(1)} fusion(bf16[128,512]{1,0:T(8,128)(2,1)S(1)} %constant_dynamic-update-slice_fusion.3, bf16[128,128]{1,0:T(8,128)(2,1)} %param.14), kind=kLoop, calls=%fused_computation.2 | loop fusion | bytes 65536
  5.9 0.8 %constant_dynamic-update-slice_fusion.1 = bf16[128,512]{1,0:T(8,128)(2,1)S(1)} fusion(bf16[128,512]{1,0:T(8,128)(2,1)S(1)} %constant_dynamic-update-slice_fusion.2, bf16[128,128]{1,0:T(8,128)(2,1)} %param.15), kind=kLoop, calls=%fused_computation.1 | loop fusion | bytes 65536
  6.7 0.8 %constant_dynamic-update-slice_fusion.weight = bf16[128,512]{1,0:T(8,128)(2,1)S(1)} fusion(bf16[128,512]{1,0:T(8,128)(2,1)S(1)} %constant_dynamic-update-slice_fusion.1, bf16[128,128]{1,0:T(8,128)(2,1)} %param.16), kind=kLoop, calls=%fused_computation | loop fusion | bytes 65536 | tf_op jit(solution)/shard_map/concatenate | solution.py:234
  7.5 0.3 collective-permute-done.own
  7.8 2.4 %collective-permute-start.1 = (bf16[14,56,128]{2,1,0:T(8,128)(2,1)S(1)}, bf16[14,56,128]{2,1,0:T(8,128)(2,1)S(1)}, u32[]{:S(2)}, u32[]{:S(2)}) collective-permute-start(bf16[14,56,128]{2,1,0:T(8,128)(2,1)S(1)} %collective-permute-done.own), channel_id=1, source_target_pairs={{0,2},{2,4},{4,6},{6,7},{7,5},{5,3},{3,1},{1,0},{8,9},{10,8},{12,1... | collective-permute-start | bytes 602120 | tf_op jit(solution)/shard_map/ppermute | solution.py:244
  10.1 0.0 collective-permute-done.2.other
  10.2 1.6 %collective-permute-start.5 = (bf16[14,56,128]{2,1,0:T(8,128)(2,1)S(1)}, bf16[14,56,128]{2,1,0:T(8,128)(2,1)S(1)}, u32[]{:S(2)}, u32[]{:S(2)}) collective-permute-start(bf16[14,56,128]{2,1,0:T(8,128)(2,1)S(1)} %collective-permute-done.2.other), channel_id=1, source_target_pairs={{0,2},{2,4},{4,6},{6,7},{7,5},{5,3},{3,1},{1,0},{8,9},{10,8},{12,1... | collective-permute-start | bytes 602120 | tf_op jit(solution)/shard_map/ppermute | solution.py:244
  12.4 0.0 copy-start.3
  12.4 0.0 collective-permute-done.3.other
  12.4 0.6 %copy-done.3 = f32[128]{0:T(128)S(1)} copy-done((f32[128]{0:T(128)S(1)}, f32[128]{0:T(128)}, u32[]{:S(2)}) %copy-start.3) | copy-done | bytes 536
  13.0 1.0 %add_both.4 = (f32[14,56,128]{2,1,0:T(8,128)S(1)}, f32[14,56,128]{2,1,0:T(8,128)S(1)}) custom-call(s32[1]{0:T(128)S(6)} %copy.14.length, f32[1,128]{1,0:T(1,128)S(1)} %bitcast.9, bf16[128,512]{1,0:T(8,128)(2,1)S(1)} %constant_dynamic-update-slice_fusion.weight, bf16[14,56,128]{2,1,0:T(8,128)(2,1)S(1)} %bitcast.7, ...), custom_call_target="tpu_custom_call" | custom-call | flops 22478848 | bytes 532996 | tf_op jit(solution)/shard_map/add_both/pallas_call | solution.py:203
  14.0 1.8 %add_both.5 = (f32[14,56,128]{2,1,0:T(8,128)S(1)}, f32[14,56,128]{2,1,0:T(8,128)S(1)}) custom-call(s32[1]{0:T(128)S(6)} %copy.14.length, f32[1,128]{1,0:T(1,128)S(1)} %bitcast.10, bf16[128,512]{1,0:T(8,128)(2,1)S(1)} %constant_dynamic-update-slice_fusion.weight, bf16[14,56,128]{2,1,0:T(8,128)(2,1)S(1)} %collective-permute-done.own, ...), custom_call_target="tpu_custom_call" | custom-call | flops 44957696 | bytes 1335812 | tf_op jit(solution)/shard_map/add_both/pallas_call | solution.py:203
  15.8 0.0 collective-permute-done.1.own
  15.8 1.7 %collective-permute-start.4 = (bf16[14,56,128]{2,1,0:T(8,128)(2,1)S(1)}, bf16[14,56,128]{2,1,0:T(8,128)(2,1)S(1)}, u32[]{:S(2)}, u32[]{:S(2)}) collective-permute-start(bf16[14,56,128]{2,1,0:T(8,128)(2,1)S(1)} %collective-permute-done.1.own), channel_id=1, source_target_pairs={{0,2},{2,4},{4,6},{6,7},{7,5},{5,3},{3,1},{1,0},{8,9},{10,8},{12,1... | collective-permute-start | bytes 602120 | tf_op jit(solution)/shard_map/ppermute | solution.py:244
  17.5 0.0 collective-permute-done.5.other
  17.5 2.3 %collective-permute-start.8 = (bf16[14,56,128]{2,1,0:T(8,128)(2,1)S(1)}, bf16[14,56,128]{2,1,0:T(8,128)(2,1)S(1)}, u32[]{:S(2)}, u32[]{:S(2)}) collective-permute-start(bf16[14,56,128]{2,1,0:T(8,128)(2,1)S(1)} %collective-permute-done.5.other), channel_id=1, source_target_pairs={{0,2},{2,4},{4,6},{6,7},{7,5},{5,3},{3,1},{1,0},{8,9},{10,8},{12,1... | collective-permute-start | bytes 602120 | tf_op jit(solution)/shard_map/ppermute | solution.py:244
  19.9 1.1 %collective-permute-start.6 = (bf16[14,16,128]{2,1,0:T(8,128)(2,1)S(1)}, bf16[14,16,128]{2,1,0:T(8,128)(2,1)S(1)}, u32[]{:S(2)}, u32[]{:S(2)}) collective-permute-start(bf16[14,16,128]{2,1,0:T(8,128)(2,1)S(1)} %pick.1), channel_id=1, source_target_pairs={{0,4},{2,6},{4,7},{6,5},{7,3},{5,1},{3,0},{1,2},{8,11},{10,9},{12,... | collective-permute-start | bytes 172040 | tf_op jit(solution)/shard_map/ppermute | solution.py:244
  20.9 1.8 %add_both.6 = (f32[14,56,128]{2,1,0:T(8,128)S(1)}, f32[14,56,128]{2,1,0:T(8,128)S(1)}) custom-call(s32[1]{0:T(128)S(6)} %copy.14.length, f32[1,128]{1,0:T(1,128)S(1)} %bitcast.11, bf16[128,512]{1,0:T(8,128)(2,1)S(1)} %constant_dynamic-update-slice_fusion.weight, bf16[14,56,128]{2,1,0:T(8,128)(2,1)S(1)} %collective-permute-done.1.own, ...), custom_call_target="tpu_custom_call" | custom-call | flops 44957696 | bytes 1335812 | tf_op jit(solution)/shard_map/add_both/pallas_call | solution.py:203
  22.7 2.9 %collective-permute-done.6.rows = bf16[14,16,128]{2,1,0:T(8,128)(2,1)S(1)} collective-permute-done((bf16[14,16,128]{2,1,0:T(8,128)(2,1)S(1)}, bf16[14,16,128]{2,1,0:T(8,128)(2,1)S(1)}, u32[]{:S(2)}, u32[]{:S(2)}) %collective-permute-start.6) | collective-permute-done | bytes 57376 | tf_op jit(solution)/shard_map/ppermute | solution.py:244
  25.6 0.0 collective-permute-done.4.own
  25.6 0.8 %collective-permute-start.7 = (bf16[14,56,128]{2,1,0:T(8,128)(2,1)S(1)}, bf16[14,56,128]{2,1,0:T(8,128)(2,1)S(1)}, u32[]{:S(2)}, u32[]{:S(2)}) collective-permute-start(bf16[14,56,128]{2,1,0:T(8,128)(2,1)S(1)} %collective-permute-done.4.own), channel_id=1, source_target_pairs={{0,2},{2,4},{4,6},{6,7},{7,5},{5,3},{3,1},{1,0},{8,9},{10,8},{12,1... | collective-permute-start | bytes 602120 | tf_op jit(solution)/shard_map/ppermute | solution.py:244
  26.5 1.8 %add_both.7 = (f32[14,56,128]{2,1,0:T(8,128)S(1)}, bf16[14,56,128]{2,1,0:T(8,128)(2,1)S(1)}) custom-call(s32[1]{0:T(128)S(6)} %copy.14.length, f32[1,128]{1,0:T(1,128)S(1)} %bitcast.12, bf16[128,512]{1,0:T(8,128)(2,1)S(1)} %constant_dynamic-update-slice_fusion.weight, bf16[14,56,128]{2,1,0:T(8,128)(2,1)S(1)} %collective-permute-done.4.own, ...), custom_call_target="tpu_custom_call" | custom-call | flops 44957696 | bytes 1335812 | tf_op jit(solution)/shard_map/add_both/pallas_call | solution.py:203
  28.2 0.0 copy-start.4
  28.3 0.1 collective-permute-start.9
  28.4 0.5 %copy-done.4 = f32[128]{0:T(128)S(1)} copy-done((f32[128]{0:T(128)S(1)}, f32[128]{0:T(128)}, u32[]{:S(2)}) %copy-start.4) | copy-done | bytes 536
  28.9 0.5 %gate.1 = (f32[14,56,128]{2,1,0:T(8,128)S(1)}, f32[1,128]{1,0:T(1,128)S(1)}, bf16[128,128]{1,0:T(8,128)(2,1)S(1)}) custom-call(bf16[14,56,128]{2,1,0:T(8,128)(2,1)S(1)} %bitcast.8, f32[1,128]{1,0:T(1,128)S(1)} %bitcast.13, bf16[128,128]{1,0:T(8,128)(2,1)S(1)} %copy-done.1, f32[1,128]{1,0:T(1,128)S(1)} %bitcast.15, bf16[128,128]{1,0:T(8,128)(2,1)S(1)} %copy-done.2), custom_call_target="tpu_custom_call" | custom-call | flops 25690112 | bytes 267264 | tf_op jit(solution)/shard_map/gate/pallas_call | solution.py:203
  29.4 2.0 %collective-permute-done.7.own = bf16[14,56,128]{2,1,0:T(8,128)(2,1)S(1)} collective-permute-done((bf16[14,56,128]{2,1,0:T(8,128)(2,1)S(1)}, bf16[14,56,128]{2,1,0:T(8,128)(2,1)S(1)}, u32[]{:S(2)}, u32[]{:S(2)}) %collective-permute-start.7) | collective-permute-done | bytes 200736 | tf_op jit(solution)/shard_map/ppermute | solution.py:244
  31.4 2.2 %finish.1 = bf16[14,56,128]{2,1,0:T(8,128)(2,1)} custom-call(s32[1]{0:T(128)S(6)} %copy.14.length, f32[1,128]{1,0:T(1,128)S(1)} %bitcast.14, bf16[128,512]{1,0:T(8,128)(2,1)S(1)} %constant_dynamic-update-slice_fusion.weight, bf16[14,56,128]{2,1,0:T(8,128)(2,1)S(1)} %collective-permute-done.7.own, bf16[14,16,128]{2,1,0:T(8,128)(2,1)S(1)} %collective-permute-done.6.rows, ...), custom_call_target="tpu_custom_call" | custom-call | flops 22478848 | bytes 1426436 | tf_op jit(solution)/shard_map/finish/pallas_call | solution.py:203
  (9 shorter events, 0.1 us)
Async XLA Ops:
  0.0 12.4 %copy-start = (bf16[56,14,128]{2,0,1:T(8,128)(2,1)S(1)}, bf16[56,14,128]{2,0,1:T(8,128)(2,1)}, u32[]{:S(2)}) copy-start(bf16[56,14,128]{2,0,1:T(8,128)(2,1)} %param.10) | copy-start | bytes 602116
  0.0 12.4 %collective-permute-start.3 = (bf16[14,56,128]{2,1,0:T(8,128)(2,1)}, bf16[14,56,128]{2,1,0:T(8,128)(2,1)S(1)}, u32[]{:S(2)}, u32[]{:S(2)}) collective-permute-start(bf16[14,56,128]{2,1,0:T(8,128)(2,1)} %bitcast.4), channel_id=1, source_target_pairs={{0,8},{8,0},{1,9},{9,1},{2,10},{10,2},{3,11},{11,3},{4,12},{12,4},... | collective-permute-start | bytes 602120 | tf_op jit(solution)/shard_map/ppermute | solution.py:247
  0.5 7.3 %collective-permute-start = (bf16[14,56,128]{2,1,0:T(8,128)(2,1)}, bf16[14,56,128]{2,1,0:T(8,128)(2,1)S(1)}, u32[]{:S(2)}, u32[]{:S(2)}) collective-permute-start(bf16[14,56,128]{2,1,0:T(8,128)(2,1)} %bitcast.5), channel_id=1, source_target_pairs={{0,2},{2,4},{4,6},{6,7},{7,5},{5,3},{3,1},{1,0},{8,9},{10,8},{12,1... | collective-permute-start | bytes 602120 | tf_op jit(solution)/shard_map/ppermute | solution.py:244
  3.1 7.1 %collective-permute-start.2 = (bf16[14,56,128]{2,1,0:T(8,128)(2,1)}, bf16[14,56,128]{2,1,0:T(8,128)(2,1)S(1)}, u32[]{:S(2)}, u32[]{:S(2)}) collective-permute-start(bf16[14,56,128]{2,1,0:T(8,128)(2,1)} %bitcast.6), channel_id=1, source_target_pairs={{0,9},{2,8},{4,10},{6,12},{7,14},{5,15},{3,13},{1,11},{8,2},{10,4}... | collective-permute-start | bytes 602120 | tf_op jit(solution)/shard_map/ppermute | solution.py:244
  7.8 8.0 %collective-permute-start.1 = (bf16[14,56,128]{2,1,0:T(8,128)(2,1)S(1)}, bf16[14,56,128]{2,1,0:T(8,128)(2,1)S(1)}, u32[]{:S(2)}, u32[]{:S(2)}) collective-permute-start(bf16[14,56,128]{2,1,0:T(8,128)(2,1)S(1)} %collective-permute-done.own), channel_id=1, source_target_pairs={{0,2},{2,4},{4,6},{6,7},{7,5},{5,3},{3,1},{1,0},{8,9},{10,8},{12,1... | collective-permute-start | bytes 602120 | tf_op jit(solution)/shard_map/ppermute | solution.py:244
  10.2 7.4 %collective-permute-start.5 = (bf16[14,56,128]{2,1,0:T(8,128)(2,1)S(1)}, bf16[14,56,128]{2,1,0:T(8,128)(2,1)S(1)}, u32[]{:S(2)}, u32[]{:S(2)}) collective-permute-start(bf16[14,56,128]{2,1,0:T(8,128)(2,1)S(1)} %collective-permute-done.2.other), channel_id=1, source_target_pairs={{0,2},{2,4},{4,6},{6,7},{7,5},{5,3},{3,1},{1,0},{8,9},{10,8},{12,1... | collective-permute-start | bytes 602120 | tf_op jit(solution)/shard_map/ppermute | solution.py:244
  12.4 0.7 %copy-start.3 = (f32[128]{0:T(128)S(1)}, f32[128]{0:T(128)}, u32[]{:S(2)}) copy-start(f32[128]{0:T(128)} %param.12) | copy-start | bytes 1540
  15.8 9.8 %collective-permute-start.4 = (bf16[14,56,128]{2,1,0:T(8,128)(2,1)S(1)}, bf16[14,56,128]{2,1,0:T(8,128)(2,1)S(1)}, u32[]{:S(2)}, u32[]{:S(2)}) collective-permute-start(bf16[14,56,128]{2,1,0:T(8,128)(2,1)S(1)} %collective-permute-done.1.own), channel_id=1, source_target_pairs={{0,2},{2,4},{4,6},{6,7},{7,5},{5,3},{3,1},{1,0},{8,9},{10,8},{12,1... | collective-permute-start | bytes 602120 | tf_op jit(solution)/shard_map/ppermute | solution.py:244
  17.5 9.0 %collective-permute-start.8 = (bf16[14,56,128]{2,1,0:T(8,128)(2,1)S(1)}, bf16[14,56,128]{2,1,0:T(8,128)(2,1)S(1)}, u32[]{:S(2)}, u32[]{:S(2)}) collective-permute-start(bf16[14,56,128]{2,1,0:T(8,128)(2,1)S(1)} %collective-permute-done.5.other), channel_id=1, source_target_pairs={{0,2},{2,4},{4,6},{6,7},{7,5},{5,3},{3,1},{1,0},{8,9},{10,8},{12,1... | collective-permute-start | bytes 602120 | tf_op jit(solution)/shard_map/ppermute | solution.py:244
  19.9 5.7 %collective-permute-start.6 = (bf16[14,16,128]{2,1,0:T(8,128)(2,1)S(1)}, bf16[14,16,128]{2,1,0:T(8,128)(2,1)S(1)}, u32[]{:S(2)}, u32[]{:S(2)}) collective-permute-start(bf16[14,16,128]{2,1,0:T(8,128)(2,1)S(1)} %pick.1), channel_id=1, source_target_pairs={{0,4},{2,6},{4,7},{6,5},{7,3},{5,1},{3,0},{1,2},{8,11},{10,9},{12,... | collective-permute-start | bytes 172040 | tf_op jit(solution)/shard_map/ppermute | solution.py:244
  25.6 2.7 %copy-start.1 = (bf16[128,128]{1,0:T(8,128)(2,1)S(1)}, bf16[128,128]{1,0:T(8,128)(2,1)}, u32[]{:S(2)}) copy-start(bf16[128,128]{1,0:T(8,128)(2,1)} %out_gate.1) | copy-start | bytes 98308
  25.6 2.7 %copy-start.2 = (bf16[128,128]{1,0:T(8,128)(2,1)S(1)}, bf16[128,128]{1,0:T(8,128)(2,1)}, u32[]{:S(2)}) copy-start(bf16[128,128]{1,0:T(8,128)(2,1)} %last_weight.1) | copy-start | bytes 98308
  25.6 5.8 %collective-permute-start.7 = (bf16[14,56,128]{2,1,0:T(8,128)(2,1)S(1)}, bf16[14,56,128]{2,1,0:T(8,128)(2,1)S(1)}, u32[]{:S(2)}, u32[]{:S(2)}) collective-permute-start(bf16[14,56,128]{2,1,0:T(8,128)(2,1)S(1)} %collective-permute-done.4.own), channel_id=1, source_target_pairs={{0,2},{2,4},{4,6},{6,7},{7,5},{5,3},{3,1},{1,0},{8,9},{10,8},{12,1... | collective-permute-start | bytes 602120 | tf_op jit(solution)/shard_map/ppermute | solution.py:244
  28.2 0.7 %copy-start.4 = (f32[128]{0:T(128)S(1)}, f32[128]{0:T(128)}, u32[]{:S(2)}) copy-start(f32[128]{0:T(128)} %param.18) | copy-start | bytes 1540
  28.3 3.2 %collective-permute-start.9 = (bf16[14,56,128]{2,1,0:T(8,128)(2,1)S(1)}, bf16[14,56,128]{2,1,0:T(8,128)(2,1)S(1)}, u32[]{:S(2)}, u32[]{:S(2)}) collective-permute-start(bf16[14,56,128]{2,1,0:T(8,128)(2,1)S(1)} %get-tuple-element.45), channel_id=1, source_target_pairs={{0,8},{8,0},{1,9},{9,1},{2,10},{10,2},{3,11},{11,3},{4,12},{12,4},... | collective-permute-start | bytes 602120 | tf_op jit(solution)/shard_map/ppermute | solution.py:247

commit v13 on v12

--- a/solution.py
+++ b/solution.py
@@ -52,12 +52,13 @@
     return jnp.dot(left, right, preferred_element_type=F32)
 
 
-def gate(s, pair, gain, out_gate, last_gain, last_weight, gating, kept_gain, kept_weight):
+def gate(s, pair, shared, out_gate, last_gain, last_weight, gating, kept_gain, kept_weight):
+    gain = Shared(s, shared).gain
     kept_gain[...] = last_gain[...]
     kept_weight[...] = last_weight[...]
     for start in range(0, s.width, s.half):
         normed = [
-            normalise(pair[start + step].astype(F32)) * gain[...] for step in range(s.half)
+            normalise(pair[start + step].astype(F32)) * gain for step in range(s.half)
         ]
         value = sigmoid(dot(jnp.concatenate(normed, 0).astype(BF16), out_gate[...]))
         for step in range(s.half):
@@ -116,38 +117,60 @@
     return column_at((place_of(col, s.cols) + step + s.cols) % s.cols, s.cols)
 
 
+class Shared:
+    def __init__(self, s, ref):
+        h = s.hidden
+        self.left = ref[: s.channels, : 2 * h].astype(BF16)
+        self.right = ref[: s.channels, 2 * h :].astype(BF16)
+        self.gain = ref[s.channels : s.channels + 1, : s.channels]
+        self.limit = ref[s.channels + 1 : s.channels + 2, :1].astype(jnp.int32)
+
+
+def join(s, length, gain, left_gate, left_value, right_gate, right_value, shared):
+    h = s.hidden
+    for at, part in enumerate((left_gate, left_value, right_gate, right_value)):
+        shared[: s.channels, at * h : (at + 1) * h] = part[...].astype(F32)
+    shared[s.channels : s.channels + 1, : s.channels] = gain[...]
+    shared[s.channels + 1 : s.channels + 2, :] = jnp.full((1, 4 * h), length[0]).astype(F32)
+
+
 def gated(s, rows, gain, weight, masks):
     h, size = s.hidden, rows[0].shape[0]
-    rows = [normalise(row) * gain[...] for row in rows]
+    rows = [normalise(row) * gain for row in rows]
     out = dot(jnp.concatenate(rows, 0).astype(BF16), weight)
     value = sigmoid(out[:, :h]) * out[:, h:]
     return [value[at * size : (at + 1) * size] * mask for at, mask in enumerate(masks)]
 
 
-def project_right(s, rows_of, base, depth, token, limit, gain, weight, partner):
+def masks_of(tokens, first, count, limit):
+    below = (lax.broadcasted_iota(jnp.int32, (count, 1), 0) + first < limit).astype(F32)
+    return [below * (token < limit).astype(F32) for token in tokens]
+
+
+def project_right(s, rows_of, base, depth, token, shared, partner):
     first = lax.axis_index("col") * s.width
-    mine = lax.broadcasted_iota(jnp.int32, (s.slots, 1), 0) + first < limit
     for start in range(0, depth, s.half):
         steps = range(start, start + s.half)
-        masks = [(mine & (token + step < limit)).astype(F32) for step in steps]
+        masks = masks_of([token + step for step in steps], first, s.slots, shared.limit)
         rows = [rows_of(base + step) for step in steps]
-        for step, part in zip(steps, gated(s, rows, gain, weight[:, 2 * s.hidden :], masks)):
+        for step, part in zip(steps, gated(s, rows, shared.gain, shared.right, masks)):
             partner[step] = part
 
 
-def project_left(s, block, row, base, depth, token, limit, gain, weight, left):
-    below = lax.broadcasted_iota(jnp.int32, (s.height, 1), 0) + row * s.height < limit
+def project_left(s, block, row, base, depth, token, shared, left):
+    first = row * s.height
     for start in range(0, depth, s.half):
         steps = range(start, start + s.half)
-        masks = [(below & (token + step < limit)).astype(F32) for step in steps]
+        masks = masks_of([token + step for step in steps], first, s.height, shared.limit)
         rows = [block[base + step].astype(F32) for step in steps]
-        for step, part in zip(steps, gated(s, rows, gain, weight[:, : 2 * s.hidden], masks)):
+        for step, part in zip(steps, gated(s, rows, shared.gain, shared.left, masks)):
             left[step] = part
 
 
-def add_both(s, distance, narrow, length, gain, weight, own, other, *refs):
+def add_both(s, distance, narrow, shared, own, other, *refs):
     before, (mine, theirs, left, right, picked, partner) = refs[:-6], refs[-6:]
-    row, col, limit = lax.axis_index("row"), lax.axis_index("col"), length[0]
+    row, col = lax.axis_index("row"), lax.axis_index("col")
+    shared = Shared(s, shared)
     depth = left.shape[0]
     base = row * s.half if distance == 0 else 0
     token = column_from(s, distance) * s.width + base
@@ -156,9 +179,9 @@
     def rows_of(at):
         return picked[at, pl.ds(offset_in(s, col), s.slots), :]
 
-    project_right(s, rows_of, base, depth, token, limit, gain, weight, partner)
-    project_left(s, own, row, base, depth, token, limit, gain, weight, left)
-    project_left(s, other, 1 - row, base, depth, token, limit, gain, weight, right)
+    project_right(s, rows_of, base, depth, token, shared, partner)
+    project_left(s, own, row, base, depth, token, shared, left)
+    project_left(s, other, 1 - row, base, depth, token, shared, right)
     old_mine, old_theirs = before if before else (None, None)
     accumulate(s, left, partner, old_mine, mine)
     if not narrow:
@@ -175,14 +198,12 @@
         rows[step] = picked[step, pl.ds(offset_in(s, col), s.slots), :].astype(BF16)
 
 
-def finish(s, length, gain, weight, own, rows, mine, given, gating, last_gain, last_weight, *refs):
+def finish(s, shared, own, rows, mine, given, gating, last_gain, last_weight, *refs):
     update, left, partner, total = refs
     token = column_from(s, s.cols // 2) * s.width
-    limit, row = length[0], lax.axis_index("row")
-    project_right(
-        s, lambda at: rows[at].astype(F32), 0, s.width, token, limit, gain, weight, partner
-    )
-    project_left(s, own, row, 0, s.width, token, limit, gain, weight, left)
+    shared = Shared(s, shared)
+    project_right(s, lambda at: rows[at].astype(F32), 0, s.width, token, shared, partner)
+    project_left(s, own, lax.axis_index("row"), 0, s.width, token, shared, left)
     accumulate(s, left, partner, mine, total)
     for start in range(0, s.width, s.half):
         settled = [
@@ -195,7 +216,7 @@
             update[start + step] = part.astype(BF16)
 
 
-def call(body, out_shape, scratch, flops, *operands):
+def call(body, out_shape, scratch, flops, *operands, grant=24):
     def space(operand):
         return pl.BlockSpec(memory_space=pltpu.SMEM if operand.dtype == jnp.int32 else pltpu.VMEM)
 
@@ -206,7 +227,7 @@
         in_specs=[space(o) for o in operands],
         out_specs=jax.tree.map(lambda _: pl.BlockSpec(memory_space=pltpu.VMEM), out_shape),
         scratch_shapes=scratch,
-        compiler_params=pltpu.CompilerParams(vmem_limit_bytes=24 * 1024 * 1024),
+        compiler_params=pltpu.CompilerParams(vmem_limit_bytes=grant * 1024 * 1024),
         cost_estimate=pl.CostEstimate(flops=flops, bytes_accessed=sent, transcendentals=0),
         name=body.func.__name__,
     )(*operands)
@@ -231,7 +252,19 @@
     shape = jax.ShapeDtypeStruct
     pair = jnp.transpose(pair_state, (1, 0, 2))
     gain = input_gain.reshape(1, channels)
-    weights = jnp.concatenate([left_gate, left_value, right_gate, right_value], 1)
+    shared = call(
+        functools.partial(join, s),
+        shape((channels + 8, 4 * hidden), F32),
+        [],
+        0,
+        valid_length,
+        gain,
+        left_gate,
+        left_value,
+        right_gate,
+        right_value,
+        grant=56,
+    )
     order = ring(s.cols)
 
     def shift(block, crossed=False, by=1):
@@ -247,7 +280,6 @@
         return lax.ppermute(block, "row", [(at, (at + 1) % s.rows) for at in range(s.rows)])
 
     sums = shape((width, height, hidden), F32)
-    common = (valid_length, gain, weights)
     product = 16 * height * width * hidden
     tokens = pltpu.VMEM((width, height, hidden), F32)
     halved = pltpu.VMEM((s.half, height, hidden), F32)
@@ -262,7 +294,7 @@
             [sums, shape(sums.shape, BF16) if narrow else sums],
             [left, left, padded, right],
             2 * left.shape[0] * product,
-            *common,
+            shared,
             own,
             other,
             *before,
@@ -276,7 +308,7 @@
     other = shift(pair, crossed=True)
     own = shift(pair)
     total = add(0, pair, swap(pair), ())
-    other, own = in_turn(other, own, weights)
+    other, own = in_turn(other, own, total)
     rows = ()
     for distance in range(1, far - 1):
         ahead = [shift(other), shift(own)]
@@ -291,8 +323,7 @@
             )
             rows = shift(rows, by=2)
         total = add(distance, own, other, total)
-        done = (total, rows)
-        other, own = in_turn(*ahead, done)
+        other, own = in_turn(*ahead, total)
     last = shift(own)
     gating = call(
         functools.partial(gate, s),
@@ -300,11 +331,12 @@
         [],
         2 * height * width * channels * channels,
         pair,
-        gain,
+        shared,
         out_gate,
         output_gain.reshape(1, hidden),
         out_weight,
     )
+    own, other, rows = lax.optimization_barrier((own, other, rows))
     mine, theirs = add(far - 1, own, other, total, narrow=True)
     given = swap(theirs)
     last, mine, gating = lax.optimization_barrier((last, mine, gating))
@@ -313,7 +345,7 @@
         shape((width, height, channels), BF16),
         [tokens, partner, pltpu.VMEM(sums.shape, F32)],
         width * product,
-        *common,
+        shared,
         last,
         rows,
         mine,

time: 34 us -> 34.7 us (1.021)
  Pallas kernels: 8.97 us -> 16.9 us
  waiting for transfers between devices: 5.28 us -> 0.45 us
  local copies, waits for them, and re-layouts: 4.26 us -> 1.53 us
  starting transfers between devices: 14.3 us -> 14.9 us
    pallas_call x7 -> x8, Pallas kernels: 8.97 us -> 16.9 us  [call(): pl.pallas_call(body, out_shape=out_shape, in_specs=[space(o) for o in ope...]
    ppermute x8, waiting for transfers between devices: 5.28 us -> 0.08 us  [shift(): return lax.ppermute(block, ('row', 'col'), pairs)]
    unnamed x13 -> x12, local copies, waits for them, and re-layouts: 3.49 us -> 1.53 us
    concatenate x1 -> x0, local copies, waits for them, and re-layouts: 0.77 us -> none  [local(): jnp.concatenate([left_gate, left_value, right_gate, right_value], 1)]
    ppermute x8, starting transfers between devices: 13.8 us -> 14.4 us  [shift(): return lax.ppermute(block, ('row', 'col'), pairs)]
    ppermute x2, waiting for transfers between devices: 0.01 us -> 0.37 us  [swap(): lax.ppermute(block, 'row', [(at, (at + 1) % s.rows) for at in range(s.row...]
  transfers between devices with their start and end apart: 10 -> 10, of which waited for: 3 -> 2; matrix products, arithmetic and copies ran while one was open for 9% -> 0% of each run, Pallas kernels for 20% -> 41%
where the time goes in v13:
time: 34.7 us; the launch traced here: 34.5 us
  Pallas kernels  16.9 us (49%)
  starting transfers between devices  14.9 us (43%)
  local copies, waits for them, and re-layouts  1.53 us (4%)
  between operations  0.8 us (2%)
  waiting for transfers between devices  0.45 us (1%)
    pallas_call x8, Pallas kernels, call(): pl.pallas_call(body, out_shape=out_shape, in_specs=[space(o) for o in ope...  16.9 us
    ppermute x8, starting transfers between devices, shift(): return lax.ppermute(block, ('row', 'col'), pairs)  14.4 us
    unnamed x12, local copies, waits for them, and re-layouts  1.53 us
  transfers between devices with their start and end apart: 10, of which 2 were waited for; matrix products, arithmetic and copies ran while one was open for 0% of the time, Pallas kernels for 41%

profile of v13, /device:TPU:0, one launch (start us, length us, event | category | flops | bytes accessed | tf_op | source)
XLA Modules:
  0.0 34.5 jit_solution(4713695867327369013)
XLA Ops:
  0.0 0.5 %collective-permute-start.1 = (bf16[14,56,128]{2,1,0:T(8,128)(2,1)}, bf16[14,56,128]{2,1,0:T(8,128)(2,1)S(1)}, u32[]{:S(2)}, u32[]{:S(2)}) collective-permute-start(bf16[14,56,128]{2,1,0:T(8,128)(2,1)} %bitcast.4), channel_id=1, source_target_pairs={{0,8},{8,0},{1,9},{9,1},{2,10},{10,2},{3,11},{11,3},{4,12},{12,4},... | collective-permute-start | bytes 602120 | tf_op jit(solution)/shard_map/ppermute | solution.py:280
  0.5 2.6 %collective-permute-start = (bf16[14,56,128]{2,1,0:T(8,128)(2,1)}, bf16[14,56,128]{2,1,0:T(8,128)(2,1)S(1)}, u32[]{:S(2)}, u32[]{:S(2)}) collective-permute-start(bf16[14,56,128]{2,1,0:T(8,128)(2,1)} %bitcast.5), channel_id=1, source_target_pairs={{0,2},{2,4},{4,6},{6,7},{7,5},{5,3},{3,1},{1,0},{8,9},{10,8},{12,1... | collective-permute-start | bytes 602120 | tf_op jit(solution)/shard_map/ppermute | solution.py:277
  3.0 1.4 %collective-permute-start.3 = (bf16[14,56,128]{2,1,0:T(8,128)(2,1)}, bf16[14,56,128]{2,1,0:T(8,128)(2,1)S(1)}, u32[]{:S(2)}, u32[]{:S(2)}) collective-permute-start(bf16[14,56,128]{2,1,0:T(8,128)(2,1)} %bitcast.6), channel_id=1, source_target_pairs={{0,9},{2,8},{4,10},{6,12},{7,14},{5,15},{3,13},{1,11},{8,2},{10,4}... | collective-permute-start | bytes 602120 | tf_op jit(solution)/shard_map/ppermute | solution.py:277
  5.0 1.6 %join.1.shared = f32[136,512]{1,0:T(8,128)} custom-call(s32[1]{0:T(128)S(6)} %copy.11.length, f32[1,128]{1,0:T(1,128)} %bitcast.10, bf16[128,128]{1,0:T(8,128)(2,1)} %left_gate.1, bf16[128,128]{1,0:T(8,128)(2,1)} %left_value.1, bf16[128,128]{1,0:T(8,128)(2,1)} %right_gate.1, bf16[128,128]{1,0:T(8,128)(2,1)} %right_value.1), custom_call_target="tpu_custom_call" | custom-call | bytes 131588 | tf_op jit(solution)/shard_map/join/pallas_call | solution.py:224
  6.6 0.0 collective-permute-done.1.other
  6.6 1.0 %copy-done = f32[136,512]{1,0:T(8,128)S(1)} copy-done((f32[136,512]{1,0:T(8,128)S(1)}, f32[136,512]{1,0:T(8,128)}, u32[]{:S(2)}) %copy-start) | copy-done | bytes 278552
  7.6 1.4 %add_both.4 = (f32[14,56,128]{2,1,0:T(8,128)S(1)}, f32[14,56,128]{2,1,0:T(8,128)S(1)}) custom-call(f32[136,512]{1,0:T(8,128)S(1)} %copy-done, bf16[14,56,128]{2,1,0:T(8,128)(2,1)S(1)} %bitcast.7, bf16[14,56,128]{2,1,0:T(8,128)(2,1)S(1)} %collective-permute-done.1.other), custom_call_target="tpu_custom_call" | custom-call | flops 22478848 | bytes 679936 | tf_op jit(solution)/shard_map/add_both/pallas_call | solution.py:224
  9.0 0.0 collective-permute-done.own
  9.0 1.1 %collective-permute-start.2 = (bf16[14,56,128]{2,1,0:T(8,128)(2,1)S(1)}, bf16[14,56,128]{2,1,0:T(8,128)(2,1)S(1)}, u32[]{:S(2)}, u32[]{:S(2)}) collective-permute-start(bf16[14,56,128]{2,1,0:T(8,128)(2,1)S(1)} %collective-permute-done.own), channel_id=1, source_target_pairs={{0,2},{2,4},{4,6},{6,7},{7,5},{5,3},{3,1},{1,0},{8,9},{10,8},{12,1... | collective-permute-start | bytes 602120 | tf_op jit(solution)/shard_map/ppermute | solution.py:277
  10.1 0.0 collective-permute-done.3.other
  10.1 1.6 %collective-permute-start.5 = (bf16[14,56,128]{2,1,0:T(8,128)(2,1)S(1)}, bf16[14,56,128]{2,1,0:T(8,128)(2,1)S(1)}, u32[]{:S(2)}, u32[]{:S(2)}) collective-permute-start(bf16[14,56,128]{2,1,0:T(8,128)(2,1)S(1)} %collective-permute-done.3.other), channel_id=1, source_target_pairs={{0,2},{2,4},{4,6},{6,7},{7,5},{5,3},{3,1},{1,0},{8,9},{10,8},{12,1... | collective-permute-start | bytes 602120 | tf_op jit(solution)/shard_map/ppermute | solution.py:277
  11.7 3.5 %add_both.5 = (f32[14,56,128]{2,1,0:T(8,128)S(1)}, f32[14,56,128]{2,1,0:T(8,128)S(1)}) custom-call(f32[136,512]{1,0:T(8,128)S(1)} %copy-done, bf16[14,56,128]{2,1,0:T(8,128)(2,1)S(1)} %collective-permute-done.own, bf16[14,56,128]{2,1,0:T(8,128)(2,1)S(1)} %collective-permute-done.3.other, f32[14,56,128]{2,1,0:T(8,128)S(1)} %get-tuple-element.30.refs_0_, ...), custom_call_target="tpu_custom_call" | custom-call | flops 44957696 | bytes 1482752 | tf_op jit(solution)/shard_map/add_both/pallas_call | solution.py:224
  15.2 0.0 collective-permute-done.2.own
  15.2 1.7 %collective-permute-start.4 = (bf16[14,56,128]{2,1,0:T(8,128)(2,1)S(1)}, bf16[14,56,128]{2,1,0:T(8,128)(2,1)S(1)}, u32[]{:S(2)}, u32[]{:S(2)}) collective-permute-start(bf16[14,56,128]{2,1,0:T(8,128)(2,1)S(1)} %collective-permute-done.2.own), channel_id=1, source_target_pairs={{0,2},{2,4},{4,6},{6,7},{7,5},{5,3},{3,1},{1,0},{8,9},{10,8},{12,1... | collective-permute-start | bytes 602120 | tf_op jit(solution)/shard_map/ppermute | solution.py:277
  16.9 0.1 collective-permute-done.5.other
  17.0 2.3 %collective-permute-start.7 = (bf16[14,56,128]{2,1,0:T(8,128)(2,1)S(1)}, bf16[14,56,128]{2,1,0:T(8,128)(2,1)S(1)}, u32[]{:S(2)}, u32[]{:S(2)}) collective-permute-start(bf16[14,56,128]{2,1,0:T(8,128)(2,1)S(1)} %collective-permute-done.5.other), channel_id=1, source_target_pairs={{0,2},{2,4},{4,6},{6,7},{7,5},{5,3},{3,1},{1,0},{8,9},{10,8},{12,1... | collective-permute-start | bytes 602120 | tf_op jit(solution)/shard_map/ppermute | solution.py:277
  19.3 1.6 %collective-permute-start.8 = (bf16[14,16,128]{2,1,0:T(8,128)(2,1)S(1)}, bf16[14,16,128]{2,1,0:T(8,128)(2,1)S(1)}, u32[]{:S(2)}, u32[]{:S(2)}) collective-permute-start(bf16[14,16,128]{2,1,0:T(8,128)(2,1)S(1)} %pick.1), channel_id=1, source_target_pairs={{0,4},{2,6},{4,7},{6,5},{7,3},{5,1},{3,0},{1,2},{8,11},{10,9},{12,... | collective-permute-start | bytes 172040 | tf_op jit(solution)/shard_map/ppermute | solution.py:277
  20.9 3.5 %add_both.6 = (f32[14,56,128]{2,1,0:T(8,128)S(1)}, f32[14,56,128]{2,1,0:T(8,128)S(1)}) custom-call(f32[136,512]{1,0:T(8,128)S(1)} %copy-done.1, bf16[14,56,128]{2,1,0:T(8,128)(2,1)S(1)} %collective-permute-done.2.own, bf16[14,56,128]{2,1,0:T(8,128)(2,1)S(1)} %collective-permute-done.5.other, f32[14,56,128]{2,1,0:T(8,128)S(1)} %get-tuple-element.34.refs_0_, ...), custom_call_target="tpu_custom_call" | custom-call | flops 44957696 | bytes 1482752 | tf_op jit(solution)/shard_map/add_both/pallas_call | solution.py:224
  24.4 0.0 collective-permute-done.4.own
  24.4 0.0 copy-start.3
  24.4 0.0 copy-start.4
  24.4 2.2 %collective-permute-start.6 = (bf16[14,56,128]{2,1,0:T(8,128)(2,1)S(1)}, bf16[14,56,128]{2,1,0:T(8,128)(2,1)S(1)}, u32[]{:S(2)}, u32[]{:S(2)}) collective-permute-start(bf16[14,56,128]{2,1,0:T(8,128)(2,1)S(1)} %collective-permute-done.4.own), channel_id=1, source_target_pairs={{0,2},{2,4},{4,6},{6,7},{7,5},{5,3},{3,1},{1,0},{8,9},{10,8},{12,1... | collective-permute-start | bytes 602120 | tf_op jit(solution)/shard_map/ppermute | solution.py:277
  26.6 0.0 collective-permute-done.7.other
  26.6 0.0 collective-permute-done.8.rows
  26.6 3.5 %add_both.7 = (f32[14,56,128]{2,1,0:T(8,128)S(1)}, bf16[14,56,128]{2,1,0:T(8,128)(2,1)S(1)}) custom-call(f32[136,512]{1,0:T(8,128)S(1)} %copy-done.1, bf16[14,56,128]{2,1,0:T(8,128)(2,1)S(1)} %collective-permute-done.4.own, bf16[14,56,128]{2,1,0:T(8,128)(2,1)S(1)} %collective-permute-done.7.other, f32[14,56,128]{2,1,0:T(8,128)S(1)} %get-tuple-element.38.refs_0_, ...), custom_call_target="tpu_custom_call" | custom-call | flops 44957696 | bytes 1482752 | tf_op jit(solution)/shard_map/add_both/pallas_call | solution.py:224
  30.2 0.0 copy-start.5
  30.2 0.1 collective-permute-start.9
  30.3 0.5 %copy-done.5 = f32[128]{0:T(128)S(1)} copy-done((f32[128]{0:T(128)S(1)}, f32[128]{0:T(128)}, u32[]{:S(2)}) %copy-start.5) | copy-done | bytes 536
  30.8 0.5 %gate.1 = (f32[14,56,128]{2,1,0:T(8,128)S(1)}, f32[1,128]{1,0:T(1,128)S(1)}, bf16[128,128]{1,0:T(8,128)(2,1)S(1)}) custom-call(bf16[14,56,128]{2,1,0:T(8,128)(2,1)S(1)} %bitcast.8, f32[136,512]{1,0:T(8,128)S(1)} %copy-done.1, bf16[128,128]{1,0:T(8,128)(2,1)S(1)} %copy-done.3, f32[1,128]{1,0:T(1,128)S(1)} %bitcast.9, bf16[128,128]{1,0:T(8,128)(2,1)S(1)} %copy-done.4), custom_call_target="tpu_custom_call" | custom-call | flops 25690112 | bytes 545280 | tf_op jit(solution)/shard_map/gate/pallas_call | solution.py:224
  31.3 0.0 collective-permute-done.6.own
  31.3 0.4 %collective-permute-done.9.given = bf16[14,56,128]{2,1,0:T(8,128)(2,1)S(1)} collective-permute-done((bf16[14,56,128]{2,1,0:T(8,128)(2,1)S(1)}, bf16[14,56,128]{2,1,0:T(8,128)(2,1)S(1)}, u32[]{:S(2)}, u32[]{:S(2)}) %collective-permute-start.9) | collective-permute-done | bytes 200736 | tf_op jit(solution)/shard_map/ppermute | solution.py:280
  31.7 2.8 %finish.1 = bf16[14,56,128]{2,1,0:T(8,128)(2,1)} custom-call(f32[136,512]{1,0:T(8,128)S(1)} %copy-done.1, bf16[14,56,128]{2,1,0:T(8,128)(2,1)S(1)} %collective-permute-done.6.own, bf16[14,16,128]{2,1,0:T(8,128)(2,1)S(1)} %collective-permute-done.8.rows, f32[14,56,128]{2,1,0:T(8,128)S(1)} %get-tuple-element.50.mine, ...), custom_call_target="tpu_custom_call" | custom-call | flops 22478848 | bytes 1573376 | tf_op jit(solution)/shard_map/finish/pallas_call | solution.py:224
  (8 shorter events, 0.0 us)
Async XLA Ops:
  0.0 6.6 %collective-permute-start.1 = (bf16[14,56,128]{2,1,0:T(8,128)(2,1)}, bf16[14,56,128]{2,1,0:T(8,128)(2,1)S(1)}, u32[]{:S(2)}, u32[]{:S(2)}) collective-permute-start(bf16[14,56,128]{2,1,0:T(8,128)(2,1)} %bitcast.4), channel_id=1, source_target_pairs={{0,8},{8,0},{1,9},{9,1},{2,10},{10,2},{3,11},{11,3},{4,12},{12,4},... | collective-permute-start | bytes 602120 | tf_op jit(solution)/shard_map/ppermute | solution.py:280
  0.5 8.6 %collective-permute-start = (bf16[14,56,128]{2,1,0:T(8,128)(2,1)}, bf16[14,56,128]{2,1,0:T(8,128)(2,1)S(1)}, u32[]{:S(2)}, u32[]{:S(2)}) collective-permute-start(bf16[14,56,128]{2,1,0:T(8,128)(2,1)} %bitcast.5), channel_id=1, source_target_pairs={{0,2},{2,4},{4,6},{6,7},{7,5},{5,3},{3,1},{1,0},{8,9},{10,8},{12,1... | collective-permute-start | bytes 602120 | tf_op jit(solution)/shard_map/ppermute | solution.py:277
  3.0 7.1 %collective-permute-start.3 = (bf16[14,56,128]{2,1,0:T(8,128)(2,1)}, bf16[14,56,128]{2,1,0:T(8,128)(2,1)S(1)}, u32[]{:S(2)}, u32[]{:S(2)}) collective-permute-start(bf16[14,56,128]{2,1,0:T(8,128)(2,1)} %bitcast.6), channel_id=1, source_target_pairs={{0,9},{2,8},{4,10},{6,12},{7,14},{5,15},{3,13},{1,11},{8,2},{10,4}... | collective-permute-start | bytes 602120 | tf_op jit(solution)/shard_map/ppermute | solution.py:277
  5.0 1.6 %copy-start.2 = (bf16[56,14,128]{2,0,1:T(8,128)(2,1)S(1)}, bf16[56,14,128]{2,0,1:T(8,128)(2,1)}, u32[]{:S(2)}) copy-start(bf16[56,14,128]{2,0,1:T(8,128)(2,1)} %param.10) | copy-start | bytes 602116
  6.6 1.0 %copy-start = (f32[136,512]{1,0:T(8,128)S(1)}, f32[136,512]{1,0:T(8,128)}, u32[]{:S(2)}) copy-start(f32[136,512]{1,0:T(8,128)} %join.1.shared) | copy-start | bytes 835588
  9.0 6.1 %collective-permute-start.2 = (bf16[14,56,128]{2,1,0:T(8,128)(2,1)S(1)}, bf16[14,56,128]{2,1,0:T(8,128)(2,1)S(1)}, u32[]{:S(2)}, u32[]{:S(2)}) collective-permute-start(bf16[14,56,128]{2,1,0:T(8,128)(2,1)S(1)} %collective-permute-done.own), channel_id=1, source_target_pairs={{0,2},{2,4},{4,6},{6,7},{7,5},{5,3},{3,1},{1,0},{8,9},{10,8},{12,1... | collective-permute-start | bytes 602120 | tf_op jit(solution)/shard_map/ppermute | solution.py:277
  10.1 6.9 %collective-permute-start.5 = (bf16[14,56,128]{2,1,0:T(8,128)(2,1)S(1)}, bf16[14,56,128]{2,1,0:T(8,128)(2,1)S(1)}, u32[]{:S(2)}, u32[]{:S(2)}) collective-permute-start(bf16[14,56,128]{2,1,0:T(8,128)(2,1)S(1)} %collective-permute-done.3.other), channel_id=1, source_target_pairs={{0,2},{2,4},{4,6},{6,7},{7,5},{5,3},{3,1},{1,0},{8,9},{10,8},{12,1... | collective-permute-start | bytes 602120 | tf_op jit(solution)/shard_map/ppermute | solution.py:277
  15.2 5.7 %copy-start.1 = (f32[136,512]{1,0:T(8,128)S(1)}, f32[136,512]{1,0:T(8,128)}, u32[]{:S(2)}) copy-start(f32[136,512]{1,0:T(8,128)} %join.1.shared) | copy-start | bytes 835588
  15.2 9.2 %collective-permute-start.4 = (bf16[14,56,128]{2,1,0:T(8,128)(2,1)S(1)}, bf16[14,56,128]{2,1,0:T(8,128)(2,1)S(1)}, u32[]{:S(2)}, u32[]{:S(2)}) collective-permute-start(bf16[14,56,128]{2,1,0:T(8,128)(2,1)S(1)} %collective-permute-done.2.own), channel_id=1, source_target_pairs={{0,2},{2,4},{4,6},{6,7},{7,5},{5,3},{3,1},{1,0},{8,9},{10,8},{12,1... | collective-permute-start | bytes 602120 | tf_op jit(solution)/shard_map/ppermute | solution.py:277
  17.0 9.7 %collective-permute-start.7 = (bf16[14,56,128]{2,1,0:T(8,128)(2,1)S(1)}, bf16[14,56,128]{2,1,0:T(8,128)(2,1)S(1)}, u32[]{:S(2)}, u32[]{:S(2)}) collective-permute-start(bf16[14,56,128]{2,1,0:T(8,128)(2,1)S(1)} %collective-permute-done.5.other), channel_id=1, source_target_pairs={{0,2},{2,4},{4,6},{6,7},{7,5},{5,3},{3,1},{1,0},{8,9},{10,8},{12,1... | collective-permute-start | bytes 602120 | tf_op jit(solution)/shard_map/ppermute | solution.py:277
  19.3 7.4 %collective-permute-start.8 = (bf16[14,16,128]{2,1,0:T(8,128)(2,1)S(1)}, bf16[14,16,128]{2,1,0:T(8,128)(2,1)S(1)}, u32[]{:S(2)}, u32[]{:S(2)}) collective-permute-start(bf16[14,16,128]{2,1,0:T(8,128)(2,1)S(1)} %pick.1), channel_id=1, source_target_pairs={{0,4},{2,6},{4,7},{6,5},{7,3},{5,1},{3,0},{1,2},{8,11},{10,9},{12,... | collective-permute-start | bytes 172040 | tf_op jit(solution)/shard_map/ppermute | solution.py:277
  24.4 5.8 %copy-start.3 = (bf16[128,128]{1,0:T(8,128)(2,1)S(1)}, bf16[128,128]{1,0:T(8,128)(2,1)}, u32[]{:S(2)}) copy-start(bf16[128,128]{1,0:T(8,128)(2,1)} %out_gate.1) | copy-start | bytes 98308
  24.4 5.8 %copy-start.4 = (bf16[128,128]{1,0:T(8,128)(2,1)S(1)}, bf16[128,128]{1,0:T(8,128)(2,1)}, u32[]{:S(2)}) copy-start(bf16[128,128]{1,0:T(8,128)(2,1)} %last_weight.1) | copy-start | bytes 98308
  24.4 6.9 %collective-permute-start.6 = (bf16[14,56,128]{2,1,0:T(8,128)(2,1)S(1)}, bf16[14,56,128]{2,1,0:T(8,128)(2,1)S(1)}, u32[]{:S(2)}, u32[]{:S(2)}) collective-permute-start(bf16[14,56,128]{2,1,0:T(8,128)(2,1)S(1)} %collective-permute-done.4.own), channel_id=1, source_target_pairs={{0,2},{2,4},{4,6},{6,7},{7,5},{5,3},{3,1},{1,0},{8,9},{10,8},{12,1... | collective-permute-start | bytes 602120 | tf_op jit(solution)/shard_map/ppermute | solution.py:277
  30.2 0.7 %copy-start.5 = (f32[128]{0:T(128)S(1)}, f32[128]{0:T(128)}, u32[]{:S(2)}) copy-start(f32[128]{0:T(128)} %param.18) | copy-start | bytes 1540
  30.2 1.5 %collective-permute-start.9 = (bf16[14,56,128]{2,1,0:T(8,128)(2,1)S(1)}, bf16[14,56,128]{2,1,0:T(8,128)(2,1)S(1)}, u32[]{:S(2)}, u32[]{:S(2)}) collective-permute-start(bf16[14,56,128]{2,1,0:T(8,128)(2,1)S(1)} %get-tuple-element.51), channel_id=1, source_target_pairs={{0,8},{8,0},{1,9},{9,1},{2,10},{10,2},{3,11},{11,3},{4,12},{12,4},... | collective-permute-start | bytes 602120 | tf_op jit(solution)/shard_map/ppermute | solution.py:280

commit v14 on v13

--- a/solution.py
+++ b/solution.py
@@ -52,8 +52,8 @@
     return jnp.dot(left, right, preferred_element_type=F32)
 
 
-def gate(s, pair, shared, out_gate, last_gain, last_weight, gating, kept_gain, kept_weight):
-    gain = Shared(s, shared).gain
+def gate(s, length, shared, pair, out_gate, last_gain, last_weight, gating, kept_gain, kept_weight):
+    gain = Shared(s, length, shared).gain
     kept_gain[...] = last_gain[...]
     kept_weight[...] = last_weight[...]
     for start in range(0, s.width, s.half):
@@ -118,20 +118,19 @@
 
 
 class Shared:
-    def __init__(self, s, ref):
+    def __init__(self, s, length, ref):
         h = s.hidden
         self.left = ref[: s.channels, : 2 * h].astype(BF16)
         self.right = ref[: s.channels, 2 * h :].astype(BF16)
         self.gain = ref[s.channels : s.channels + 1, : s.channels]
-        self.limit = ref[s.channels + 1 : s.channels + 2, :1].astype(jnp.int32)
-
-
-def join(s, length, gain, left_gate, left_value, right_gate, right_value, shared):
+        self.limit = length[0]
+
+
+def join(s, gain, left_gate, left_value, right_gate, right_value, shared):
     h = s.hidden
     for at, part in enumerate((left_gate, left_value, right_gate, right_value)):
         shared[: s.channels, at * h : (at + 1) * h] = part[...].astype(F32)
     shared[s.channels : s.channels + 1, : s.channels] = gain[...]
-    shared[s.channels + 1 : s.channels + 2, :] = jnp.full((1, 4 * h), length[0]).astype(F32)
 
 
 def gated(s, rows, gain, weight, masks):
@@ -143,8 +142,8 @@
 
 
 def masks_of(tokens, first, count, limit):
-    below = (lax.broadcasted_iota(jnp.int32, (count, 1), 0) + first < limit).astype(F32)
-    return [below * (token < limit).astype(F32) for token in tokens]
+    below = lax.broadcasted_iota(jnp.int32, (count, 1), 0) + first < limit
+    return [(below & (token < limit)).astype(F32) for token in tokens]
 
 
 def project_right(s, rows_of, base, depth, token, shared, partner):
@@ -167,10 +166,10 @@
             left[step] = part
 
 
-def add_both(s, distance, narrow, shared, own, other, *refs):
+def add_both(s, distance, narrow, length, shared, own, other, *refs):
     before, (mine, theirs, left, right, picked, partner) = refs[:-6], refs[-6:]
     row, col = lax.axis_index("row"), lax.axis_index("col")
-    shared = Shared(s, shared)
+    shared = Shared(s, length, shared)
     depth = left.shape[0]
     base = row * s.half if distance == 0 else 0
     token = column_from(s, distance) * s.width + base
@@ -198,10 +197,10 @@
         rows[step] = picked[step, pl.ds(offset_in(s, col), s.slots), :].astype(BF16)
 
 
-def finish(s, shared, own, rows, mine, given, gating, last_gain, last_weight, *refs):
+def finish(s, length, shared, own, rows, mine, given, gating, last_gain, last_weight, *refs):
     update, left, partner, total = refs
     token = column_from(s, s.cols // 2) * s.width
-    shared = Shared(s, shared)
+    shared = Shared(s, length, shared)
     project_right(s, lambda at: rows[at].astype(F32), 0, s.width, token, shared, partner)
     project_left(s, own, lax.axis_index("row"), 0, s.width, token, shared, left)
     accumulate(s, left, partner, mine, total)
@@ -257,7 +256,6 @@
         shape((channels + 8, 4 * hidden), F32),
         [],
         0,
-        valid_length,
         gain,
         left_gate,
         left_value,
@@ -265,6 +263,7 @@
         right_value,
         grant=56,
     )
+    shared = (valid_length, shared)
     order = ring(s.cols)
 
     def shift(block, crossed=False, by=1):
@@ -294,7 +293,7 @@
             [sums, shape(sums.shape, BF16) if narrow else sums],
             [left, left, padded, right],
             2 * left.shape[0] * product,
-            shared,
+            *shared,
             own,
             other,
             *before,
@@ -330,8 +329,8 @@
         [sums, shape((1, hidden), F32), shape(out_weight.shape, BF16)],
         [],
         2 * height * width * channels * channels,
+        *shared,
         pair,
-        shared,
         out_gate,
         output_gain.reshape(1, hidden),
         out_weight,
@@ -345,7 +344,7 @@
         shape((width, height, channels), BF16),
         [tokens, partner, pltpu.VMEM(sums.shape, F32)],
         width * product,
-        shared,
+        *shared,
         last,
         rows,
         mine,

time: 34.7 us -> 30.8 us (0.89)
  Pallas kernels: 16.9 us -> 10.6 us
  waiting for transfers between devices: 0.45 us -> 2.27 us
  starting transfers between devices: 14.9 us -> 15.5 us
    pallas_call x8, Pallas kernels: 16.9 us -> 10.6 us  [call(): pl.pallas_call(body, out_shape=out_shape, in_specs=[space(o) for o in ope...]
    ppermute x8, waiting for transfers between devices: 0.08 us -> 2.27 us  [shift(): return lax.ppermute(block, ('row', 'col'), pairs)]
    ppermute x8, starting transfers between devices: 14.4 us -> 14.9 us  [shift(): return lax.ppermute(block, ('row', 'col'), pairs)]
    ppermute x2, waiting for transfers between devices: 0.37 us -> 0.01 us  [swap(): lax.ppermute(block, 'row', [(at, (at + 1) % s.rows) for at in range(s.row...]
  transfers between devices with their start and end apart: 10 -> 10, of which waited for: 2 -> 3; matrix products, arithmetic and copies ran while one was open for 0% -> 0% of each run, Pallas kernels for 41% -> 27%
where the time goes in v14:
time: 30.8 us; the launch traced here: 30.7 us
  starting transfers between devices  15.5 us (50%)
  Pallas kernels  10.6 us (34%)
  waiting for transfers between devices  2.27 us (7%)
  local copies, waits for them, and re-layouts  1.53 us (5%)
  between operations  0.79 us (3%)
    ppermute x8, starting transfers between devices, shift(): return lax.ppermute(block, ('row', 'col'), pairs)  14.9 us
    pallas_call x8, Pallas kernels, call(): pl.pallas_call(body, out_shape=out_shape, in_specs=[space(o) for o in ope...  10.6 us
    ppermute x8, waiting for transfers between devices, shift(): return lax.ppermute(block, ('row', 'col'), pairs)  2.27 us
    unnamed x12, local copies, waits for them, and re-layouts  1.53 us
  transfers between devices with their start and end apart: 10, of which 3 were waited for; matrix products, arithmetic and copies ran while one was open for 0% of the time, Pallas kernels for 27%

profile of v14, /device:TPU:0, one launch (start us, length us, event | category | flops | bytes accessed | tf_op | source)
XLA Modules:
  0.0 30.7 jit_solution(644539592998390875)
XLA Ops:
  0.0 0.5 %collective-permute-start.1 = (bf16[14,56,128]{2,1,0:T(8,128)(2,1)}, bf16[14,56,128]{2,1,0:T(8,128)(2,1)S(1)}, u32[]{:S(2)}, u32[]{:S(2)}) collective-permute-start(bf16[14,56,128]{2,1,0:T(8,128)(2,1)} %bitcast.4), channel_id=1, source_target_pairs={{0,8},{8,0},{1,9},{9,1},{2,10},{10,2},{3,11},{11,3},{4,12},{12,4},... | collective-permute-start | bytes 602120 | tf_op jit(solution)/shard_map/ppermute | solution.py:279
  0.5 2.6 %collective-permute-start = (bf16[14,56,128]{2,1,0:T(8,128)(2,1)}, bf16[14,56,128]{2,1,0:T(8,128)(2,1)S(1)}, u32[]{:S(2)}, u32[]{:S(2)}) collective-permute-start(bf16[14,56,128]{2,1,0:T(8,128)(2,1)} %bitcast.5), channel_id=1, source_target_pairs={{0,2},{2,4},{4,6},{6,7},{7,5},{5,3},{3,1},{1,0},{8,9},{10,8},{12,1... | collective-permute-start | bytes 602120 | tf_op jit(solution)/shard_map/ppermute | solution.py:276
  3.0 1.4 %collective-permute-start.3 = (bf16[14,56,128]{2,1,0:T(8,128)(2,1)}, bf16[14,56,128]{2,1,0:T(8,128)(2,1)S(1)}, u32[]{:S(2)}, u32[]{:S(2)}) collective-permute-start(bf16[14,56,128]{2,1,0:T(8,128)(2,1)} %bitcast.6), channel_id=1, source_target_pairs={{0,9},{2,8},{4,10},{6,12},{7,14},{5,15},{3,13},{1,11},{8,2},{10,4}... | collective-permute-start | bytes 602120 | tf_op jit(solution)/shard_map/ppermute | solution.py:276
  5.0 1.6 %join.1.shared = f32[136,512]{1,0:T(8,128)} custom-call(f32[1,128]{1,0:T(1,128)} %bitcast.10, bf16[128,128]{1,0:T(8,128)(2,1)} %left_gate.1, bf16[128,128]{1,0:T(8,128)(2,1)} %left_value.1, bf16[128,128]{1,0:T(8,128)(2,1)} %right_gate.1, bf16[128,128]{1,0:T(8,128)(2,1)} %right_value.1), custom_call_target="tpu_custom_call" | custom-call | bytes 131584 | tf_op jit(solution)/shard_map/join/pallas_call | solution.py:223
  6.6 0.0 collective-permute-done.1.other
  6.6 1.0 %copy-done = f32[136,512]{1,0:T(8,128)S(1)} copy-done((f32[136,512]{1,0:T(8,128)S(1)}, f32[136,512]{1,0:T(8,128)}, u32[]{:S(2)}) %copy-start) | copy-done | bytes 278552
  7.6 1.0 %add_both.4 = (f32[14,56,128]{2,1,0:T(8,128)S(1)}, f32[14,56,128]{2,1,0:T(8,128)S(1)}) custom-call(s32[1]{0:T(128)S(6)} %copy.11.length, f32[136,512]{1,0:T(8,128)S(1)} %copy-done, bf16[14,56,128]{2,1,0:T(8,128)(2,1)S(1)} %bitcast.7, bf16[14,56,128]{2,1,0:T(8,128)(2,1)S(1)} %collective-permute-done.1.other), custom_call_target="tpu_custom_call" | custom-call | flops 22478848 | bytes 679940 | tf_op jit(solution)/shard_map/add_both/pallas_call | solution.py:223
  8.6 0.0 collective-permute-done.own
  8.6 1.5 %collective-permute-start.2 = (bf16[14,56,128]{2,1,0:T(8,128)(2,1)S(1)}, bf16[14,56,128]{2,1,0:T(8,128)(2,1)S(1)}, u32[]{:S(2)}, u32[]{:S(2)}) collective-permute-start(bf16[14,56,128]{2,1,0:T(8,128)(2,1)S(1)} %collective-permute-done.own), channel_id=1, source_target_pairs={{0,2},{2,4},{4,6},{6,7},{7,5},{5,3},{3,1},{1,0},{8,9},{10,8},{12,1... | collective-permute-start | bytes 602120 | tf_op jit(solution)/shard_map/ppermute | solution.py:276
  10.1 0.0 collective-permute-done.3.other
  10.1 1.6 %collective-permute-start.5 = (bf16[14,56,128]{2,1,0:T(8,128)(2,1)S(1)}, bf16[14,56,128]{2,1,0:T(8,128)(2,1)S(1)}, u32[]{:S(2)}, u32[]{:S(2)}) collective-permute-start(bf16[14,56,128]{2,1,0:T(8,128)(2,1)S(1)} %collective-permute-done.3.other), channel_id=1, source_target_pairs={{0,2},{2,4},{4,6},{6,7},{7,5},{5,3},{3,1},{1,0},{8,9},{10,8},{12,1... | collective-permute-start | bytes 602120 | tf_op jit(solution)/shard_map/ppermute | solution.py:276
  11.7 1.8 %add_both.5 = (f32[14,56,128]{2,1,0:T(8,128)S(1)}, f32[14,56,128]{2,1,0:T(8,128)S(1)}) custom-call(s32[1]{0:T(128)S(6)} %copy.11.length, f32[136,512]{1,0:T(8,128)S(1)} %copy-done, bf16[14,56,128]{2,1,0:T(8,128)(2,1)S(1)} %collective-permute-done.own, bf16[14,56,128]{2,1,0:T(8,128)(2,1)S(1)} %collective-permute-done.3.other, ...), custom_call_target="tpu_custom_call" | custom-call | flops 44957696 | bytes 1482756 | tf_op jit(solution)/shard_map/add_both/pallas_call | solution.py:223
  13.5 0.9 %collective-permute-done.2.own = bf16[14,56,128]{2,1,0:T(8,128)(2,1)S(1)} collective-permute-done((bf16[14,56,128]{2,1,0:T(8,128)(2,1)S(1)}, bf16[14,56,128]{2,1,0:T(8,128)(2,1)S(1)}, u32[]{:S(2)}, u32[]{:S(2)}) %collective-permute-start.2) | collective-permute-done | bytes 200736 | tf_op jit(solution)/shard_map/ppermute | solution.py:276
  14.4 1.4 %collective-permute-start.4 = (bf16[14,56,128]{2,1,0:T(8,128)(2,1)S(1)}, bf16[14,56,128]{2,1,0:T(8,128)(2,1)S(1)}, u32[]{:S(2)}, u32[]{:S(2)}) collective-permute-start(bf16[14,56,128]{2,1,0:T(8,128)(2,1)S(1)} %collective-permute-done.2.own), channel_id=1, source_target_pairs={{0,2},{2,4},{4,6},{6,7},{7,5},{5,3},{3,1},{1,0},{8,9},{10,8},{12,1... | collective-permute-start | bytes 602120 | tf_op jit(solution)/shard_map/ppermute | solution.py:276
  15.8 0.7 %collective-permute-done.5.other = bf16[14,56,128]{2,1,0:T(8,128)(2,1)S(1)} collective-permute-done((bf16[14,56,128]{2,1,0:T(8,128)(2,1)S(1)}, bf16[14,56,128]{2,1,0:T(8,128)(2,1)S(1)}, u32[]{:S(2)}, u32[]{:S(2)}) %collective-permute-start.5) | collective-permute-done | bytes 200736 | tf_op jit(solution)/shard_map/ppermute | solution.py:276
  16.5 1.4 %collective-permute-start.7 = (bf16[14,56,128]{2,1,0:T(8,128)(2,1)S(1)}, bf16[14,56,128]{2,1,0:T(8,128)(2,1)S(1)}, u32[]{:S(2)}, u32[]{:S(2)}) collective-permute-start(bf16[14,56,128]{2,1,0:T(8,128)(2,1)S(1)} %collective-permute-done.5.other), channel_id=1, source_target_pairs={{0,2},{2,4},{4,6},{6,7},{7,5},{5,3},{3,1},{1,0},{8,9},{10,8},{12,1... | collective-permute-start | bytes 602120 | tf_op jit(solution)/shard_map/ppermute | solution.py:276
  18.0 2.9 %collective-permute-start.8 = (bf16[14,16,128]{2,1,0:T(8,128)(2,1)S(1)}, bf16[14,16,128]{2,1,0:T(8,128)(2,1)S(1)}, u32[]{:S(2)}, u32[]{:S(2)}) collective-permute-start(bf16[14,16,128]{2,1,0:T(8,128)(2,1)S(1)} %pick.1), channel_id=1, source_target_pairs={{0,4},{2,6},{4,7},{6,5},{7,3},{5,1},{3,0},{1,2},{8,11},{10,9},{12,... | collective-permute-start | bytes 172040 | tf_op jit(solution)/shard_map/ppermute | solution.py:276
  20.9 1.8 %add_both.6 = (f32[14,56,128]{2,1,0:T(8,128)S(1)}, f32[14,56,128]{2,1,0:T(8,128)S(1)}) custom-call(s32[1]{0:T(128)S(6)} %copy.11.length, f32[136,512]{1,0:T(8,128)S(1)} %copy-done.1, bf16[14,56,128]{2,1,0:T(8,128)(2,1)S(1)} %collective-permute-done.2.own, bf16[14,56,128]{2,1,0:T(8,128)(2,1)S(1)} %collective-permute-done.5.other, ...), custom_call_target="tpu_custom_call" | custom-call | flops 44957696 | bytes 1482756 | tf_op jit(solution)/shard_map/add_both/pallas_call | solution.py:223
  22.7 0.0 collective-permute-done.4.own
  22.7 0.0 copy-start.3
  22.7 0.0 copy-start.4
  22.7 2.2 %collective-permute-start.6 = (bf16[14,56,128]{2,1,0:T(8,128)(2,1)S(1)}, bf16[14,56,128]{2,1,0:T(8,128)(2,1)S(1)}, u32[]{:S(2)}, u32[]{:S(2)}) collective-permute-start(bf16[14,56,128]{2,1,0:T(8,128)(2,1)S(1)} %collective-permute-done.4.own), channel_id=1, source_target_pairs={{0,2},{2,4},{4,6},{6,7},{7,5},{5,3},{3,1},{1,0},{8,9},{10,8},{12,1... | collective-permute-start | bytes 602120 | tf_op jit(solution)/shard_map/ppermute | solution.py:276
  24.9 0.0 collective-permute-done.7.other
  24.9 0.0 collective-permute-done.8.rows
  24.9 1.8 %add_both.7 = (f32[14,56,128]{2,1,0:T(8,128)S(1)}, bf16[14,56,128]{2,1,0:T(8,128)(2,1)S(1)}) custom-call(s32[1]{0:T(128)S(6)} %copy.11.length, f32[136,512]{1,0:T(8,128)S(1)} %copy-done.1, bf16[14,56,128]{2,1,0:T(8,128)(2,1)S(1)} %collective-permute-done.4.own, bf16[14,56,128]{2,1,0:T(8,128)(2,1)S(1)} %collective-permute-done.7.other, ...), custom_call_target="tpu_custom_call" | custom-call | flops 44957696 | bytes 1482756 | tf_op jit(solution)/shard_map/add_both/pallas_call | solution.py:223
  26.7 0.0 copy-start.5
  26.7 0.1 collective-permute-start.9
  26.8 0.5 %copy-done.5 = f32[128]{0:T(128)S(1)} copy-done((f32[128]{0:T(128)S(1)}, f32[128]{0:T(128)}, u32[]{:S(2)}) %copy-start.5) | copy-done | bytes 536
  27.4 0.5 %gate.1 = (f32[14,56,128]{2,1,0:T(8,128)S(1)}, f32[1,128]{1,0:T(1,128)S(1)}, bf16[128,128]{1,0:T(8,128)(2,1)S(1)}) custom-call(s32[1]{0:T(128)S(6)} %copy.11.length, f32[136,512]{1,0:T(8,128)S(1)} %copy-done.1, bf16[14,56,128]{2,1,0:T(8,128)(2,1)S(1)} %bitcast.8, bf16[128,128]{1,0:T(8,128)(2,1)S(1)} %copy-done.3, f32[1,128]{1,0:T(1,128)S(1)} %bitcast.9, ...), custom_call_target="tpu_custom_call" | custom-call | flops 25690112 | bytes 545284 | tf_op jit(solution)/shard_map/gate/pallas_call | solution.py:223
  27.9 0.6 %collective-permute-done.6.own = bf16[14,56,128]{2,1,0:T(8,128)(2,1)S(1)} collective-permute-done((bf16[14,56,128]{2,1,0:T(8,128)(2,1)S(1)}, bf16[14,56,128]{2,1,0:T(8,128)(2,1)S(1)}, u32[]{:S(2)}, u32[]{:S(2)}) %collective-permute-start.6) | collective-permute-done | bytes 200736 | tf_op jit(solution)/shard_map/ppermute | solution.py:276
  28.5 0.0 collective-permute-done.9.given
  28.5 2.2 %finish.1 = bf16[14,56,128]{2,1,0:T(8,128)(2,1)} custom-call(s32[1]{0:T(128)S(6)} %copy.11.length, f32[136,512]{1,0:T(8,128)S(1)} %copy-done.1, bf16[14,56,128]{2,1,0:T(8,128)(2,1)S(1)} %collective-permute-done.6.own, bf16[14,16,128]{2,1,0:T(8,128)(2,1)S(1)} %collective-permute-done.8.rows, f32[14,56,128]{2,1,0:T(8,128)S(1)} %get-tuple-element.50.mine, ...), custom_call_target="tpu_custom_call" | custom-call | flops 22478848 | bytes 1573380 | tf_op jit(solution)/shard_map/finish/pallas_call | solution.py:223
  (8 shorter events, 0.0 us)
Async XLA Ops:
  0.0 6.6 %collective-permute-start.1 = (bf16[14,56,128]{2,1,0:T(8,128)(2,1)}, bf16[14,56,128]{2,1,0:T(8,128)(2,1)S(1)}, u32[]{:S(2)}, u32[]{:S(2)}) collective-permute-start(bf16[14,56,128]{2,1,0:T(8,128)(2,1)} %bitcast.4), channel_id=1, source_target_pairs={{0,8},{8,0},{1,9},{9,1},{2,10},{10,2},{3,11},{11,3},{4,12},{12,4},... | collective-permute-start | bytes 602120 | tf_op jit(solution)/shard_map/ppermute | solution.py:279
  0.5 8.2 %collective-permute-start = (bf16[14,56,128]{2,1,0:T(8,128)(2,1)}, bf16[14,56,128]{2,1,0:T(8,128)(2,1)S(1)}, u32[]{:S(2)}, u32[]{:S(2)}) collective-permute-start(bf16[14,56,128]{2,1,0:T(8,128)(2,1)} %bitcast.5), channel_id=1, source_target_pairs={{0,2},{2,4},{4,6},{6,7},{7,5},{5,3},{3,1},{1,0},{8,9},{10,8},{12,1... | collective-permute-start | bytes 602120 | tf_op jit(solution)/shard_map/ppermute | solution.py:276
  3.0 7.1 %collective-permute-start.3 = (bf16[14,56,128]{2,1,0:T(8,128)(2,1)}, bf16[14,56,128]{2,1,0:T(8,128)(2,1)S(1)}, u32[]{:S(2)}, u32[]{:S(2)}) collective-permute-start(bf16[14,56,128]{2,1,0:T(8,128)(2,1)} %bitcast.6), channel_id=1, source_target_pairs={{0,9},{2,8},{4,10},{6,12},{7,14},{5,15},{3,13},{1,11},{8,2},{10,4}... | collective-permute-start | bytes 602120 | tf_op jit(solution)/shard_map/ppermute | solution.py:276
  5.0 1.6 %copy-start.2 = (bf16[56,14,128]{2,0,1:T(8,128)(2,1)S(1)}, bf16[56,14,128]{2,0,1:T(8,128)(2,1)}, u32[]{:S(2)}) copy-start(bf16[56,14,128]{2,0,1:T(8,128)(2,1)} %param.10) | copy-start | bytes 602116
  6.6 1.0 %copy-start = (f32[136,512]{1,0:T(8,128)S(1)}, f32[136,512]{1,0:T(8,128)}, u32[]{:S(2)}) copy-start(f32[136,512]{1,0:T(8,128)} %join.1.shared) | copy-start | bytes 835588
  8.6 5.8 %collective-permute-start.2 = (bf16[14,56,128]{2,1,0:T(8,128)(2,1)S(1)}, bf16[14,56,128]{2,1,0:T(8,128)(2,1)S(1)}, u32[]{:S(2)}, u32[]{:S(2)}) collective-permute-start(bf16[14,56,128]{2,1,0:T(8,128)(2,1)S(1)} %collective-permute-done.own), channel_id=1, source_target_pairs={{0,2},{2,4},{4,6},{6,7},{7,5},{5,3},{3,1},{1,0},{8,9},{10,8},{12,1... | collective-permute-start | bytes 602120 | tf_op jit(solution)/shard_map/ppermute | solution.py:276
  10.1 6.4 %collective-permute-start.5 = (bf16[14,56,128]{2,1,0:T(8,128)(2,1)S(1)}, bf16[14,56,128]{2,1,0:T(8,128)(2,1)S(1)}, u32[]{:S(2)}, u32[]{:S(2)}) collective-permute-start(bf16[14,56,128]{2,1,0:T(8,128)(2,1)S(1)} %collective-permute-done.3.other), channel_id=1, source_target_pairs={{0,2},{2,4},{4,6},{6,7},{7,5},{5,3},{3,1},{1,0},{8,9},{10,8},{12,1... | collective-permute-start | bytes 602120 | tf_op jit(solution)/shard_map/ppermute | solution.py:276
  13.5 7.4 %copy-start.1 = (f32[136,512]{1,0:T(8,128)S(1)}, f32[136,512]{1,0:T(8,128)}, u32[]{:S(2)}) copy-start(f32[136,512]{1,0:T(8,128)} %join.1.shared) | copy-start | bytes 835588
  14.4 8.3 %collective-permute-start.4 = (bf16[14,56,128]{2,1,0:T(8,128)(2,1)S(1)}, bf16[14,56,128]{2,1,0:T(8,128)(2,1)S(1)}, u32[]{:S(2)}, u32[]{:S(2)}) collective-permute-start(bf16[14,56,128]{2,1,0:T(8,128)(2,1)S(1)} %collective-permute-done.2.own), channel_id=1, source_target_pairs={{0,2},{2,4},{4,6},{6,7},{7,5},{5,3},{3,1},{1,0},{8,9},{10,8},{12,1... | collective-permute-start | bytes 602120 | tf_op jit(solution)/shard_map/ppermute | solution.py:276
  16.5 8.4 %collective-permute-start.7 = (bf16[14,56,128]{2,1,0:T(8,128)(2,1)S(1)}, bf16[14,56,128]{2,1,0:T(8,128)(2,1)S(1)}, u32[]{:S(2)}, u32[]{:S(2)}) collective-permute-start(bf16[14,56,128]{2,1,0:T(8,128)(2,1)S(1)} %collective-permute-done.5.other), channel_id=1, source_target_pairs={{0,2},{2,4},{4,6},{6,7},{7,5},{5,3},{3,1},{1,0},{8,9},{10,8},{12,1... | collective-permute-start | bytes 602120 | tf_op jit(solution)/shard_map/ppermute | solution.py:276
  18.0 6.9 %collective-permute-start.8 = (bf16[14,16,128]{2,1,0:T(8,128)(2,1)S(1)}, bf16[14,16,128]{2,1,0:T(8,128)(2,1)S(1)}, u32[]{:S(2)}, u32[]{:S(2)}) collective-permute-start(bf16[14,16,128]{2,1,0:T(8,128)(2,1)S(1)} %pick.1), channel_id=1, source_target_pairs={{0,4},{2,6},{4,7},{6,5},{7,3},{5,1},{3,0},{1,2},{8,11},{10,9},{12,... | collective-permute-start | bytes 172040 | tf_op jit(solution)/shard_map/ppermute | solution.py:276
  22.7 4.1 %copy-start.3 = (bf16[128,128]{1,0:T(8,128)(2,1)S(1)}, bf16[128,128]{1,0:T(8,128)(2,1)}, u32[]{:S(2)}) copy-start(bf16[128,128]{1,0:T(8,128)(2,1)} %out_gate.1) | copy-start | bytes 98308
  22.7 4.1 %copy-start.4 = (bf16[128,128]{1,0:T(8,128)(2,1)S(1)}, bf16[128,128]{1,0:T(8,128)(2,1)}, u32[]{:S(2)}) copy-start(bf16[128,128]{1,0:T(8,128)(2,1)} %last_weight.1) | copy-start | bytes 98308
  22.7 5.8 %collective-permute-start.6 = (bf16[14,56,128]{2,1,0:T(8,128)(2,1)S(1)}, bf16[14,56,128]{2,1,0:T(8,128)(2,1)S(1)}, u32[]{:S(2)}, u32[]{:S(2)}) collective-permute-start(bf16[14,56,128]{2,1,0:T(8,128)(2,1)S(1)} %collective-permute-done.4.own), channel_id=1, source_target_pairs={{0,2},{2,4},{4,6},{6,7},{7,5},{5,3},{3,1},{1,0},{8,9},{10,8},{12,1... | collective-permute-start | bytes 602120 | tf_op jit(solution)/shard_map/ppermute | solution.py:276
  26.7 0.7 %copy-start.5 = (f32[128]{0:T(128)S(1)}, f32[128]{0:T(128)}, u32[]{:S(2)}) copy-start(f32[128]{0:T(128)} %param.18) | copy-start | bytes 1540
  26.7 1.8 %collective-permute-start.9 = (bf16[14,56,128]{2,1,0:T(8,128)(2,1)S(1)}, bf16[14,56,128]{2,1,0:T(8,128)(2,1)S(1)}, u32[]{:S(2)}, u32[]{:S(2)}) collective-permute-start(bf16[14,56,128]{2,1,0:T(8,128)(2,1)S(1)} %get-tuple-element.51), channel_id=1, source_target_pairs={{0,8},{8,0},{1,9},{9,1},{2,10},{10,2},{3,11},{11,3},{4,12},{12,4},... | collective-permute-start | bytes 602120 | tf_op jit(solution)/shard_map/ppermute | solution.py:279

commit v15 on v14

--- a/solution.py
+++ b/solution.py
@@ -190,8 +190,8 @@
         theirs[...] = picked[:, : s.height].astype(BF16)
 
 
-def pick(s, own, other, rows, picked):
-    col = column_from(s, -2)
+def pick(s, ahead, own, other, rows, picked):
+    col = column_from(s, -ahead)
     choose(lax.axis_index("row") == owner_of(s, col), own, other, picked.at[:, : s.height])
     for step in range(s.width):
         rows[step] = picked[step, pl.ds(offset_in(s, col), s.slots), :].astype(BF16)
@@ -308,34 +308,36 @@
     own = shift(pair)
     total = add(0, pair, swap(pair), ())
     other, own = in_turn(other, own, total)
-    rows = ()
+    early = min(3, far - 1)
     for distance in range(1, far - 1):
         ahead = [shift(other), shift(own)]
-        if distance == far - 2:
+        if distance == far - early:
             rows = call(
-                functools.partial(pick, s),
+                functools.partial(pick, s, early),
                 shape((width, s.slots, channels), BF16),
                 [padded],
                 0,
                 own,
                 other,
             )
-            rows = shift(rows, by=2)
+            rows = shift(rows, by=early)
         total = add(distance, own, other, total)
         other, own = in_turn(*ahead, total)
+        if distance == far - early:
+            later = lax.optimization_barrier((pair, own))[0]
+            gating = call(
+                functools.partial(gate, s),
+                [sums, shape((1, hidden), F32), shape(out_weight.shape, BF16)],
+                [],
+                2 * height * width * channels * channels,
+                *shared,
+                later,
+                out_gate,
+                output_gain.reshape(1, hidden),
+                out_weight,
+            )
+            other, rows, gating = lax.optimization_barrier((other, rows, gating))
     last = shift(own)
-    gating = call(
-        functools.partial(gate, s),
-        [sums, shape((1, hidden), F32), shape(out_weight.shape, BF16)],
-        [],
-        2 * height * width * channels * channels,
-        *shared,
-        pair,
-        out_gate,
-        output_gain.reshape(1, hidden),
-        out_weight,
-    )
-    own, other, rows = lax.optimization_barrier((own, other, rows))
     mine, theirs = add(far - 1, own, other, total, narrow=True)
     given = swap(theirs)
     last, mine, gating = lax.optimization_barrier((last, mine, gating))

time: 30.8 us -> 31.4 us (1.019)
  waiting for transfers between devices: 2.27 us -> 5.84 us
  starting transfers between devices: 15.5 us -> 12.5 us
    ppermute x8, starting transfers between devices: 14.9 us -> 11.9 us  [shift(): return lax.ppermute(block, ('row', 'col'), pairs)]
    ppermute x8, waiting for transfers between devices: 2.27 us -> 5.18 us  [shift(): return lax.ppermute(block, ('row', 'col'), pairs)]
    ppermute x2, waiting for transfers between devices: 0.01 us -> 0.66 us  [swap(): lax.ppermute(block, 'row', [(at, (at + 1) % s.rows) for at in range(s.row...]
  transfers between devices with their start and end apart: 10 -> 10, of which waited for: 3 -> 5; matrix products, arithmetic and copies ran while one was open for 0% -> 0% of each run, Pallas kernels for 27% -> 27%
where the time goes in v15:
time: 31.4 us; the launch traced here: 31.2 us
  starting transfers between devices  12.5 us (40%)
  Pallas kernels  10.6 us (34%)
  waiting for transfers between devices  5.84 us (19%)
  local copies, waits for them, and re-layouts  1.53 us (5%)
  between operations  0.78 us (2%)
    ppermute x8, starting transfers between devices, shift(): return lax.ppermute(block, ('row', 'col'), pairs)  11.9 us
    pallas_call x8, Pallas kernels, call(): pl.pallas_call(body, out_shape=out_shape, in_specs=[space(o) for o in ope...  10.6 us
    ppermute x8, waiting for transfers between devices, shift(): return lax.ppermute(block, ('row', 'col'), pairs)  5.18 us
    unnamed x12, local copies, waits for them, and re-layouts  1.53 us
    ppermute x2, waiting for transfers between devices, swap(): lax.ppermute(block, 'row', [(at, (at + 1) % s.rows) for at in range(s.row...  0.66 us
  transfers between devices with their start and end apart: 10, of which 5 were waited for; matrix products, arithmetic and copies ran while one was open for 0% of the time, Pallas kernels for 27%

profile of v15, /device:TPU:0, one launch (start us, length us, event | category | flops | bytes accessed | tf_op | source)
XLA Modules:
  0.0 31.2 jit_solution(12471918382840934589)
XLA Ops:
  0.0 0.5 %collective-permute-start.1 = (bf16[14,56,128]{2,1,0:T(8,128)(2,1)}, bf16[14,56,128]{2,1,0:T(8,128)(2,1)S(1)}, u32[]{:S(2)}, u32[]{:S(2)}) collective-permute-start(bf16[14,56,128]{2,1,0:T(8,128)(2,1)} %bitcast.4), channel_id=1, source_target_pairs={{0,8},{8,0},{1,9},{9,1},{2,10},{10,2},{3,11},{11,3},{4,12},{12,4},... | collective-permute-start | bytes 602120 | tf_op jit(solution)/shard_map/ppermute | solution.py:279
  0.5 2.6 %collective-permute-start = (bf16[14,56,128]{2,1,0:T(8,128)(2,1)}, bf16[14,56,128]{2,1,0:T(8,128)(2,1)S(1)}, u32[]{:S(2)}, u32[]{:S(2)}) collective-permute-start(bf16[14,56,128]{2,1,0:T(8,128)(2,1)} %bitcast.5), channel_id=1, source_target_pairs={{0,2},{2,4},{4,6},{6,7},{7,5},{5,3},{3,1},{1,0},{8,9},{10,8},{12,1... | collective-permute-start | bytes 602120 | tf_op jit(solution)/shard_map/ppermute | solution.py:276
  3.0 1.4 %collective-permute-start.3 = (bf16[14,56,128]{2,1,0:T(8,128)(2,1)}, bf16[14,56,128]{2,1,0:T(8,128)(2,1)S(1)}, u32[]{:S(2)}, u32[]{:S(2)}) collective-permute-start(bf16[14,56,128]{2,1,0:T(8,128)(2,1)} %bitcast.6), channel_id=1, source_target_pairs={{0,9},{2,8},{4,10},{6,12},{7,14},{5,15},{3,13},{1,11},{8,2},{10,4}... | collective-permute-start | bytes 602120 | tf_op jit(solution)/shard_map/ppermute | solution.py:276
  5.0 1.6 %join.1.shared = f32[136,512]{1,0:T(8,128)} custom-call(f32[1,128]{1,0:T(1,128)} %bitcast.10, bf16[128,128]{1,0:T(8,128)(2,1)} %left_gate.1, bf16[128,128]{1,0:T(8,128)(2,1)} %left_value.1, bf16[128,128]{1,0:T(8,128)(2,1)} %right_gate.1, bf16[128,128]{1,0:T(8,128)(2,1)} %right_value.1), custom_call_target="tpu_custom_call" | custom-call | bytes 131584 | tf_op jit(solution)/shard_map/join/pallas_call | solution.py:223
  6.6 0.0 collective-permute-done.1.other
  6.6 1.0 %copy-done = f32[136,512]{1,0:T(8,128)S(1)} copy-done((f32[136,512]{1,0:T(8,128)S(1)}, f32[136,512]{1,0:T(8,128)}, u32[]{:S(2)}) %copy-start) | copy-done | bytes 278552
  7.6 1.0 %add_both.4 = (f32[14,56,128]{2,1,0:T(8,128)S(1)}, f32[14,56,128]{2,1,0:T(8,128)S(1)}) custom-call(s32[1]{0:T(128)S(6)} %copy.11.length, f32[136,512]{1,0:T(8,128)S(1)} %copy-done, bf16[14,56,128]{2,1,0:T(8,128)(2,1)S(1)} %bitcast.7, bf16[14,56,128]{2,1,0:T(8,128)(2,1)S(1)} %collective-permute-done.1.other), custom_call_target="tpu_custom_call" | custom-call | flops 22478848 | bytes 679940 | tf_op jit(solution)/shard_map/add_both/pallas_call | solution.py:223
  8.6 0.0 collective-permute-done.own
  8.6 1.5 %collective-permute-start.2 = (bf16[14,56,128]{2,1,0:T(8,128)(2,1)S(1)}, bf16[14,56,128]{2,1,0:T(8,128)(2,1)S(1)}, u32[]{:S(2)}, u32[]{:S(2)}) collective-permute-start(bf16[14,56,128]{2,1,0:T(8,128)(2,1)S(1)} %collective-permute-done.own), channel_id=1, source_target_pairs={{0,2},{2,4},{4,6},{6,7},{7,5},{5,3},{3,1},{1,0},{8,9},{10,8},{12,1... | collective-permute-start | bytes 602120 | tf_op jit(solution)/shard_map/ppermute | solution.py:276
  10.1 0.0 collective-permute-done.3.other
  10.1 1.6 %collective-permute-start.5 = (bf16[14,56,128]{2,1,0:T(8,128)(2,1)S(1)}, bf16[14,56,128]{2,1,0:T(8,128)(2,1)S(1)}, u32[]{:S(2)}, u32[]{:S(2)}) collective-permute-start(bf16[14,56,128]{2,1,0:T(8,128)(2,1)S(1)} %collective-permute-done.3.other), channel_id=1, source_target_pairs={{0,2},{2,4},{4,6},{6,7},{7,5},{5,3},{3,1},{1,0},{8,9},{10,8},{12,1... | collective-permute-start | bytes 602120 | tf_op jit(solution)/shard_map/ppermute | solution.py:276
  11.7 0.0 copy-start.3
  11.7 0.0 copy-start.4
  11.7 3.4 %collective-permute-start.6 = (bf16[14,16,128]{2,1,0:T(8,128)(2,1)S(1)}, bf16[14,16,128]{2,1,0:T(8,128)(2,1)S(1)}, u32[]{:S(2)}, u32[]{:S(2)}) collective-permute-start(bf16[14,16,128]{2,1,0:T(8,128)(2,1)S(1)} %pick.1), channel_id=1, source_target_pairs={{0,6},{2,7},{4,5},{6,3},{7,1},{5,0},{3,2},{1,4},{8,13},{10,11},{12... | collective-permute-start | bytes 172040 | tf_op jit(solution)/shard_map/ppermute | solution.py:276
  15.1 1.8 %add_both.5 = (f32[14,56,128]{2,1,0:T(8,128)S(1)}, f32[14,56,128]{2,1,0:T(8,128)S(1)}) custom-call(s32[1]{0:T(128)S(6)} %copy.11.length, f32[136,512]{1,0:T(8,128)S(1)} %copy-done.1, bf16[14,56,128]{2,1,0:T(8,128)(2,1)S(1)} %collective-permute-done.own, bf16[14,56,128]{2,1,0:T(8,128)(2,1)S(1)} %collective-permute-done.3.other, ...), custom_call_target="tpu_custom_call" | custom-call | flops 44957696 | bytes 1482756 | tf_op jit(solution)/shard_map/add_both/pallas_call | solution.py:223
  16.9 0.0 collective-permute-done.2.own
  16.9 0.0 copy-start.5
  16.9 0.1 collective-permute-start.4
  17.0 0.0 collective-permute-done.5.other
  17.0 0.6 %copy-done.5 = f32[128]{0:T(128)S(1)} copy-done((f32[128]{0:T(128)S(1)}, f32[128]{0:T(128)}, u32[]{:S(2)}) %copy-start.5) | copy-done | bytes 536
  17.5 0.5 %gate.1 = (f32[14,56,128]{2,1,0:T(8,128)S(1)}, f32[1,128]{1,0:T(1,128)S(1)}, bf16[128,128]{1,0:T(8,128)(2,1)S(1)}) custom-call(s32[1]{0:T(128)S(6)} %copy.11.length, f32[136,512]{1,0:T(8,128)S(1)} %copy-done.1, bf16[14,56,128]{2,1,0:T(8,128)(2,1)S(1)} %bitcast.8, bf16[128,128]{1,0:T(8,128)(2,1)S(1)} %copy-done.3, f32[1,128]{1,0:T(1,128)S(1)} %bitcast.9, ...), custom_call_target="tpu_custom_call" | custom-call | flops 25690112 | bytes 545284 | tf_op jit(solution)/shard_map/gate/pallas_call | solution.py:223
  18.0 2.0 %collective-permute-done.6.rows = bf16[14,16,128]{2,1,0:T(8,128)(2,1)S(1)} collective-permute-done((bf16[14,16,128]{2,1,0:T(8,128)(2,1)S(1)}, bf16[14,16,128]{2,1,0:T(8,128)(2,1)S(1)}, u32[]{:S(2)}, u32[]{:S(2)}) %collective-permute-start.6) | collective-permute-done | bytes 57376 | tf_op jit(solution)/shard_map/ppermute | solution.py:276
  20.0 0.0 collective-permute-start.8
  20.0 1.8 %add_both.6 = (f32[14,56,128]{2,1,0:T(8,128)S(1)}, f32[14,56,128]{2,1,0:T(8,128)S(1)}) custom-call(s32[1]{0:T(128)S(6)} %copy.11.length, f32[136,512]{1,0:T(8,128)S(1)} %copy-done.1, bf16[14,56,128]{2,1,0:T(8,128)(2,1)S(1)} %collective-permute-done.2.own, bf16[14,56,128]{2,1,0:T(8,128)(2,1)S(1)} %collective-permute-done.5.other, ...), custom_call_target="tpu_custom_call" | custom-call | flops 44957696 | bytes 1482756 | tf_op jit(solution)/shard_map/add_both/pallas_call | solution.py:223
  21.8 0.9 %collective-permute-done.4.own = bf16[14,56,128]{2,1,0:T(8,128)(2,1)S(1)} collective-permute-done((bf16[14,56,128]{2,1,0:T(8,128)(2,1)S(1)}, bf16[14,56,128]{2,1,0:T(8,128)(2,1)S(1)}, u32[]{:S(2)}, u32[]{:S(2)}) %collective-permute-start.4) | collective-permute-done | bytes 200736 | tf_op jit(solution)/shard_map/ppermute | solution.py:276
  22.7 1.5 %collective-permute-start.7 = (bf16[14,56,128]{2,1,0:T(8,128)(2,1)S(1)}, bf16[14,56,128]{2,1,0:T(8,128)(2,1)S(1)}, u32[]{:S(2)}, u32[]{:S(2)}) collective-permute-start(bf16[14,56,128]{2,1,0:T(8,128)(2,1)S(1)} %collective-permute-done.4.own), channel_id=1, source_target_pairs={{0,2},{2,4},{4,6},{6,7},{7,5},{5,3},{3,1},{1,0},{8,9},{10,8},{12,1... | collective-permute-start | bytes 602120 | tf_op jit(solution)/shard_map/ppermute | solution.py:276
  24.2 1.5 %collective-permute-done.8.other = bf16[14,56,128]{2,1,0:T(8,128)(2,1)S(1)} collective-permute-done((bf16[14,56,128]{2,1,0:T(8,128)(2,1)S(1)}, bf16[14,56,128]{2,1,0:T(8,128)(2,1)S(1)}, u32[]{:S(2)}, u32[]{:S(2)}) %collective-permute-start.8) | collective-permute-done | bytes 200736 | tf_op jit(solution)/shard_map/ppermute | solution.py:276
  25.7 1.8 %add_both.7 = (f32[14,56,128]{2,1,0:T(8,128)S(1)}, bf16[14,56,128]{2,1,0:T(8,128)(2,1)S(1)}) custom-call(s32[1]{0:T(128)S(6)} %copy.11.length, f32[136,512]{1,0:T(8,128)S(1)} %copy-done.1, bf16[14,56,128]{2,1,0:T(8,128)(2,1)S(1)} %collective-permute-done.4.own, bf16[14,56,128]{2,1,0:T(8,128)(2,1)S(1)} %collective-permute-done.8.other, ...), custom_call_target="tpu_custom_call" | custom-call | flops 44957696 | bytes 1482756 | tf_op jit(solution)/shard_map/add_both/pallas_call | solution.py:223
  27.5 0.1 collective-permute-start.9
  27.6 0.8 %collective-permute-done.7.own = bf16[14,56,128]{2,1,0:T(8,128)(2,1)S(1)} collective-permute-done((bf16[14,56,128]{2,1,0:T(8,128)(2,1)S(1)}, bf16[14,56,128]{2,1,0:T(8,128)(2,1)S(1)}, u32[]{:S(2)}, u32[]{:S(2)}) %collective-permute-start.7) | collective-permute-done | bytes 200736 | tf_op jit(solution)/shard_map/ppermute | solution.py:276
  28.4 0.7 %collective-permute-done.9.given = bf16[14,56,128]{2,1,0:T(8,128)(2,1)S(1)} collective-permute-done((bf16[14,56,128]{2,1,0:T(8,128)(2,1)S(1)}, bf16[14,56,128]{2,1,0:T(8,128)(2,1)S(1)}, u32[]{:S(2)}, u32[]{:S(2)}) %collective-permute-start.9) | collective-permute-done | bytes 200736 | tf_op jit(solution)/shard_map/ppermute | solution.py:279
  29.0 2.2 %finish.1 = bf16[14,56,128]{2,1,0:T(8,128)(2,1)} custom-call(s32[1]{0:T(128)S(6)} %copy.11.length, f32[136,512]{1,0:T(8,128)S(1)} %copy-done.1, bf16[14,56,128]{2,1,0:T(8,128)(2,1)S(1)} %collective-permute-done.7.own, bf16[14,16,128]{2,1,0:T(8,128)(2,1)S(1)} %collective-permute-done.6.rows, f32[14,56,128]{2,1,0:T(8,128)S(1)} %get-tuple-element.56.mine, ...), custom_call_target="tpu_custom_call" | custom-call | flops 22478848 | bytes 1573380 | tf_op jit(solution)/shard_map/finish/pallas_call | solution.py:223
  (8 shorter events, 0.0 us)
Async XLA Ops:
  0.0 6.6 %collective-permute-start.1 = (bf16[14,56,128]{2,1,0:T(8,128)(2,1)}, bf16[14,56,128]{2,1,0:T(8,128)(2,1)S(1)}, u32[]{:S(2)}, u32[]{:S(2)}) collective-permute-start(bf16[14,56,128]{2,1,0:T(8,128)(2,1)} %bitcast.4), channel_id=1, source_target_pairs={{0,8},{8,0},{1,9},{9,1},{2,10},{10,2},{3,11},{11,3},{4,12},{12,4},... | collective-permute-start | bytes 602120 | tf_op jit(solution)/shard_map/ppermute | solution.py:279
  0.5 8.2 %collective-permute-start = (bf16[14,56,128]{2,1,0:T(8,128)(2,1)}, bf16[14,56,128]{2,1,0:T(8,128)(2,1)S(1)}, u32[]{:S(2)}, u32[]{:S(2)}) collective-permute-start(bf16[14,56,128]{2,1,0:T(8,128)(2,1)} %bitcast.5), channel_id=1, source_target_pairs={{0,2},{2,4},{4,6},{6,7},{7,5},{5,3},{3,1},{1,0},{8,9},{10,8},{12,1... | collective-permute-start | bytes 602120 | tf_op jit(solution)/shard_map/ppermute | solution.py:276
  3.0 7.1 %collective-permute-start.3 = (bf16[14,56,128]{2,1,0:T(8,128)(2,1)}, bf16[14,56,128]{2,1,0:T(8,128)(2,1)S(1)}, u32[]{:S(2)}, u32[]{:S(2)}) collective-permute-start(bf16[14,56,128]{2,1,0:T(8,128)(2,1)} %bitcast.6), channel_id=1, source_target_pairs={{0,9},{2,8},{4,10},{6,12},{7,14},{5,15},{3,13},{1,11},{8,2},{10,4}... | collective-permute-start | bytes 602120 | tf_op jit(solution)/shard_map/ppermute | solution.py:276
  5.0 1.6 %copy-start.2 = (bf16[56,14,128]{2,0,1:T(8,128)(2,1)S(1)}, bf16[56,14,128]{2,0,1:T(8,128)(2,1)}, u32[]{:S(2)}) copy-start(bf16[56,14,128]{2,0,1:T(8,128)(2,1)} %param.10) | copy-start | bytes 602116
  6.6 1.0 %copy-start = (f32[136,512]{1,0:T(8,128)S(1)}, f32[136,512]{1,0:T(8,128)}, u32[]{:S(2)}) copy-start(f32[136,512]{1,0:T(8,128)} %join.1.shared) | copy-start | bytes 835588
  8.6 6.5 %copy-start.1 = (f32[136,512]{1,0:T(8,128)S(1)}, f32[136,512]{1,0:T(8,128)}, u32[]{:S(2)}) copy-start(f32[136,512]{1,0:T(8,128)} %join.1.shared) | copy-start | bytes 835588
  8.6 8.3 %collective-permute-start.2 = (bf16[14,56,128]{2,1,0:T(8,128)(2,1)S(1)}, bf16[14,56,128]{2,1,0:T(8,128)(2,1)S(1)}, u32[]{:S(2)}, u32[]{:S(2)}) collective-permute-start(bf16[14,56,128]{2,1,0:T(8,128)(2,1)S(1)} %collective-permute-done.own), channel_id=1, source_target_pairs={{0,2},{2,4},{4,6},{6,7},{7,5},{5,3},{3,1},{1,0},{8,9},{10,8},{12,1... | collective-permute-start | bytes 602120 | tf_op jit(solution)/shard_map/ppermute | solution.py:276
  10.1 6.9 %collective-permute-start.5 = (bf16[14,56,128]{2,1,0:T(8,128)(2,1)S(1)}, bf16[14,56,128]{2,1,0:T(8,128)(2,1)S(1)}, u32[]{:S(2)}, u32[]{:S(2)}) collective-permute-start(bf16[14,56,128]{2,1,0:T(8,128)(2,1)S(1)} %collective-permute-done.3.other), channel_id=1, source_target_pairs={{0,2},{2,4},{4,6},{6,7},{7,5},{5,3},{3,1},{1,0},{8,9},{10,8},{12,1... | collective-permute-start | bytes 602120 | tf_op jit(solution)/shard_map/ppermute | solution.py:276
  11.7 5.3 %copy-start.3 = (bf16[128,128]{1,0:T(8,128)(2,1)S(1)}, bf16[128,128]{1,0:T(8,128)(2,1)}, u32[]{:S(2)}) copy-start(bf16[128,128]{1,0:T(8,128)(2,1)} %out_gate.1) | copy-start | bytes 98308
  11.7 5.3 %copy-start.4 = (bf16[128,128]{1,0:T(8,128)(2,1)S(1)}, bf16[128,128]{1,0:T(8,128)(2,1)}, u32[]{:S(2)}) copy-start(bf16[128,128]{1,0:T(8,128)(2,1)} %last_weight.1) | copy-start | bytes 98308
  11.7 8.3 %collective-permute-start.6 = (bf16[14,16,128]{2,1,0:T(8,128)(2,1)S(1)}, bf16[14,16,128]{2,1,0:T(8,128)(2,1)S(1)}, u32[]{:S(2)}, u32[]{:S(2)}) collective-permute-start(bf16[14,16,128]{2,1,0:T(8,128)(2,1)S(1)} %pick.1), channel_id=1, source_target_pairs={{0,6},{2,7},{4,5},{6,3},{7,1},{5,0},{3,2},{1,4},{8,13},{10,11},{12... | collective-permute-start | bytes 172040 | tf_op jit(solution)/shard_map/ppermute | solution.py:276
  16.9 0.7 %copy-start.5 = (f32[128]{0:T(128)S(1)}, f32[128]{0:T(128)}, u32[]{:S(2)}) copy-start(f32[128]{0:T(128)} %param.18) | copy-start | bytes 1540
  16.9 5.8 %collective-permute-start.4 = (bf16[14,56,128]{2,1,0:T(8,128)(2,1)S(1)}, bf16[14,56,128]{2,1,0:T(8,128)(2,1)S(1)}, u32[]{:S(2)}, u32[]{:S(2)}) collective-permute-start(bf16[14,56,128]{2,1,0:T(8,128)(2,1)S(1)} %collective-permute-done.2.own), channel_id=1, source_target_pairs={{0,2},{2,4},{4,6},{6,7},{7,5},{5,3},{3,1},{1,0},{8,9},{10,8},{12,1... | collective-permute-start | bytes 602120 | tf_op jit(solution)/shard_map/ppermute | solution.py:276
  20.0 5.7 %collective-permute-start.8 = (bf16[14,56,128]{2,1,0:T(8,128)(2,1)S(1)}, bf16[14,56,128]{2,1,0:T(8,128)(2,1)S(1)}, u32[]{:S(2)}, u32[]{:S(2)}) collective-permute-start(bf16[14,56,128]{2,1,0:T(8,128)(2,1)S(1)} %collective-permute-done.5.other), channel_id=1, source_target_pairs={{0,2},{2,4},{4,6},{6,7},{7,5},{5,3},{3,1},{1,0},{8,9},{10,8},{12,1... | collective-permute-start | bytes 602120 | tf_op jit(solution)/shard_map/ppermute | solution.py:276
  22.7 5.7 %collective-permute-start.7 = (bf16[14,56,128]{2,1,0:T(8,128)(2,1)S(1)}, bf16[14,56,128]{2,1,0:T(8,128)(2,1)S(1)}, u32[]{:S(2)}, u32[]{:S(2)}) collective-permute-start(bf16[14,56,128]{2,1,0:T(8,128)(2,1)S(1)} %collective-permute-done.4.own), channel_id=1, source_target_pairs={{0,2},{2,4},{4,6},{6,7},{7,5},{5,3},{3,1},{1,0},{8,9},{10,8},{12,1... | collective-permute-start | bytes 602120 | tf_op jit(solution)/shard_map/ppermute | solution.py:276
  27.5 1.5 %collective-permute-start.9 = (bf16[14,56,128]{2,1,0:T(8,128)(2,1)S(1)}, bf16[14,56,128]{2,1,0:T(8,128)(2,1)S(1)}, u32[]{:S(2)}, u32[]{:S(2)}) collective-permute-start(bf16[14,56,128]{2,1,0:T(8,128)(2,1)S(1)} %get-tuple-element.57), channel_id=1, source_target_pairs={{0,8},{8,0},{1,9},{9,1},{2,10},{10,2},{3,11},{11,3},{4,12},{12,4},... | collective-permute-start | bytes 602120 | tf_op jit(solution)/shard_map/ppermute | solution.py:279

commit v16 on v15

--- a/solution.py
+++ b/solution.py
@@ -190,19 +190,28 @@
         theirs[...] = picked[:, : s.height].astype(BF16)
 
 
-def pick(s, ahead, own, other, rows, picked):
-    col = column_from(s, -ahead)
-    choose(lax.axis_index("row") == owner_of(s, col), own, other, picked.at[:, : s.height])
-    for step in range(s.width):
-        rows[step] = picked[step, pl.ds(offset_in(s, col), s.slots), :].astype(BF16)
-
-
-def finish(s, length, shared, own, rows, mine, given, gating, last_gain, last_weight, *refs):
-    update, left, partner, total = refs
+def last_right(s, length, shared, own, right, picked, partner):
+    shared = Shared(s, length, shared)
+    picked[:, : s.height] = own[...].astype(F32)
+    offset = offset_in(s, lax.axis_index("col"))
     token = column_from(s, s.cols // 2) * s.width
+
+    def rows_of(at):
+        return picked[at, pl.ds(offset, s.slots), :]
+
+    project_right(s, rows_of, 0, s.width, token, shared, partner)
+    right[...] = partner[...].astype(BF16)
+
+
+def last_left(s, length, shared, own, left):
     shared = Shared(s, length, shared)
-    project_right(s, lambda at: rows[at].astype(F32), 0, s.width, token, shared, partner)
+    token = column_from(s, s.cols // 2) * s.width
     project_left(s, own, lax.axis_index("row"), 0, s.width, token, shared, left)
+
+
+def finish(s, left, right, other, mine, given, gating, last_gain, last_weight, *refs):
+    update, partner, total = refs
+    choose(lax.axis_index("row") == owner_of(s, lax.axis_index("col")), right, other, partner)
     accumulate(s, left, partner, mine, total)
     for start in range(0, s.width, s.half):
         settled = [
@@ -308,47 +317,44 @@
     own = shift(pair)
     total = add(0, pair, swap(pair), ())
     other, own = in_turn(other, own, total)
-    early = min(3, far - 1)
     for distance in range(1, far - 1):
         ahead = [shift(other), shift(own)]
-        if distance == far - early:
-            rows = call(
-                functools.partial(pick, s, early),
-                shape((width, s.slots, channels), BF16),
-                [padded],
-                0,
-                own,
-                other,
-            )
-            rows = shift(rows, by=early)
         total = add(distance, own, other, total)
-        other, own = in_turn(*ahead, total)
-        if distance == far - early:
-            later = lax.optimization_barrier((pair, own))[0]
+        if distance == 1:
             gating = call(
                 functools.partial(gate, s),
                 [sums, shape((1, hidden), F32), shape(out_weight.shape, BF16)],
                 [],
                 2 * height * width * channels * channels,
                 *shared,
-                later,
+                pair,
                 out_gate,
                 output_gain.reshape(1, hidden),
                 out_weight,
             )
-            other, rows, gating = lax.optimization_barrier((other, rows, gating))
+        other, own = in_turn(*ahead, (total, gating))
     last = shift(own)
     mine, theirs = add(far - 1, own, other, total, narrow=True)
     given = swap(theirs)
     last, mine, gating = lax.optimization_barrier((last, mine, gating))
+    right = call(
+        functools.partial(last_right, s),
+        shape((width, s.slots, hidden), BF16),
+        [padded, partner],
+        0,
+        *shared,
+        last,
+    )
+    swapped = swap(right)
+    left = call(functools.partial(last_left, s), sums, [], 0, *shared, last)
     update = call(
         functools.partial(finish, s),
         shape((width, height, channels), BF16),
-        [tokens, partner, pltpu.VMEM(sums.shape, F32)],
+        [partner, pltpu.VMEM(sums.shape, F32)],
         width * product,
-        *shared,
-        last,
-        rows,
+        left,
+        right,
+        swapped,
         mine,
         given,
         *gating,

time: 31.4 us -> 29.3 us (0.933)
  waiting for transfers between devices: 5.84 us -> 4.68 us
  starting transfers between devices: 12.5 us -> 11.8 us
  local copies, waits for them, and re-layouts: 1.53 us -> 0.97 us
    ppermute x8 -> x7, waiting for transfers between devices: 5.18 us -> 3.94 us  [shift(): return lax.ppermute(block, ('row', 'col'), pairs)]
    ppermute x8 -> x7, starting transfers between devices: 11.9 us -> 11.2 us  [shift(): return lax.ppermute(block, ('row', 'col'), pairs)]
    unnamed x12 -> x10, local copies, waits for them, and re-layouts: 1.53 us -> 0.97 us
    pallas_call x8 -> x9, Pallas kernels: 10.6 us -> 10.9 us  [call(): pl.pallas_call(body, out_shape=out_shape, in_specs=[space(o) for o in ope...]
    ppermute x2 -> x3, waiting for transfers between devices: 0.66 us -> 0.73 us  [swap(): lax.ppermute(block, 'row', [(at, (at + 1) % s.rows) for at in range(s.row...]
  transfers between devices with their start and end apart: 10 -> 10, of which waited for: 5 -> 6; matrix products, arithmetic and copies ran while one was open for 0% -> 0% of each run, Pallas kernels for 27% -> 32%
where the time goes in v16:
time: 29.3 us; the launch traced here: 29.1 us
  starting transfers between devices  11.8 us (40%)
  Pallas kernels  10.9 us (37%)
  waiting for transfers between devices  4.68 us (16%)
  local copies, waits for them, and re-layouts  0.97 us (3%)
  between operations  0.77 us (3%)
    ppermute x7, starting transfers between devices, shift(): return lax.ppermute(block, ('row', 'col'), pairs)  11.2 us
    pallas_call x9, Pallas kernels, call(): pl.pallas_call(body, out_shape=out_shape, in_specs=[space(o) for o in ope...  10.9 us
    ppermute x7, waiting for transfers between devices, shift(): return lax.ppermute(block, ('row', 'col'), pairs)  3.94 us
    unnamed x10, local copies, waits for them, and re-layouts  0.97 us
    ppermute x3, waiting for transfers between devices, swap(): lax.ppermute(block, 'row', [(at, (at + 1) % s.rows) for at in range(s.row...  0.73 us
    ppermute x3, starting transfers between devices, swap(): lax.ppermute(block, 'row', [(at, (at + 1) % s.rows) for at in range(s.row...  0.59 us
  transfers between devices with their start and end apart: 10, of which 6 were waited for; matrix products, arithmetic and copies ran while one was open for 0% of the time, Pallas kernels for 32%

profile of v16, /device:TPU:0, one launch (start us, length us, event | category | flops | bytes accessed | tf_op | source)
XLA Modules:
  0.0 29.1 jit_solution(13845397611607272586)
XLA Ops:
  0.0 0.5 %collective-permute-start.1 = (bf16[14,56,128]{2,1,0:T(8,128)(2,1)}, bf16[14,56,128]{2,1,0:T(8,128)(2,1)S(1)}, u32[]{:S(2)}, u32[]{:S(2)}) collective-permute-start(bf16[14,56,128]{2,1,0:T(8,128)(2,1)} %bitcast.4), channel_id=1, source_target_pairs={{0,8},{8,0},{1,9},{9,1},{2,10},{10,2},{3,11},{11,3},{4,12},{12,4},... | collective-permute-start | bytes 602120 | tf_op jit(solution)/shard_map/ppermute | solution.py:288
  0.5 2.6 %collective-permute-start = (bf16[14,56,128]{2,1,0:T(8,128)(2,1)}, bf16[14,56,128]{2,1,0:T(8,128)(2,1)S(1)}, u32[]{:S(2)}, u32[]{:S(2)}) collective-permute-start(bf16[14,56,128]{2,1,0:T(8,128)(2,1)} %bitcast.5), channel_id=1, source_target_pairs={{0,2},{2,4},{4,6},{6,7},{7,5},{5,3},{3,1},{1,0},{8,9},{10,8},{12,1... | collective-permute-start | bytes 602120 | tf_op jit(solution)/shard_map/ppermute | solution.py:285
  3.0 1.4 %collective-permute-start.3 = (bf16[14,56,128]{2,1,0:T(8,128)(2,1)}, bf16[14,56,128]{2,1,0:T(8,128)(2,1)S(1)}, u32[]{:S(2)}, u32[]{:S(2)}) collective-permute-start(bf16[14,56,128]{2,1,0:T(8,128)(2,1)} %bitcast.6), channel_id=1, source_target_pairs={{0,9},{2,8},{4,10},{6,12},{7,14},{5,15},{3,13},{1,11},{8,2},{10,4}... | collective-permute-start | bytes 602120 | tf_op jit(solution)/shard_map/ppermute | solution.py:285
  5.0 1.6 %join.1.shared = f32[136,512]{1,0:T(8,128)} custom-call(f32[1,128]{1,0:T(1,128)} %bitcast.10, bf16[128,128]{1,0:T(8,128)(2,1)} %left_gate.1, bf16[128,128]{1,0:T(8,128)(2,1)} %left_value.1, bf16[128,128]{1,0:T(8,128)(2,1)} %right_gate.1, bf16[128,128]{1,0:T(8,128)(2,1)} %right_value.1), custom_call_target="tpu_custom_call" | custom-call | bytes 131584 | tf_op jit(solution)/shard_map/join/pallas_call | solution.py:232
  6.6 0.0 collective-permute-done.1.other
  6.6 0.0 copy-done.1
  6.6 1.0 %copy-done = f32[136,512]{1,0:T(8,128)S(1)} copy-done((f32[136,512]{1,0:T(8,128)S(1)}, f32[136,512]{1,0:T(8,128)}, u32[]{:S(2)}) %copy-start) | copy-done | bytes 278552
  7.6 1.0 %add_both.4 = (f32[14,56,128]{2,1,0:T(8,128)S(1)}, f32[14,56,128]{2,1,0:T(8,128)S(1)}) custom-call(s32[1]{0:T(128)S(6)} %copy.11.length, f32[136,512]{1,0:T(8,128)S(1)} %copy-done, bf16[14,56,128]{2,1,0:T(8,128)(2,1)S(1)} %bitcast.7, bf16[14,56,128]{2,1,0:T(8,128)(2,1)S(1)} %collective-permute-done.1.other), custom_call_target="tpu_custom_call" | custom-call | flops 22478848 | bytes 679940 | tf_op jit(solution)/shard_map/add_both/pallas_call | solution.py:232
  8.6 0.0 collective-permute-done.own
  8.6 0.0 copy-start.4
  8.6 1.5 %collective-permute-start.2 = (bf16[14,56,128]{2,1,0:T(8,128)(2,1)S(1)}, bf16[14,56,128]{2,1,0:T(8,128)(2,1)S(1)}, u32[]{:S(2)}, u32[]{:S(2)}) collective-permute-start(bf16[14,56,128]{2,1,0:T(8,128)(2,1)S(1)} %collective-permute-done.own), channel_id=1, source_target_pairs={{0,2},{2,4},{4,6},{6,7},{7,5},{5,3},{3,1},{1,0},{8,9},{10,8},{12,1... | collective-permute-start | bytes 602120 | tf_op jit(solution)/shard_map/ppermute | solution.py:285
  10.1 0.0 collective-permute-done.3.other
  10.1 1.6 %collective-permute-start.5 = (bf16[14,56,128]{2,1,0:T(8,128)(2,1)S(1)}, bf16[14,56,128]{2,1,0:T(8,128)(2,1)S(1)}, u32[]{:S(2)}, u32[]{:S(2)}) collective-permute-start(bf16[14,56,128]{2,1,0:T(8,128)(2,1)S(1)} %collective-permute-done.3.other), channel_id=1, source_target_pairs={{0,2},{2,4},{4,6},{6,7},{7,5},{5,3},{3,1},{1,0},{8,9},{10,8},{12,1... | collective-permute-start | bytes 602120 | tf_op jit(solution)/shard_map/ppermute | solution.py:285
  11.7 0.5 %gate.1 = (f32[14,56,128]{2,1,0:T(8,128)S(1)}, f32[1,128]{1,0:T(1,128)S(1)}, bf16[128,128]{1,0:T(8,128)(2,1)S(1)}) custom-call(s32[1]{0:T(128)S(6)} %copy.11.length, f32[136,512]{1,0:T(8,128)S(1)} %copy-done, bf16[14,56,128]{2,1,0:T(8,128)(2,1)S(1)} %bitcast.8, bf16[128,128]{1,0:T(8,128)(2,1)S(1)} %copy-done.2, f32[1,128]{1,0:T(1,128)S(1)} %bitcast.9, ...), custom_call_target="tpu_custom_call" | custom-call | flops 25690112 | bytes 545284 | tf_op jit(solution)/shard_map/gate/pallas_call | solution.py:232
  12.2 1.8 %add_both.5 = (f32[14,56,128]{2,1,0:T(8,128)S(1)}, f32[14,56,128]{2,1,0:T(8,128)S(1)}) custom-call(s32[1]{0:T(128)S(6)} %copy.11.length, f32[136,512]{1,0:T(8,128)S(1)} %copy-done, bf16[14,56,128]{2,1,0:T(8,128)(2,1)S(1)} %collective-permute-done.own, bf16[14,56,128]{2,1,0:T(8,128)(2,1)S(1)} %collective-permute-done.3.other, ...), custom_call_target="tpu_custom_call" | custom-call | flops 44957696 | bytes 1482756 | tf_op jit(solution)/shard_map/add_both/pallas_call | solution.py:232
  14.0 0.4 %collective-permute-done.2.own = bf16[14,56,128]{2,1,0:T(8,128)(2,1)S(1)} collective-permute-done((bf16[14,56,128]{2,1,0:T(8,128)(2,1)S(1)}, bf16[14,56,128]{2,1,0:T(8,128)(2,1)S(1)}, u32[]{:S(2)}, u32[]{:S(2)}) %collective-permute-start.2) | collective-permute-done | bytes 200736 | tf_op jit(solution)/shard_map/ppermute | solution.py:285
  14.4 1.4 %collective-permute-start.4 = (bf16[14,56,128]{2,1,0:T(8,128)(2,1)S(1)}, bf16[14,56,128]{2,1,0:T(8,128)(2,1)S(1)}, u32[]{:S(2)}, u32[]{:S(2)}) collective-permute-start(bf16[14,56,128]{2,1,0:T(8,128)(2,1)S(1)} %collective-permute-done.2.own), channel_id=1, source_target_pairs={{0,2},{2,4},{4,6},{6,7},{7,5},{5,3},{3,1},{1,0},{8,9},{10,8},{12,1... | collective-permute-start | bytes 602120 | tf_op jit(solution)/shard_map/ppermute | solution.py:285
  15.8 0.7 %collective-permute-done.5.other = bf16[14,56,128]{2,1,0:T(8,128)(2,1)S(1)} collective-permute-done((bf16[14,56,128]{2,1,0:T(8,128)(2,1)S(1)}, bf16[14,56,128]{2,1,0:T(8,128)(2,1)S(1)}, u32[]{:S(2)}, u32[]{:S(2)}) %collective-permute-start.5) | collective-permute-done | bytes 200736 | tf_op jit(solution)/shard_map/ppermute | solution.py:285
  16.6 1.5 %collective-permute-start.7 = (bf16[14,56,128]{2,1,0:T(8,128)(2,1)S(1)}, bf16[14,56,128]{2,1,0:T(8,128)(2,1)S(1)}, u32[]{:S(2)}, u32[]{:S(2)}) collective-permute-start(bf16[14,56,128]{2,1,0:T(8,128)(2,1)S(1)} %collective-permute-done.5.other), channel_id=1, source_target_pairs={{0,2},{2,4},{4,6},{6,7},{7,5},{5,3},{3,1},{1,0},{8,9},{10,8},{12,1... | collective-permute-start | bytes 602120 | tf_op jit(solution)/shard_map/ppermute | solution.py:285
  18.0 1.8 %add_both.6 = (f32[14,56,128]{2,1,0:T(8,128)S(1)}, f32[14,56,128]{2,1,0:T(8,128)S(1)}) custom-call(s32[1]{0:T(128)S(6)} %copy.11.length, f32[136,512]{1,0:T(8,128)S(1)} %copy-done, bf16[14,56,128]{2,1,0:T(8,128)(2,1)S(1)} %collective-permute-done.2.own, bf16[14,56,128]{2,1,0:T(8,128)(2,1)S(1)} %collective-permute-done.5.other, ...), custom_call_target="tpu_custom_call" | custom-call | flops 44957696 | bytes 1482756 | tf_op jit(solution)/shard_map/add_both/pallas_call | solution.py:232
  19.8 0.3 %collective-permute-done.4.own = bf16[14,56,128]{2,1,0:T(8,128)(2,1)S(1)} collective-permute-done((bf16[14,56,128]{2,1,0:T(8,128)(2,1)S(1)}, bf16[14,56,128]{2,1,0:T(8,128)(2,1)S(1)}, u32[]{:S(2)}, u32[]{:S(2)}) %collective-permute-start.4) | collective-permute-done | bytes 200736 | tf_op jit(solution)/shard_map/ppermute | solution.py:285
  20.1 1.4 %collective-permute-start.6 = (bf16[14,56,128]{2,1,0:T(8,128)(2,1)S(1)}, bf16[14,56,128]{2,1,0:T(8,128)(2,1)S(1)}, u32[]{:S(2)}, u32[]{:S(2)}) collective-permute-start(bf16[14,56,128]{2,1,0:T(8,128)(2,1)S(1)} %collective-permute-done.4.own), channel_id=1, source_target_pairs={{0,2},{2,4},{4,6},{6,7},{7,5},{5,3},{3,1},{1,0},{8,9},{10,8},{12,1... | collective-permute-start | bytes 602120 | tf_op jit(solution)/shard_map/ppermute | solution.py:285
  21.5 0.7 %collective-permute-done.7.other = bf16[14,56,128]{2,1,0:T(8,128)(2,1)S(1)} collective-permute-done((bf16[14,56,128]{2,1,0:T(8,128)(2,1)S(1)}, bf16[14,56,128]{2,1,0:T(8,128)(2,1)S(1)}, u32[]{:S(2)}, u32[]{:S(2)}) %collective-permute-start.7) | collective-permute-done | bytes 200736 | tf_op jit(solution)/shard_map/ppermute | solution.py:285
  22.3 1.8 %add_both.7 = (f32[14,56,128]{2,1,0:T(8,128)S(1)}, bf16[14,56,128]{2,1,0:T(8,128)(2,1)S(1)}) custom-call(s32[1]{0:T(128)S(6)} %copy.11.length, f32[136,512]{1,0:T(8,128)S(1)} %copy-done, bf16[14,56,128]{2,1,0:T(8,128)(2,1)S(1)} %collective-permute-done.4.own, bf16[14,56,128]{2,1,0:T(8,128)(2,1)S(1)} %collective-permute-done.7.other, ...), custom_call_target="tpu_custom_call" | custom-call | flops 44957696 | bytes 1482756 | tf_op jit(solution)/shard_map/add_both/pallas_call | solution.py:232
  24.1 0.1 collective-permute-start.9
  24.1 1.7 %collective-permute-done.6.own = bf16[14,56,128]{2,1,0:T(8,128)(2,1)S(1)} collective-permute-done((bf16[14,56,128]{2,1,0:T(8,128)(2,1)S(1)}, bf16[14,56,128]{2,1,0:T(8,128)(2,1)S(1)}, u32[]{:S(2)}, u32[]{:S(2)}) %collective-permute-start.6) | collective-permute-done | bytes 200736 | tf_op jit(solution)/shard_map/ppermute | solution.py:285
  25.8 0.4 %last_right.1.right = bf16[14,16,128]{2,1,0:T(8,128)(2,1)S(1)} custom-call(s32[1]{0:T(128)S(6)} %copy.11.length, f32[136,512]{1,0:T(8,128)S(1)} %copy-done, bf16[14,56,128]{2,1,0:T(8,128)(2,1)S(1)} %collective-permute-done.6.own), custom_call_target="tpu_custom_call" | custom-call | bytes 479236 | tf_op jit(solution)/shard_map/last_right/pallas_call | solution.py:232
  26.2 0.1 collective-permute-start.8
  26.3 0.5 %last_left.1.left = f32[14,56,128]{2,1,0:T(8,128)S(1)} custom-call(s32[1]{0:T(128)S(6)} %copy.11.length, f32[136,512]{1,0:T(8,128)S(1)} %copy-done, bf16[14,56,128]{2,1,0:T(8,128)(2,1)S(1)} %collective-permute-done.6.own), custom_call_target="tpu_custom_call" | custom-call | bytes 479236 | tf_op jit(solution)/shard_map/last_left/pallas_call | solution.py:232
  26.8 0.0 collective-permute-done.9.given
  26.8 0.7 %collective-permute-done.8.other = bf16[14,16,128]{2,1,0:T(8,128)(2,1)S(1)} collective-permute-done((bf16[14,16,128]{2,1,0:T(8,128)(2,1)S(1)}, bf16[14,16,128]{2,1,0:T(8,128)(2,1)S(1)}, u32[]{:S(2)}, u32[]{:S(2)}) %collective-permute-start.8) | collective-permute-done | bytes 57376 | tf_op jit(solution)/shard_map/ppermute | solution.py:288
  27.5 1.6 %finish.1 = bf16[14,56,128]{2,1,0:T(8,128)(2,1)} custom-call(f32[14,56,128]{2,1,0:T(8,128)S(1)} %last_left.1.left, bf16[14,16,128]{2,1,0:T(8,128)(2,1)S(1)} %last_right.1.right, bf16[14,16,128]{2,1,0:T(8,128)(2,1)S(1)} %collective-permute-done.8.other, f32[14,56,128]{2,1,0:T(8,128)S(1)} %get-tuple-element.44.mine, ...), custom_call_target="tpu_custom_call" | custom-call | flops 22478848 | bytes 1552896 | tf_op jit(solution)/shard_map/finish/pallas_call | solution.py:232
  (7 shorter events, 0.0 us)
Async XLA Ops:
  0.0 6.6 %collective-permute-start.1 = (bf16[14,56,128]{2,1,0:T(8,128)(2,1)}, bf16[14,56,128]{2,1,0:T(8,128)(2,1)S(1)}, u32[]{:S(2)}, u32[]{:S(2)}) collective-permute-start(bf16[14,56,128]{2,1,0:T(8,128)(2,1)} %bitcast.4), channel_id=1, source_target_pairs={{0,8},{8,0},{1,9},{9,1},{2,10},{10,2},{3,11},{11,3},{4,12},{12,4},... | collective-permute-start | bytes 602120 | tf_op jit(solution)/shard_map/ppermute | solution.py:288
  0.5 8.2 %collective-permute-start = (bf16[14,56,128]{2,1,0:T(8,128)(2,1)}, bf16[14,56,128]{2,1,0:T(8,128)(2,1)S(1)}, u32[]{:S(2)}, u32[]{:S(2)}) collective-permute-start(bf16[14,56,128]{2,1,0:T(8,128)(2,1)} %bitcast.5), channel_id=1, source_target_pairs={{0,2},{2,4},{4,6},{6,7},{7,5},{5,3},{3,1},{1,0},{8,9},{10,8},{12,1... | collective-permute-start | bytes 602120 | tf_op jit(solution)/shard_map/ppermute | solution.py:285
  3.0 7.1 %collective-permute-start.3 = (bf16[14,56,128]{2,1,0:T(8,128)(2,1)}, bf16[14,56,128]{2,1,0:T(8,128)(2,1)S(1)}, u32[]{:S(2)}, u32[]{:S(2)}) collective-permute-start(bf16[14,56,128]{2,1,0:T(8,128)(2,1)} %bitcast.6), channel_id=1, source_target_pairs={{0,9},{2,8},{4,10},{6,12},{7,14},{5,15},{3,13},{1,11},{8,2},{10,4}... | collective-permute-start | bytes 602120 | tf_op jit(solution)/shard_map/ppermute | solution.py:285
  5.0 1.6 %copy-start.1 = (bf16[56,14,128]{2,0,1:T(8,128)(2,1)S(1)}, bf16[56,14,128]{2,0,1:T(8,128)(2,1)}, u32[]{:S(2)}) copy-start(bf16[56,14,128]{2,0,1:T(8,128)(2,1)} %param.10) | copy-start | bytes 602116
  6.6 1.0 %copy-start = (f32[136,512]{1,0:T(8,128)S(1)}, f32[136,512]{1,0:T(8,128)}, u32[]{:S(2)}) copy-start(f32[136,512]{1,0:T(8,128)} %join.1.shared) | copy-start | bytes 835588
  7.6 4.1 %copy-start.2 = (bf16[128,128]{1,0:T(8,128)(2,1)S(1)}, bf16[128,128]{1,0:T(8,128)(2,1)}, u32[]{:S(2)}) copy-start(bf16[128,128]{1,0:T(8,128)(2,1)} %out_gate.1) | copy-start | bytes 98308
  7.6 4.1 %copy-start.3 = (bf16[128,128]{1,0:T(8,128)(2,1)S(1)}, bf16[128,128]{1,0:T(8,128)(2,1)}, u32[]{:S(2)}) copy-start(bf16[128,128]{1,0:T(8,128)(2,1)} %last_weight.1) | copy-start | bytes 98308
  8.6 3.1 %copy-start.4 = (f32[128]{0:T(128)S(1)}, f32[128]{0:T(128)}, u32[]{:S(2)}) copy-start(f32[128]{0:T(128)} %param.18) | copy-start | bytes 1540
  8.6 5.8 %collective-permute-start.2 = (bf16[14,56,128]{2,1,0:T(8,128)(2,1)S(1)}, bf16[14,56,128]{2,1,0:T(8,128)(2,1)S(1)}, u32[]{:S(2)}, u32[]{:S(2)}) collective-permute-start(bf16[14,56,128]{2,1,0:T(8,128)(2,1)S(1)} %collective-permute-done.own), channel_id=1, source_target_pairs={{0,2},{2,4},{4,6},{6,7},{7,5},{5,3},{3,1},{1,0},{8,9},{10,8},{12,1... | collective-permute-start | bytes 602120 | tf_op jit(solution)/shard_map/ppermute | solution.py:285
  10.1 6.4 %collective-permute-start.5 = (bf16[14,56,128]{2,1,0:T(8,128)(2,1)S(1)}, bf16[14,56,128]{2,1,0:T(8,128)(2,1)S(1)}, u32[]{:S(2)}, u32[]{:S(2)}) collective-permute-start(bf16[14,56,128]{2,1,0:T(8,128)(2,1)S(1)} %collective-permute-done.3.other), channel_id=1, source_target_pairs={{0,2},{2,4},{4,6},{6,7},{7,5},{5,3},{3,1},{1,0},{8,9},{10,8},{12,1... | collective-permute-start | bytes 602120 | tf_op jit(solution)/shard_map/ppermute | solution.py:285
  14.4 5.7 %collective-permute-start.4 = (bf16[14,56,128]{2,1,0:T(8,128)(2,1)S(1)}, bf16[14,56,128]{2,1,0:T(8,128)(2,1)S(1)}, u32[]{:S(2)}, u32[]{:S(2)}) collective-permute-start(bf16[14,56,128]{2,1,0:T(8,128)(2,1)S(1)} %collective-permute-done.2.own), channel_id=1, source_target_pairs={{0,2},{2,4},{4,6},{6,7},{7,5},{5,3},{3,1},{1,0},{8,9},{10,8},{12,1... | collective-permute-start | bytes 602120 | tf_op jit(solution)/shard_map/ppermute | solution.py:285
  16.6 5.7 %collective-permute-start.7 = (bf16[14,56,128]{2,1,0:T(8,128)(2,1)S(1)}, bf16[14,56,128]{2,1,0:T(8,128)(2,1)S(1)}, u32[]{:S(2)}, u32[]{:S(2)}) collective-permute-start(bf16[14,56,128]{2,1,0:T(8,128)(2,1)S(1)} %collective-permute-done.5.other), channel_id=1, source_target_pairs={{0,2},{2,4},{4,6},{6,7},{7,5},{5,3},{3,1},{1,0},{8,9},{10,8},{12,1... | collective-permute-start | bytes 602120 | tf_op jit(solution)/shard_map/ppermute | solution.py:285
  20.1 5.7 %collective-permute-start.6 = (bf16[14,56,128]{2,1,0:T(8,128)(2,1)S(1)}, bf16[14,56,128]{2,1,0:T(8,128)(2,1)S(1)}, u32[]{:S(2)}, u32[]{:S(2)}) collective-permute-start(bf16[14,56,128]{2,1,0:T(8,128)(2,1)S(1)} %collective-permute-done.4.own), channel_id=1, source_target_pairs={{0,2},{2,4},{4,6},{6,7},{7,5},{5,3},{3,1},{1,0},{8,9},{10,8},{12,1... | collective-permute-start | bytes 602120 | tf_op jit(solution)/shard_map/ppermute | solution.py:285
  24.1 2.7 %collective-permute-start.9 = (bf16[14,56,128]{2,1,0:T(8,128)(2,1)S(1)}, bf16[14,56,128]{2,1,0:T(8,128)(2,1)S(1)}, u32[]{:S(2)}, u32[]{:S(2)}) collective-permute-start(bf16[14,56,128]{2,1,0:T(8,128)(2,1)S(1)} %get-tuple-element.45), channel_id=1, source_target_pairs={{0,8},{8,0},{1,9},{9,1},{2,10},{10,2},{3,11},{11,3},{4,12},{12,4},... | collective-permute-start | bytes 602120 | tf_op jit(solution)/shard_map/ppermute | solution.py:288
  26.2 1.3 %collective-permute-start.8 = (bf16[14,16,128]{2,1,0:T(8,128)(2,1)S(1)}, bf16[14,16,128]{2,1,0:T(8,128)(2,1)S(1)}, u32[]{:S(2)}, u32[]{:S(2)}) collective-permute-start(bf16[14,16,128]{2,1,0:T(8,128)(2,1)S(1)} %last_right.1.right), channel_id=1, source_target_pairs={{0,8},{8,0},{1,9},{9,1},{2,10},{10,2},{3,11},{11,3},{4,12},{12,4},... | collective-permute-start | bytes 172040 | tf_op jit(solution)/shard_map/ppermute | solution.py:288

commit v17 on v16

--- a/solution.py
+++ b/solution.py
@@ -44,6 +44,14 @@
     return centered * lax.rsqrt(variance + EPS)
 
 
+def normalise_tokens(values):
+    channels = values.shape[-1]
+    mean = jnp.full((channels, channels), 1.0 / channels, BF16)
+    centered = values - dot(values.astype(BF16), mean)
+    variance = dot((centered * centered).astype(BF16), mean)
+    return centered * lax.rsqrt(variance + EPS)
+
+
 def sigmoid(values):
     return 0.5 * jnp.tanh(0.5 * values) + 0.5
 
@@ -57,10 +65,8 @@
     kept_gain[...] = last_gain[...]
     kept_weight[...] = last_weight[...]
     for start in range(0, s.width, s.half):
-        normed = [
-            normalise(pair[start + step].astype(F32)) * gain for step in range(s.half)
-        ]
-        value = sigmoid(dot(jnp.concatenate(normed, 0).astype(BF16), out_gate[...]))
+        rows = jnp.concatenate([pair[start + step].astype(F32) for step in range(s.half)], 0)
+        value = sigmoid(dot((normalise_tokens(rows) * gain).astype(BF16), out_gate[...]))
         for step in range(s.half):
             gating[start + step] = value[step * s.height : (step + 1) * s.height]
 
@@ -129,15 +135,15 @@
 def join(s, gain, left_gate, left_value, right_gate, right_value, shared):
     h = s.hidden
     for at, part in enumerate((left_gate, left_value, right_gate, right_value)):
-        shared[: s.channels, at * h : (at + 1) * h] = part[...].astype(F32)
+        shared[: s.channels, at * h : (at + 1) * h] = 0.5 * part[...].astype(F32)
     shared[s.channels : s.channels + 1, : s.channels] = gain[...]
 
 
 def gated(s, rows, gain, weight, masks):
     h, size = s.hidden, rows[0].shape[0]
-    rows = [normalise(row) * gain for row in rows]
-    out = dot(jnp.concatenate(rows, 0).astype(BF16), weight)
-    value = sigmoid(out[:, :h]) * out[:, h:]
+    rows = normalise_tokens(jnp.concatenate(rows, 0)) * gain
+    out = dot(rows.astype(BF16), weight)
+    value = (jnp.tanh(out[:, :h]) + 1.0) * out[:, h:]
     return [value[at * size : (at + 1) * size] * mask for at, mask in enumerate(masks)]
 
 

time: 29.3 us -> 30.9 us (1.055)
  Pallas kernels: 10.9 us -> 14 us
  waiting for transfers between devices: 4.68 us -> 3.04 us
    pallas_call x9, Pallas kernels: 10.9 us -> 14 us  [call(): pl.pallas_call(body, out_shape=out_shape, in_specs=[space(o) for o in ope...]
    ppermute x7, waiting for transfers between devices: 3.94 us -> 2.54 us  [shift(): return lax.ppermute(block, ('row', 'col'), pairs)]
  transfers between devices with their start and end apart: 10 -> 10, of which waited for: 6 -> 4; matrix products, arithmetic and copies ran while one was open for 0% -> 0% of each run, Pallas kernels for 32% -> 40%
where the time goes in v17:
time: 30.9 us; the launch traced here: 30.7 us
  Pallas kernels  14 us (45%)
  starting transfers between devices  12 us (39%)
  waiting for transfers between devices  3.04 us (10%)
  local copies, waits for them, and re-layouts  0.97 us (3%)
  between operations  0.78 us (3%)
    pallas_call x9, Pallas kernels, call(): pl.pallas_call(body, out_shape=out_shape, in_specs=[space(o) for o in ope...  14 us
    ppermute x7, starting transfers between devices, shift(): return lax.ppermute(block, ('row', 'col'), pairs)  11.4 us
    ppermute x7, waiting for transfers between devices, shift(): return lax.ppermute(block, ('row', 'col'), pairs)  2.54 us
    unnamed x10, local copies, waits for them, and re-layouts  0.97 us
  transfers between devices with their start and end apart: 10, of which 4 were waited for; matrix products, arithmetic and copies ran while one was open for 0% of the time, Pallas kernels for 40%

profile of v17, /device:TPU:0, one launch (start us, length us, event | category | flops | bytes accessed | tf_op | source)
XLA Modules:
  0.0 30.7 jit_solution(2203872912222220665)
XLA Ops:
  0.0 0.5 %collective-permute-start.1 = (bf16[14,56,128]{2,1,0:T(8,128)(2,1)}, bf16[14,56,128]{2,1,0:T(8,128)(2,1)S(1)}, u32[]{:S(2)}, u32[]{:S(2)}) collective-permute-start(bf16[14,56,128]{2,1,0:T(8,128)(2,1)} %bitcast.4), channel_id=1, source_target_pairs={{0,8},{8,0},{1,9},{9,1},{2,10},{10,2},{3,11},{11,3},{4,12},{12,4},... | collective-permute-start | bytes 602120 | tf_op jit(solution)/shard_map/ppermute | solution.py:294
  0.5 2.6 %collective-permute-start = (bf16[14,56,128]{2,1,0:T(8,128)(2,1)}, bf16[14,56,128]{2,1,0:T(8,128)(2,1)S(1)}, u32[]{:S(2)}, u32[]{:S(2)}) collective-permute-start(bf16[14,56,128]{2,1,0:T(8,128)(2,1)} %bitcast.5), channel_id=1, source_target_pairs={{0,2},{2,4},{4,6},{6,7},{7,5},{5,3},{3,1},{1,0},{8,9},{10,8},{12,1... | collective-permute-start | bytes 602120 | tf_op jit(solution)/shard_map/ppermute | solution.py:291
  3.0 1.4 %collective-permute-start.3 = (bf16[14,56,128]{2,1,0:T(8,128)(2,1)}, bf16[14,56,128]{2,1,0:T(8,128)(2,1)S(1)}, u32[]{:S(2)}, u32[]{:S(2)}) collective-permute-start(bf16[14,56,128]{2,1,0:T(8,128)(2,1)} %bitcast.6), channel_id=1, source_target_pairs={{0,9},{2,8},{4,10},{6,12},{7,14},{5,15},{3,13},{1,11},{8,2},{10,4}... | collective-permute-start | bytes 602120 | tf_op jit(solution)/shard_map/ppermute | solution.py:291
  5.0 1.6 %join.1.shared = f32[136,512]{1,0:T(8,128)} custom-call(f32[1,128]{1,0:T(1,128)} %bitcast.10, bf16[128,128]{1,0:T(8,128)(2,1)} %left_gate.1, bf16[128,128]{1,0:T(8,128)(2,1)} %left_value.1, bf16[128,128]{1,0:T(8,128)(2,1)} %right_gate.1, bf16[128,128]{1,0:T(8,128)(2,1)} %right_value.1), custom_call_target="tpu_custom_call" | custom-call | bytes 131584 | tf_op jit(solution)/shard_map/join/pallas_call | solution.py:238
  6.6 0.0 collective-permute-done.1.other
  6.7 1.0 %copy-done = f32[136,512]{1,0:T(8,128)S(1)} copy-done((f32[136,512]{1,0:T(8,128)S(1)}, f32[136,512]{1,0:T(8,128)}, u32[]{:S(2)}) %copy-start) | copy-done | bytes 278552
  7.6 1.3 %add_both.4 = (f32[14,56,128]{2,1,0:T(8,128)S(1)}, f32[14,56,128]{2,1,0:T(8,128)S(1)}) custom-call(s32[1]{0:T(128)S(6)} %copy.11.length, f32[136,512]{1,0:T(8,128)S(1)} %copy-done, bf16[14,56,128]{2,1,0:T(8,128)(2,1)S(1)} %bitcast.7, bf16[14,56,128]{2,1,0:T(8,128)(2,1)S(1)} %collective-permute-done.1.other), custom_call_target="tpu_custom_call" | custom-call | flops 22478848 | bytes 679940 | tf_op jit(solution)/shard_map/add_both/pallas_call | solution.py:238
  8.9 0.0 collective-permute-done.own
  8.9 0.0 copy-start.4
  8.9 1.2 %collective-permute-start.2 = (bf16[14,56,128]{2,1,0:T(8,128)(2,1)S(1)}, bf16[14,56,128]{2,1,0:T(8,128)(2,1)S(1)}, u32[]{:S(2)}, u32[]{:S(2)}) collective-permute-start(bf16[14,56,128]{2,1,0:T(8,128)(2,1)S(1)} %collective-permute-done.own), channel_id=1, source_target_pairs={{0,2},{2,4},{4,6},{6,7},{7,5},{5,3},{3,1},{1,0},{8,9},{10,8},{12,1... | collective-permute-start | bytes 602120 | tf_op jit(solution)/shard_map/ppermute | solution.py:291
  10.1 0.0 collective-permute-done.3.other
  10.1 1.6 %collective-permute-start.5 = (bf16[14,56,128]{2,1,0:T(8,128)(2,1)S(1)}, bf16[14,56,128]{2,1,0:T(8,128)(2,1)S(1)}, u32[]{:S(2)}, u32[]{:S(2)}) collective-permute-start(bf16[14,56,128]{2,1,0:T(8,128)(2,1)S(1)} %collective-permute-done.3.other), channel_id=1, source_target_pairs={{0,2},{2,4},{4,6},{6,7},{7,5},{5,3},{3,1},{1,0},{8,9},{10,8},{12,1... | collective-permute-start | bytes 602120 | tf_op jit(solution)/shard_map/ppermute | solution.py:291
  11.7 0.0 copy-done.3
  11.7 0.7 %gate.1 = (f32[14,56,128]{2,1,0:T(8,128)S(1)}, f32[1,128]{1,0:T(1,128)S(1)}, bf16[128,128]{1,0:T(8,128)(2,1)S(1)}) custom-call(s32[1]{0:T(128)S(6)} %copy.11.length, f32[136,512]{1,0:T(8,128)S(1)} %copy-done, bf16[14,56,128]{2,1,0:T(8,128)(2,1)S(1)} %bitcast.8, bf16[128,128]{1,0:T(8,128)(2,1)S(1)} %copy-done.2, f32[1,128]{1,0:T(1,128)S(1)} %bitcast.9, ...), custom_call_target="tpu_custom_call" | custom-call | flops 25690112 | bytes 545284 | tf_op jit(solution)/shard_map/gate/pallas_call | solution.py:238
  12.4 2.5 %add_both.5 = (f32[14,56,128]{2,1,0:T(8,128)S(1)}, f32[14,56,128]{2,1,0:T(8,128)S(1)}) custom-call(s32[1]{0:T(128)S(6)} %copy.11.length, f32[136,512]{1,0:T(8,128)S(1)} %copy-done, bf16[14,56,128]{2,1,0:T(8,128)(2,1)S(1)} %collective-permute-done.own, bf16[14,56,128]{2,1,0:T(8,128)(2,1)S(1)} %collective-permute-done.3.other, ...), custom_call_target="tpu_custom_call" | custom-call | flops 44957696 | bytes 1482756 | tf_op jit(solution)/shard_map/add_both/pallas_call | solution.py:238
  14.9 0.0 collective-permute-done.2.own
  14.9 1.7 %collective-permute-start.4 = (bf16[14,56,128]{2,1,0:T(8,128)(2,1)S(1)}, bf16[14,56,128]{2,1,0:T(8,128)(2,1)S(1)}, u32[]{:S(2)}, u32[]{:S(2)}) collective-permute-start(bf16[14,56,128]{2,1,0:T(8,128)(2,1)S(1)} %collective-permute-done.2.own), channel_id=1, source_target_pairs={{0,2},{2,4},{4,6},{6,7},{7,5},{5,3},{3,1},{1,0},{8,9},{10,8},{12,1... | collective-permute-start | bytes 602120 | tf_op jit(solution)/shard_map/ppermute | solution.py:291
  16.6 0.2 collective-permute-done.5.other
  16.8 2.1 %collective-permute-start.7 = (bf16[14,56,128]{2,1,0:T(8,128)(2,1)S(1)}, bf16[14,56,128]{2,1,0:T(8,128)(2,1)S(1)}, u32[]{:S(2)}, u32[]{:S(2)}) collective-permute-start(bf16[14,56,128]{2,1,0:T(8,128)(2,1)S(1)} %collective-permute-done.5.other), channel_id=1, source_target_pairs={{0,2},{2,4},{4,6},{6,7},{7,5},{5,3},{3,1},{1,0},{8,9},{10,8},{12,1... | collective-permute-start | bytes 602120 | tf_op jit(solution)/shard_map/ppermute | solution.py:291
  18.9 2.5 %add_both.6 = (f32[14,56,128]{2,1,0:T(8,128)S(1)}, f32[14,56,128]{2,1,0:T(8,128)S(1)}) custom-call(s32[1]{0:T(128)S(6)} %copy.11.length, f32[136,512]{1,0:T(8,128)S(1)} %copy-done, bf16[14,56,128]{2,1,0:T(8,128)(2,1)S(1)} %collective-permute-done.2.own, bf16[14,56,128]{2,1,0:T(8,128)(2,1)S(1)} %collective-permute-done.5.other, ...), custom_call_target="tpu_custom_call" | custom-call | flops 44957696 | bytes 1482756 | tf_op jit(solution)/shard_map/add_both/pallas_call | solution.py:238
  21.4 0.0 collective-permute-done.4.own
  21.4 0.9 %collective-permute-start.6 = (bf16[14,56,128]{2,1,0:T(8,128)(2,1)S(1)}, bf16[14,56,128]{2,1,0:T(8,128)(2,1)S(1)}, u32[]{:S(2)}, u32[]{:S(2)}) collective-permute-start(bf16[14,56,128]{2,1,0:T(8,128)(2,1)S(1)} %collective-permute-done.4.own), channel_id=1, source_target_pairs={{0,2},{2,4},{4,6},{6,7},{7,5},{5,3},{3,1},{1,0},{8,9},{10,8},{12,1... | collective-permute-start | bytes 602120 | tf_op jit(solution)/shard_map/ppermute | solution.py:291
  22.3 0.5 %collective-permute-done.7.other = bf16[14,56,128]{2,1,0:T(8,128)(2,1)S(1)} collective-permute-done((bf16[14,56,128]{2,1,0:T(8,128)(2,1)S(1)}, bf16[14,56,128]{2,1,0:T(8,128)(2,1)S(1)}, u32[]{:S(2)}, u32[]{:S(2)}) %collective-permute-start.7) | collective-permute-done | bytes 200736 | tf_op jit(solution)/shard_map/ppermute | solution.py:291
  22.8 2.5 %add_both.7 = (f32[14,56,128]{2,1,0:T(8,128)S(1)}, bf16[14,56,128]{2,1,0:T(8,128)(2,1)S(1)}) custom-call(s32[1]{0:T(128)S(6)} %copy.11.length, f32[136,512]{1,0:T(8,128)S(1)} %copy-done, bf16[14,56,128]{2,1,0:T(8,128)(2,1)S(1)} %collective-permute-done.4.own, bf16[14,56,128]{2,1,0:T(8,128)(2,1)S(1)} %collective-permute-done.7.other, ...), custom_call_target="tpu_custom_call" | custom-call | flops 44957696 | bytes 1482756 | tf_op jit(solution)/shard_map/add_both/pallas_call | solution.py:238
  25.3 0.1 collective-permute-start.9
  25.4 1.8 %collective-permute-done.6.own = bf16[14,56,128]{2,1,0:T(8,128)(2,1)S(1)} collective-permute-done((bf16[14,56,128]{2,1,0:T(8,128)(2,1)S(1)}, bf16[14,56,128]{2,1,0:T(8,128)(2,1)S(1)}, u32[]{:S(2)}, u32[]{:S(2)}) %collective-permute-start.6) | collective-permute-done | bytes 200736 | tf_op jit(solution)/shard_map/ppermute | solution.py:291
  27.2 0.6 %last_right.1.right = bf16[14,16,128]{2,1,0:T(8,128)(2,1)S(1)} custom-call(s32[1]{0:T(128)S(6)} %copy.11.length, f32[136,512]{1,0:T(8,128)S(1)} %copy-done, bf16[14,56,128]{2,1,0:T(8,128)(2,1)S(1)} %collective-permute-done.6.own), custom_call_target="tpu_custom_call" | custom-call | bytes 479236 | tf_op jit(solution)/shard_map/last_right/pallas_call | solution.py:238
  27.8 0.1 collective-permute-start.8
  27.9 0.7 %last_left.1.left = f32[14,56,128]{2,1,0:T(8,128)S(1)} custom-call(s32[1]{0:T(128)S(6)} %copy.11.length, f32[136,512]{1,0:T(8,128)S(1)} %copy-done, bf16[14,56,128]{2,1,0:T(8,128)(2,1)S(1)} %collective-permute-done.6.own), custom_call_target="tpu_custom_call" | custom-call | bytes 479236 | tf_op jit(solution)/shard_map/last_left/pallas_call | solution.py:238
  28.6 0.0 collective-permute-done.9.given
  28.6 0.5 %collective-permute-done.8.other = bf16[14,16,128]{2,1,0:T(8,128)(2,1)S(1)} collective-permute-done((bf16[14,16,128]{2,1,0:T(8,128)(2,1)S(1)}, bf16[14,16,128]{2,1,0:T(8,128)(2,1)S(1)}, u32[]{:S(2)}, u32[]{:S(2)}) %collective-permute-start.8) | collective-permute-done | bytes 57376 | tf_op jit(solution)/shard_map/ppermute | solution.py:294
  29.1 1.6 %finish.1 = bf16[14,56,128]{2,1,0:T(8,128)(2,1)} custom-call(f32[14,56,128]{2,1,0:T(8,128)S(1)} %last_left.1.left, bf16[14,16,128]{2,1,0:T(8,128)(2,1)S(1)} %last_right.1.right, bf16[14,16,128]{2,1,0:T(8,128)(2,1)S(1)} %collective-permute-done.8.other, f32[14,56,128]{2,1,0:T(8,128)S(1)} %get-tuple-element.44.mine, ...), custom_call_target="tpu_custom_call" | custom-call | flops 22478848 | bytes 1552896 | tf_op jit(solution)/shard_map/finish/pallas_call | solution.py:238
  (7 shorter events, 0.0 us)
Async XLA Ops:
  0.0 6.6 %collective-permute-start.1 = (bf16[14,56,128]{2,1,0:T(8,128)(2,1)}, bf16[14,56,128]{2,1,0:T(8,128)(2,1)S(1)}, u32[]{:S(2)}, u32[]{:S(2)}) collective-permute-start(bf16[14,56,128]{2,1,0:T(8,128)(2,1)} %bitcast.4), channel_id=1, source_target_pairs={{0,8},{8,0},{1,9},{9,1},{2,10},{10,2},{3,11},{11,3},{4,12},{12,4},... | collective-permute-start | bytes 602120 | tf_op jit(solution)/shard_map/ppermute | solution.py:294
  0.5 8.4 %collective-permute-start = (bf16[14,56,128]{2,1,0:T(8,128)(2,1)}, bf16[14,56,128]{2,1,0:T(8,128)(2,1)S(1)}, u32[]{:S(2)}, u32[]{:S(2)}) collective-permute-start(bf16[14,56,128]{2,1,0:T(8,128)(2,1)} %bitcast.5), channel_id=1, source_target_pairs={{0,2},{2,4},{4,6},{6,7},{7,5},{5,3},{3,1},{1,0},{8,9},{10,8},{12,1... | collective-permute-start | bytes 602120 | tf_op jit(solution)/shard_map/ppermute | solution.py:291
  3.0 7.1 %collective-permute-start.3 = (bf16[14,56,128]{2,1,0:T(8,128)(2,1)}, bf16[14,56,128]{2,1,0:T(8,128)(2,1)S(1)}, u32[]{:S(2)}, u32[]{:S(2)}) collective-permute-start(bf16[14,56,128]{2,1,0:T(8,128)(2,1)} %bitcast.6), channel_id=1, source_target_pairs={{0,9},{2,8},{4,10},{6,12},{7,14},{5,15},{3,13},{1,11},{8,2},{10,4}... | collective-permute-start | bytes 602120 | tf_op jit(solution)/shard_map/ppermute | solution.py:291
  5.0 1.6 %copy-start.1 = (bf16[56,14,128]{2,0,1:T(8,128)(2,1)S(1)}, bf16[56,14,128]{2,0,1:T(8,128)(2,1)}, u32[]{:S(2)}) copy-start(bf16[56,14,128]{2,0,1:T(8,128)(2,1)} %param.10) | copy-start | bytes 602116
  6.6 1.0 %copy-start = (f32[136,512]{1,0:T(8,128)S(1)}, f32[136,512]{1,0:T(8,128)}, u32[]{:S(2)}) copy-start(f32[136,512]{1,0:T(8,128)} %join.1.shared) | copy-start | bytes 835588
  7.6 4.1 %copy-start.2 = (bf16[128,128]{1,0:T(8,128)(2,1)S(1)}, bf16[128,128]{1,0:T(8,128)(2,1)}, u32[]{:S(2)}) copy-start(bf16[128,128]{1,0:T(8,128)(2,1)} %out_gate.1) | copy-start | bytes 98308
  7.6 4.1 %copy-start.3 = (bf16[128,128]{1,0:T(8,128)(2,1)S(1)}, bf16[128,128]{1,0:T(8,128)(2,1)}, u32[]{:S(2)}) copy-start(bf16[128,128]{1,0:T(8,128)(2,1)} %last_weight.1) | copy-start | bytes 98308
  8.9 2.8 %copy-start.4 = (f32[128]{0:T(128)S(1)}, f32[128]{0:T(128)}, u32[]{:S(2)}) copy-start(f32[128]{0:T(128)} %param.18) | copy-start | bytes 1540
  8.9 6.0 %collective-permute-start.2 = (bf16[14,56,128]{2,1,0:T(8,128)(2,1)S(1)}, bf16[14,56,128]{2,1,0:T(8,128)(2,1)S(1)}, u32[]{:S(2)}, u32[]{:S(2)}) collective-permute-start(bf16[14,56,128]{2,1,0:T(8,128)(2,1)S(1)} %collective-permute-done.own), channel_id=1, source_target_pairs={{0,2},{2,4},{4,6},{6,7},{7,5},{5,3},{3,1},{1,0},{8,9},{10,8},{12,1... | collective-permute-start | bytes 602120 | tf_op jit(solution)/shard_map/ppermute | solution.py:291
  10.1 6.7 %collective-permute-start.5 = (bf16[14,56,128]{2,1,0:T(8,128)(2,1)S(1)}, bf16[14,56,128]{2,1,0:T(8,128)(2,1)S(1)}, u32[]{:S(2)}, u32[]{:S(2)}) collective-permute-start(bf16[14,56,128]{2,1,0:T(8,128)(2,1)S(1)} %collective-permute-done.3.other), channel_id=1, source_target_pairs={{0,2},{2,4},{4,6},{6,7},{7,5},{5,3},{3,1},{1,0},{8,9},{10,8},{12,1... | collective-permute-start | bytes 602120 | tf_op jit(solution)/shard_map/ppermute | solution.py:291
  14.9 6.5 %collective-permute-start.4 = (bf16[14,56,128]{2,1,0:T(8,128)(2,1)S(1)}, bf16[14,56,128]{2,1,0:T(8,128)(2,1)S(1)}, u32[]{:S(2)}, u32[]{:S(2)}) collective-permute-start(bf16[14,56,128]{2,1,0:T(8,128)(2,1)S(1)} %collective-permute-done.2.own), channel_id=1, source_target_pairs={{0,2},{2,4},{4,6},{6,7},{7,5},{5,3},{3,1},{1,0},{8,9},{10,8},{12,1... | collective-permute-start | bytes 602120 | tf_op jit(solution)/shard_map/ppermute | solution.py:291
  16.8 6.0 %collective-permute-start.7 = (bf16[14,56,128]{2,1,0:T(8,128)(2,1)S(1)}, bf16[14,56,128]{2,1,0:T(8,128)(2,1)S(1)}, u32[]{:S(2)}, u32[]{:S(2)}) collective-permute-start(bf16[14,56,128]{2,1,0:T(8,128)(2,1)S(1)} %collective-permute-done.5.other), channel_id=1, source_target_pairs={{0,2},{2,4},{4,6},{6,7},{7,5},{5,3},{3,1},{1,0},{8,9},{10,8},{12,1... | collective-permute-start | bytes 602120 | tf_op jit(solution)/shard_map/ppermute | solution.py:291
  21.4 5.8 %collective-permute-start.6 = (bf16[14,56,128]{2,1,0:T(8,128)(2,1)S(1)}, bf16[14,56,128]{2,1,0:T(8,128)(2,1)S(1)}, u32[]{:S(2)}, u32[]{:S(2)}) collective-permute-start(bf16[14,56,128]{2,1,0:T(8,128)(2,1)S(1)} %collective-permute-done.4.own), channel_id=1, source_target_pairs={{0,2},{2,4},{4,6},{6,7},{7,5},{5,3},{3,1},{1,0},{8,9},{10,8},{12,1... | collective-permute-start | bytes 602120 | tf_op jit(solution)/shard_map/ppermute | solution.py:291
  25.3 3.3 %collective-permute-start.9 = (bf16[14,56,128]{2,1,0:T(8,128)(2,1)S(1)}, bf16[14,56,128]{2,1,0:T(8,128)(2,1)S(1)}, u32[]{:S(2)}, u32[]{:S(2)}) collective-permute-start(bf16[14,56,128]{2,1,0:T(8,128)(2,1)S(1)} %get-tuple-element.45), channel_id=1, source_target_pairs={{0,8},{8,0},{1,9},{9,1},{2,10},{10,2},{3,11},{11,3},{4,12},{12,4},... | collective-permute-start | bytes 602120 | tf_op jit(solution)/shard_map/ppermute | solution.py:294
  27.8 1.3 %collective-permute-start.8 = (bf16[14,16,128]{2,1,0:T(8,128)(2,1)S(1)}, bf16[14,16,128]{2,1,0:T(8,128)(2,1)S(1)}, u32[]{:S(2)}, u32[]{:S(2)}) collective-permute-start(bf16[14,16,128]{2,1,0:T(8,128)(2,1)S(1)} %last_right.1.right), channel_id=1, source_target_pairs={{0,8},{8,0},{1,9},{9,1},{2,10},{10,2},{3,11},{11,3},{4,12},{12,4},... | collective-permute-start | bytes 172040 | tf_op jit(solution)/shard_map/ppermute | solution.py:294

commit v18 on v16

--- a/solution.py
+++ b/solution.py
@@ -129,7 +129,7 @@
 def join(s, gain, left_gate, left_value, right_gate, right_value, shared):
     h = s.hidden
     for at, part in enumerate((left_gate, left_value, right_gate, right_value)):
-        shared[: s.channels, at * h : (at + 1) * h] = part[...].astype(F32)
+        shared[: s.channels, at * h : (at + 1) * h] = 0.5 * part[...].astype(F32)
     shared[s.channels : s.channels + 1, : s.channels] = gain[...]
 
 
@@ -137,7 +137,7 @@
     h, size = s.hidden, rows[0].shape[0]
     rows = [normalise(row) * gain for row in rows]
     out = dot(jnp.concatenate(rows, 0).astype(BF16), weight)
-    value = sigmoid(out[:, :h]) * out[:, h:]
+    value = (jnp.tanh(out[:, :h]) + 1.0) * out[:, h:]
     return [value[at * size : (at + 1) * size] * mask for at, mask in enumerate(masks)]
 
 
@@ -313,13 +313,13 @@
         return lax.optimization_barrier((other, own))[0], own
 
     far = s.cols // 2
+    given = swap(pair)
     other = shift(pair, crossed=True)
     own = shift(pair)
-    total = add(0, pair, swap(pair), ())
+    total = add(0, pair, given, ())
     other, own = in_turn(other, own, total)
     for distance in range(1, far - 1):
         ahead = [shift(other), shift(own)]
-        total = add(distance, own, other, total)
         if distance == 1:
             gating = call(
                 functools.partial(gate, s),
@@ -332,6 +332,7 @@
                 output_gain.reshape(1, hidden),
                 out_weight,
             )
+        total = add(distance, own, other, total)
         other, own = in_turn(*ahead, (total, gating))
     last = shift(own)
     mine, theirs = add(far - 1, own, other, total, narrow=True)

time: 29.3 us -> 29.3 us (level)
  no operation moved by 1% of the time
where the time goes in v18:
time: 29.3 us; the launch traced here: 29.1 us
  starting transfers between devices  11.8 us (40%)
  Pallas kernels  10.8 us (37%)
  waiting for transfers between devices  4.74 us (16%)
  local copies, waits for them, and re-layouts  0.97 us (3%)
  between operations  0.77 us (3%)
    ppermute x7, starting transfers between devices, shift(): return lax.ppermute(block, ('row', 'col'), pairs)  11.3 us
    pallas_call x9, Pallas kernels, call(): pl.pallas_call(body, out_shape=out_shape, in_specs=[space(o) for o in ope...  10.8 us
    ppermute x7, waiting for transfers between devices, shift(): return lax.ppermute(block, ('row', 'col'), pairs)  4 us
    unnamed x10, local copies, waits for them, and re-layouts  0.97 us
    ppermute x3, waiting for transfers between devices, swap(): lax.ppermute(block, 'row', [(at, (at + 1) % s.rows) for at in range(s.row...  0.73 us
    ppermute x3, starting transfers between devices, swap(): lax.ppermute(block, 'row', [(at, (at + 1) % s.rows) for at in range(s.row...  0.59 us
  transfers between devices with their start and end apart: 10, of which 6 were waited for; matrix products, arithmetic and copies ran while one was open for 0% of the time, Pallas kernels for 32%

profile of v18, /device:TPU:0, one launch (start us, length us, event | category | flops | bytes accessed | tf_op | source)
XLA Modules:
  0.0 29.1 jit_solution(955017441620200200)
XLA Ops:
  0.0 0.5 %collective-permute-start.1 = (bf16[14,56,128]{2,1,0:T(8,128)(2,1)}, bf16[14,56,128]{2,1,0:T(8,128)(2,1)S(1)}, u32[]{:S(2)}, u32[]{:S(2)}) collective-permute-start(bf16[14,56,128]{2,1,0:T(8,128)(2,1)} %bitcast.4), channel_id=1, source_target_pairs={{0,8},{8,0},{1,9},{9,1},{2,10},{10,2},{3,11},{11,3},{4,12},{12,4},... | collective-permute-start | bytes 602120 | tf_op jit(solution)/shard_map/ppermute | solution.py:288
  0.5 2.6 %collective-permute-start = (bf16[14,56,128]{2,1,0:T(8,128)(2,1)}, bf16[14,56,128]{2,1,0:T(8,128)(2,1)S(1)}, u32[]{:S(2)}, u32[]{:S(2)}) collective-permute-start(bf16[14,56,128]{2,1,0:T(8,128)(2,1)} %bitcast.5), channel_id=1, source_target_pairs={{0,2},{2,4},{4,6},{6,7},{7,5},{5,3},{3,1},{1,0},{8,9},{10,8},{12,1... | collective-permute-start | bytes 602120 | tf_op jit(solution)/shard_map/ppermute | solution.py:285
  3.0 1.4 %collective-permute-start.3 = (bf16[14,56,128]{2,1,0:T(8,128)(2,1)}, bf16[14,56,128]{2,1,0:T(8,128)(2,1)S(1)}, u32[]{:S(2)}, u32[]{:S(2)}) collective-permute-start(bf16[14,56,128]{2,1,0:T(8,128)(2,1)} %bitcast.6), channel_id=1, source_target_pairs={{0,9},{2,8},{4,10},{6,12},{7,14},{5,15},{3,13},{1,11},{8,2},{10,4}... | collective-permute-start | bytes 602120 | tf_op jit(solution)/shard_map/ppermute | solution.py:285
  5.0 1.6 %join.1.shared = f32[136,512]{1,0:T(8,128)} custom-call(f32[1,128]{1,0:T(1,128)} %bitcast.10, bf16[128,128]{1,0:T(8,128)(2,1)} %left_gate.1, bf16[128,128]{1,0:T(8,128)(2,1)} %left_value.1, bf16[128,128]{1,0:T(8,128)(2,1)} %right_gate.1, bf16[128,128]{1,0:T(8,128)(2,1)} %right_value.1), custom_call_target="tpu_custom_call" | custom-call | bytes 131584 | tf_op jit(solution)/shard_map/join/pallas_call | solution.py:232
  6.6 0.0 collective-permute-done.1.other
  6.7 1.0 %copy-done = f32[136,512]{1,0:T(8,128)S(1)} copy-done((f32[136,512]{1,0:T(8,128)S(1)}, f32[136,512]{1,0:T(8,128)}, u32[]{:S(2)}) %copy-start) | copy-done | bytes 278552
  7.6 1.0 %add_both.4 = (f32[14,56,128]{2,1,0:T(8,128)S(1)}, f32[14,56,128]{2,1,0:T(8,128)S(1)}) custom-call(s32[1]{0:T(128)S(6)} %copy.11.length, f32[136,512]{1,0:T(8,128)S(1)} %copy-done, bf16[14,56,128]{2,1,0:T(8,128)(2,1)S(1)} %bitcast.7, bf16[14,56,128]{2,1,0:T(8,128)(2,1)S(1)} %collective-permute-done.1.other), custom_call_target="tpu_custom_call" | custom-call | flops 22478848 | bytes 679940 | tf_op jit(solution)/shard_map/add_both/pallas_call | solution.py:232
  8.6 0.0 collective-permute-done.own
  8.6 0.0 copy-start.4
  8.6 1.5 %collective-permute-start.2 = (bf16[14,56,128]{2,1,0:T(8,128)(2,1)S(1)}, bf16[14,56,128]{2,1,0:T(8,128)(2,1)S(1)}, u32[]{:S(2)}, u32[]{:S(2)}) collective-permute-start(bf16[14,56,128]{2,1,0:T(8,128)(2,1)S(1)} %collective-permute-done.own), channel_id=1, source_target_pairs={{0,2},{2,4},{4,6},{6,7},{7,5},{5,3},{3,1},{1,0},{8,9},{10,8},{12,1... | collective-permute-start | bytes 602120 | tf_op jit(solution)/shard_map/ppermute | solution.py:285
  10.1 0.0 collective-permute-done.3.other
  10.1 1.6 %collective-permute-start.5 = (bf16[14,56,128]{2,1,0:T(8,128)(2,1)S(1)}, bf16[14,56,128]{2,1,0:T(8,128)(2,1)S(1)}, u32[]{:S(2)}, u32[]{:S(2)}) collective-permute-start(bf16[14,56,128]{2,1,0:T(8,128)(2,1)S(1)} %collective-permute-done.3.other), channel_id=1, source_target_pairs={{0,2},{2,4},{4,6},{6,7},{7,5},{5,3},{3,1},{1,0},{8,9},{10,8},{12,1... | collective-permute-start | bytes 602120 | tf_op jit(solution)/shard_map/ppermute | solution.py:285
  11.7 0.0 copy-done.2
  11.7 0.5 %gate.1 = (f32[14,56,128]{2,1,0:T(8,128)S(1)}, f32[1,128]{1,0:T(1,128)S(1)}, bf16[128,128]{1,0:T(8,128)(2,1)S(1)}) custom-call(s32[1]{0:T(128)S(6)} %copy.11.length, f32[136,512]{1,0:T(8,128)S(1)} %copy-done, bf16[14,56,128]{2,1,0:T(8,128)(2,1)S(1)} %bitcast.8, bf16[128,128]{1,0:T(8,128)(2,1)S(1)} %copy-done.2, f32[1,128]{1,0:T(1,128)S(1)} %bitcast.9, ...), custom_call_target="tpu_custom_call" | custom-call | flops 25690112 | bytes 545284 | tf_op jit(solution)/shard_map/gate/pallas_call | solution.py:232
  12.2 1.8 %add_both.5 = (f32[14,56,128]{2,1,0:T(8,128)S(1)}, f32[14,56,128]{2,1,0:T(8,128)S(1)}) custom-call(s32[1]{0:T(128)S(6)} %copy.11.length, f32[136,512]{1,0:T(8,128)S(1)} %copy-done, bf16[14,56,128]{2,1,0:T(8,128)(2,1)S(1)} %collective-permute-done.own, bf16[14,56,128]{2,1,0:T(8,128)(2,1)S(1)} %collective-permute-done.3.other, ...), custom_call_target="tpu_custom_call" | custom-call | flops 44957696 | bytes 1482756 | tf_op jit(solution)/shard_map/add_both/pallas_call | solution.py:232
  13.9 0.5 %collective-permute-done.2.own = bf16[14,56,128]{2,1,0:T(8,128)(2,1)S(1)} collective-permute-done((bf16[14,56,128]{2,1,0:T(8,128)(2,1)S(1)}, bf16[14,56,128]{2,1,0:T(8,128)(2,1)S(1)}, u32[]{:S(2)}, u32[]{:S(2)}) %collective-permute-start.2) | collective-permute-done | bytes 200736 | tf_op jit(solution)/shard_map/ppermute | solution.py:285
  14.4 1.4 %collective-permute-start.4 = (bf16[14,56,128]{2,1,0:T(8,128)(2,1)S(1)}, bf16[14,56,128]{2,1,0:T(8,128)(2,1)S(1)}, u32[]{:S(2)}, u32[]{:S(2)}) collective-permute-start(bf16[14,56,128]{2,1,0:T(8,128)(2,1)S(1)} %collective-permute-done.2.own), channel_id=1, source_target_pairs={{0,2},{2,4},{4,6},{6,7},{7,5},{5,3},{3,1},{1,0},{8,9},{10,8},{12,1... | collective-permute-start | bytes 602120 | tf_op jit(solution)/shard_map/ppermute | solution.py:285
  15.8 0.7 %collective-permute-done.5.other = bf16[14,56,128]{2,1,0:T(8,128)(2,1)S(1)} collective-permute-done((bf16[14,56,128]{2,1,0:T(8,128)(2,1)S(1)}, bf16[14,56,128]{2,1,0:T(8,128)(2,1)S(1)}, u32[]{:S(2)}, u32[]{:S(2)}) %collective-permute-start.5) | collective-permute-done | bytes 200736 | tf_op jit(solution)/shard_map/ppermute | solution.py:285
  16.5 1.4 %collective-permute-start.7 = (bf16[14,56,128]{2,1,0:T(8,128)(2,1)S(1)}, bf16[14,56,128]{2,1,0:T(8,128)(2,1)S(1)}, u32[]{:S(2)}, u32[]{:S(2)}) collective-permute-start(bf16[14,56,128]{2,1,0:T(8,128)(2,1)S(1)} %collective-permute-done.5.other), channel_id=1, source_target_pairs={{0,2},{2,4},{4,6},{6,7},{7,5},{5,3},{3,1},{1,0},{8,9},{10,8},{12,1... | collective-permute-start | bytes 602120 | tf_op jit(solution)/shard_map/ppermute | solution.py:285
  18.0 1.7 %add_both.6 = (f32[14,56,128]{2,1,0:T(8,128)S(1)}, f32[14,56,128]{2,1,0:T(8,128)S(1)}) custom-call(s32[1]{0:T(128)S(6)} %copy.11.length, f32[136,512]{1,0:T(8,128)S(1)} %copy-done, bf16[14,56,128]{2,1,0:T(8,128)(2,1)S(1)} %collective-permute-done.2.own, bf16[14,56,128]{2,1,0:T(8,128)(2,1)S(1)} %collective-permute-done.5.other, ...), custom_call_target="tpu_custom_call" | custom-call | flops 44957696 | bytes 1482756 | tf_op jit(solution)/shard_map/add_both/pallas_call | solution.py:232
  19.7 0.4 %collective-permute-done.4.own = bf16[14,56,128]{2,1,0:T(8,128)(2,1)S(1)} collective-permute-done((bf16[14,56,128]{2,1,0:T(8,128)(2,1)S(1)}, bf16[14,56,128]{2,1,0:T(8,128)(2,1)S(1)}, u32[]{:S(2)}, u32[]{:S(2)}) %collective-permute-start.4) | collective-permute-done | bytes 200736 | tf_op jit(solution)/shard_map/ppermute | solution.py:285
  20.1 1.4 %collective-permute-start.6 = (bf16[14,56,128]{2,1,0:T(8,128)(2,1)S(1)}, bf16[14,56,128]{2,1,0:T(8,128)(2,1)S(1)}, u32[]{:S(2)}, u32[]{:S(2)}) collective-permute-start(bf16[14,56,128]{2,1,0:T(8,128)(2,1)S(1)} %collective-permute-done.4.own), channel_id=1, source_target_pairs={{0,2},{2,4},{4,6},{6,7},{7,5},{5,3},{3,1},{1,0},{8,9},{10,8},{12,1... | collective-permute-start | bytes 602120 | tf_op jit(solution)/shard_map/ppermute | solution.py:285
  21.5 0.7 %collective-permute-done.7.other = bf16[14,56,128]{2,1,0:T(8,128)(2,1)S(1)} collective-permute-done((bf16[14,56,128]{2,1,0:T(8,128)(2,1)S(1)}, bf16[14,56,128]{2,1,0:T(8,128)(2,1)S(1)}, u32[]{:S(2)}, u32[]{:S(2)}) %collective-permute-start.7) | collective-permute-done | bytes 200736 | tf_op jit(solution)/shard_map/ppermute | solution.py:285
  22.3 1.8 %add_both.7 = (f32[14,56,128]{2,1,0:T(8,128)S(1)}, bf16[14,56,128]{2,1,0:T(8,128)(2,1)S(1)}) custom-call(s32[1]{0:T(128)S(6)} %copy.11.length, f32[136,512]{1,0:T(8,128)S(1)} %copy-done, bf16[14,56,128]{2,1,0:T(8,128)(2,1)S(1)} %collective-permute-done.4.own, bf16[14,56,128]{2,1,0:T(8,128)(2,1)S(1)} %collective-permute-done.7.other, ...), custom_call_target="tpu_custom_call" | custom-call | flops 44957696 | bytes 1482756 | tf_op jit(solution)/shard_map/add_both/pallas_call | solution.py:232
  24.0 0.1 collective-permute-start.9
  24.1 1.7 %collective-permute-done.6.own = bf16[14,56,128]{2,1,0:T(8,128)(2,1)S(1)} collective-permute-done((bf16[14,56,128]{2,1,0:T(8,128)(2,1)S(1)}, bf16[14,56,128]{2,1,0:T(8,128)(2,1)S(1)}, u32[]{:S(2)}, u32[]{:S(2)}) %collective-permute-start.6) | collective-permute-done | bytes 200736 | tf_op jit(solution)/shard_map/ppermute | solution.py:285
  25.8 0.4 %last_right.1.right = bf16[14,16,128]{2,1,0:T(8,128)(2,1)S(1)} custom-call(s32[1]{0:T(128)S(6)} %copy.11.length, f32[136,512]{1,0:T(8,128)S(1)} %copy-done, bf16[14,56,128]{2,1,0:T(8,128)(2,1)S(1)} %collective-permute-done.6.own), custom_call_target="tpu_custom_call" | custom-call | bytes 479236 | tf_op jit(solution)/shard_map/last_right/pallas_call | solution.py:232
  26.2 0.1 collective-permute-start.8
  26.3 0.5 %last_left.1.left = f32[14,56,128]{2,1,0:T(8,128)S(1)} custom-call(s32[1]{0:T(128)S(6)} %copy.11.length, f32[136,512]{1,0:T(8,128)S(1)} %copy-done, bf16[14,56,128]{2,1,0:T(8,128)(2,1)S(1)} %collective-permute-done.6.own), custom_call_target="tpu_custom_call" | custom-call | bytes 479236 | tf_op jit(solution)/shard_map/last_left/pallas_call | solution.py:232
  26.8 0.0 collective-permute-done.9.given
  26.8 0.7 %collective-permute-done.8.other = bf16[14,16,128]{2,1,0:T(8,128)(2,1)S(1)} collective-permute-done((bf16[14,16,128]{2,1,0:T(8,128)(2,1)S(1)}, bf16[14,16,128]{2,1,0:T(8,128)(2,1)S(1)}, u32[]{:S(2)}, u32[]{:S(2)}) %collective-permute-start.8) | collective-permute-done | bytes 57376 | tf_op jit(solution)/shard_map/ppermute | solution.py:288
  27.5 1.6 %finish.1 = bf16[14,56,128]{2,1,0:T(8,128)(2,1)} custom-call(f32[14,56,128]{2,1,0:T(8,128)S(1)} %last_left.1.left, bf16[14,16,128]{2,1,0:T(8,128)(2,1)S(1)} %last_right.1.right, bf16[14,16,128]{2,1,0:T(8,128)(2,1)S(1)} %collective-permute-done.8.other, f32[14,56,128]{2,1,0:T(8,128)S(1)} %get-tuple-element.44.mine, ...), custom_call_target="tpu_custom_call" | custom-call | flops 22478848 | bytes 1552896 | tf_op jit(solution)/shard_map/finish/pallas_call | solution.py:232
  (7 shorter events, 0.0 us)
Async XLA Ops:
  0.0 6.6 %collective-permute-start.1 = (bf16[14,56,128]{2,1,0:T(8,128)(2,1)}, bf16[14,56,128]{2,1,0:T(8,128)(2,1)S(1)}, u32[]{:S(2)}, u32[]{:S(2)}) collective-permute-start(bf16[14,56,128]{2,1,0:T(8,128)(2,1)} %bitcast.4), channel_id=1, source_target_pairs={{0,8},{8,0},{1,9},{9,1},{2,10},{10,2},{3,11},{11,3},{4,12},{12,4},... | collective-permute-start | bytes 602120 | tf_op jit(solution)/shard_map/ppermute | solution.py:288
  0.5 8.2 %collective-permute-start = (bf16[14,56,128]{2,1,0:T(8,128)(2,1)}, bf16[14,56,128]{2,1,0:T(8,128)(2,1)S(1)}, u32[]{:S(2)}, u32[]{:S(2)}) collective-permute-start(bf16[14,56,128]{2,1,0:T(8,128)(2,1)} %bitcast.5), channel_id=1, source_target_pairs={{0,2},{2,4},{4,6},{6,7},{7,5},{5,3},{3,1},{1,0},{8,9},{10,8},{12,1... | collective-permute-start | bytes 602120 | tf_op jit(solution)/shard_map/ppermute | solution.py:285
  3.0 7.1 %collective-permute-start.3 = (bf16[14,56,128]{2,1,0:T(8,128)(2,1)}, bf16[14,56,128]{2,1,0:T(8,128)(2,1)S(1)}, u32[]{:S(2)}, u32[]{:S(2)}) collective-permute-start(bf16[14,56,128]{2,1,0:T(8,128)(2,1)} %bitcast.6), channel_id=1, source_target_pairs={{0,9},{2,8},{4,10},{6,12},{7,14},{5,15},{3,13},{1,11},{8,2},{10,4}... | collective-permute-start | bytes 602120 | tf_op jit(solution)/shard_map/ppermute | solution.py:285
  5.0 1.6 %copy-start.1 = (bf16[56,14,128]{2,0,1:T(8,128)(2,1)S(1)}, bf16[56,14,128]{2,0,1:T(8,128)(2,1)}, u32[]{:S(2)}) copy-start(bf16[56,14,128]{2,0,1:T(8,128)(2,1)} %param.10) | copy-start | bytes 602116
  6.6 1.0 %copy-start = (f32[136,512]{1,0:T(8,128)S(1)}, f32[136,512]{1,0:T(8,128)}, u32[]{:S(2)}) copy-start(f32[136,512]{1,0:T(8,128)} %join.1.shared) | copy-start | bytes 835588
  7.6 4.1 %copy-start.2 = (bf16[128,128]{1,0:T(8,128)(2,1)S(1)}, bf16[128,128]{1,0:T(8,128)(2,1)}, u32[]{:S(2)}) copy-start(bf16[128,128]{1,0:T(8,128)(2,1)} %out_gate.1) | copy-start | bytes 98308
  7.6 4.1 %copy-start.3 = (bf16[128,128]{1,0:T(8,128)(2,1)S(1)}, bf16[128,128]{1,0:T(8,128)(2,1)}, u32[]{:S(2)}) copy-start(bf16[128,128]{1,0:T(8,128)(2,1)} %last_weight.1) | copy-start | bytes 98308
  8.6 3.1 %copy-start.4 = (f32[128]{0:T(128)S(1)}, f32[128]{0:T(128)}, u32[]{:S(2)}) copy-start(f32[128]{0:T(128)} %param.18) | copy-start | bytes 1540
  8.6 5.8 %collective-permute-start.2 = (bf16[14,56,128]{2,1,0:T(8,128)(2,1)S(1)}, bf16[14,56,128]{2,1,0:T(8,128)(2,1)S(1)}, u32[]{:S(2)}, u32[]{:S(2)}) collective-permute-start(bf16[14,56,128]{2,1,0:T(8,128)(2,1)S(1)} %collective-permute-done.own), channel_id=1, source_target_pairs={{0,2},{2,4},{4,6},{6,7},{7,5},{5,3},{3,1},{1,0},{8,9},{10,8},{12,1... | collective-permute-start | bytes 602120 | tf_op jit(solution)/shard_map/ppermute | solution.py:285
  10.1 6.4 %collective-permute-start.5 = (bf16[14,56,128]{2,1,0:T(8,128)(2,1)S(1)}, bf16[14,56,128]{2,1,0:T(8,128)(2,1)S(1)}, u32[]{:S(2)}, u32[]{:S(2)}) collective-permute-start(bf16[14,56,128]{2,1,0:T(8,128)(2,1)S(1)} %collective-permute-done.3.other), channel_id=1, source_target_pairs={{0,2},{2,4},{4,6},{6,7},{7,5},{5,3},{3,1},{1,0},{8,9},{10,8},{12,1... | collective-permute-start | bytes 602120 | tf_op jit(solution)/shard_map/ppermute | solution.py:285
  14.4 5.7 %collective-permute-start.4 = (bf16[14,56,128]{2,1,0:T(8,128)(2,1)S(1)}, bf16[14,56,128]{2,1,0:T(8,128)(2,1)S(1)}, u32[]{:S(2)}, u32[]{:S(2)}) collective-permute-start(bf16[14,56,128]{2,1,0:T(8,128)(2,1)S(1)} %collective-permute-done.2.own), channel_id=1, source_target_pairs={{0,2},{2,4},{4,6},{6,7},{7,5},{5,3},{3,1},{1,0},{8,9},{10,8},{12,1... | collective-permute-start | bytes 602120 | tf_op jit(solution)/shard_map/ppermute | solution.py:285
  16.5 5.7 %collective-permute-start.7 = (bf16[14,56,128]{2,1,0:T(8,128)(2,1)S(1)}, bf16[14,56,128]{2,1,0:T(8,128)(2,1)S(1)}, u32[]{:S(2)}, u32[]{:S(2)}) collective-permute-start(bf16[14,56,128]{2,1,0:T(8,128)(2,1)S(1)} %collective-permute-done.5.other), channel_id=1, source_target_pairs={{0,2},{2,4},{4,6},{6,7},{7,5},{5,3},{3,1},{1,0},{8,9},{10,8},{12,1... | collective-permute-start | bytes 602120 | tf_op jit(solution)/shard_map/ppermute | solution.py:285
  20.1 5.7 %collective-permute-start.6 = (bf16[14,56,128]{2,1,0:T(8,128)(2,1)S(1)}, bf16[14,56,128]{2,1,0:T(8,128)(2,1)S(1)}, u32[]{:S(2)}, u32[]{:S(2)}) collective-permute-start(bf16[14,56,128]{2,1,0:T(8,128)(2,1)S(1)} %collective-permute-done.4.own), channel_id=1, source_target_pairs={{0,2},{2,4},{4,6},{6,7},{7,5},{5,3},{3,1},{1,0},{8,9},{10,8},{12,1... | collective-permute-start | bytes 602120 | tf_op jit(solution)/shard_map/ppermute | solution.py:285
  24.0 2.7 %collective-permute-start.9 = (bf16[14,56,128]{2,1,0:T(8,128)(2,1)S(1)}, bf16[14,56,128]{2,1,0:T(8,128)(2,1)S(1)}, u32[]{:S(2)}, u32[]{:S(2)}) collective-permute-start(bf16[14,56,128]{2,1,0:T(8,128)(2,1)S(1)} %get-tuple-element.45), channel_id=1, source_target_pairs={{0,8},{8,0},{1,9},{9,1},{2,10},{10,2},{3,11},{11,3},{4,12},{12,4},... | collective-permute-start | bytes 602120 | tf_op jit(solution)/shard_map/ppermute | solution.py:288
  26.2 1.3 %collective-permute-start.8 = (bf16[14,16,128]{2,1,0:T(8,128)(2,1)S(1)}, bf16[14,16,128]{2,1,0:T(8,128)(2,1)S(1)}, u32[]{:S(2)}, u32[]{:S(2)}) collective-permute-start(bf16[14,16,128]{2,1,0:T(8,128)(2,1)S(1)} %last_right.1.right), channel_id=1, source_target_pairs={{0,8},{8,0},{1,9},{9,1},{2,10},{10,2},{3,11},{11,3},{4,12},{12,4},... | collective-permute-start | bytes 172040 | tf_op jit(solution)/shard_map/ppermute | solution.py:288

commit v19 on v16

--- a/solution.py
+++ b/solution.py
@@ -171,16 +171,15 @@
     row, col = lax.axis_index("row"), lax.axis_index("col")
     shared = Shared(s, length, shared)
     depth = left.shape[0]
-    base = row * s.half if distance == 0 else 0
-    token = column_from(s, distance) * s.width + base
+    token = column_from(s, distance) * s.width
     choose(row == owner_of(s, col), own, other, picked.at[:, : s.height])
 
     def rows_of(at):
         return picked[at, pl.ds(offset_in(s, col), s.slots), :]
 
-    project_right(s, rows_of, base, depth, token, shared, partner)
-    project_left(s, own, row, base, depth, token, shared, left)
-    project_left(s, other, 1 - row, base, depth, token, shared, right)
+    project_right(s, rows_of, 0, depth, token, shared, partner)
+    project_left(s, own, row, 0, depth, token, shared, left)
+    project_left(s, other, 1 - row, 0, depth, token, shared, right)
     old_mine, old_theirs = before if before else (None, None)
     accumulate(s, left, partner, old_mine, mine)
     if not narrow:
@@ -190,11 +189,11 @@
         theirs[...] = picked[:, : s.height].astype(BF16)
 
 
-def last_right(s, length, shared, own, right, picked, partner):
+def own_right(s, distance, length, shared, own, right, picked, partner):
     shared = Shared(s, length, shared)
     picked[:, : s.height] = own[...].astype(F32)
     offset = offset_in(s, lax.axis_index("col"))
-    token = column_from(s, s.cols // 2) * s.width
+    token = column_from(s, distance) * s.width
 
     def rows_of(at):
         return picked[at, pl.ds(offset, s.slots), :]
@@ -203,10 +202,15 @@
     right[...] = partner[...].astype(BF16)
 
 
-def last_left(s, length, shared, own, left):
+def own_left(s, distance, length, shared, own, left):
     shared = Shared(s, length, shared)
-    token = column_from(s, s.cols // 2) * s.width
+    token = column_from(s, distance) * s.width
     project_left(s, own, lax.axis_index("row"), 0, s.width, token, shared, left)
+
+
+def add_own(s, left, right, other, before, mine, partner):
+    choose(lax.axis_index("row") == owner_of(s, lax.axis_index("col")), right, other, partner)
+    accumulate(s, left, partner, before, mine)
 
 
 def finish(s, left, right, other, mine, given, gating, last_gain, last_weight, *refs):
@@ -290,18 +294,15 @@
     sums = shape((width, height, hidden), F32)
     product = 16 * height * width * hidden
     tokens = pltpu.VMEM((width, height, hidden), F32)
-    halved = pltpu.VMEM((s.half, height, hidden), F32)
     padded = pltpu.VMEM((width, height + TILE, channels), F32)
     partner = pltpu.VMEM((width, s.slots, hidden), F32)
-    few = pltpu.VMEM((s.half, s.slots, hidden), F32)
 
     def add(distance, own, other, before, narrow=False):
-        left, right = (halved, few) if distance == 0 else (tokens, partner)
         return call(
             functools.partial(add_both, s, distance, narrow),
             [sums, shape(sums.shape, BF16) if narrow else sums],
-            [left, left, padded, right],
-            2 * left.shape[0] * product,
+            [tokens, tokens, padded, partner],
+            2 * width * product,
             *shared,
             own,
             other,
@@ -313,14 +314,24 @@
         return lax.optimization_barrier((other, own))[0], own
 
     far = s.cols // 2
+    def right_of(distance, block):
+        out = shape((width, s.slots, hidden), BF16)
+        body = functools.partial(own_right, s, distance)
+        return call(body, out, [padded, partner], 0, *shared, block)
+
+    def left_of(distance, block):
+        return call(functools.partial(own_left, s, distance), sums, [], 0, *shared, block)
+
     other = shift(pair, crossed=True)
     own = shift(pair)
-    total = add(0, pair, swap(pair), ())
-    other, own = in_turn(other, own, total)
+    right = right_of(0, pair)
+    swapped = swap(right)
+    other, own = in_turn(other, own, right)
+    total = ()
     for distance in range(1, far - 1):
         ahead = [shift(other), shift(own)]
-        total = add(distance, own, other, total)
         if distance == 1:
+            left = left_of(0, pair)
             gating = call(
                 functools.partial(gate, s),
                 [sums, shape((1, hidden), F32), shape(out_weight.shape, BF16)],
@@ -332,21 +343,27 @@
                 output_gain.reshape(1, hidden),
                 out_weight,
             )
+        elif distance == 2:
+            mine = call(
+                functools.partial(add_own, s),
+                sums,
+                [partner],
+                width * product,
+                left,
+                right,
+                swapped,
+                lax.optimization_barrier((total[0], own))[0],
+            )
+            total = mine, total[1]
+        total = add(distance, own, other, total)
         other, own = in_turn(*ahead, (total, gating))
     last = shift(own)
     mine, theirs = add(far - 1, own, other, total, narrow=True)
     given = swap(theirs)
     last, mine, gating = lax.optimization_barrier((last, mine, gating))
-    right = call(
-        functools.partial(last_right, s),
-        shape((width, s.slots, hidden), BF16),
-        [padded, partner],
-        0,
-        *shared,
-        last,
-    )
+    right = right_of(far, last)
     swapped = swap(right)
-    left = call(functools.partial(last_left, s), sums, [], 0, *shared, last)
+    left = left_of(far, last)
     update = call(
         functools.partial(finish, s),
         shape((width, height, channels), BF16),

time: 29.3 us -> 30.7 us (1.048)
  waiting for transfers between devices: 4.68 us -> 5.99 us
    ppermute x3, waiting for transfers between devices: 0.73 us -> 1.46 us  [swap(): lax.ppermute(block, 'row', [(at, (at + 1) % s.rows) for at in range(s.row...]
    ppermute x7, waiting for transfers between devices: 3.94 us -> 4.53 us  [shift(): return lax.ppermute(block, ('row', 'col'), pairs)]
    ppermute x3, starting transfers between devices: 0.59 us -> 0.14 us  [swap(): lax.ppermute(block, 'row', [(at, (at + 1) % s.rows) for at in range(s.row...]
    pallas_call x9 -> x11, Pallas kernels: 10.9 us -> 11.2 us  [call(): pl.pallas_call(body, out_shape=out_shape, in_specs=[space(o) for o in ope...]
    unnamed x10 -> x12, local copies, waits for them, and re-layouts: 0.97 us -> 0.98 us
  transfers between devices with their start and end apart: 10 -> 10, of which waited for: 6 -> 6; matrix products, arithmetic and copies ran while one was open for 0% -> 0% of each run, Pallas kernels for 32% -> 31%
where the time goes in v19:
time: 30.7 us; the launch traced here: 30.6 us
  starting transfers between devices  11.6 us (38%)
  Pallas kernels  11.2 us (36%)
  waiting for transfers between devices  5.99 us (20%)
  local copies, waits for them, and re-layouts  0.98 us (3%)
  between operations  0.79 us (3%)
    ppermute x7, starting transfers between devices, shift(): return lax.ppermute(block, ('row', 'col'), pairs)  11.5 us
    pallas_call x11, Pallas kernels, call(): pl.pallas_call(body, out_shape=out_shape, in_specs=[space(o) for o in ope...  11.2 us
    ppermute x7, waiting for transfers between devices, shift(): return lax.ppermute(block, ('row', 'col'), pairs)  4.53 us
    ppermute x3, waiting for transfers between devices, swap(): lax.ppermute(block, 'row', [(at, (at + 1) % s.rows) for at in range(s.row...  1.46 us
    unnamed x12, local copies, waits for them, and re-layouts  0.98 us
  transfers between devices with their start and end apart: 10, of which 6 were waited for; matrix products, arithmetic and copies ran while one was open for 0% of the time, Pallas kernels for 31%

profile of v19, /device:TPU:0, one launch (start us, length us, event | category | flops | bytes accessed | tf_op | source)
XLA Modules:
  0.0 30.6 jit_solution(8070418368336539)
XLA Ops:
  0.0 3.0 %collective-permute-start = (bf16[14,56,128]{2,1,0:T(8,128)(2,1)}, bf16[14,56,128]{2,1,0:T(8,128)(2,1)S(1)}, u32[]{:S(2)}, u32[]{:S(2)}) collective-permute-start(bf16[14,56,128]{2,1,0:T(8,128)(2,1)} %bitcast.4), channel_id=1, source_target_pairs={{0,2},{2,4},{4,6},{6,7},{7,5},{5,3},{3,1},{1,0},{8,9},{10,8},{12,1... | collective-permute-start | bytes 602120 | tf_op jit(solution)/shard_map/ppermute | solution.py:289
  3.0 0.7 %collective-permute-start.2 = (bf16[14,56,128]{2,1,0:T(8,128)(2,1)}, bf16[14,56,128]{2,1,0:T(8,128)(2,1)S(1)}, u32[]{:S(2)}, u32[]{:S(2)}) collective-permute-start(bf16[14,56,128]{2,1,0:T(8,128)(2,1)} %bitcast.5), channel_id=1, source_target_pairs={{0,9},{2,8},{4,10},{6,12},{7,14},{5,15},{3,13},{1,11},{8,2},{10,4}... | collective-permute-start | bytes 602120 | tf_op jit(solution)/shard_map/ppermute | solution.py:289
  4.4 1.6 %join.1.shared = f32[136,512]{1,0:T(8,128)} custom-call(f32[1,128]{1,0:T(1,128)} %bitcast.10, bf16[128,128]{1,0:T(8,128)(2,1)} %left_gate.1, bf16[128,128]{1,0:T(8,128)(2,1)} %left_value.1, bf16[128,128]{1,0:T(8,128)(2,1)} %right_gate.1, bf16[128,128]{1,0:T(8,128)(2,1)} %right_value.1), custom_call_target="tpu_custom_call" | custom-call | bytes 131584 | tf_op jit(solution)/shard_map/join/pallas_call | solution.py:236
  6.0 1.0 %copy-done = f32[136,512]{1,0:T(8,128)S(1)} copy-done((f32[136,512]{1,0:T(8,128)S(1)}, f32[136,512]{1,0:T(8,128)}, u32[]{:S(2)}) %copy-start) | copy-done | bytes 278552
  6.9 0.4 %own_right.2.right = bf16[14,16,128]{2,1,0:T(8,128)(2,1)S(1)} custom-call(s32[1]{0:T(128)S(6)} %copy.11.length, f32[136,512]{1,0:T(8,128)S(1)} %copy-done, bf16[14,56,128]{2,1,0:T(8,128)(2,1)S(1)} %bitcast.6), custom_call_target="tpu_custom_call" | custom-call | bytes 479236 | tf_op jit(solution)/shard_map/own_right/pallas_call | solution.py:236
  7.3 0.0 copy-start.5
  7.3 0.4 %collective-permute-done.own = bf16[14,56,128]{2,1,0:T(8,128)(2,1)S(1)} collective-permute-done((bf16[14,56,128]{2,1,0:T(8,128)(2,1)}, bf16[14,56,128]{2,1,0:T(8,128)(2,1)S(1)}, u32[]{:S(2)}, u32[]{:S(2)}) %collective-permute-start) | collective-permute-done | bytes 200736 | tf_op jit(solution)/shard_map/ppermute | solution.py:289
  7.7 2.4 %collective-permute-start.1 = (bf16[14,56,128]{2,1,0:T(8,128)(2,1)S(1)}, bf16[14,56,128]{2,1,0:T(8,128)(2,1)S(1)}, u32[]{:S(2)}, u32[]{:S(2)}) collective-permute-start(bf16[14,56,128]{2,1,0:T(8,128)(2,1)S(1)} %collective-permute-done.own), channel_id=1, source_target_pairs={{0,2},{2,4},{4,6},{6,7},{7,5},{5,3},{3,1},{1,0},{8,9},{10,8},{12,1... | collective-permute-start | bytes 602120 | tf_op jit(solution)/shard_map/ppermute | solution.py:289
  10.1 0.0 collective-permute-done.2.other
  10.1 1.6 %collective-permute-start.4 = (bf16[14,56,128]{2,1,0:T(8,128)(2,1)S(1)}, bf16[14,56,128]{2,1,0:T(8,128)(2,1)S(1)}, u32[]{:S(2)}, u32[]{:S(2)}) collective-permute-start(bf16[14,56,128]{2,1,0:T(8,128)(2,1)S(1)} %collective-permute-done.2.other), channel_id=1, source_target_pairs={{0,2},{2,4},{4,6},{6,7},{7,5},{5,3},{3,1},{1,0},{8,9},{10,8},{12,1... | collective-permute-start | bytes 602120 | tf_op jit(solution)/shard_map/ppermute | solution.py:289
  11.7 0.5 %gate.1 = (f32[14,56,128]{2,1,0:T(8,128)S(1)}, f32[1,128]{1,0:T(1,128)S(1)}, bf16[128,128]{1,0:T(8,128)(2,1)S(1)}) custom-call(s32[1]{0:T(128)S(6)} %copy.11.length, f32[136,512]{1,0:T(8,128)S(1)} %copy-done, bf16[14,56,128]{2,1,0:T(8,128)(2,1)S(1)} %bitcast.7, bf16[128,128]{1,0:T(8,128)(2,1)S(1)} %copy-done.3, f32[1,128]{1,0:T(1,128)S(1)} %bitcast.9, ...), custom_call_target="tpu_custom_call" | custom-call | flops 25690112 | bytes 545284 | tf_op jit(solution)/shard_map/gate/pallas_call | solution.py:236
  12.2 1.8 %add_both.3 = (f32[14,56,128]{2,1,0:T(8,128)S(1)}, f32[14,56,128]{2,1,0:T(8,128)S(1)}) custom-call(s32[1]{0:T(128)S(6)} %copy.11.length, f32[136,512]{1,0:T(8,128)S(1)} %copy-done, bf16[14,56,128]{2,1,0:T(8,128)(2,1)S(1)} %collective-permute-done.own, bf16[14,56,128]{2,1,0:T(8,128)(2,1)S(1)} %collective-permute-done.2.other), custom_call_target="tpu_custom_call" | custom-call | flops 44957696 | bytes 679940 | tf_op jit(solution)/shard_map/add_both/pallas_call | solution.py:236
  13.9 0.8 %collective-permute-done.1.own = bf16[14,56,128]{2,1,0:T(8,128)(2,1)S(1)} collective-permute-done((bf16[14,56,128]{2,1,0:T(8,128)(2,1)S(1)}, bf16[14,56,128]{2,1,0:T(8,128)(2,1)S(1)}, u32[]{:S(2)}, u32[]{:S(2)}) %collective-permute-start.1) | collective-permute-done | bytes 200736 | tf_op jit(solution)/shard_map/ppermute | solution.py:289
  14.7 1.1 %collective-permute-start.3 = (bf16[14,56,128]{2,1,0:T(8,128)(2,1)S(1)}, bf16[14,56,128]{2,1,0:T(8,128)(2,1)S(1)}, u32[]{:S(2)}, u32[]{:S(2)}) collective-permute-start(bf16[14,56,128]{2,1,0:T(8,128)(2,1)S(1)} %collective-permute-done.1.own), channel_id=1, source_target_pairs={{0,2},{2,4},{4,6},{6,7},{7,5},{5,3},{3,1},{1,0},{8,9},{10,8},{12,1... | collective-permute-start | bytes 602120 | tf_op jit(solution)/shard_map/ppermute | solution.py:289
  15.8 1.0 %collective-permute-done.4.other = bf16[14,56,128]{2,1,0:T(8,128)(2,1)S(1)} collective-permute-done((bf16[14,56,128]{2,1,0:T(8,128)(2,1)S(1)}, bf16[14,56,128]{2,1,0:T(8,128)(2,1)S(1)}, u32[]{:S(2)}, u32[]{:S(2)}) %collective-permute-start.4) | collective-permute-done | bytes 200736 | tf_op jit(solution)/shard_map/ppermute | solution.py:289
  16.9 1.1 %collective-permute-start.7 = (bf16[14,56,128]{2,1,0:T(8,128)(2,1)S(1)}, bf16[14,56,128]{2,1,0:T(8,128)(2,1)S(1)}, u32[]{:S(2)}, u32[]{:S(2)}) collective-permute-start(bf16[14,56,128]{2,1,0:T(8,128)(2,1)S(1)} %collective-permute-done.4.other), channel_id=1, source_target_pairs={{0,2},{2,4},{4,6},{6,7},{7,5},{5,3},{3,1},{1,0},{8,9},{10,8},{12,1... | collective-permute-start | bytes 602120 | tf_op jit(solution)/shard_map/ppermute | solution.py:289
  18.0 0.0 collective-permute-start.5
  18.0 0.5 %own_left.2.left = f32[14,56,128]{2,1,0:T(8,128)S(1)} custom-call(s32[1]{0:T(128)S(6)} %copy.11.length, f32[136,512]{1,0:T(8,128)S(1)} %copy-done, bf16[14,56,128]{2,1,0:T(8,128)(2,1)S(1)} %bitcast.8), custom_call_target="tpu_custom_call" | custom-call | bytes 479236 | tf_op jit(solution)/shard_map/own_left/pallas_call | solution.py:236
  18.5 0.7 %collective-permute-done.5.other = bf16[14,16,128]{2,1,0:T(8,128)(2,1)S(1)} collective-permute-done((bf16[14,16,128]{2,1,0:T(8,128)(2,1)S(1)}, bf16[14,16,128]{2,1,0:T(8,128)(2,1)S(1)}, u32[]{:S(2)}, u32[]{:S(2)}) %collective-permute-start.5) | collective-permute-done | bytes 57376 | tf_op jit(solution)/shard_map/ppermute | solution.py:292
  19.2 0.5 %add_own.1.refs_0_ = f32[14,56,128]{2,1,0:T(8,128)S(1)} custom-call(f32[14,56,128]{2,1,0:T(8,128)S(1)} %own_left.2.left, bf16[14,16,128]{2,1,0:T(8,128)(2,1)S(1)} %own_right.2.right, bf16[14,16,128]{2,1,0:T(8,128)(2,1)S(1)} %collective-permute-done.5.other, f32[14,56,128]{2,1,0:T(8,128)S(1)} %get-tuple-element.35.before), custom_call_target="tpu_custom_call" | custom-call | flops 22478848 | bytes 917504 | tf_op jit(solution)/shard_map/add_own/pallas_call | solution.py:236
  19.7 1.8 %add_both.4 = (f32[14,56,128]{2,1,0:T(8,128)S(1)}, f32[14,56,128]{2,1,0:T(8,128)S(1)}) custom-call(s32[1]{0:T(128)S(6)} %copy.11.length, f32[136,512]{1,0:T(8,128)S(1)} %copy-done.1, bf16[14,56,128]{2,1,0:T(8,128)(2,1)S(1)} %collective-permute-done.1.own, bf16[14,56,128]{2,1,0:T(8,128)(2,1)S(1)} %collective-permute-done.4.other, ...), custom_call_target="tpu_custom_call" | custom-call | flops 44957696 | bytes 1482756 | tf_op jit(solution)/shard_map/add_both/pallas_call | solution.py:236
  21.5 0.0 collective-permute-done.3.own
  21.5 1.6 %collective-permute-start.6 = (bf16[14,56,128]{2,1,0:T(8,128)(2,1)S(1)}, bf16[14,56,128]{2,1,0:T(8,128)(2,1)S(1)}, u32[]{:S(2)}, u32[]{:S(2)}) collective-permute-start(bf16[14,56,128]{2,1,0:T(8,128)(2,1)S(1)} %collective-permute-done.3.own), channel_id=1, source_target_pairs={{0,2},{2,4},{4,6},{6,7},{7,5},{5,3},{3,1},{1,0},{8,9},{10,8},{12,1... | collective-permute-start | bytes 602120 | tf_op jit(solution)/shard_map/ppermute | solution.py:289
  23.1 0.0 collective-permute-done.7.other
  23.1 1.8 %add_both.5 = (f32[14,56,128]{2,1,0:T(8,128)S(1)}, bf16[14,56,128]{2,1,0:T(8,128)(2,1)S(1)}) custom-call(s32[1]{0:T(128)S(6)} %copy.11.length, f32[136,512]{1,0:T(8,128)S(1)} %copy-done.1, bf16[14,56,128]{2,1,0:T(8,128)(2,1)S(1)} %collective-permute-done.3.own, bf16[14,56,128]{2,1,0:T(8,128)(2,1)S(1)} %collective-permute-done.7.other, ...), custom_call_target="tpu_custom_call" | custom-call | flops 44957696 | bytes 1482756 | tf_op jit(solution)/shard_map/add_both/pallas_call | solution.py:236
  24.9 0.1 collective-permute-start.9
  25.0 2.3 %collective-permute-done.6.own = bf16[14,56,128]{2,1,0:T(8,128)(2,1)S(1)} collective-permute-done((bf16[14,56,128]{2,1,0:T(8,128)(2,1)S(1)}, bf16[14,56,128]{2,1,0:T(8,128)(2,1)S(1)}, u32[]{:S(2)}, u32[]{:S(2)}) %collective-permute-start.6) | collective-permute-done | bytes 200736 | tf_op jit(solution)/shard_map/ppermute | solution.py:289
  27.3 0.4 %own_right.3.right = bf16[14,16,128]{2,1,0:T(8,128)(2,1)S(1)} custom-call(s32[1]{0:T(128)S(6)} %copy.11.length, f32[136,512]{1,0:T(8,128)S(1)} %copy-done.1, bf16[14,56,128]{2,1,0:T(8,128)(2,1)S(1)} %collective-permute-done.6.own), custom_call_target="tpu_custom_call" | custom-call | bytes 479236 | tf_op jit(solution)/shard_map/own_right/pallas_call | solution.py:236
  27.6 0.1 collective-permute-start.8
  27.7 0.5 %own_left.3.left = f32[14,56,128]{2,1,0:T(8,128)S(1)} custom-call(s32[1]{0:T(128)S(6)} %copy.11.length, f32[136,512]{1,0:T(8,128)S(1)} %copy-done.1, bf16[14,56,128]{2,1,0:T(8,128)(2,1)S(1)} %collective-permute-done.6.own), custom_call_target="tpu_custom_call" | custom-call | bytes 479236 | tf_op jit(solution)/shard_map/own_left/pallas_call | solution.py:236
  28.2 0.7 %collective-permute-done.8.other = bf16[14,16,128]{2,1,0:T(8,128)(2,1)S(1)} collective-permute-done((bf16[14,16,128]{2,1,0:T(8,128)(2,1)S(1)}, bf16[14,16,128]{2,1,0:T(8,128)(2,1)S(1)}, u32[]{:S(2)}, u32[]{:S(2)}) %collective-permute-start.8) | collective-permute-done | bytes 57376 | tf_op jit(solution)/shard_map/ppermute | solution.py:292
  28.9 1.6 %finish.1 = bf16[14,56,128]{2,1,0:T(8,128)(2,1)} custom-call(f32[14,56,128]{2,1,0:T(8,128)S(1)} %own_left.3.left, bf16[14,16,128]{2,1,0:T(8,128)(2,1)S(1)} %own_right.3.right, bf16[14,16,128]{2,1,0:T(8,128)(2,1)S(1)} %collective-permute-done.8.other, f32[14,56,128]{2,1,0:T(8,128)S(1)} %get-tuple-element.42.mine, ...), custom_call_target="tpu_custom_call" | custom-call | flops 22478848 | bytes 1552896 | tf_op jit(solution)/shard_map/finish/pallas_call | solution.py:236
  (11 shorter events, 0.0 us)
Async XLA Ops:
  0.0 7.7 %collective-permute-start = (bf16[14,56,128]{2,1,0:T(8,128)(2,1)}, bf16[14,56,128]{2,1,0:T(8,128)(2,1)S(1)}, u32[]{:S(2)}, u32[]{:S(2)}) collective-permute-start(bf16[14,56,128]{2,1,0:T(8,128)(2,1)} %bitcast.4), channel_id=1, source_target_pairs={{0,2},{2,4},{4,6},{6,7},{7,5},{5,3},{3,1},{1,0},{8,9},{10,8},{12,1... | collective-permute-start | bytes 602120 | tf_op jit(solution)/shard_map/ppermute | solution.py:289
  3.0 7.1 %collective-permute-start.2 = (bf16[14,56,128]{2,1,0:T(8,128)(2,1)}, bf16[14,56,128]{2,1,0:T(8,128)(2,1)S(1)}, u32[]{:S(2)}, u32[]{:S(2)}) collective-permute-start(bf16[14,56,128]{2,1,0:T(8,128)(2,1)} %bitcast.5), channel_id=1, source_target_pairs={{0,9},{2,8},{4,10},{6,12},{7,14},{5,15},{3,13},{1,11},{8,2},{10,4}... | collective-permute-start | bytes 602120 | tf_op jit(solution)/shard_map/ppermute | solution.py:289
  4.4 1.6 %copy-start.2 = (bf16[56,14,128]{2,0,1:T(8,128)(2,1)S(1)}, bf16[56,14,128]{2,0,1:T(8,128)(2,1)}, u32[]{:S(2)}) copy-start(bf16[56,14,128]{2,0,1:T(8,128)(2,1)} %param.10) | copy-start | bytes 602116
  6.0 1.0 %copy-start = (f32[136,512]{1,0:T(8,128)S(1)}, f32[136,512]{1,0:T(8,128)}, u32[]{:S(2)}) copy-start(f32[136,512]{1,0:T(8,128)} %join.1.shared) | copy-start | bytes 835588
  6.9 4.8 %copy-start.3 = (bf16[128,128]{1,0:T(8,128)(2,1)S(1)}, bf16[128,128]{1,0:T(8,128)(2,1)}, u32[]{:S(2)}) copy-start(bf16[128,128]{1,0:T(8,128)(2,1)} %out_gate.1) | copy-start | bytes 98308
  6.9 4.8 %copy-start.4 = (bf16[128,128]{1,0:T(8,128)(2,1)S(1)}, bf16[128,128]{1,0:T(8,128)(2,1)}, u32[]{:S(2)}) copy-start(bf16[128,128]{1,0:T(8,128)(2,1)} %last_weight.1) | copy-start | bytes 98308
  7.3 4.4 %copy-start.5 = (f32[128]{0:T(128)S(1)}, f32[128]{0:T(128)}, u32[]{:S(2)}) copy-start(f32[128]{0:T(128)} %param.18) | copy-start | bytes 1540
  7.7 7.0 %collective-permute-start.1 = (bf16[14,56,128]{2,1,0:T(8,128)(2,1)S(1)}, bf16[14,56,128]{2,1,0:T(8,128)(2,1)S(1)}, u32[]{:S(2)}, u32[]{:S(2)}) collective-permute-start(bf16[14,56,128]{2,1,0:T(8,128)(2,1)S(1)} %collective-permute-done.own), channel_id=1, source_target_pairs={{0,2},{2,4},{4,6},{6,7},{7,5},{5,3},{3,1},{1,0},{8,9},{10,8},{12,1... | collective-permute-start | bytes 602120 | tf_op jit(solution)/shard_map/ppermute | solution.py:289
  10.1 6.8 %collective-permute-start.4 = (bf16[14,56,128]{2,1,0:T(8,128)(2,1)S(1)}, bf16[14,56,128]{2,1,0:T(8,128)(2,1)S(1)}, u32[]{:S(2)}, u32[]{:S(2)}) collective-permute-start(bf16[14,56,128]{2,1,0:T(8,128)(2,1)S(1)} %collective-permute-done.2.other), channel_id=1, source_target_pairs={{0,2},{2,4},{4,6},{6,7},{7,5},{5,3},{3,1},{1,0},{8,9},{10,8},{12,1... | collective-permute-start | bytes 602120 | tf_op jit(solution)/shard_map/ppermute | solution.py:289
  14.7 6.8 %collective-permute-start.3 = (bf16[14,56,128]{2,1,0:T(8,128)(2,1)S(1)}, bf16[14,56,128]{2,1,0:T(8,128)(2,1)S(1)}, u32[]{:S(2)}, u32[]{:S(2)}) collective-permute-start(bf16[14,56,128]{2,1,0:T(8,128)(2,1)S(1)} %collective-permute-done.1.own), channel_id=1, source_target_pairs={{0,2},{2,4},{4,6},{6,7},{7,5},{5,3},{3,1},{1,0},{8,9},{10,8},{12,1... | collective-permute-start | bytes 602120 | tf_op jit(solution)/shard_map/ppermute | solution.py:289
  16.9 6.3 %collective-permute-start.7 = (bf16[14,56,128]{2,1,0:T(8,128)(2,1)S(1)}, bf16[14,56,128]{2,1,0:T(8,128)(2,1)S(1)}, u32[]{:S(2)}, u32[]{:S(2)}) collective-permute-start(bf16[14,56,128]{2,1,0:T(8,128)(2,1)S(1)} %collective-permute-done.4.other), channel_id=1, source_target_pairs={{0,2},{2,4},{4,6},{6,7},{7,5},{5,3},{3,1},{1,0},{8,9},{10,8},{12,1... | collective-permute-start | bytes 602120 | tf_op jit(solution)/shard_map/ppermute | solution.py:289
  18.0 1.2 %collective-permute-start.5 = (bf16[14,16,128]{2,1,0:T(8,128)(2,1)S(1)}, bf16[14,16,128]{2,1,0:T(8,128)(2,1)S(1)}, u32[]{:S(2)}, u32[]{:S(2)}) collective-permute-start(bf16[14,16,128]{2,1,0:T(8,128)(2,1)S(1)} %own_right.2.right), channel_id=1, source_target_pairs={{0,8},{8,0},{1,9},{9,1},{2,10},{10,2},{3,11},{11,3},{4,12},{12,4},... | collective-permute-start | bytes 172040 | tf_op jit(solution)/shard_map/ppermute | solution.py:292
  18.5 1.2 %copy-start.1 = (f32[136,512]{1,0:T(8,128)S(1)}, f32[136,512]{1,0:T(8,128)}, u32[]{:S(2)}) copy-start(f32[136,512]{1,0:T(8,128)} %join.1.shared) | copy-start | bytes 835588
  21.5 5.8 %collective-permute-start.6 = (bf16[14,56,128]{2,1,0:T(8,128)(2,1)S(1)}, bf16[14,56,128]{2,1,0:T(8,128)(2,1)S(1)}, u32[]{:S(2)}, u32[]{:S(2)}) collective-permute-start(bf16[14,56,128]{2,1,0:T(8,128)(2,1)S(1)} %collective-permute-done.3.own), channel_id=1, source_target_pairs={{0,2},{2,4},{4,6},{6,7},{7,5},{5,3},{3,1},{1,0},{8,9},{10,8},{12,1... | collective-permute-start | bytes 602120 | tf_op jit(solution)/shard_map/ppermute | solution.py:289
  24.9 3.3 %collective-permute-start.9 = (bf16[14,56,128]{2,1,0:T(8,128)(2,1)S(1)}, bf16[14,56,128]{2,1,0:T(8,128)(2,1)S(1)}, u32[]{:S(2)}, u32[]{:S(2)}) collective-permute-start(bf16[14,56,128]{2,1,0:T(8,128)(2,1)S(1)} %get-tuple-element.43), channel_id=1, source_target_pairs={{0,8},{8,0},{1,9},{9,1},{2,10},{10,2},{3,11},{11,3},{4,12},{12,4},... | collective-permute-start | bytes 602120 | tf_op jit(solution)/shard_map/ppermute | solution.py:292
  27.6 1.3 %collective-permute-start.8 = (bf16[14,16,128]{2,1,0:T(8,128)(2,1)S(1)}, bf16[14,16,128]{2,1,0:T(8,128)(2,1)S(1)}, u32[]{:S(2)}, u32[]{:S(2)}) collective-permute-start(bf16[14,16,128]{2,1,0:T(8,128)(2,1)S(1)} %own_right.3.right), channel_id=1, source_target_pairs={{0,8},{8,0},{1,9},{9,1},{2,10},{10,2},{3,11},{11,3},{4,12},{12,4},... | collective-permute-start | bytes 172040 | tf_op jit(solution)/shard_map/ppermute | solution.py:292

commit v20 on v14

v20 whole, which is shorter than its diff:
```python
import functools

import jax
import jax.numpy as jnp
from jax import lax
from jax.experimental import pallas as pl
from jax.experimental.pallas import tpu as pltpu
from jax.sharding import PartitionSpec as P

F32 = jnp.float32
BF16 = jnp.bfloat16
EPS = 1e-05
TILE = 16
CHUNK = 56
GROUP = 7


class Sizes:
    def __init__(self, mesh, height, width, channels, hidden):
        self.rows = mesh.shape["row"]
        self.cols = mesh.shape["col"]
        self.height, self.width = height, width
        self.channels, self.hidden = channels, hidden
        self.half = width // 2
        self.slots = -(-width // TILE) * TILE
        self.both = 2 * width


def normalise(values):
    average = jnp.mean(values, -1, keepdims=True)
    centered = values - average
    variance = jnp.mean(centered * centered, -1, keepdims=True)
    return centered * lax.rsqrt(variance + EPS)


def sigmoid(values):
    return 0.5 * jnp.tanh(0.5 * values) + 0.5


def dot(left, right):
    return jnp.dot(left, right, preferred_element_type=F32)


def gate(s, length, shared, pair, out_gate, last_gain, last_weight, gating, kept_gain, kept_weight):
    gain = Shared(s, length, shared).gain
    kept_gain[...] = last_gain[...]
    kept_weight[...] = last_weight[...]
    for start in range(0, s.width, s.half):
        normed = [
            normalise(pair[start + step].astype(F32)) * gain for step in range(s.half)
        ]
        value = sigmoid(dot(jnp.concatenate(normed, 0).astype(BF16), out_gate[...]))
        for step in range(s.half):
            gating[start + step] = value[step * s.height : (step + 1) * s.height]


def accumulate(s, left, partner, shift, before, total):
    depth = left.shape[0]
    size = CHUNK if s.height % CHUNK == 0 else s.height
    group = GROUP if s.width % GROUP == 0 else 1

    def chunk(index, carry):
        at = pl.ds(pl.multiple_of(index * size, 8), size)
        for first in range(0, s.width, group):
            members = range(first, first + group)
            if before is None:
                sums = tuple(jnp.zeros((size, s.hidden), F32) for _ in members)
            else:
                sums = tuple(before[j, at] for j in members)

            def step(k, sums):
                value = left[k, at]
                return tuple(
                    so_far + value * partner[k, shift + j : shift + j + 1] for so_far, j in zip(sums, members)
                )

            sums = lax.fori_loop(0, depth, step, sums, unroll=s.half)
            for so_far, j in zip(sums, members):
                total[j, at] = so_far
        return carry

    lax.fori_loop(0, s.height // size, chunk, 0)


def split(s):
    col = lax.axis_index("col")
    return col // 2, col % 2


def choose(s, right, other, partner):
    hi, _ = split(s)
    mine = lax.axis_index("row") == hi // (s.height // s.both)

    @pl.when(mine)
    def _():
        partner[...] = right[...].astype(F32)

    @pl.when(jnp.logical_not(mine))
    def _():
        partner[...] = other[...].astype(F32)


class Shared:
    def __init__(self, s, length, ref):
        h = s.hidden
        self.left = ref[: s.channels, : 2 * h].astype(BF16)
        self.right = ref[: s.channels, 2 * h :].astype(BF16)
        self.gain = ref[s.channels : s.channels + 1, : s.channels]
        self.limit = length[0]


def join(s, gain, left_gate, left_value, right_gate, right_value, shared):
    h = s.hidden
    for at, part in enumerate((left_gate, left_value, right_gate, right_value)):
        shared[: s.channels, at * h : (at + 1) * h] = part[...].astype(F32)
    shared[s.channels : s.channels + 1, : s.channels] = gain[...]


def gated(s, rows, gain, weight, masks):
    h, size = s.hidden, rows[0].shape[0]
    rows = [normalise(row) * gain for row in rows]
    out = dot(jnp.concatenate(rows, 0).astype(BF16), weight)
    value = sigmoid(out[:, :h]) * out[:, h:]
    return [value[at * size : (at + 1) * size] * mask for at, mask in enumerate(masks)]


def masks_of(tokens, first, count, limit):
    below = lax.broadcasted_iota(jnp.int32, (count, 1), 0) + first < limit
    return [(below & (token < limit)).astype(F32) for token in tokens]


def project_left(s, block, row, base, depth, token, shared, left):
    first = row * s.height
    for start in range(0, depth, s.half):
        steps = range(start, start + s.half)
        masks = masks_of([token + step for step in steps], first, s.height, shared.limit)
        rows = [block[base + step].astype(F32) for step in steps]
        for step, part in zip(steps, gated(s, rows, shared.gain, shared.left, masks)):
            left[step] = part


def project(s, mask, length, shared, block, left, right, picked):
    hi, lo = split(s)
    shared = Shared(s, length, shared)
    token = ((hi ^ mask) * 2 + lo) * s.width
    project_left(s, block, lax.axis_index("row"), 0, s.width, token, shared, left)
    picked[:, : s.height] = block[...].astype(F32)
    offset = (hi % (s.height // s.both)) * s.both
    for side, which in enumerate((lo, 1 - lo)):
        first = hi * s.both + which * s.width
        place = pl.ds(offset + which * s.width, s.slots)
        for start in range(0, s.width, s.half):
            steps = range(start, start + s.half)
            masks = masks_of([token + step for step in steps], first, s.slots, shared.limit)
            rows = [picked[step, place, :] for step in steps]
            for step, part in zip(steps, gated(s, rows, shared.gain, shared.right, masks)):
                right[step, side * s.slots : (side + 1) * s.slots] = part.astype(BF16)


def add(s, left, right, other, *refs):
    *before, mine, theirs, partner = refs
    choose(s, right, other, partner)
    old_mine, old_theirs = before if before else (None, None)
    accumulate(s, left, partner, 0, old_mine, mine)
    accumulate(s, left, partner, s.slots, old_theirs, theirs)


def add_theirs(s, left, right, other, before, theirs, partner, total):
    choose(s, right, other, partner)
    accumulate(s, left, partner, s.slots, before, total)
    theirs[...] = total[...].astype(BF16)


def add_mine(s, left, right, other, before, mine, partner):
    choose(s, right, other, partner)
    accumulate(s, left, partner, 0, before, mine)


def finish(s, mine, given, gating, last_gain, last_weight, update):
    for start in range(0, s.width, s.half):
        settled = [
            normalise(mine[start + step] + given[start + step].astype(F32)) * last_gain[...]
            for step in range(s.half)
        ]
        value = dot(jnp.concatenate(settled, 0).astype(BF16), last_weight[...])
        for step in range(s.half):
            part = gating[start + step] * value[step * s.height : (step + 1) * s.height]
            update[start + step] = part.astype(BF16)


def call(body, out_shape, scratch, flops, *operands, grant=24):
    def space(operand):
        return pl.BlockSpec(memory_space=pltpu.SMEM if operand.dtype == jnp.int32 else pltpu.VMEM)

    sent = sum(o.size * o.dtype.itemsize for o in operands)
    return pl.pallas_call(
        body,
        out_shape=out_shape,
        in_specs=[space(o) for o in operands],
        out_specs=jax.tree.map(lambda _: pl.BlockSpec(memory_space=pltpu.VMEM), out_shape),
        scratch_shapes=scratch,
        compiler_params=pltpu.CompilerParams(vmem_limit_bytes=grant * 1024 * 1024),
        cost_estimate=pl.CostEstimate(flops=flops, bytes_accessed=sent, transcendentals=0),
        name=body.func.__name__,
    )(*operands)


def local(
    mesh,
    pair_state,
    valid_length,
    input_gain,
    left_gate,
    left_value,
    right_gate,
    right_value,
    out_gate,
    output_gain,
    out_weight,
):
    height, width, channels = pair_state.shape
    hidden = left_gate.shape[1]
    s = Sizes(mesh, height, width, channels, hidden)
    shape = jax.ShapeDtypeStruct
    pair = jnp.transpose(pair_state, (1, 0, 2))
    gain = input_gain.reshape(1, channels)
    shared = call(
        functools.partial(join, s),
        shape((channels + 8, 4 * hidden), F32),
        [],
        0,
        gain,
        left_gate,
        left_value,
        right_gate,
        right_value,
        grant=56,
    )
    shared = (valid_length, shared)
    def xor(block, mask):
        return lax.ppermute(block, "col", [(at, at ^ mask) for at in range(s.cols)])

    def swap(block):
        return lax.ppermute(block, "row", [(at, (at + 1) % s.rows) for at in range(s.rows)])

    sums = shape((width, height, hidden), F32)
    sent = shape(sums.shape, BF16)
    partner = pltpu.VMEM((width, 2 * s.slots, hidden), F32)
    picked = pltpu.VMEM((width, height + TILE, channels), F32)
    product = 16 * width * height * width * hidden

    blocks = [pair] + [xor(pair, 2 * mask) for mask in range(1, s.cols // 2)]
    total, terms = (), None
    for mask, block in enumerate(blocks):
        if total:
            block, total = lax.optimization_barrier((block, total))
        left, right = call(
            functools.partial(project, s, mask),
            [sums, shape((width, 2 * s.slots, hidden), BF16)],
            [picked],
            4 * width * height * channels * hidden,
            *shared,
            block,
        )
        before, terms = terms, (left, right, swap(right))
        if before:
            total = call(
                functools.partial(add, s), [sums, sums], [partner], 2 * product, *before, *total
            )
    theirs = call(
        functools.partial(add_theirs, s),
        sent,
        [partner, pltpu.VMEM(sums.shape, F32)],
        product,
        *terms,
        total[1],
    )
    given = xor(theirs, 1)
    mine = call(functools.partial(add_mine, s), sums, [partner], product, *terms, total[0])
    gating = call(
        functools.partial(gate, s),
        [sums, shape((1, hidden), F32), shape(out_weight.shape, BF16)],
        [],
        2 * height * width * channels * channels,
        *shared,
        pair,
        out_gate,
        output_gain.reshape(1, hidden),
        out_weight,
    )
    update = call(
        functools.partial(finish, s),
        shape((width, height, channels), BF16),
        [],
        2 * height * width * channels * hidden,
        mine,
        given,
        *gating,
    )
    return jnp.transpose(update, (1, 0, 2))


def solution(mesh):
    return jax.shard_map(
        functools.partial(local, mesh),
        mesh=mesh,
        in_specs=(P(("parts", "row"), "col", None), P("parts")) + (P(),) * 8,
        out_specs=P(("parts", "row"), "col", None),
        check_vma=False,
    )
```

time: 30.8 us -> 33.7 us (1.094)
  waiting for transfers between devices: 2.27 us -> 14.2 us
  starting transfers between devices: 15.5 us -> 7.95 us
  Pallas kernels: 10.6 us -> 9.58 us
  local copies, waits for them, and re-layouts: 1.53 us -> 0.98 us
    ppermute x8 -> x4, waiting for transfers between devices: 2.27 us -> 14.1 us  [xor(): return lax.ppermute(block, 'col', [(at, at ^ mask) for at in range(s.cols)])]
    ppermute x8 -> x4, starting transfers between devices: 14.9 us -> 7.21 us  [xor(): return lax.ppermute(block, 'col', [(at, at ^ mask) for at in range(s.cols)])]
    pallas_call x8 -> x12, Pallas kernels: 10.6 us -> 9.58 us  [call(): pl.pallas_call(body, out_shape=out_shape, in_specs=[space(o) for o in ope...]
    unnamed x12, local copies, waits for them, and re-layouts: 1.53 us -> 0.98 us
    ppermute x2 -> x4, starting transfers between devices: 0.52 us -> 0.74 us  [swap(): lax.ppermute(block, 'row', [(at, (at + 1) % s.rows) for at in range(s.row...]
  transfers between devices with their start and end apart: 10 -> 8, of which waited for: 3 -> 3; matrix products, arithmetic and copies ran while one was open for 0% -> 0% of each run, Pallas kernels for 27% -> 24%
where the time goes in v20:
time: 33.7 us; the launch traced here: 33.5 us
  waiting for transfers between devices  14.2 us (42%)
  Pallas kernels  9.58 us (28%)
  starting transfers between devices  7.95 us (24%)
  local copies, waits for them, and re-layouts  0.98 us (3%)
  between operations  0.8 us (2%)
    ppermute x4, waiting for transfers between devices, xor(): return lax.ppermute(block, 'col', [(at, at ^ mask) for at in range(s.cols)])  14.1 us
    pallas_call x12, Pallas kernels, call(): pl.pallas_call(body, out_shape=out_shape, in_specs=[space(o) for o in ope...  9.58 us
    ppermute x4, starting transfers between devices, xor(): return lax.ppermute(block, 'col', [(at, at ^ mask) for at in range(s.cols)])  7.21 us
    unnamed x12, local copies, waits for them, and re-layouts  0.98 us
    ppermute x4, starting transfers between devices, swap(): lax.ppermute(block, 'row', [(at, (at + 1) % s.rows) for at in range(s.row...  0.74 us
  transfers between devices with their start and end apart: 8, of which 3 were waited for; matrix products, arithmetic and copies ran while one was open for 0% of the time, Pallas kernels for 24%

profile of v20, /device:TPU:0, one launch (start us, length us, event | category | flops | bytes accessed | tf_op | source)
XLA Modules:
  0.0 33.5 jit_solution(9013493680235986803)
XLA Ops:
  0.0 3.0 %collective-permute-start.1 = (bf16[14,56,128]{2,1,0:T(8,128)(2,1)}, bf16[14,56,128]{2,1,0:T(8,128)(2,1)S(1)}, u32[]{:S(2)}, u32[]{:S(2)}) collective-permute-start(bf16[14,56,128]{2,1,0:T(8,128)(2,1)} %bitcast.4), channel_id=1, source_target_pairs={{0,2},{1,3},{2,0},{3,1},{4,6},{5,7},{6,4},{7,5},{8,10},{9,11},{10,... | collective-permute-start | bytes 602120 | tf_op jit(solution)/shard_map/ppermute | solution.py:241
  3.0 2.6 %collective-permute-start.3 = (bf16[14,56,128]{2,1,0:T(8,128)(2,1)}, bf16[14,56,128]{2,1,0:T(8,128)(2,1)S(1)}, u32[]{:S(2)}, u32[]{:S(2)}) collective-permute-start(bf16[14,56,128]{2,1,0:T(8,128)(2,1)} %bitcast.5), channel_id=1, source_target_pairs={{0,4},{1,5},{2,6},{3,7},{4,0},{5,1},{6,2},{7,3},{8,12},{9,13},{10,... | collective-permute-start | bytes 602120 | tf_op jit(solution)/shard_map/ppermute | solution.py:241
  5.6 0.0 collective-permute-start
  6.3 0.0 copy-start.2
  6.3 1.6 %join.1.shared = f32[136,512]{1,0:T(8,128)} custom-call(f32[1,128]{1,0:T(1,128)} %bitcast.10, bf16[128,128]{1,0:T(8,128)(2,1)} %left_gate.1, bf16[128,128]{1,0:T(8,128)(2,1)} %left_value.1, bf16[128,128]{1,0:T(8,128)(2,1)} %right_gate.1, bf16[128,128]{1,0:T(8,128)(2,1)} %right_value.1), custom_call_target="tpu_custom_call" | custom-call | bytes 131584 | tf_op jit(solution)/shard_map/join/pallas_call | solution.py:196
  7.9 0.0 copy-done.2
  7.9 1.0 %copy-done = f32[136,512]{1,0:T(8,128)S(1)} copy-done((f32[136,512]{1,0:T(8,128)S(1)}, f32[136,512]{1,0:T(8,128)}, u32[]{:S(2)}) %copy-start) | copy-done | bytes 278552
  8.8 0.6 %project.5 = (f32[14,56,128]{2,1,0:T(8,128)S(1)}, bf16[14,32,128]{2,1,0:T(8,128)(2,1)S(1)}) custom-call(s32[1]{0:T(128)S(6)} %copy.11.length, f32[136,512]{1,0:T(8,128)S(1)} %copy-done, bf16[14,56,128]{2,1,0:T(8,128)(2,1)S(1)} %bitcast.7), custom_call_target="tpu_custom_call" | custom-call | flops 51380224 | bytes 479236 | tf_op jit(solution)/shard_map/project/pallas_call | solution.py:196
  9.4 0.1 collective-permute-start.4
  9.5 2.2 %collective-permute-done.1.block = bf16[14,56,128]{2,1,0:T(8,128)(2,1)S(1)} collective-permute-done((bf16[14,56,128]{2,1,0:T(8,128)(2,1)}, bf16[14,56,128]{2,1,0:T(8,128)(2,1)S(1)}, u32[]{:S(2)}, u32[]{:S(2)}) %collective-permute-start.1) | collective-permute-done | bytes 200736 | tf_op jit(solution)/shard_map/ppermute | solution.py:241
  11.8 0.6 %project.4 = (f32[14,56,128]{2,1,0:T(8,128)S(1)}, bf16[14,32,128]{2,1,0:T(8,128)(2,1)S(1)}) custom-call(s32[1]{0:T(128)S(6)} %copy.11.length, f32[136,512]{1,0:T(8,128)S(1)} %copy-done, bf16[14,56,128]{2,1,0:T(8,128)(2,1)S(1)} %collective-permute-done.1.block), custom_call_target="tpu_custom_call" | custom-call | flops 51380224 | bytes 479236 | tf_op jit(solution)/shard_map/project/pallas_call | solution.py:196
  12.4 0.1 collective-permute-start.2
  12.5 0.0 collective-permute-done.4.other
  12.5 0.9 %add.3 = (f32[14,56,128]{2,1,0:T(8,128)S(1)}, f32[14,56,128]{2,1,0:T(8,128)S(1)}) custom-call(f32[14,56,128]{2,1,0:T(8,128)S(1)} %get-tuple-element.30.left, bf16[14,32,128]{2,1,0:T(8,128)(2,1)S(1)} %get-tuple-element.31.right, bf16[14,32,128]{2,1,0:T(8,128)(2,1)S(1)} %collective-permute-done.4.other), custom_call_target="tpu_custom_call" | custom-call | flops 44957696 | bytes 630784 | tf_op jit(solution)/shard_map/add/pallas_call | solution.py:196
  13.4 7.2 %collective-permute-done.3.block = bf16[14,56,128]{2,1,0:T(8,128)(2,1)S(1)} collective-permute-done((bf16[14,56,128]{2,1,0:T(8,128)(2,1)}, bf16[14,56,128]{2,1,0:T(8,128)(2,1)S(1)}, u32[]{:S(2)}, u32[]{:S(2)}) %collective-permute-start.3) | collective-permute-done | bytes 200736 | tf_op jit(solution)/shard_map/ppermute | solution.py:241
  20.7 0.6 %project.7 = (f32[14,56,128]{2,1,0:T(8,128)S(1)}, bf16[14,32,128]{2,1,0:T(8,128)(2,1)S(1)}) custom-call(s32[1]{0:T(128)S(6)} %copy.11.length, f32[136,512]{1,0:T(8,128)S(1)} %copy-done.1, bf16[14,56,128]{2,1,0:T(8,128)(2,1)S(1)} %collective-permute-done.3.block), custom_call_target="tpu_custom_call" | custom-call | flops 51380224 | bytes 479236 | tf_op jit(solution)/shard_map/project/pallas_call | solution.py:196
  21.3 0.1 collective-permute-start.6
  21.4 0.0 collective-permute-done.2.other
  21.4 1.0 %add.4 = (f32[14,56,128]{2,1,0:T(8,128)S(1)}, f32[14,56,128]{2,1,0:T(8,128)S(1)}) custom-call(f32[14,56,128]{2,1,0:T(8,128)S(1)} %get-tuple-element.28.left, bf16[14,32,128]{2,1,0:T(8,128)(2,1)S(1)} %get-tuple-element.29.right, bf16[14,32,128]{2,1,0:T(8,128)(2,1)S(1)} %collective-permute-done.2.other, f32[14,56,128]{2,1,0:T(8,128)S(1)} %get-tuple-element.34.refs_0_, ...), custom_call_target="tpu_custom_call" | custom-call | flops 44957696 | bytes 1433600 | tf_op jit(solution)/shard_map/add/pallas_call | solution.py:196
  22.3 0.0 collective-permute-done.block
  22.4 0.6 %project.6 = (f32[14,56,128]{2,1,0:T(8,128)S(1)}, bf16[14,32,128]{2,1,0:T(8,128)(2,1)S(1)}) custom-call(s32[1]{0:T(128)S(6)} %copy.11.length, f32[136,512]{1,0:T(8,128)S(1)} %copy-done.1, bf16[14,56,128]{2,1,0:T(8,128)(2,1)S(1)} %collective-permute-done.block), custom_call_target="tpu_custom_call" | custom-call | flops 51380224 | bytes 479236 | tf_op jit(solution)/shard_map/project/pallas_call | solution.py:196
  23.0 0.5 %collective-permute-start.5 = (bf16[14,32,128]{2,1,0:T(8,128)(2,1)S(1)}, bf16[14,32,128]{2,1,0:T(8,128)(2,1)S(1)}, u32[]{:S(2)}, u32[]{:S(2)}) collective-permute-start(bf16[14,32,128]{2,1,0:T(8,128)(2,1)S(1)} %get-tuple-element.40.right), channel_id=1, source_target_pairs={{0,8},{8,0},{1,9},{9,1},{2,10},{10,2},{3,11},{11,3},{4,12},{12,4},... | collective-permute-start | bytes 344072 | tf_op jit(solution)/shard_map/ppermute | solution.py:244
  23.5 0.0 collective-permute-done.6.other
  23.5 0.9 %add.5 = (f32[14,56,128]{2,1,0:T(8,128)S(1)}, f32[14,56,128]{2,1,0:T(8,128)S(1)}) custom-call(f32[14,56,128]{2,1,0:T(8,128)S(1)} %get-tuple-element.42.left, bf16[14,32,128]{2,1,0:T(8,128)(2,1)S(1)} %get-tuple-element.43.right, bf16[14,32,128]{2,1,0:T(8,128)(2,1)S(1)} %collective-permute-done.6.other, f32[14,56,128]{2,1,0:T(8,128)S(1)} %get-tuple-element.44.refs_0_, ...), custom_call_target="tpu_custom_call" | custom-call | flops 44957696 | bytes 1433600 | tf_op jit(solution)/shard_map/add/pallas_call | solution.py:196
  24.4 0.0 collective-permute-done.5.other
  24.5 0.5 %add_theirs.1 = bf16[14,56,128]{2,1,0:T(8,128)(2,1)S(1)} custom-call(f32[14,56,128]{2,1,0:T(8,128)S(1)} %get-tuple-element.39.left, bf16[14,32,128]{2,1,0:T(8,128)(2,1)S(1)} %get-tuple-element.40.right, bf16[14,32,128]{2,1,0:T(8,128)(2,1)S(1)} %collective-permute-done.5.other, f32[14,56,128]{2,1,0:T(8,128)S(1)} %get-tuple-element.47.before), custom_call_target="tpu_custom_call" | custom-call | flops 22478848 | bytes 1032192 | tf_op jit(solution)/shard_map/add_theirs/pallas_call | solution.py:196
  25.0 0.0 copy-start.5
  25.0 1.6 %collective-permute-start.7 = (bf16[14,56,128]{2,1,0:T(8,128)(2,1)S(1)}, bf16[14,56,128]{2,1,0:T(8,128)(2,1)S(1)}, u32[]{:S(2)}, u32[]{:S(2)}) collective-permute-start(bf16[14,56,128]{2,1,0:T(8,128)(2,1)S(1)} %add_theirs.1), channel_id=1, source_target_pairs={{0,1},{1,0},{2,3},{3,2},{4,5},{5,4},{6,7},{7,6},{8,9},{9,8},{10,11... | collective-permute-start | bytes 602120 | tf_op jit(solution)/shard_map/ppermute | solution.py:241
  26.6 0.5 %gate.1 = (f32[14,56,128]{2,1,0:T(8,128)S(1)}, f32[1,128]{1,0:T(1,128)S(1)}, bf16[128,128]{1,0:T(8,128)(2,1)S(1)}) custom-call(s32[1]{0:T(128)S(6)} %copy.11.length, f32[136,512]{1,0:T(8,128)S(1)} %copy-done.1, bf16[14,56,128]{2,1,0:T(8,128)(2,1)S(1)} %bitcast.8, bf16[128,128]{1,0:T(8,128)(2,1)S(1)} %copy-done.3, f32[1,128]{1,0:T(1,128)S(1)} %bitcast.9, ...), custom_call_target="tpu_custom_call" | custom-call | flops 25690112 | bytes 545284 | tf_op jit(solution)/shard_map/gate/pallas_call | solution.py:196
  27.1 0.5 %add_mine.1.mine = f32[14,56,128]{2,1,0:T(8,128)S(1)} custom-call(f32[14,56,128]{2,1,0:T(8,128)S(1)} %get-tuple-element.39.left, bf16[14,32,128]{2,1,0:T(8,128)(2,1)S(1)} %get-tuple-element.40.right, bf16[14,32,128]{2,1,0:T(8,128)(2,1)S(1)} %collective-permute-done.5.other, f32[14,56,128]{2,1,0:T(8,128)S(1)} %get-tuple-element.46.before), custom_call_target="tpu_custom_call" | custom-call | flops 22478848 | bytes 1032192 | tf_op jit(solution)/shard_map/add_mine/pallas_call | solution.py:196
  27.6 4.7 %collective-permute-done.7.given = bf16[14,56,128]{2,1,0:T(8,128)(2,1)S(1)} collective-permute-done((bf16[14,56,128]{2,1,0:T(8,128)(2,1)S(1)}, bf16[14,56,128]{2,1,0:T(8,128)(2,1)S(1)}, u32[]{:S(2)}, u32[]{:S(2)}) %collective-permute-start.7) | collective-permute-done | bytes 200736 | tf_op jit(solution)/shard_map/ppermute | solution.py:241
  32.3 1.2 %finish.1 = bf16[14,56,128]{2,1,0:T(8,128)(2,1)} custom-call(f32[14,56,128]{2,1,0:T(8,128)S(1)} %add_mine.1.mine, bf16[14,56,128]{2,1,0:T(8,128)(2,1)S(1)} %collective-permute-done.7.given, f32[14,56,128]{2,1,0:T(8,128)S(1)} %get-tuple-element.48.gating, f32[1,128]{1,0:T(1,128)S(1)} %get-tuple-element.49.last_gain, ...), custom_call_target="tpu_custom_call" | custom-call | flops 25690112 | bytes 1036800 | tf_op jit(solution)/shard_map/finish/pallas_call | solution.py:196
  (8 shorter events, 0.0 us)
Async XLA Ops:
  0.0 11.8 %collective-permute-start.1 = (bf16[14,56,128]{2,1,0:T(8,128)(2,1)}, bf16[14,56,128]{2,1,0:T(8,128)(2,1)S(1)}, u32[]{:S(2)}, u32[]{:S(2)}) collective-permute-start(bf16[14,56,128]{2,1,0:T(8,128)(2,1)} %bitcast.4), channel_id=1, source_target_pairs={{0,2},{1,3},{2,0},{3,1},{4,6},{5,7},{6,4},{7,5},{8,10},{9,11},{10,... | collective-permute-start | bytes 602120 | tf_op jit(solution)/shard_map/ppermute | solution.py:241
  3.0 17.6 %collective-permute-start.3 = (bf16[14,56,128]{2,1,0:T(8,128)(2,1)}, bf16[14,56,128]{2,1,0:T(8,128)(2,1)S(1)}, u32[]{:S(2)}, u32[]{:S(2)}) collective-permute-start(bf16[14,56,128]{2,1,0:T(8,128)(2,1)} %bitcast.5), channel_id=1, source_target_pairs={{0,4},{1,5},{2,6},{3,7},{4,0},{5,1},{6,2},{7,3},{8,12},{9,13},{10,... | collective-permute-start | bytes 602120 | tf_op jit(solution)/shard_map/ppermute | solution.py:241
  5.6 16.7 %collective-permute-start = (bf16[14,56,128]{2,1,0:T(8,128)(2,1)}, bf16[14,56,128]{2,1,0:T(8,128)(2,1)S(1)}, u32[]{:S(2)}, u32[]{:S(2)}) collective-permute-start(bf16[14,56,128]{2,1,0:T(8,128)(2,1)} %bitcast.6), channel_id=1, source_target_pairs={{0,6},{1,7},{2,4},{3,5},{4,2},{5,3},{6,0},{7,1},{8,14},{9,15},{10,... | collective-permute-start | bytes 602120 | tf_op jit(solution)/shard_map/ppermute | solution.py:241
  6.3 1.6 %copy-start.2 = (bf16[56,14,128]{2,0,1:T(8,128)(2,1)S(1)}, bf16[56,14,128]{2,0,1:T(8,128)(2,1)}, u32[]{:S(2)}) copy-start(bf16[56,14,128]{2,0,1:T(8,128)(2,1)} %param.10) | copy-start | bytes 602116
  7.9 1.0 %copy-start = (f32[136,512]{1,0:T(8,128)S(1)}, f32[136,512]{1,0:T(8,128)}, u32[]{:S(2)}) copy-start(f32[136,512]{1,0:T(8,128)} %join.1.shared) | copy-start | bytes 835588
  9.4 3.0 %collective-permute-start.4 = (bf16[14,32,128]{2,1,0:T(8,128)(2,1)S(1)}, bf16[14,32,128]{2,1,0:T(8,128)(2,1)S(1)}, u32[]{:S(2)}, u32[]{:S(2)}) collective-permute-start(bf16[14,32,128]{2,1,0:T(8,128)(2,1)S(1)} %get-tuple-element.31.right), channel_id=1, source_target_pairs={{0,8},{8,0},{1,9},{9,1},{2,10},{10,2},{3,11},{11,3},{4,12},{12,4},... | collective-permute-start | bytes 344072 | tf_op jit(solution)/shard_map/ppermute | solution.py:244
  12.4 9.0 %collective-permute-start.2 = (bf16[14,32,128]{2,1,0:T(8,128)(2,1)S(1)}, bf16[14,32,128]{2,1,0:T(8,128)(2,1)S(1)}, u32[]{:S(2)}, u32[]{:S(2)}) collective-permute-start(bf16[14,32,128]{2,1,0:T(8,128)(2,1)S(1)} %get-tuple-element.29.right), channel_id=1, source_target_pairs={{0,8},{8,0},{1,9},{9,1},{2,10},{10,2},{3,11},{11,3},{4,12},{12,4},... | collective-permute-start | bytes 344072 | tf_op jit(solution)/shard_map/ppermute | solution.py:244
  12.5 8.2 %copy-start.1 = (f32[136,512]{1,0:T(8,128)S(1)}, f32[136,512]{1,0:T(8,128)}, u32[]{:S(2)}) copy-start(f32[136,512]{1,0:T(8,128)} %join.1.shared) | copy-start | bytes 835588
  21.3 2.2 %collective-permute-start.6 = (bf16[14,32,128]{2,1,0:T(8,128)(2,1)S(1)}, bf16[14,32,128]{2,1,0:T(8,128)(2,1)S(1)}, u32[]{:S(2)}, u32[]{:S(2)}) collective-permute-start(bf16[14,32,128]{2,1,0:T(8,128)(2,1)S(1)} %get-tuple-element.43.right), channel_id=1, source_target_pairs={{0,8},{8,0},{1,9},{9,1},{2,10},{10,2},{3,11},{11,3},{4,12},{12,4},... | collective-permute-start | bytes 344072 | tf_op jit(solution)/shard_map/ppermute | solution.py:244
  23.0 1.5 %collective-permute-start.5 = (bf16[14,32,128]{2,1,0:T(8,128)(2,1)S(1)}, bf16[14,32,128]{2,1,0:T(8,128)(2,1)S(1)}, u32[]{:S(2)}, u32[]{:S(2)}) collective-permute-start(bf16[14,32,128]{2,1,0:T(8,128)(2,1)S(1)} %get-tuple-element.40.right), channel_id=1, source_target_pairs={{0,8},{8,0},{1,9},{9,1},{2,10},{10,2},{3,11},{11,3},{4,12},{12,4},... | collective-permute-start | bytes 344072 | tf_op jit(solution)/shard_map/ppermute | solution.py:244
  24.5 2.2 %copy-start.3 = (bf16[128,128]{1,0:T(8,128)(2,1)S(1)}, bf16[128,128]{1,0:T(8,128)(2,1)}, u32[]{:S(2)}) copy-start(bf16[128,128]{1,0:T(8,128)(2,1)} %out_gate.1) | copy-start | bytes 98308
  24.5 2.2 %copy-start.4 = (bf16[128,128]{1,0:T(8,128)(2,1)S(1)}, bf16[128,128]{1,0:T(8,128)(2,1)}, u32[]{:S(2)}) copy-start(bf16[128,128]{1,0:T(8,128)(2,1)} %last_weight.1) | copy-start | bytes 98308
  25.0 1.6 %copy-start.5 = (f32[128]{0:T(128)S(1)}, f32[128]{0:T(128)}, u32[]{:S(2)}) copy-start(f32[128]{0:T(128)} %param.18) | copy-start | bytes 1540
  25.0 7.3 %collective-permute-start.7 = (bf16[14,56,128]{2,1,0:T(8,128)(2,1)S(1)}, bf16[14,56,128]{2,1,0:T(8,128)(2,1)S(1)}, u32[]{:S(2)}, u32[]{:S(2)}) collective-permute-start(bf16[14,56,128]{2,1,0:T(8,128)(2,1)S(1)} %add_theirs.1), channel_id=1, source_target_pairs={{0,1},{1,0},{2,3},{3,2},{4,5},{5,4},{6,7},{7,6},{8,9},{9,8},{10,11... | collective-permute-start | bytes 602120 | tf_op jit(solution)/shard_map/ppermute | solution.py:241

commit v21 on v19

--- a/solution.py
+++ b/solution.py
@@ -325,24 +325,23 @@
     other = shift(pair, crossed=True)
     own = shift(pair)
     right = right_of(0, pair)
-    swapped = swap(right)
-    other, own = in_turn(other, own, right)
+    gating = call(
+        functools.partial(gate, s),
+        [sums, shape((1, hidden), F32), shape(out_weight.shape, BF16)],
+        [],
+        2 * height * width * channels * channels,
+        *shared,
+        pair,
+        out_gate,
+        output_gain.reshape(1, hidden),
+        out_weight,
+    )
+    other, own = in_turn(other, own, (right, gating))
     total = ()
     for distance in range(1, far - 1):
         ahead = [shift(other), shift(own)]
         if distance == 1:
-            left = left_of(0, pair)
-            gating = call(
-                functools.partial(gate, s),
-                [sums, shape((1, hidden), F32), shape(out_weight.shape, BF16)],
-                [],
-                2 * height * width * channels * channels,
-                *shared,
-                pair,
-                out_gate,
-                output_gain.reshape(1, hidden),
-                out_weight,
-            )
+            left, swapped = left_of(0, pair), swap(lax.optimization_barrier((right, own))[0])
         elif distance == 2:
             mine = call(
                 functools.partial(add_own, s),
@@ -356,7 +355,9 @@
             )
             total = mine, total[1]
         total = add(distance, own, other, total)
-        other, own = in_turn(*ahead, (total, gating))
+        other, own = in_turn(*ahead, (total, left))
+        if distance == 1:
+            other, swapped = lax.optimization_barrier((other, swapped))
     last = shift(own)
     mine, theirs = add(far - 1, own, other, total, narrow=True)
     given = swap(theirs)

time: 30.7 us -> 29.7 us (0.967)
  waiting for transfers between devices: 5.99 us -> 4.94 us
  starting transfers between devices: 11.6 us -> 10.9 us
  local copies, waits for them, and re-layouts: 0.98 us -> 1.62 us
    ppermute x7, starting transfers between devices: 11.5 us -> 10.7 us  [shift(): return lax.ppermute(block, ('row', 'col'), pairs)]
    ppermute x3, waiting for transfers between devices: 1.46 us -> 0.73 us  [swap(): lax.ppermute(block, 'row', [(at, (at + 1) % s.rows) for at in range(s.row...]
    unnamed x12, local copies, waits for them, and re-layouts: 0.98 us -> 1.62 us
    ppermute x7, waiting for transfers between devices: 4.53 us -> 4.21 us  [shift(): return lax.ppermute(block, ('row', 'col'), pairs)]
  transfers between devices with their start and end apart: 10 -> 10, of which waited for: 6 -> 6; matrix products, arithmetic and copies ran while one was open for 0% -> 0% of each run, Pallas kernels for 31% -> 32%
where the time goes in v21:
time: 29.7 us; the launch traced here: 29.4 us
  Pallas kernels  11.2 us (38%)
  starting transfers between devices  10.9 us (37%)
  waiting for transfers between devices  4.94 us (17%)
  local copies, waits for them, and re-layouts  1.62 us (5%)
  between operations  0.79 us (3%)
    pallas_call x11, Pallas kernels, call(): pl.pallas_call(body, out_shape=out_shape, in_specs=[space(o) for o in ope...  11.2 us
    ppermute x7, starting transfers between devices, shift(): return lax.ppermute(block, ('row', 'col'), pairs)  10.7 us
    ppermute x7, waiting for transfers between devices, shift(): return lax.ppermute(block, ('row', 'col'), pairs)  4.21 us
    unnamed x12, local copies, waits for them, and re-layouts  1.62 us
    ppermute x3, waiting for transfers between devices, swap(): lax.ppermute(block, 'row', [(at, (at + 1) % s.rows) for at in range(s.row...  0.73 us
  transfers between devices with their start and end apart: 10, of which 6 were waited for; matrix products, arithmetic and copies ran while one was open for 0% of the time, Pallas kernels for 32%

profile of v21, /device:TPU:0, one launch (start us, length us, event | category | flops | bytes accessed | tf_op | source)
XLA Modules:
  0.0 29.4 jit_solution(12779376036126145147)
XLA Ops:
  0.0 3.0 %collective-permute-start = (bf16[14,56,128]{2,1,0:T(8,128)(2,1)}, bf16[14,56,128]{2,1,0:T(8,128)(2,1)S(1)}, u32[]{:S(2)}, u32[]{:S(2)}) collective-permute-start(bf16[14,56,128]{2,1,0:T(8,128)(2,1)} %bitcast.4), channel_id=1, source_target_pairs={{0,2},{2,4},{4,6},{6,7},{7,5},{5,3},{3,1},{1,0},{8,9},{10,8},{12,1... | collective-permute-start | bytes 602120 | tf_op jit(solution)/shard_map/ppermute | solution.py:289
  3.0 0.7 %collective-permute-start.2 = (bf16[14,56,128]{2,1,0:T(8,128)(2,1)}, bf16[14,56,128]{2,1,0:T(8,128)(2,1)S(1)}, u32[]{:S(2)}, u32[]{:S(2)}) collective-permute-start(bf16[14,56,128]{2,1,0:T(8,128)(2,1)} %bitcast.5), channel_id=1, source_target_pairs={{0,9},{2,8},{4,10},{6,12},{7,14},{5,15},{3,13},{1,11},{8,2},{10,4}... | collective-permute-start | bytes 602120 | tf_op jit(solution)/shard_map/ppermute | solution.py:289
  4.4 1.6 %join.1.shared = f32[136,512]{1,0:T(8,128)} custom-call(f32[1,128]{1,0:T(1,128)} %bitcast.10, bf16[128,128]{1,0:T(8,128)(2,1)} %left_gate.1, bf16[128,128]{1,0:T(8,128)(2,1)} %left_value.1, bf16[128,128]{1,0:T(8,128)(2,1)} %right_gate.1, bf16[128,128]{1,0:T(8,128)(2,1)} %right_value.1), custom_call_target="tpu_custom_call" | custom-call | bytes 131584 | tf_op jit(solution)/shard_map/join/pallas_call | solution.py:236
  6.0 1.0 %copy-done = f32[136,512]{1,0:T(8,128)S(1)} copy-done((f32[136,512]{1,0:T(8,128)S(1)}, f32[136,512]{1,0:T(8,128)}, u32[]{:S(2)}) %copy-start) | copy-done | bytes 278552
  6.9 0.4 %own_right.2.right = bf16[14,16,128]{2,1,0:T(8,128)(2,1)S(1)} custom-call(s32[1]{0:T(128)S(6)} %copy.11.length, f32[136,512]{1,0:T(8,128)S(1)} %copy-done, bf16[14,56,128]{2,1,0:T(8,128)(2,1)S(1)} %bitcast.6), custom_call_target="tpu_custom_call" | custom-call | bytes 479236 | tf_op jit(solution)/shard_map/own_right/pallas_call | solution.py:236
  7.3 0.0 copy-start.5
  7.3 0.4 %copy-done.3 = bf16[128,128]{1,0:T(8,128)(2,1)S(1)} copy-done((bf16[128,128]{1,0:T(8,128)(2,1)S(1)}, bf16[128,128]{1,0:T(8,128)(2,1)}, u32[]{:S(2)}) %copy-start.3) | copy-done | bytes 32792
  7.7 0.0 copy-done.4
  7.7 0.3 copy-done.5
  8.0 0.5 %gate.1 = (f32[14,56,128]{2,1,0:T(8,128)S(1)}, f32[1,128]{1,0:T(1,128)S(1)}, bf16[128,128]{1,0:T(8,128)(2,1)S(1)}) custom-call(s32[1]{0:T(128)S(6)} %copy.11.length, f32[136,512]{1,0:T(8,128)S(1)} %copy-done, bf16[14,56,128]{2,1,0:T(8,128)(2,1)S(1)} %bitcast.7, bf16[128,128]{1,0:T(8,128)(2,1)S(1)} %copy-done.3, f32[1,128]{1,0:T(1,128)S(1)} %bitcast.9, ...), custom_call_target="tpu_custom_call" | custom-call | flops 25690112 | bytes 545284 | tf_op jit(solution)/shard_map/gate/pallas_call | solution.py:236
  8.5 1.6 %collective-permute-start.1 = (bf16[14,56,128]{2,1,0:T(8,128)(2,1)S(1)}, bf16[14,56,128]{2,1,0:T(8,128)(2,1)S(1)}, u32[]{:S(2)}, u32[]{:S(2)}) collective-permute-start(bf16[14,56,128]{2,1,0:T(8,128)(2,1)S(1)} %collective-permute-done.own), channel_id=1, source_target_pairs={{0,2},{2,4},{4,6},{6,7},{7,5},{5,3},{3,1},{1,0},{8,9},{10,8},{12,1... | collective-permute-start | bytes 602120 | tf_op jit(solution)/shard_map/ppermute | solution.py:289
  10.1 1.6 %collective-permute-start.4 = (bf16[14,56,128]{2,1,0:T(8,128)(2,1)S(1)}, bf16[14,56,128]{2,1,0:T(8,128)(2,1)S(1)}, u32[]{:S(2)}, u32[]{:S(2)}) collective-permute-start(bf16[14,56,128]{2,1,0:T(8,128)(2,1)S(1)} %collective-permute-done.2.other), channel_id=1, source_target_pairs={{0,2},{2,4},{4,6},{6,7},{7,5},{5,3},{3,1},{1,0},{8,9},{10,8},{12,1... | collective-permute-start | bytes 602120 | tf_op jit(solution)/shard_map/ppermute | solution.py:289
  11.7 0.5 %own_left.2.left = f32[14,56,128]{2,1,0:T(8,128)S(1)} custom-call(s32[1]{0:T(128)S(6)} %copy.11.length, f32[136,512]{1,0:T(8,128)S(1)} %copy-done, bf16[14,56,128]{2,1,0:T(8,128)(2,1)S(1)} %bitcast.8), custom_call_target="tpu_custom_call" | custom-call | bytes 479236 | tf_op jit(solution)/shard_map/own_left/pallas_call | solution.py:236
  12.2 0.1 collective-permute-start.5
  12.2 1.8 %add_both.3 = (f32[14,56,128]{2,1,0:T(8,128)S(1)}, f32[14,56,128]{2,1,0:T(8,128)S(1)}) custom-call(s32[1]{0:T(128)S(6)} %copy.11.length, f32[136,512]{1,0:T(8,128)S(1)} %copy-done, bf16[14,56,128]{2,1,0:T(8,128)(2,1)S(1)} %collective-permute-done.own, bf16[14,56,128]{2,1,0:T(8,128)(2,1)S(1)} %collective-permute-done.2.other), custom_call_target="tpu_custom_call" | custom-call | flops 44957696 | bytes 679940 | tf_op jit(solution)/shard_map/add_both/pallas_call | solution.py:236
  14.0 0.7 %collective-permute-done.1.own = bf16[14,56,128]{2,1,0:T(8,128)(2,1)S(1)} collective-permute-done((bf16[14,56,128]{2,1,0:T(8,128)(2,1)S(1)}, bf16[14,56,128]{2,1,0:T(8,128)(2,1)S(1)}, u32[]{:S(2)}, u32[]{:S(2)}) %collective-permute-start.1) | collective-permute-done | bytes 200736 | tf_op jit(solution)/shard_map/ppermute | solution.py:289
  14.7 1.1 %collective-permute-start.3 = (bf16[14,56,128]{2,1,0:T(8,128)(2,1)S(1)}, bf16[14,56,128]{2,1,0:T(8,128)(2,1)S(1)}, u32[]{:S(2)}, u32[]{:S(2)}) collective-permute-start(bf16[14,56,128]{2,1,0:T(8,128)(2,1)S(1)} %collective-permute-done.1.own), channel_id=1, source_target_pairs={{0,2},{2,4},{4,6},{6,7},{7,5},{5,3},{3,1},{1,0},{8,9},{10,8},{12,1... | collective-permute-start | bytes 602120 | tf_op jit(solution)/shard_map/ppermute | solution.py:289
  15.8 1.0 %collective-permute-done.4.other = bf16[14,56,128]{2,1,0:T(8,128)(2,1)S(1)} collective-permute-done((bf16[14,56,128]{2,1,0:T(8,128)(2,1)S(1)}, bf16[14,56,128]{2,1,0:T(8,128)(2,1)S(1)}, u32[]{:S(2)}, u32[]{:S(2)}) %collective-permute-start.4) | collective-permute-done | bytes 200736 | tf_op jit(solution)/shard_map/ppermute | solution.py:289
  16.9 1.2 %collective-permute-start.7 = (bf16[14,56,128]{2,1,0:T(8,128)(2,1)S(1)}, bf16[14,56,128]{2,1,0:T(8,128)(2,1)S(1)}, u32[]{:S(2)}, u32[]{:S(2)}) collective-permute-start(bf16[14,56,128]{2,1,0:T(8,128)(2,1)S(1)} %collective-permute-done.4.other), channel_id=1, source_target_pairs={{0,2},{2,4},{4,6},{6,7},{7,5},{5,3},{3,1},{1,0},{8,9},{10,8},{12,1... | collective-permute-start | bytes 602120 | tf_op jit(solution)/shard_map/ppermute | solution.py:289
  18.1 0.5 %add_own.1.refs_0_ = f32[14,56,128]{2,1,0:T(8,128)S(1)} custom-call(f32[14,56,128]{2,1,0:T(8,128)S(1)} %own_left.2.left, bf16[14,16,128]{2,1,0:T(8,128)(2,1)S(1)} %own_right.2.right, bf16[14,16,128]{2,1,0:T(8,128)(2,1)S(1)} %collective-permute-done.5.other, f32[14,56,128]{2,1,0:T(8,128)S(1)} %get-tuple-element.41.before), custom_call_target="tpu_custom_call" | custom-call | flops 22478848 | bytes 917504 | tf_op jit(solution)/shard_map/add_own/pallas_call | solution.py:236
  18.6 1.8 %add_both.4 = (f32[14,56,128]{2,1,0:T(8,128)S(1)}, f32[14,56,128]{2,1,0:T(8,128)S(1)}) custom-call(s32[1]{0:T(128)S(6)} %copy.11.length, f32[136,512]{1,0:T(8,128)S(1)} %copy-done.1, bf16[14,56,128]{2,1,0:T(8,128)(2,1)S(1)} %collective-permute-done.1.own, bf16[14,56,128]{2,1,0:T(8,128)(2,1)S(1)} %collective-permute-done.4.other, ...), custom_call_target="tpu_custom_call" | custom-call | flops 44957696 | bytes 1482756 | tf_op jit(solution)/shard_map/add_both/pallas_call | solution.py:236
  20.3 0.1 collective-permute-done.3.own
  20.4 1.5 %collective-permute-start.6 = (bf16[14,56,128]{2,1,0:T(8,128)(2,1)S(1)}, bf16[14,56,128]{2,1,0:T(8,128)(2,1)S(1)}, u32[]{:S(2)}, u32[]{:S(2)}) collective-permute-start(bf16[14,56,128]{2,1,0:T(8,128)(2,1)S(1)} %collective-permute-done.3.own), channel_id=1, source_target_pairs={{0,2},{2,4},{4,6},{6,7},{7,5},{5,3},{3,1},{1,0},{8,9},{10,8},{12,1... | collective-permute-start | bytes 602120 | tf_op jit(solution)/shard_map/ppermute | solution.py:289
  21.9 0.7 %collective-permute-done.7.other = bf16[14,56,128]{2,1,0:T(8,128)(2,1)S(1)} collective-permute-done((bf16[14,56,128]{2,1,0:T(8,128)(2,1)S(1)}, bf16[14,56,128]{2,1,0:T(8,128)(2,1)S(1)}, u32[]{:S(2)}, u32[]{:S(2)}) %collective-permute-start.7) | collective-permute-done | bytes 200736 | tf_op jit(solution)/shard_map/ppermute | solution.py:289
  22.6 1.8 %add_both.5 = (f32[14,56,128]{2,1,0:T(8,128)S(1)}, bf16[14,56,128]{2,1,0:T(8,128)(2,1)S(1)}) custom-call(s32[1]{0:T(128)S(6)} %copy.11.length, f32[136,512]{1,0:T(8,128)S(1)} %copy-done.1, bf16[14,56,128]{2,1,0:T(8,128)(2,1)S(1)} %collective-permute-done.3.own, bf16[14,56,128]{2,1,0:T(8,128)(2,1)S(1)} %collective-permute-done.7.other, ...), custom_call_target="tpu_custom_call" | custom-call | flops 44957696 | bytes 1482756 | tf_op jit(solution)/shard_map/add_both/pallas_call | solution.py:236
  24.4 0.1 collective-permute-start.9
  24.4 1.7 %collective-permute-done.6.own = bf16[14,56,128]{2,1,0:T(8,128)(2,1)S(1)} collective-permute-done((bf16[14,56,128]{2,1,0:T(8,128)(2,1)S(1)}, bf16[14,56,128]{2,1,0:T(8,128)(2,1)S(1)}, u32[]{:S(2)}, u32[]{:S(2)}) %collective-permute-start.6) | collective-permute-done | bytes 200736 | tf_op jit(solution)/shard_map/ppermute | solution.py:289
  26.1 0.4 %own_right.3.right = bf16[14,16,128]{2,1,0:T(8,128)(2,1)S(1)} custom-call(s32[1]{0:T(128)S(6)} %copy.11.length, f32[136,512]{1,0:T(8,128)S(1)} %copy-done.1, bf16[14,56,128]{2,1,0:T(8,128)(2,1)S(1)} %collective-permute-done.6.own), custom_call_target="tpu_custom_call" | custom-call | bytes 479236 | tf_op jit(solution)/shard_map/own_right/pallas_call | solution.py:236
  26.5 0.1 collective-permute-start.8
  26.6 0.5 %own_left.3.left = f32[14,56,128]{2,1,0:T(8,128)S(1)} custom-call(s32[1]{0:T(128)S(6)} %copy.11.length, f32[136,512]{1,0:T(8,128)S(1)} %copy-done.1, bf16[14,56,128]{2,1,0:T(8,128)(2,1)S(1)} %collective-permute-done.6.own), custom_call_target="tpu_custom_call" | custom-call | bytes 479236 | tf_op jit(solution)/shard_map/own_left/pallas_call | solution.py:236
  27.1 0.7 %collective-permute-done.8.other = bf16[14,16,128]{2,1,0:T(8,128)(2,1)S(1)} collective-permute-done((bf16[14,16,128]{2,1,0:T(8,128)(2,1)S(1)}, bf16[14,16,128]{2,1,0:T(8,128)(2,1)S(1)}, u32[]{:S(2)}, u32[]{:S(2)}) %collective-permute-start.8) | collective-permute-done | bytes 57376 | tf_op jit(solution)/shard_map/ppermute | solution.py:292
  27.8 1.6 %finish.1 = bf16[14,56,128]{2,1,0:T(8,128)(2,1)} custom-call(f32[14,56,128]{2,1,0:T(8,128)S(1)} %own_left.3.left, bf16[14,16,128]{2,1,0:T(8,128)(2,1)S(1)} %own_right.3.right, bf16[14,16,128]{2,1,0:T(8,128)(2,1)S(1)} %collective-permute-done.8.other, f32[14,56,128]{2,1,0:T(8,128)S(1)} %get-tuple-element.48.mine, ...), custom_call_target="tpu_custom_call" | custom-call | flops 22478848 | bytes 1552896 | tf_op jit(solution)/shard_map/finish/pallas_call | solution.py:236
  (11 shorter events, 0.0 us)
Async XLA Ops:
  0.0 8.4 %collective-permute-start = (bf16[14,56,128]{2,1,0:T(8,128)(2,1)}, bf16[14,56,128]{2,1,0:T(8,128)(2,1)S(1)}, u32[]{:S(2)}, u32[]{:S(2)}) collective-permute-start(bf16[14,56,128]{2,1,0:T(8,128)(2,1)} %bitcast.4), channel_id=1, source_target_pairs={{0,2},{2,4},{4,6},{6,7},{7,5},{5,3},{3,1},{1,0},{8,9},{10,8},{12,1... | collective-permute-start | bytes 602120 | tf_op jit(solution)/shard_map/ppermute | solution.py:289
  3.0 7.1 %collective-permute-start.2 = (bf16[14,56,128]{2,1,0:T(8,128)(2,1)}, bf16[14,56,128]{2,1,0:T(8,128)(2,1)S(1)}, u32[]{:S(2)}, u32[]{:S(2)}) collective-permute-start(bf16[14,56,128]{2,1,0:T(8,128)(2,1)} %bitcast.5), channel_id=1, source_target_pairs={{0,9},{2,8},{4,10},{6,12},{7,14},{5,15},{3,13},{1,11},{8,2},{10,4}... | collective-permute-start | bytes 602120 | tf_op jit(solution)/shard_map/ppermute | solution.py:289
  4.4 1.6 %copy-start.2 = (bf16[56,14,128]{2,0,1:T(8,128)(2,1)S(1)}, bf16[56,14,128]{2,0,1:T(8,128)(2,1)}, u32[]{:S(2)}) copy-start(bf16[56,14,128]{2,0,1:T(8,128)(2,1)} %param.10) | copy-start | bytes 602116
  6.0 1.0 %copy-start = (f32[136,512]{1,0:T(8,128)S(1)}, f32[136,512]{1,0:T(8,128)}, u32[]{:S(2)}) copy-start(f32[136,512]{1,0:T(8,128)} %join.1.shared) | copy-start | bytes 835588
  6.9 0.8 %copy-start.3 = (bf16[128,128]{1,0:T(8,128)(2,1)S(1)}, bf16[128,128]{1,0:T(8,128)(2,1)}, u32[]{:S(2)}) copy-start(bf16[128,128]{1,0:T(8,128)(2,1)} %out_gate.1) | copy-start | bytes 98308
  6.9 0.8 %copy-start.4 = (bf16[128,128]{1,0:T(8,128)(2,1)S(1)}, bf16[128,128]{1,0:T(8,128)(2,1)}, u32[]{:S(2)}) copy-start(bf16[128,128]{1,0:T(8,128)(2,1)} %last_weight.1) | copy-start | bytes 98308
  7.3 0.7 %copy-start.5 = (f32[128]{0:T(128)S(1)}, f32[128]{0:T(128)}, u32[]{:S(2)}) copy-start(f32[128]{0:T(128)} %param.18) | copy-start | bytes 1540
  8.5 6.3 %collective-permute-start.1 = (bf16[14,56,128]{2,1,0:T(8,128)(2,1)S(1)}, bf16[14,56,128]{2,1,0:T(8,128)(2,1)S(1)}, u32[]{:S(2)}, u32[]{:S(2)}) collective-permute-start(bf16[14,56,128]{2,1,0:T(8,128)(2,1)S(1)} %collective-permute-done.own), channel_id=1, source_target_pairs={{0,2},{2,4},{4,6},{6,7},{7,5},{5,3},{3,1},{1,0},{8,9},{10,8},{12,1... | collective-permute-start | bytes 602120 | tf_op jit(solution)/shard_map/ppermute | solution.py:289
  10.1 6.8 %collective-permute-start.4 = (bf16[14,56,128]{2,1,0:T(8,128)(2,1)S(1)}, bf16[14,56,128]{2,1,0:T(8,128)(2,1)S(1)}, u32[]{:S(2)}, u32[]{:S(2)}) collective-permute-start(bf16[14,56,128]{2,1,0:T(8,128)(2,1)S(1)} %collective-permute-done.2.other), channel_id=1, source_target_pairs={{0,2},{2,4},{4,6},{6,7},{7,5},{5,3},{3,1},{1,0},{8,9},{10,8},{12,1... | collective-permute-start | bytes 602120 | tf_op jit(solution)/shard_map/ppermute | solution.py:289
  12.2 4.7 %collective-permute-start.5 = (bf16[14,16,128]{2,1,0:T(8,128)(2,1)S(1)}, bf16[14,16,128]{2,1,0:T(8,128)(2,1)S(1)}, u32[]{:S(2)}, u32[]{:S(2)}) collective-permute-start(bf16[14,16,128]{2,1,0:T(8,128)(2,1)S(1)} %own_right.2.right), channel_id=1, source_target_pairs={{0,8},{8,0},{1,9},{9,1},{2,10},{10,2},{3,11},{11,3},{4,12},{12,4},... | collective-permute-start | bytes 172040 | tf_op jit(solution)/shard_map/ppermute | solution.py:292
  14.7 3.8 %copy-start.1 = (f32[136,512]{1,0:T(8,128)S(1)}, f32[136,512]{1,0:T(8,128)}, u32[]{:S(2)}) copy-start(f32[136,512]{1,0:T(8,128)} %join.1.shared) | copy-start | bytes 835588
  14.7 5.7 %collective-permute-start.3 = (bf16[14,56,128]{2,1,0:T(8,128)(2,1)S(1)}, bf16[14,56,128]{2,1,0:T(8,128)(2,1)S(1)}, u32[]{:S(2)}, u32[]{:S(2)}) collective-permute-start(bf16[14,56,128]{2,1,0:T(8,128)(2,1)S(1)} %collective-permute-done.1.own), channel_id=1, source_target_pairs={{0,2},{2,4},{4,6},{6,7},{7,5},{5,3},{3,1},{1,0},{8,9},{10,8},{12,1... | collective-permute-start | bytes 602120 | tf_op jit(solution)/shard_map/ppermute | solution.py:289
  16.9 5.7 %collective-permute-start.7 = (bf16[14,56,128]{2,1,0:T(8,128)(2,1)S(1)}, bf16[14,56,128]{2,1,0:T(8,128)(2,1)S(1)}, u32[]{:S(2)}, u32[]{:S(2)}) collective-permute-start(bf16[14,56,128]{2,1,0:T(8,128)(2,1)S(1)} %collective-permute-done.4.other), channel_id=1, source_target_pairs={{0,2},{2,4},{4,6},{6,7},{7,5},{5,3},{3,1},{1,0},{8,9},{10,8},{12,1... | collective-permute-start | bytes 602120 | tf_op jit(solution)/shard_map/ppermute | solution.py:289
  20.4 5.7 %collective-permute-start.6 = (bf16[14,56,128]{2,1,0:T(8,128)(2,1)S(1)}, bf16[14,56,128]{2,1,0:T(8,128)(2,1)S(1)}, u32[]{:S(2)}, u32[]{:S(2)}) collective-permute-start(bf16[14,56,128]{2,1,0:T(8,128)(2,1)S(1)} %collective-permute-done.3.own), channel_id=1, source_target_pairs={{0,2},{2,4},{4,6},{6,7},{7,5},{5,3},{3,1},{1,0},{8,9},{10,8},{12,1... | collective-permute-start | bytes 602120 | tf_op jit(solution)/shard_map/ppermute | solution.py:289
  24.4 2.7 %collective-permute-start.9 = (bf16[14,56,128]{2,1,0:T(8,128)(2,1)S(1)}, bf16[14,56,128]{2,1,0:T(8,128)(2,1)S(1)}, u32[]{:S(2)}, u32[]{:S(2)}) collective-permute-start(bf16[14,56,128]{2,1,0:T(8,128)(2,1)S(1)} %get-tuple-element.49), channel_id=1, source_target_pairs={{0,8},{8,0},{1,9},{9,1},{2,10},{10,2},{3,11},{11,3},{4,12},{12,4},... | collective-permute-start | bytes 602120 | tf_op jit(solution)/shard_map/ppermute | solution.py:292
  26.5 1.3 %collective-permute-start.8 = (bf16[14,16,128]{2,1,0:T(8,128)(2,1)S(1)}, bf16[14,16,128]{2,1,0:T(8,128)(2,1)S(1)}, u32[]{:S(2)}, u32[]{:S(2)}) collective-permute-start(bf16[14,16,128]{2,1,0:T(8,128)(2,1)S(1)} %own_right.3.right), channel_id=1, source_target_pairs={{0,8},{8,0},{1,9},{9,1},{2,10},{10,2},{3,11},{11,3},{4,12},{12,4},... | collective-permute-start | bytes 172040 | tf_op jit(solution)/shard_map/ppermute | solution.py:292

commit v22 on v21

--- a/solution.py
+++ b/solution.py
@@ -325,18 +325,7 @@
     other = shift(pair, crossed=True)
     own = shift(pair)
     right = right_of(0, pair)
-    gating = call(
-        functools.partial(gate, s),
-        [sums, shape((1, hidden), F32), shape(out_weight.shape, BF16)],
-        [],
-        2 * height * width * channels * channels,
-        *shared,
-        pair,
-        out_gate,
-        output_gain.reshape(1, hidden),
-        out_weight,
-    )
-    other, own = in_turn(other, own, (right, gating))
+    other, own = in_turn(other, own, right)
     total = ()
     for distance in range(1, far - 1):
         ahead = [shift(other), shift(own)]
@@ -359,6 +348,17 @@
         if distance == 1:
             other, swapped = lax.optimization_barrier((other, swapped))
     last = shift(own)
+    gating = call(
+        functools.partial(gate, s),
+        [sums, shape((1, hidden), F32), shape(out_weight.shape, BF16)],
+        [],
+        2 * height * width * channels * channels,
+        *shared,
+        pair,
+        out_gate,
+        output_gain.reshape(1, hidden),
+        out_weight,
+    )
     mine, theirs = add(far - 1, own, other, total, narrow=True)
     given = swap(theirs)
     last, mine, gating = lax.optimization_barrier((last, mine, gating))

time: 29.7 us -> 29.6 us (level)
  starting transfers between devices: 10.9 us -> 11.7 us
  waiting for transfers between devices: 4.94 us -> 4.29 us
    ppermute x7, starting transfers between devices: 10.7 us -> 11.4 us  [shift(): return lax.ppermute(block, ('row', 'col'), pairs)]
    ppermute x7, waiting for transfers between devices: 4.21 us -> 3.56 us  [shift(): return lax.ppermute(block, ('row', 'col'), pairs)]
  transfers between devices with their start and end apart: 10 -> 10, of which waited for: 6 -> 7; matrix products, arithmetic and copies ran while one was open for 0% -> 0% of each run, Pallas kernels for 32% -> 32%
where the time goes in v22:
time: 29.6 us; the launch traced here: 29.4 us
  starting transfers between devices  11.7 us (40%)
  Pallas kernels  11.2 us (38%)
  waiting for transfers between devices  4.29 us (14%)
  local copies, waits for them, and re-layouts  1.52 us (5%)
  between operations  0.8 us (3%)
    ppermute x7, starting transfers between devices, shift(): return lax.ppermute(block, ('row', 'col'), pairs)  11.4 us
    pallas_call x11, Pallas kernels, call(): pl.pallas_call(body, out_shape=out_shape, in_specs=[space(o) for o in ope...  11.2 us
    ppermute x7, waiting for transfers between devices, shift(): return lax.ppermute(block, ('row', 'col'), pairs)  3.56 us
    unnamed x12, local copies, waits for them, and re-layouts  1.52 us
    ppermute x3, waiting for transfers between devices, swap(): lax.ppermute(block, 'row', [(at, (at + 1) % s.rows) for at in range(s.row...  0.73 us
  transfers between devices with their start and end apart: 10, of which 7 were waited for; matrix products, arithmetic and copies ran while one was open for 0% of the time, Pallas kernels for 32%

profile of v22, /device:TPU:0, one launch (start us, length us, event | category | flops | bytes accessed | tf_op | source)
XLA Modules:
  0.0 29.4 jit_solution(9675013384300206530)
XLA Ops:
  0.0 3.0 %collective-permute-start = (bf16[14,56,128]{2,1,0:T(8,128)(2,1)}, bf16[14,56,128]{2,1,0:T(8,128)(2,1)S(1)}, u32[]{:S(2)}, u32[]{:S(2)}) collective-permute-start(bf16[14,56,128]{2,1,0:T(8,128)(2,1)} %bitcast.4), channel_id=1, source_target_pairs={{0,2},{2,4},{4,6},{6,7},{7,5},{5,3},{3,1},{1,0},{8,9},{10,8},{12,1... | collective-permute-start | bytes 602120 | tf_op jit(solution)/shard_map/ppermute | solution.py:289
  3.0 0.7 %collective-permute-start.2 = (bf16[14,56,128]{2,1,0:T(8,128)(2,1)}, bf16[14,56,128]{2,1,0:T(8,128)(2,1)S(1)}, u32[]{:S(2)}, u32[]{:S(2)}) collective-permute-start(bf16[14,56,128]{2,1,0:T(8,128)(2,1)} %bitcast.5), channel_id=1, source_target_pairs={{0,9},{2,8},{4,10},{6,12},{7,14},{5,15},{3,13},{1,11},{8,2},{10,4}... | collective-permute-start | bytes 602120 | tf_op jit(solution)/shard_map/ppermute | solution.py:289
  4.4 1.6 %join.1.shared = f32[136,512]{1,0:T(8,128)} custom-call(f32[1,128]{1,0:T(1,128)} %bitcast.10, bf16[128,128]{1,0:T(8,128)(2,1)} %left_gate.1, bf16[128,128]{1,0:T(8,128)(2,1)} %left_value.1, bf16[128,128]{1,0:T(8,128)(2,1)} %right_gate.1, bf16[128,128]{1,0:T(8,128)(2,1)} %right_value.1), custom_call_target="tpu_custom_call" | custom-call | bytes 131584 | tf_op jit(solution)/shard_map/join/pallas_call | solution.py:236
  6.0 1.0 %copy-done = f32[136,512]{1,0:T(8,128)S(1)} copy-done((f32[136,512]{1,0:T(8,128)S(1)}, f32[136,512]{1,0:T(8,128)}, u32[]{:S(2)}) %copy-start) | copy-done | bytes 278552
  6.9 0.4 %own_right.2.right = bf16[14,16,128]{2,1,0:T(8,128)(2,1)S(1)} custom-call(s32[1]{0:T(128)S(6)} %copy.11.length, f32[136,512]{1,0:T(8,128)S(1)} %copy-done, bf16[14,56,128]{2,1,0:T(8,128)(2,1)S(1)} %bitcast.6), custom_call_target="tpu_custom_call" | custom-call | bytes 479236 | tf_op jit(solution)/shard_map/own_right/pallas_call | solution.py:236
  7.3 0.4 %collective-permute-done.own = bf16[14,56,128]{2,1,0:T(8,128)(2,1)S(1)} collective-permute-done((bf16[14,56,128]{2,1,0:T(8,128)(2,1)}, bf16[14,56,128]{2,1,0:T(8,128)(2,1)S(1)}, u32[]{:S(2)}, u32[]{:S(2)}) %collective-permute-start) | collective-permute-done | bytes 200736 | tf_op jit(solution)/shard_map/ppermute | solution.py:289
  7.7 2.4 %collective-permute-start.1 = (bf16[14,56,128]{2,1,0:T(8,128)(2,1)S(1)}, bf16[14,56,128]{2,1,0:T(8,128)(2,1)S(1)}, u32[]{:S(2)}, u32[]{:S(2)}) collective-permute-start(bf16[14,56,128]{2,1,0:T(8,128)(2,1)S(1)} %collective-permute-done.own), channel_id=1, source_target_pairs={{0,2},{2,4},{4,6},{6,7},{7,5},{5,3},{3,1},{1,0},{8,9},{10,8},{12,1... | collective-permute-start | bytes 602120 | tf_op jit(solution)/shard_map/ppermute | solution.py:289
  10.1 0.0 collective-permute-done.2.other
  10.1 1.6 %collective-permute-start.4 = (bf16[14,56,128]{2,1,0:T(8,128)(2,1)S(1)}, bf16[14,56,128]{2,1,0:T(8,128)(2,1)S(1)}, u32[]{:S(2)}, u32[]{:S(2)}) collective-permute-start(bf16[14,56,128]{2,1,0:T(8,128)(2,1)S(1)} %collective-permute-done.2.other), channel_id=1, source_target_pairs={{0,2},{2,4},{4,6},{6,7},{7,5},{5,3},{3,1},{1,0},{8,9},{10,8},{12,1... | collective-permute-start | bytes 602120 | tf_op jit(solution)/shard_map/ppermute | solution.py:289
  11.7 0.5 %own_left.2.left = f32[14,56,128]{2,1,0:T(8,128)S(1)} custom-call(s32[1]{0:T(128)S(6)} %copy.11.length, f32[136,512]{1,0:T(8,128)S(1)} %copy-done, bf16[14,56,128]{2,1,0:T(8,128)(2,1)S(1)} %bitcast.7), custom_call_target="tpu_custom_call" | custom-call | bytes 479236 | tf_op jit(solution)/shard_map/own_left/pallas_call | solution.py:236
  12.2 0.1 collective-permute-start.5
  12.2 1.8 %add_both.3 = (f32[14,56,128]{2,1,0:T(8,128)S(1)}, f32[14,56,128]{2,1,0:T(8,128)S(1)}) custom-call(s32[1]{0:T(128)S(6)} %copy.11.length, f32[136,512]{1,0:T(8,128)S(1)} %copy-done, bf16[14,56,128]{2,1,0:T(8,128)(2,1)S(1)} %collective-permute-done.own, bf16[14,56,128]{2,1,0:T(8,128)(2,1)S(1)} %collective-permute-done.2.other), custom_call_target="tpu_custom_call" | custom-call | flops 44957696 | bytes 679940 | tf_op jit(solution)/shard_map/add_both/pallas_call | solution.py:236
  14.0 0.7 %collective-permute-done.1.own = bf16[14,56,128]{2,1,0:T(8,128)(2,1)S(1)} collective-permute-done((bf16[14,56,128]{2,1,0:T(8,128)(2,1)S(1)}, bf16[14,56,128]{2,1,0:T(8,128)(2,1)S(1)}, u32[]{:S(2)}, u32[]{:S(2)}) %collective-permute-start.1) | collective-permute-done | bytes 200736 | tf_op jit(solution)/shard_map/ppermute | solution.py:289
  14.7 1.1 %collective-permute-start.3 = (bf16[14,56,128]{2,1,0:T(8,128)(2,1)S(1)}, bf16[14,56,128]{2,1,0:T(8,128)(2,1)S(1)}, u32[]{:S(2)}, u32[]{:S(2)}) collective-permute-start(bf16[14,56,128]{2,1,0:T(8,128)(2,1)S(1)} %collective-permute-done.1.own), channel_id=1, source_target_pairs={{0,2},{2,4},{4,6},{6,7},{7,5},{5,3},{3,1},{1,0},{8,9},{10,8},{12,1... | collective-permute-start | bytes 602120 | tf_op jit(solution)/shard_map/ppermute | solution.py:289
  15.8 1.0 %collective-permute-done.4.other = bf16[14,56,128]{2,1,0:T(8,128)(2,1)S(1)} collective-permute-done((bf16[14,56,128]{2,1,0:T(8,128)(2,1)S(1)}, bf16[14,56,128]{2,1,0:T(8,128)(2,1)S(1)}, u32[]{:S(2)}, u32[]{:S(2)}) %collective-permute-start.4) | collective-permute-done | bytes 200736 | tf_op jit(solution)/shard_map/ppermute | solution.py:289
  16.9 1.2 %collective-permute-start.7 = (bf16[14,56,128]{2,1,0:T(8,128)(2,1)S(1)}, bf16[14,56,128]{2,1,0:T(8,128)(2,1)S(1)}, u32[]{:S(2)}, u32[]{:S(2)}) collective-permute-start(bf16[14,56,128]{2,1,0:T(8,128)(2,1)S(1)} %collective-permute-done.4.other), channel_id=1, source_target_pairs={{0,2},{2,4},{4,6},{6,7},{7,5},{5,3},{3,1},{1,0},{8,9},{10,8},{12,1... | collective-permute-start | bytes 602120 | tf_op jit(solution)/shard_map/ppermute | solution.py:289
  18.1 0.5 %add_own.1.refs_0_ = f32[14,56,128]{2,1,0:T(8,128)S(1)} custom-call(f32[14,56,128]{2,1,0:T(8,128)S(1)} %own_left.2.left, bf16[14,16,128]{2,1,0:T(8,128)(2,1)S(1)} %own_right.2.right, bf16[14,16,128]{2,1,0:T(8,128)(2,1)S(1)} %collective-permute-done.5.other, f32[14,56,128]{2,1,0:T(8,128)S(1)} %get-tuple-element.38.before), custom_call_target="tpu_custom_call" | custom-call | flops 22478848 | bytes 917504 | tf_op jit(solution)/shard_map/add_own/pallas_call | solution.py:236
  18.6 1.8 %add_both.4 = (f32[14,56,128]{2,1,0:T(8,128)S(1)}, f32[14,56,128]{2,1,0:T(8,128)S(1)}) custom-call(s32[1]{0:T(128)S(6)} %copy.11.length, f32[136,512]{1,0:T(8,128)S(1)} %copy-done.1, bf16[14,56,128]{2,1,0:T(8,128)(2,1)S(1)} %collective-permute-done.1.own, bf16[14,56,128]{2,1,0:T(8,128)(2,1)S(1)} %collective-permute-done.4.other, ...), custom_call_target="tpu_custom_call" | custom-call | flops 44957696 | bytes 1482756 | tf_op jit(solution)/shard_map/add_both/pallas_call | solution.py:236
  20.3 0.1 collective-permute-done.3.own
  20.4 1.5 %collective-permute-start.6 = (bf16[14,56,128]{2,1,0:T(8,128)(2,1)S(1)}, bf16[14,56,128]{2,1,0:T(8,128)(2,1)S(1)}, u32[]{:S(2)}, u32[]{:S(2)}) collective-permute-start(bf16[14,56,128]{2,1,0:T(8,128)(2,1)S(1)} %collective-permute-done.3.own), channel_id=1, source_target_pairs={{0,2},{2,4},{4,6},{6,7},{7,5},{5,3},{3,1},{1,0},{8,9},{10,8},{12,1... | collective-permute-start | bytes 602120 | tf_op jit(solution)/shard_map/ppermute | solution.py:289
  21.9 0.7 %collective-permute-done.7.other = bf16[14,56,128]{2,1,0:T(8,128)(2,1)S(1)} collective-permute-done((bf16[14,56,128]{2,1,0:T(8,128)(2,1)S(1)}, bf16[14,56,128]{2,1,0:T(8,128)(2,1)S(1)}, u32[]{:S(2)}, u32[]{:S(2)}) %collective-permute-start.7) | collective-permute-done | bytes 200736 | tf_op jit(solution)/shard_map/ppermute | solution.py:289
  22.6 1.8 %add_both.5 = (f32[14,56,128]{2,1,0:T(8,128)S(1)}, bf16[14,56,128]{2,1,0:T(8,128)(2,1)S(1)}) custom-call(s32[1]{0:T(128)S(6)} %copy.11.length, f32[136,512]{1,0:T(8,128)S(1)} %copy-done.1, bf16[14,56,128]{2,1,0:T(8,128)(2,1)S(1)} %collective-permute-done.3.own, bf16[14,56,128]{2,1,0:T(8,128)(2,1)S(1)} %collective-permute-done.7.other, ...), custom_call_target="tpu_custom_call" | custom-call | flops 44957696 | bytes 1482756 | tf_op jit(solution)/shard_map/add_both/pallas_call | solution.py:236
  24.4 0.0 copy-start.5
  24.4 0.1 collective-permute-start.9
  24.5 0.5 %copy-done.5 = f32[128]{0:T(128)S(1)} copy-done((f32[128]{0:T(128)S(1)}, f32[128]{0:T(128)}, u32[]{:S(2)}) %copy-start.5) | copy-done | bytes 536
  25.0 0.5 %gate.1 = (f32[14,56,128]{2,1,0:T(8,128)S(1)}, f32[1,128]{1,0:T(1,128)S(1)}, bf16[128,128]{1,0:T(8,128)(2,1)S(1)}) custom-call(s32[1]{0:T(128)S(6)} %copy.11.length, f32[136,512]{1,0:T(8,128)S(1)} %copy-done.1, bf16[14,56,128]{2,1,0:T(8,128)(2,1)S(1)} %bitcast.8, bf16[128,128]{1,0:T(8,128)(2,1)S(1)} %copy-done.3, f32[1,128]{1,0:T(1,128)S(1)} %bitcast.9, ...), custom_call_target="tpu_custom_call" | custom-call | flops 25690112 | bytes 545284 | tf_op jit(solution)/shard_map/gate/pallas_call | solution.py:236
  25.5 0.6 %collective-permute-done.6.own = bf16[14,56,128]{2,1,0:T(8,128)(2,1)S(1)} collective-permute-done((bf16[14,56,128]{2,1,0:T(8,128)(2,1)S(1)}, bf16[14,56,128]{2,1,0:T(8,128)(2,1)S(1)}, u32[]{:S(2)}, u32[]{:S(2)}) %collective-permute-start.6) | collective-permute-done | bytes 200736 | tf_op jit(solution)/shard_map/ppermute | solution.py:289
  26.1 0.4 %own_right.3.right = bf16[14,16,128]{2,1,0:T(8,128)(2,1)S(1)} custom-call(s32[1]{0:T(128)S(6)} %copy.11.length, f32[136,512]{1,0:T(8,128)S(1)} %copy-done.1, bf16[14,56,128]{2,1,0:T(8,128)(2,1)S(1)} %collective-permute-done.6.own), custom_call_target="tpu_custom_call" | custom-call | bytes 479236 | tf_op jit(solution)/shard_map/own_right/pallas_call | solution.py:236
  26.5 0.1 collective-permute-start.8
  26.6 0.5 %own_left.3.left = f32[14,56,128]{2,1,0:T(8,128)S(1)} custom-call(s32[1]{0:T(128)S(6)} %copy.11.length, f32[136,512]{1,0:T(8,128)S(1)} %copy-done.1, bf16[14,56,128]{2,1,0:T(8,128)(2,1)S(1)} %collective-permute-done.6.own), custom_call_target="tpu_custom_call" | custom-call | bytes 479236 | tf_op jit(solution)/shard_map/own_left/pallas_call | solution.py:236
  27.1 0.7 %collective-permute-done.8.other = bf16[14,16,128]{2,1,0:T(8,128)(2,1)S(1)} collective-permute-done((bf16[14,16,128]{2,1,0:T(8,128)(2,1)S(1)}, bf16[14,16,128]{2,1,0:T(8,128)(2,1)S(1)}, u32[]{:S(2)}, u32[]{:S(2)}) %collective-permute-start.8) | collective-permute-done | bytes 57376 | tf_op jit(solution)/shard_map/ppermute | solution.py:292
  27.8 1.6 %finish.1 = bf16[14,56,128]{2,1,0:T(8,128)(2,1)} custom-call(f32[14,56,128]{2,1,0:T(8,128)S(1)} %own_left.3.left, bf16[14,16,128]{2,1,0:T(8,128)(2,1)S(1)} %own_right.3.right, bf16[14,16,128]{2,1,0:T(8,128)(2,1)S(1)} %collective-permute-done.8.other, f32[14,56,128]{2,1,0:T(8,128)S(1)} %get-tuple-element.48.mine, ...), custom_call_target="tpu_custom_call" | custom-call | flops 22478848 | bytes 1552896 | tf_op jit(solution)/shard_map/finish/pallas_call | solution.py:236
  (11 shorter events, 0.0 us)
Async XLA Ops:
  0.0 7.7 %collective-permute-start = (bf16[14,56,128]{2,1,0:T(8,128)(2,1)}, bf16[14,56,128]{2,1,0:T(8,128)(2,1)S(1)}, u32[]{:S(2)}, u32[]{:S(2)}) collective-permute-start(bf16[14,56,128]{2,1,0:T(8,128)(2,1)} %bitcast.4), channel_id=1, source_target_pairs={{0,2},{2,4},{4,6},{6,7},{7,5},{5,3},{3,1},{1,0},{8,9},{10,8},{12,1... | collective-permute-start | bytes 602120 | tf_op jit(solution)/shard_map/ppermute | solution.py:289
  3.0 7.1 %collective-permute-start.2 = (bf16[14,56,128]{2,1,0:T(8,128)(2,1)}, bf16[14,56,128]{2,1,0:T(8,128)(2,1)S(1)}, u32[]{:S(2)}, u32[]{:S(2)}) collective-permute-start(bf16[14,56,128]{2,1,0:T(8,128)(2,1)} %bitcast.5), channel_id=1, source_target_pairs={{0,9},{2,8},{4,10},{6,12},{7,14},{5,15},{3,13},{1,11},{8,2},{10,4}... | collective-permute-start | bytes 602120 | tf_op jit(solution)/shard_map/ppermute | solution.py:289
  4.4 1.6 %copy-start.2 = (bf16[56,14,128]{2,0,1:T(8,128)(2,1)S(1)}, bf16[56,14,128]{2,0,1:T(8,128)(2,1)}, u32[]{:S(2)}) copy-start(bf16[56,14,128]{2,0,1:T(8,128)(2,1)} %param.10) | copy-start | bytes 602116
  6.0 1.0 %copy-start = (f32[136,512]{1,0:T(8,128)S(1)}, f32[136,512]{1,0:T(8,128)}, u32[]{:S(2)}) copy-start(f32[136,512]{1,0:T(8,128)} %join.1.shared) | copy-start | bytes 835588
  7.7 7.0 %collective-permute-start.1 = (bf16[14,56,128]{2,1,0:T(8,128)(2,1)S(1)}, bf16[14,56,128]{2,1,0:T(8,128)(2,1)S(1)}, u32[]{:S(2)}, u32[]{:S(2)}) collective-permute-start(bf16[14,56,128]{2,1,0:T(8,128)(2,1)S(1)} %collective-permute-done.own), channel_id=1, source_target_pairs={{0,2},{2,4},{4,6},{6,7},{7,5},{5,3},{3,1},{1,0},{8,9},{10,8},{12,1... | collective-permute-start | bytes 602120 | tf_op jit(solution)/shard_map/ppermute | solution.py:289
  10.1 6.8 %collective-permute-start.4 = (bf16[14,56,128]{2,1,0:T(8,128)(2,1)S(1)}, bf16[14,56,128]{2,1,0:T(8,128)(2,1)S(1)}, u32[]{:S(2)}, u32[]{:S(2)}) collective-permute-start(bf16[14,56,128]{2,1,0:T(8,128)(2,1)S(1)} %collective-permute-done.2.other), channel_id=1, source_target_pairs={{0,2},{2,4},{4,6},{6,7},{7,5},{5,3},{3,1},{1,0},{8,9},{10,8},{12,1... | collective-permute-start | bytes 602120 | tf_op jit(solution)/shard_map/ppermute | solution.py:289
  12.2 4.7 %collective-permute-start.5 = (bf16[14,16,128]{2,1,0:T(8,128)(2,1)S(1)}, bf16[14,16,128]{2,1,0:T(8,128)(2,1)S(1)}, u32[]{:S(2)}, u32[]{:S(2)}) collective-permute-start(bf16[14,16,128]{2,1,0:T(8,128)(2,1)S(1)} %own_right.2.right), channel_id=1, source_target_pairs={{0,8},{8,0},{1,9},{9,1},{2,10},{10,2},{3,11},{11,3},{4,12},{12,4},... | collective-permute-start | bytes 172040 | tf_op jit(solution)/shard_map/ppermute | solution.py:292
  14.7 3.8 %copy-start.1 = (f32[136,512]{1,0:T(8,128)S(1)}, f32[136,512]{1,0:T(8,128)}, u32[]{:S(2)}) copy-start(f32[136,512]{1,0:T(8,128)} %join.1.shared) | copy-start | bytes 835588
  14.7 5.7 %collective-permute-start.3 = (bf16[14,56,128]{2,1,0:T(8,128)(2,1)S(1)}, bf16[14,56,128]{2,1,0:T(8,128)(2,1)S(1)}, u32[]{:S(2)}, u32[]{:S(2)}) collective-permute-start(bf16[14,56,128]{2,1,0:T(8,128)(2,1)S(1)} %collective-permute-done.1.own), channel_id=1, source_target_pairs={{0,2},{2,4},{4,6},{6,7},{7,5},{5,3},{3,1},{1,0},{8,9},{10,8},{12,1... | collective-permute-start | bytes 602120 | tf_op jit(solution)/shard_map/ppermute | solution.py:289
  16.9 5.7 %collective-permute-start.7 = (bf16[14,56,128]{2,1,0:T(8,128)(2,1)S(1)}, bf16[14,56,128]{2,1,0:T(8,128)(2,1)S(1)}, u32[]{:S(2)}, u32[]{:S(2)}) collective-permute-start(bf16[14,56,128]{2,1,0:T(8,128)(2,1)S(1)} %collective-permute-done.4.other), channel_id=1, source_target_pairs={{0,2},{2,4},{4,6},{6,7},{7,5},{5,3},{3,1},{1,0},{8,9},{10,8},{12,1... | collective-permute-start | bytes 602120 | tf_op jit(solution)/shard_map/ppermute | solution.py:289
  20.4 4.0 %copy-start.3 = (bf16[128,128]{1,0:T(8,128)(2,1)S(1)}, bf16[128,128]{1,0:T(8,128)(2,1)}, u32[]{:S(2)}) copy-start(bf16[128,128]{1,0:T(8,128)(2,1)} %out_gate.1) | copy-start | bytes 98308
  20.4 4.0 %copy-start.4 = (bf16[128,128]{1,0:T(8,128)(2,1)S(1)}, bf16[128,128]{1,0:T(8,128)(2,1)}, u32[]{:S(2)}) copy-start(bf16[128,128]{1,0:T(8,128)(2,1)} %last_weight.1) | copy-start | bytes 98308
  20.4 5.7 %collective-permute-start.6 = (bf16[14,56,128]{2,1,0:T(8,128)(2,1)S(1)}, bf16[14,56,128]{2,1,0:T(8,128)(2,1)S(1)}, u32[]{:S(2)}, u32[]{:S(2)}) collective-permute-start(bf16[14,56,128]{2,1,0:T(8,128)(2,1)S(1)} %collective-permute-done.3.own), channel_id=1, source_target_pairs={{0,2},{2,4},{4,6},{6,7},{7,5},{5,3},{3,1},{1,0},{8,9},{10,8},{12,1... | collective-permute-start | bytes 602120 | tf_op jit(solution)/shard_map/ppermute | solution.py:289
  24.4 0.7 %copy-start.5 = (f32[128]{0:T(128)S(1)}, f32[128]{0:T(128)}, u32[]{:S(2)}) copy-start(f32[128]{0:T(128)} %param.18) | copy-start | bytes 1540
  24.4 2.7 %collective-permute-start.9 = (bf16[14,56,128]{2,1,0:T(8,128)(2,1)S(1)}, bf16[14,56,128]{2,1,0:T(8,128)(2,1)S(1)}, u32[]{:S(2)}, u32[]{:S(2)}) collective-permute-start(bf16[14,56,128]{2,1,0:T(8,128)(2,1)S(1)} %get-tuple-element.49), channel_id=1, source_target_pairs={{0,8},{8,0},{1,9},{9,1},{2,10},{10,2},{3,11},{11,3},{4,12},{12,4},... | collective-permute-start | bytes 602120 | tf_op jit(solution)/shard_map/ppermute | solution.py:292
  26.5 1.3 %collective-permute-start.8 = (bf16[14,16,128]{2,1,0:T(8,128)(2,1)S(1)}, bf16[14,16,128]{2,1,0:T(8,128)(2,1)S(1)}, u32[]{:S(2)}, u32[]{:S(2)}) collective-permute-start(bf16[14,16,128]{2,1,0:T(8,128)(2,1)S(1)} %own_right.3.right), channel_id=1, source_target_pairs={{0,8},{8,0},{1,9},{9,1},{2,10},{10,2},{3,11},{11,3},{4,12},{12,4},... | collective-permute-start | bytes 172040 | tf_op jit(solution)/shard_map/ppermute | solution.py:292

commit v23 on v16

--- a/solution.py
+++ b/solution.py
@@ -113,7 +113,7 @@
 
 def column_from(s, distance):
     row, col = lax.axis_index("row"), lax.axis_index("col")
-    step = distance * (2 * row - 1)
+    step = distance * (1 - 2 * row)
     return column_at((place_of(col, s.cols) + step + s.cols) % s.cols, s.cols)
 
 
@@ -280,7 +280,7 @@
         for row in range(s.rows):
             target = s.rows - 1 - row if crossed else row
             for at in range(s.cols):
-                to = (at + by * (1 - 2 * target)) % s.cols
+                to = (at + by * (2 * target - 1)) % s.cols
                 pairs.append((row * s.cols + order[at], target * s.cols + order[to]))
         return lax.ppermute(block, ("row", "col"), pairs)
 

time: 29.3 us -> 29.4 us (level)
  waiting for transfers between devices: 4.68 us -> 5.02 us
    ppermute x7, waiting for transfers between devices: 3.94 us -> 4.29 us  [shift(): return lax.ppermute(block, ('row', 'col'), pairs)]
where the time goes in v23:
time: 29.4 us; the launch traced here: 29.2 us
  starting transfers between devices  11.6 us (39%)
  Pallas kernels  10.9 us (37%)
  waiting for transfers between devices  5.02 us (17%)
  local copies, waits for them, and re-layouts  0.97 us (3%)
  between operations  0.77 us (3%)
    ppermute x7, starting transfers between devices, shift(): return lax.ppermute(block, ('row', 'col'), pairs)  11 us
    pallas_call x9, Pallas kernels, call(): pl.pallas_call(body, out_shape=out_shape, in_specs=[space(o) for o in ope...  10.9 us
    ppermute x7, waiting for transfers between devices, shift(): return lax.ppermute(block, ('row', 'col'), pairs)  4.29 us
    unnamed x10, local copies, waits for them, and re-layouts  0.97 us
    ppermute x3, waiting for transfers between devices, swap(): lax.ppermute(block, 'row', [(at, (at + 1) % s.rows) for at in range(s.row...  0.73 us
    ppermute x3, starting transfers between devices, swap(): lax.ppermute(block, 'row', [(at, (at + 1) % s.rows) for at in range(s.row...  0.59 us
  transfers between devices with their start and end apart: 10, of which 6 were waited for; matrix products, arithmetic and copies ran while one was open for 0% of the time, Pallas kernels for 32%

profile of v23, /device:TPU:0, one launch (start us, length us, event | category | flops | bytes accessed | tf_op | source)
XLA Modules:
  0.0 29.2 jit_solution(13515486058420035649)
XLA Ops:
  0.0 0.5 %collective-permute-start.1 = (bf16[14,56,128]{2,1,0:T(8,128)(2,1)}, bf16[14,56,128]{2,1,0:T(8,128)(2,1)S(1)}, u32[]{:S(2)}, u32[]{:S(2)}) collective-permute-start(bf16[14,56,128]{2,1,0:T(8,128)(2,1)} %bitcast.4), channel_id=1, source_target_pairs={{0,8},{8,0},{1,9},{9,1},{2,10},{10,2},{3,11},{11,3},{4,12},{12,4},... | collective-permute-start | bytes 602120 | tf_op jit(solution)/shard_map/ppermute | solution.py:288
  0.5 2.5 %collective-permute-start = (bf16[14,56,128]{2,1,0:T(8,128)(2,1)}, bf16[14,56,128]{2,1,0:T(8,128)(2,1)S(1)}, u32[]{:S(2)}, u32[]{:S(2)}) collective-permute-start(bf16[14,56,128]{2,1,0:T(8,128)(2,1)} %bitcast.5), channel_id=1, source_target_pairs={{0,1},{2,0},{4,2},{6,4},{7,6},{5,7},{3,5},{1,3},{8,10},{10,12},{12... | collective-permute-start | bytes 602120 | tf_op jit(solution)/shard_map/ppermute | solution.py:285
  3.0 1.5 %collective-permute-start.3 = (bf16[14,56,128]{2,1,0:T(8,128)(2,1)}, bf16[14,56,128]{2,1,0:T(8,128)(2,1)S(1)}, u32[]{:S(2)}, u32[]{:S(2)}) collective-permute-start(bf16[14,56,128]{2,1,0:T(8,128)(2,1)} %bitcast.6), channel_id=1, source_target_pairs={{0,10},{2,12},{4,14},{6,15},{7,13},{5,11},{3,9},{1,8},{8,1},{10,0}... | collective-permute-start | bytes 602120 | tf_op jit(solution)/shard_map/ppermute | solution.py:285
  5.1 1.6 %join.1.shared = f32[136,512]{1,0:T(8,128)} custom-call(f32[1,128]{1,0:T(1,128)} %bitcast.10, bf16[128,128]{1,0:T(8,128)(2,1)} %left_gate.1, bf16[128,128]{1,0:T(8,128)(2,1)} %left_value.1, bf16[128,128]{1,0:T(8,128)(2,1)} %right_gate.1, bf16[128,128]{1,0:T(8,128)(2,1)} %right_value.1), custom_call_target="tpu_custom_call" | custom-call | bytes 131584 | tf_op jit(solution)/shard_map/join/pallas_call | solution.py:232
  6.7 0.0 collective-permute-done.1.other
  6.7 0.0 copy-done.1
  6.7 1.0 %copy-done = f32[136,512]{1,0:T(8,128)S(1)} copy-done((f32[136,512]{1,0:T(8,128)S(1)}, f32[136,512]{1,0:T(8,128)}, u32[]{:S(2)}) %copy-start) | copy-done | bytes 278552
  7.7 1.0 %add_both.4 = (f32[14,56,128]{2,1,0:T(8,128)S(1)}, f32[14,56,128]{2,1,0:T(8,128)S(1)}) custom-call(s32[1]{0:T(128)S(6)} %copy.11.length, f32[136,512]{1,0:T(8,128)S(1)} %copy-done, bf16[14,56,128]{2,1,0:T(8,128)(2,1)S(1)} %bitcast.7, bf16[14,56,128]{2,1,0:T(8,128)(2,1)S(1)} %collective-permute-done.1.other), custom_call_target="tpu_custom_call" | custom-call | flops 22478848 | bytes 679940 | tf_op jit(solution)/shard_map/add_both/pallas_call | solution.py:232
  8.7 0.0 collective-permute-done.own
  8.7 0.0 copy-start.4
  8.7 1.4 %collective-permute-start.2 = (bf16[14,56,128]{2,1,0:T(8,128)(2,1)S(1)}, bf16[14,56,128]{2,1,0:T(8,128)(2,1)S(1)}, u32[]{:S(2)}, u32[]{:S(2)}) collective-permute-start(bf16[14,56,128]{2,1,0:T(8,128)(2,1)S(1)} %collective-permute-done.own), channel_id=1, source_target_pairs={{0,1},{2,0},{4,2},{6,4},{7,6},{5,7},{3,5},{1,3},{8,10},{10,12},{12... | collective-permute-start | bytes 602120 | tf_op jit(solution)/shard_map/ppermute | solution.py:285
  10.0 0.0 collective-permute-done.3.other
  10.0 1.6 %collective-permute-start.5 = (bf16[14,56,128]{2,1,0:T(8,128)(2,1)S(1)}, bf16[14,56,128]{2,1,0:T(8,128)(2,1)S(1)}, u32[]{:S(2)}, u32[]{:S(2)}) collective-permute-start(bf16[14,56,128]{2,1,0:T(8,128)(2,1)S(1)} %collective-permute-done.3.other), channel_id=1, source_target_pairs={{0,1},{2,0},{4,2},{6,4},{7,6},{5,7},{3,5},{1,3},{8,10},{10,12},{12... | collective-permute-start | bytes 602120 | tf_op jit(solution)/shard_map/ppermute | solution.py:285
  11.6 0.5 %gate.1 = (f32[14,56,128]{2,1,0:T(8,128)S(1)}, f32[1,128]{1,0:T(1,128)S(1)}, bf16[128,128]{1,0:T(8,128)(2,1)S(1)}) custom-call(s32[1]{0:T(128)S(6)} %copy.11.length, f32[136,512]{1,0:T(8,128)S(1)} %copy-done, bf16[14,56,128]{2,1,0:T(8,128)(2,1)S(1)} %bitcast.8, bf16[128,128]{1,0:T(8,128)(2,1)S(1)} %copy-done.2, f32[1,128]{1,0:T(1,128)S(1)} %bitcast.9, ...), custom_call_target="tpu_custom_call" | custom-call | flops 25690112 | bytes 545284 | tf_op jit(solution)/shard_map/gate/pallas_call | solution.py:232
  12.1 1.8 %add_both.5 = (f32[14,56,128]{2,1,0:T(8,128)S(1)}, f32[14,56,128]{2,1,0:T(8,128)S(1)}) custom-call(s32[1]{0:T(128)S(6)} %copy.11.length, f32[136,512]{1,0:T(8,128)S(1)} %copy-done, bf16[14,56,128]{2,1,0:T(8,128)(2,1)S(1)} %collective-permute-done.own, bf16[14,56,128]{2,1,0:T(8,128)(2,1)S(1)} %collective-permute-done.3.other, ...), custom_call_target="tpu_custom_call" | custom-call | flops 44957696 | bytes 1482756 | tf_op jit(solution)/shard_map/add_both/pallas_call | solution.py:232
  13.9 0.6 %collective-permute-done.2.own = bf16[14,56,128]{2,1,0:T(8,128)(2,1)S(1)} collective-permute-done((bf16[14,56,128]{2,1,0:T(8,128)(2,1)S(1)}, bf16[14,56,128]{2,1,0:T(8,128)(2,1)S(1)}, u32[]{:S(2)}, u32[]{:S(2)}) %collective-permute-start.2) | collective-permute-done | bytes 200736 | tf_op jit(solution)/shard_map/ppermute | solution.py:285
  14.5 1.3 %collective-permute-start.4 = (bf16[14,56,128]{2,1,0:T(8,128)(2,1)S(1)}, bf16[14,56,128]{2,1,0:T(8,128)(2,1)S(1)}, u32[]{:S(2)}, u32[]{:S(2)}) collective-permute-start(bf16[14,56,128]{2,1,0:T(8,128)(2,1)S(1)} %collective-permute-done.2.own), channel_id=1, source_target_pairs={{0,1},{2,0},{4,2},{6,4},{7,6},{5,7},{3,5},{1,3},{8,10},{10,12},{12... | collective-permute-start | bytes 602120 | tf_op jit(solution)/shard_map/ppermute | solution.py:285
  15.8 0.9 %collective-permute-done.5.other = bf16[14,56,128]{2,1,0:T(8,128)(2,1)S(1)} collective-permute-done((bf16[14,56,128]{2,1,0:T(8,128)(2,1)S(1)}, bf16[14,56,128]{2,1,0:T(8,128)(2,1)S(1)}, u32[]{:S(2)}, u32[]{:S(2)}) %collective-permute-start.5) | collective-permute-done | bytes 200736 | tf_op jit(solution)/shard_map/ppermute | solution.py:285
  16.6 1.5 %collective-permute-start.7 = (bf16[14,56,128]{2,1,0:T(8,128)(2,1)S(1)}, bf16[14,56,128]{2,1,0:T(8,128)(2,1)S(1)}, u32[]{:S(2)}, u32[]{:S(2)}) collective-permute-start(bf16[14,56,128]{2,1,0:T(8,128)(2,1)S(1)} %collective-permute-done.5.other), channel_id=1, source_target_pairs={{0,1},{2,0},{4,2},{6,4},{7,6},{5,7},{3,5},{1,3},{8,10},{10,12},{12... | collective-permute-start | bytes 602120 | tf_op jit(solution)/shard_map/ppermute | solution.py:285
  18.1 1.8 %add_both.6 = (f32[14,56,128]{2,1,0:T(8,128)S(1)}, f32[14,56,128]{2,1,0:T(8,128)S(1)}) custom-call(s32[1]{0:T(128)S(6)} %copy.11.length, f32[136,512]{1,0:T(8,128)S(1)} %copy-done, bf16[14,56,128]{2,1,0:T(8,128)(2,1)S(1)} %collective-permute-done.2.own, bf16[14,56,128]{2,1,0:T(8,128)(2,1)S(1)} %collective-permute-done.5.other, ...), custom_call_target="tpu_custom_call" | custom-call | flops 44957696 | bytes 1482756 | tf_op jit(solution)/shard_map/add_both/pallas_call | solution.py:232
  19.8 0.3 %collective-permute-done.4.own = bf16[14,56,128]{2,1,0:T(8,128)(2,1)S(1)} collective-permute-done((bf16[14,56,128]{2,1,0:T(8,128)(2,1)S(1)}, bf16[14,56,128]{2,1,0:T(8,128)(2,1)S(1)}, u32[]{:S(2)}, u32[]{:S(2)}) %collective-permute-start.4) | collective-permute-done | bytes 200736 | tf_op jit(solution)/shard_map/ppermute | solution.py:285
  20.2 1.3 %collective-permute-start.6 = (bf16[14,56,128]{2,1,0:T(8,128)(2,1)S(1)}, bf16[14,56,128]{2,1,0:T(8,128)(2,1)S(1)}, u32[]{:S(2)}, u32[]{:S(2)}) collective-permute-start(bf16[14,56,128]{2,1,0:T(8,128)(2,1)S(1)} %collective-permute-done.4.own), channel_id=1, source_target_pairs={{0,1},{2,0},{4,2},{6,4},{7,6},{5,7},{3,5},{1,3},{8,10},{10,12},{12... | collective-permute-start | bytes 602120 | tf_op jit(solution)/shard_map/ppermute | solution.py:285
  21.5 0.9 %collective-permute-done.7.other = bf16[14,56,128]{2,1,0:T(8,128)(2,1)S(1)} collective-permute-done((bf16[14,56,128]{2,1,0:T(8,128)(2,1)S(1)}, bf16[14,56,128]{2,1,0:T(8,128)(2,1)S(1)}, u32[]{:S(2)}, u32[]{:S(2)}) %collective-permute-start.7) | collective-permute-done | bytes 200736 | tf_op jit(solution)/shard_map/ppermute | solution.py:285
  22.3 1.8 %add_both.7 = (f32[14,56,128]{2,1,0:T(8,128)S(1)}, bf16[14,56,128]{2,1,0:T(8,128)(2,1)S(1)}) custom-call(s32[1]{0:T(128)S(6)} %copy.11.length, f32[136,512]{1,0:T(8,128)S(1)} %copy-done, bf16[14,56,128]{2,1,0:T(8,128)(2,1)S(1)} %collective-permute-done.4.own, bf16[14,56,128]{2,1,0:T(8,128)(2,1)S(1)} %collective-permute-done.7.other, ...), custom_call_target="tpu_custom_call" | custom-call | flops 44957696 | bytes 1482756 | tf_op jit(solution)/shard_map/add_both/pallas_call | solution.py:232
  24.1 0.1 collective-permute-start.9
  24.2 1.7 %collective-permute-done.6.own = bf16[14,56,128]{2,1,0:T(8,128)(2,1)S(1)} collective-permute-done((bf16[14,56,128]{2,1,0:T(8,128)(2,1)S(1)}, bf16[14,56,128]{2,1,0:T(8,128)(2,1)S(1)}, u32[]{:S(2)}, u32[]{:S(2)}) %collective-permute-start.6) | collective-permute-done | bytes 200736 | tf_op jit(solution)/shard_map/ppermute | solution.py:285
  25.9 0.4 %last_right.1.right = bf16[14,16,128]{2,1,0:T(8,128)(2,1)S(1)} custom-call(s32[1]{0:T(128)S(6)} %copy.11.length, f32[136,512]{1,0:T(8,128)S(1)} %copy-done, bf16[14,56,128]{2,1,0:T(8,128)(2,1)S(1)} %collective-permute-done.6.own), custom_call_target="tpu_custom_call" | custom-call | bytes 479236 | tf_op jit(solution)/shard_map/last_right/pallas_call | solution.py:232
  26.3 0.1 collective-permute-start.8
  26.3 0.5 %last_left.1.left = f32[14,56,128]{2,1,0:T(8,128)S(1)} custom-call(s32[1]{0:T(128)S(6)} %copy.11.length, f32[136,512]{1,0:T(8,128)S(1)} %copy-done, bf16[14,56,128]{2,1,0:T(8,128)(2,1)S(1)} %collective-permute-done.6.own), custom_call_target="tpu_custom_call" | custom-call | bytes 479236 | tf_op jit(solution)/shard_map/last_left/pallas_call | solution.py:232
  26.8 0.0 collective-permute-done.9.given
  26.8 0.7 %collective-permute-done.8.other = bf16[14,16,128]{2,1,0:T(8,128)(2,1)S(1)} collective-permute-done((bf16[14,16,128]{2,1,0:T(8,128)(2,1)S(1)}, bf16[14,16,128]{2,1,0:T(8,128)(2,1)S(1)}, u32[]{:S(2)}, u32[]{:S(2)}) %collective-permute-start.8) | collective-permute-done | bytes 57376 | tf_op jit(solution)/shard_map/ppermute | solution.py:288
  27.6 1.6 %finish.1 = bf16[14,56,128]{2,1,0:T(8,128)(2,1)} custom-call(f32[14,56,128]{2,1,0:T(8,128)S(1)} %last_left.1.left, bf16[14,16,128]{2,1,0:T(8,128)(2,1)S(1)} %last_right.1.right, bf16[14,16,128]{2,1,0:T(8,128)(2,1)S(1)} %collective-permute-done.8.other, f32[14,56,128]{2,1,0:T(8,128)S(1)} %get-tuple-element.44.mine, ...), custom_call_target="tpu_custom_call" | custom-call | flops 22478848 | bytes 1552896 | tf_op jit(solution)/shard_map/finish/pallas_call | solution.py:232
  (7 shorter events, 0.0 us)
Async XLA Ops:
  0.0 6.7 %collective-permute-start.1 = (bf16[14,56,128]{2,1,0:T(8,128)(2,1)}, bf16[14,56,128]{2,1,0:T(8,128)(2,1)S(1)}, u32[]{:S(2)}, u32[]{:S(2)}) collective-permute-start(bf16[14,56,128]{2,1,0:T(8,128)(2,1)} %bitcast.4), channel_id=1, source_target_pairs={{0,8},{8,0},{1,9},{9,1},{2,10},{10,2},{3,11},{11,3},{4,12},{12,4},... | collective-permute-start | bytes 602120 | tf_op jit(solution)/shard_map/ppermute | solution.py:288
  0.5 8.2 %collective-permute-start = (bf16[14,56,128]{2,1,0:T(8,128)(2,1)}, bf16[14,56,128]{2,1,0:T(8,128)(2,1)S(1)}, u32[]{:S(2)}, u32[]{:S(2)}) collective-permute-start(bf16[14,56,128]{2,1,0:T(8,128)(2,1)} %bitcast.5), channel_id=1, source_target_pairs={{0,1},{2,0},{4,2},{6,4},{7,6},{5,7},{3,5},{1,3},{8,10},{10,12},{12... | collective-permute-start | bytes 602120 | tf_op jit(solution)/shard_map/ppermute | solution.py:285
  3.0 7.1 %collective-permute-start.3 = (bf16[14,56,128]{2,1,0:T(8,128)(2,1)}, bf16[14,56,128]{2,1,0:T(8,128)(2,1)S(1)}, u32[]{:S(2)}, u32[]{:S(2)}) collective-permute-start(bf16[14,56,128]{2,1,0:T(8,128)(2,1)} %bitcast.6), channel_id=1, source_target_pairs={{0,10},{2,12},{4,14},{6,15},{7,13},{5,11},{3,9},{1,8},{8,1},{10,0}... | collective-permute-start | bytes 602120 | tf_op jit(solution)/shard_map/ppermute | solution.py:285
  5.1 1.6 %copy-start.1 = (bf16[56,14,128]{2,0,1:T(8,128)(2,1)S(1)}, bf16[56,14,128]{2,0,1:T(8,128)(2,1)}, u32[]{:S(2)}) copy-start(bf16[56,14,128]{2,0,1:T(8,128)(2,1)} %param.10) | copy-start | bytes 602116
  6.7 1.0 %copy-start = (f32[136,512]{1,0:T(8,128)S(1)}, f32[136,512]{1,0:T(8,128)}, u32[]{:S(2)}) copy-start(f32[136,512]{1,0:T(8,128)} %join.1.shared) | copy-start | bytes 835588
  7.7 4.0 %copy-start.2 = (bf16[128,128]{1,0:T(8,128)(2,1)S(1)}, bf16[128,128]{1,0:T(8,128)(2,1)}, u32[]{:S(2)}) copy-start(bf16[128,128]{1,0:T(8,128)(2,1)} %out_gate.1) | copy-start | bytes 98308
  7.7 4.0 %copy-start.3 = (bf16[128,128]{1,0:T(8,128)(2,1)S(1)}, bf16[128,128]{1,0:T(8,128)(2,1)}, u32[]{:S(2)}) copy-start(bf16[128,128]{1,0:T(8,128)(2,1)} %last_weight.1) | copy-start | bytes 98308
  8.7 3.0 %copy-start.4 = (f32[128]{0:T(128)S(1)}, f32[128]{0:T(128)}, u32[]{:S(2)}) copy-start(f32[128]{0:T(128)} %param.18) | copy-start | bytes 1540
  8.7 5.8 %collective-permute-start.2 = (bf16[14,56,128]{2,1,0:T(8,128)(2,1)S(1)}, bf16[14,56,128]{2,1,0:T(8,128)(2,1)S(1)}, u32[]{:S(2)}, u32[]{:S(2)}) collective-permute-start(bf16[14,56,128]{2,1,0:T(8,128)(2,1)S(1)} %collective-permute-done.own), channel_id=1, source_target_pairs={{0,1},{2,0},{4,2},{6,4},{7,6},{5,7},{3,5},{1,3},{8,10},{10,12},{12... | collective-permute-start | bytes 602120 | tf_op jit(solution)/shard_map/ppermute | solution.py:285
  10.0 6.6 %collective-permute-start.5 = (bf16[14,56,128]{2,1,0:T(8,128)(2,1)S(1)}, bf16[14,56,128]{2,1,0:T(8,128)(2,1)S(1)}, u32[]{:S(2)}, u32[]{:S(2)}) collective-permute-start(bf16[14,56,128]{2,1,0:T(8,128)(2,1)S(1)} %collective-permute-done.3.other), channel_id=1, source_target_pairs={{0,1},{2,0},{4,2},{6,4},{7,6},{5,7},{3,5},{1,3},{8,10},{10,12},{12... | collective-permute-start | bytes 602120 | tf_op jit(solution)/shard_map/ppermute | solution.py:285
  14.5 5.7 %collective-permute-start.4 = (bf16[14,56,128]{2,1,0:T(8,128)(2,1)S(1)}, bf16[14,56,128]{2,1,0:T(8,128)(2,1)S(1)}, u32[]{:S(2)}, u32[]{:S(2)}) collective-permute-start(bf16[14,56,128]{2,1,0:T(8,128)(2,1)S(1)} %collective-permute-done.2.own), channel_id=1, source_target_pairs={{0,1},{2,0},{4,2},{6,4},{7,6},{5,7},{3,5},{1,3},{8,10},{10,12},{12... | collective-permute-start | bytes 602120 | tf_op jit(solution)/shard_map/ppermute | solution.py:285
  16.6 5.7 %collective-permute-start.7 = (bf16[14,56,128]{2,1,0:T(8,128)(2,1)S(1)}, bf16[14,56,128]{2,1,0:T(8,128)(2,1)S(1)}, u32[]{:S(2)}, u32[]{:S(2)}) collective-permute-start(bf16[14,56,128]{2,1,0:T(8,128)(2,1)S(1)} %collective-permute-done.5.other), channel_id=1, source_target_pairs={{0,1},{2,0},{4,2},{6,4},{7,6},{5,7},{3,5},{1,3},{8,10},{10,12},{12... | collective-permute-start | bytes 602120 | tf_op jit(solution)/shard_map/ppermute | solution.py:285
  20.2 5.7 %collective-permute-start.6 = (bf16[14,56,128]{2,1,0:T(8,128)(2,1)S(1)}, bf16[14,56,128]{2,1,0:T(8,128)(2,1)S(1)}, u32[]{:S(2)}, u32[]{:S(2)}) collective-permute-start(bf16[14,56,128]{2,1,0:T(8,128)(2,1)S(1)} %collective-permute-done.4.own), channel_id=1, source_target_pairs={{0,1},{2,0},{4,2},{6,4},{7,6},{5,7},{3,5},{1,3},{8,10},{10,12},{12... | collective-permute-start | bytes 602120 | tf_op jit(solution)/shard_map/ppermute | solution.py:285
  24.1 2.7 %collective-permute-start.9 = (bf16[14,56,128]{2,1,0:T(8,128)(2,1)S(1)}, bf16[14,56,128]{2,1,0:T(8,128)(2,1)S(1)}, u32[]{:S(2)}, u32[]{:S(2)}) collective-permute-start(bf16[14,56,128]{2,1,0:T(8,128)(2,1)S(1)} %get-tuple-element.45), channel_id=1, source_target_pairs={{0,8},{8,0},{1,9},{9,1},{2,10},{10,2},{3,11},{11,3},{4,12},{12,4},... | collective-permute-start | bytes 602120 | tf_op jit(solution)/shard_map/ppermute | solution.py:288
  26.3 1.3 %collective-permute-start.8 = (bf16[14,16,128]{2,1,0:T(8,128)(2,1)S(1)}, bf16[14,16,128]{2,1,0:T(8,128)(2,1)S(1)}, u32[]{:S(2)}, u32[]{:S(2)}) collective-permute-start(bf16[14,16,128]{2,1,0:T(8,128)(2,1)S(1)} %last_right.1.right), channel_id=1, source_target_pairs={{0,8},{8,0},{1,9},{9,1},{2,10},{10,2},{3,11},{11,3},{4,12},{12,4},... | collective-permute-start | bytes 172040 | tf_op jit(solution)/shard_map/ppermute | solution.py:288

commit v24 on v16

--- a/solution.py
+++ b/solution.py
@@ -192,39 +192,51 @@
 
 def last_right(s, length, shared, own, right, picked, partner):
     shared = Shared(s, length, shared)
-    picked[:, : s.height] = own[...].astype(F32)
     offset = offset_in(s, lax.axis_index("col"))
+    for at in range(0, s.height, s.width):
+
+        @pl.when(offset == at)
+        def _(at=at):
+            picked[:, : s.width] = own[:, at : at + s.width].astype(F32)
+
     token = column_from(s, s.cols // 2) * s.width
 
     def rows_of(at):
-        return picked[at, pl.ds(offset, s.slots), :]
+        return picked[at, : s.slots, :]
 
     project_right(s, rows_of, 0, s.width, token, shared, partner)
     right[...] = partner[...].astype(BF16)
 
 
-def last_left(s, length, shared, own, left):
+def last_left(s, length, shared, own, mine, given, left, total):
+    total[...] = mine[...] + given[...].astype(F32)
     shared = Shared(s, length, shared)
     token = column_from(s, s.cols // 2) * s.width
     project_left(s, own, lax.axis_index("row"), 0, s.width, token, shared, left)
 
 
-def finish(s, left, right, other, mine, given, gating, last_gain, last_weight, *refs):
-    update, partner, total = refs
+def finish(s, left, right, other, mine, gating, last_gain, last_weight, *refs):
+    update, partner, total, held, sent = refs
+    copies = []
     choose(lax.axis_index("row") == owner_of(s, lax.axis_index("col")), right, other, partner)
     accumulate(s, left, partner, mine, total)
     for start in range(0, s.width, s.half):
         settled = [
-            normalise(total[start + step] + given[start + step].astype(F32)) * last_gain[...]
+            normalise(total[start + step]) * last_gain[...]
             for step in range(s.half)
         ]
         value = dot(jnp.concatenate(settled, 0).astype(BF16), last_weight[...])
         for step in range(s.half):
             part = gating[start + step] * value[step * s.height : (step + 1) * s.height]
-            update[start + step] = part.astype(BF16)
-
-
-def call(body, out_shape, scratch, flops, *operands, grant=24):
+            held[start + step] = part.astype(BF16)
+        part = pl.ds(start, s.half)
+        copies.append(pltpu.make_async_copy(held.at[part], update.at[part], sent.at[len(copies)]))
+        copies[-1].start()
+    for copy in copies:
+        copy.wait()
+
+
+def call(body, out_shape, scratch, flops, *operands, grant=24, out_memory=pltpu.VMEM):
     def space(operand):
         return pl.BlockSpec(memory_space=pltpu.SMEM if operand.dtype == jnp.int32 else pltpu.VMEM)
 
@@ -233,7 +245,7 @@
         body,
         out_shape=out_shape,
         in_specs=[space(o) for o in operands],
-        out_specs=jax.tree.map(lambda _: pl.BlockSpec(memory_space=pltpu.VMEM), out_shape),
+        out_specs=jax.tree.map(lambda _: pl.BlockSpec(memory_space=out_memory), out_shape),
         scratch_shapes=scratch,
         compiler_params=pltpu.CompilerParams(vmem_limit_bytes=grant * 1024 * 1024),
         cost_estimate=pl.CostEstimate(flops=flops, bytes_accessed=sent, transcendentals=0),
@@ -346,18 +358,25 @@
         last,
     )
     swapped = swap(right)
-    left = call(functools.partial(last_left, s), sums, [], 0, *shared, last)
+    left, mine = call(
+        functools.partial(last_left, s), [sums, sums], [], 0, *shared, last, mine, given
+    )
     update = call(
         functools.partial(finish, s),
         shape((width, height, channels), BF16),
-        [partner, pltpu.VMEM(sums.shape, F32)],
+        [
+            partner,
+            pltpu.VMEM(sums.shape, F32),
+            pltpu.VMEM(sums.shape, BF16),
+            pltpu.SemaphoreType.DMA((2,)),
+        ],
         width * product,
         left,
         right,
         swapped,
         mine,
-        given,
         *gating,
+        out_memory=pl.ANY,
     )
     return jnp.transpose(update, (1, 0, 2))
 

time: 29.3 us -> 29.3 us (level)
  no operation moved by 1% of the time
where the time goes in v24:
time: 29.3 us; the launch traced here: 29.1 us
  starting transfers between devices  11.9 us (41%)
  Pallas kernels  10.9 us (37%)
  waiting for transfers between devices  4.64 us (16%)
  local copies, waits for them, and re-layouts  0.97 us (3%)
  between operations  0.76 us (3%)
    ppermute x7, starting transfers between devices, shift(): return lax.ppermute(block, ('row', 'col'), pairs)  11.3 us
    pallas_call x9, Pallas kernels, call(): pl.pallas_call(body, out_shape=out_shape, in_specs=[space(o) for o in ope...  10.9 us
    ppermute x7, waiting for transfers between devices, shift(): return lax.ppermute(block, ('row', 'col'), pairs)  3.92 us
    unnamed x10, local copies, waits for them, and re-layouts  0.97 us
    ppermute x3, waiting for transfers between devices, swap(): lax.ppermute(block, 'row', [(at, (at + 1) % s.rows) for at in range(s.row...  0.72 us
    ppermute x3, starting transfers between devices, swap(): lax.ppermute(block, 'row', [(at, (at + 1) % s.rows) for at in range(s.row...  0.59 us
  transfers between devices with their start and end apart: 10, of which 6 were waited for; matrix products, arithmetic and copies ran while one was open for 0% of the time, Pallas kernels for 32%

profile of v24, /device:TPU:0, one launch (start us, length us, event | category | flops | bytes accessed | tf_op | source)
XLA Modules:
  0.0 29.1 jit_solution(4736738070598499528)
XLA Ops:
  0.0 0.5 %collective-permute-start.1 = (bf16[14,56,128]{2,1,0:T(8,128)(2,1)}, bf16[14,56,128]{2,1,0:T(8,128)(2,1)S(1)}, u32[]{:S(2)}, u32[]{:S(2)}) collective-permute-start(bf16[14,56,128]{2,1,0:T(8,128)(2,1)} %bitcast.4), channel_id=1, source_target_pairs={{0,8},{8,0},{1,9},{9,1},{2,10},{10,2},{3,11},{11,3},{4,12},{12,4},... | collective-permute-start | bytes 602120 | tf_op jit(solution)/shard_map/ppermute | solution.py:300
  0.5 2.6 %collective-permute-start = (bf16[14,56,128]{2,1,0:T(8,128)(2,1)}, bf16[14,56,128]{2,1,0:T(8,128)(2,1)S(1)}, u32[]{:S(2)}, u32[]{:S(2)}) collective-permute-start(bf16[14,56,128]{2,1,0:T(8,128)(2,1)} %bitcast.5), channel_id=1, source_target_pairs={{0,2},{2,4},{4,6},{6,7},{7,5},{5,3},{3,1},{1,0},{8,9},{10,8},{12,1... | collective-permute-start | bytes 602120 | tf_op jit(solution)/shard_map/ppermute | solution.py:297
  3.0 1.4 %collective-permute-start.3 = (bf16[14,56,128]{2,1,0:T(8,128)(2,1)}, bf16[14,56,128]{2,1,0:T(8,128)(2,1)S(1)}, u32[]{:S(2)}, u32[]{:S(2)}) collective-permute-start(bf16[14,56,128]{2,1,0:T(8,128)(2,1)} %bitcast.6), channel_id=1, source_target_pairs={{0,9},{2,8},{4,10},{6,12},{7,14},{5,15},{3,13},{1,11},{8,2},{10,4}... | collective-permute-start | bytes 602120 | tf_op jit(solution)/shard_map/ppermute | solution.py:297
  5.0 1.6 %join.1.shared = f32[136,512]{1,0:T(8,128)} custom-call(f32[1,128]{1,0:T(1,128)} %bitcast.10, bf16[128,128]{1,0:T(8,128)(2,1)} %left_gate.1, bf16[128,128]{1,0:T(8,128)(2,1)} %left_value.1, bf16[128,128]{1,0:T(8,128)(2,1)} %right_gate.1, bf16[128,128]{1,0:T(8,128)(2,1)} %right_value.1), custom_call_target="tpu_custom_call" | custom-call | bytes 131584 | tf_op jit(solution)/shard_map/join/pallas_call | solution.py:244
  6.6 0.0 collective-permute-done.1.other
  6.6 1.0 %copy-done = f32[136,512]{1,0:T(8,128)S(1)} copy-done((f32[136,512]{1,0:T(8,128)S(1)}, f32[136,512]{1,0:T(8,128)}, u32[]{:S(2)}) %copy-start) | copy-done | bytes 278552
  7.6 1.0 %add_both.4 = (f32[14,56,128]{2,1,0:T(8,128)S(1)}, f32[14,56,128]{2,1,0:T(8,128)S(1)}) custom-call(s32[1]{0:T(128)S(6)} %copy.11.length, f32[136,512]{1,0:T(8,128)S(1)} %copy-done, bf16[14,56,128]{2,1,0:T(8,128)(2,1)S(1)} %bitcast.7, bf16[14,56,128]{2,1,0:T(8,128)(2,1)S(1)} %collective-permute-done.1.other), custom_call_target="tpu_custom_call" | custom-call | flops 22478848 | bytes 679940 | tf_op jit(solution)/shard_map/add_both/pallas_call | solution.py:244
  8.6 0.0 collective-permute-done.own
  8.6 0.0 copy-start.4
  8.6 1.5 %collective-permute-start.2 = (bf16[14,56,128]{2,1,0:T(8,128)(2,1)S(1)}, bf16[14,56,128]{2,1,0:T(8,128)(2,1)S(1)}, u32[]{:S(2)}, u32[]{:S(2)}) collective-permute-start(bf16[14,56,128]{2,1,0:T(8,128)(2,1)S(1)} %collective-permute-done.own), channel_id=1, source_target_pairs={{0,2},{2,4},{4,6},{6,7},{7,5},{5,3},{3,1},{1,0},{8,9},{10,8},{12,1... | collective-permute-start | bytes 602120 | tf_op jit(solution)/shard_map/ppermute | solution.py:297
  10.1 0.0 collective-permute-done.3.other
  10.1 1.6 %collective-permute-start.5 = (bf16[14,56,128]{2,1,0:T(8,128)(2,1)S(1)}, bf16[14,56,128]{2,1,0:T(8,128)(2,1)S(1)}, u32[]{:S(2)}, u32[]{:S(2)}) collective-permute-start(bf16[14,56,128]{2,1,0:T(8,128)(2,1)S(1)} %collective-permute-done.3.other), channel_id=1, source_target_pairs={{0,2},{2,4},{4,6},{6,7},{7,5},{5,3},{3,1},{1,0},{8,9},{10,8},{12,1... | collective-permute-start | bytes 602120 | tf_op jit(solution)/shard_map/ppermute | solution.py:297
  11.7 0.0 copy-done.4
  11.7 0.5 %gate.1 = (f32[14,56,128]{2,1,0:T(8,128)S(1)}, f32[1,128]{1,0:T(1,128)S(1)}, bf16[128,128]{1,0:T(8,128)(2,1)S(1)}) custom-call(s32[1]{0:T(128)S(6)} %copy.11.length, f32[136,512]{1,0:T(8,128)S(1)} %copy-done, bf16[14,56,128]{2,1,0:T(8,128)(2,1)S(1)} %bitcast.8, bf16[128,128]{1,0:T(8,128)(2,1)S(1)} %copy-done.2, f32[1,128]{1,0:T(1,128)S(1)} %bitcast.9, ...), custom_call_target="tpu_custom_call" | custom-call | flops 25690112 | bytes 545284 | tf_op jit(solution)/shard_map/gate/pallas_call | solution.py:244
  12.2 1.8 %add_both.5 = (f32[14,56,128]{2,1,0:T(8,128)S(1)}, f32[14,56,128]{2,1,0:T(8,128)S(1)}) custom-call(s32[1]{0:T(128)S(6)} %copy.11.length, f32[136,512]{1,0:T(8,128)S(1)} %copy-done, bf16[14,56,128]{2,1,0:T(8,128)(2,1)S(1)} %collective-permute-done.own, bf16[14,56,128]{2,1,0:T(8,128)(2,1)S(1)} %collective-permute-done.3.other, ...), custom_call_target="tpu_custom_call" | custom-call | flops 44957696 | bytes 1482756 | tf_op jit(solution)/shard_map/add_both/pallas_call | solution.py:244
  14.0 0.4 %collective-permute-done.2.own = bf16[14,56,128]{2,1,0:T(8,128)(2,1)S(1)} collective-permute-done((bf16[14,56,128]{2,1,0:T(8,128)(2,1)S(1)}, bf16[14,56,128]{2,1,0:T(8,128)(2,1)S(1)}, u32[]{:S(2)}, u32[]{:S(2)}) %collective-permute-start.2) | collective-permute-done | bytes 200736 | tf_op jit(solution)/shard_map/ppermute | solution.py:297
  14.4 1.4 %collective-permute-start.4 = (bf16[14,56,128]{2,1,0:T(8,128)(2,1)S(1)}, bf16[14,56,128]{2,1,0:T(8,128)(2,1)S(1)}, u32[]{:S(2)}, u32[]{:S(2)}) collective-permute-start(bf16[14,56,128]{2,1,0:T(8,128)(2,1)S(1)} %collective-permute-done.2.own), channel_id=1, source_target_pairs={{0,2},{2,4},{4,6},{6,7},{7,5},{5,3},{3,1},{1,0},{8,9},{10,8},{12,1... | collective-permute-start | bytes 602120 | tf_op jit(solution)/shard_map/ppermute | solution.py:297
  15.8 0.7 %collective-permute-done.5.other = bf16[14,56,128]{2,1,0:T(8,128)(2,1)S(1)} collective-permute-done((bf16[14,56,128]{2,1,0:T(8,128)(2,1)S(1)}, bf16[14,56,128]{2,1,0:T(8,128)(2,1)S(1)}, u32[]{:S(2)}, u32[]{:S(2)}) %collective-permute-start.5) | collective-permute-done | bytes 200736 | tf_op jit(solution)/shard_map/ppermute | solution.py:297
  16.5 1.5 %collective-permute-start.7 = (bf16[14,56,128]{2,1,0:T(8,128)(2,1)S(1)}, bf16[14,56,128]{2,1,0:T(8,128)(2,1)S(1)}, u32[]{:S(2)}, u32[]{:S(2)}) collective-permute-start(bf16[14,56,128]{2,1,0:T(8,128)(2,1)S(1)} %collective-permute-done.5.other), channel_id=1, source_target_pairs={{0,2},{2,4},{4,6},{6,7},{7,5},{5,3},{3,1},{1,0},{8,9},{10,8},{12,1... | collective-permute-start | bytes 602120 | tf_op jit(solution)/shard_map/ppermute | solution.py:297
  18.0 1.8 %add_both.6 = (f32[14,56,128]{2,1,0:T(8,128)S(1)}, f32[14,56,128]{2,1,0:T(8,128)S(1)}) custom-call(s32[1]{0:T(128)S(6)} %copy.11.length, f32[136,512]{1,0:T(8,128)S(1)} %copy-done, bf16[14,56,128]{2,1,0:T(8,128)(2,1)S(1)} %collective-permute-done.2.own, bf16[14,56,128]{2,1,0:T(8,128)(2,1)S(1)} %collective-permute-done.5.other, ...), custom_call_target="tpu_custom_call" | custom-call | flops 44957696 | bytes 1482756 | tf_op jit(solution)/shard_map/add_both/pallas_call | solution.py:244
  19.8 0.3 %collective-permute-done.4.own = bf16[14,56,128]{2,1,0:T(8,128)(2,1)S(1)} collective-permute-done((bf16[14,56,128]{2,1,0:T(8,128)(2,1)S(1)}, bf16[14,56,128]{2,1,0:T(8,128)(2,1)S(1)}, u32[]{:S(2)}, u32[]{:S(2)}) %collective-permute-start.4) | collective-permute-done | bytes 200736 | tf_op jit(solution)/shard_map/ppermute | solution.py:297
  20.1 1.4 %collective-permute-start.6 = (bf16[14,56,128]{2,1,0:T(8,128)(2,1)S(1)}, bf16[14,56,128]{2,1,0:T(8,128)(2,1)S(1)}, u32[]{:S(2)}, u32[]{:S(2)}) collective-permute-start(bf16[14,56,128]{2,1,0:T(8,128)(2,1)S(1)} %collective-permute-done.4.own), channel_id=1, source_target_pairs={{0,2},{2,4},{4,6},{6,7},{7,5},{5,3},{3,1},{1,0},{8,9},{10,8},{12,1... | collective-permute-start | bytes 602120 | tf_op jit(solution)/shard_map/ppermute | solution.py:297
  21.5 0.7 %collective-permute-done.7.other = bf16[14,56,128]{2,1,0:T(8,128)(2,1)S(1)} collective-permute-done((bf16[14,56,128]{2,1,0:T(8,128)(2,1)S(1)}, bf16[14,56,128]{2,1,0:T(8,128)(2,1)S(1)}, u32[]{:S(2)}, u32[]{:S(2)}) %collective-permute-start.7) | collective-permute-done | bytes 200736 | tf_op jit(solution)/shard_map/ppermute | solution.py:297
  22.3 1.8 %add_both.7 = (f32[14,56,128]{2,1,0:T(8,128)S(1)}, bf16[14,56,128]{2,1,0:T(8,128)(2,1)S(1)}) custom-call(s32[1]{0:T(128)S(6)} %copy.11.length, f32[136,512]{1,0:T(8,128)S(1)} %copy-done, bf16[14,56,128]{2,1,0:T(8,128)(2,1)S(1)} %collective-permute-done.4.own, bf16[14,56,128]{2,1,0:T(8,128)(2,1)S(1)} %collective-permute-done.7.other, ...), custom_call_target="tpu_custom_call" | custom-call | flops 44957696 | bytes 1482756 | tf_op jit(solution)/shard_map/add_both/pallas_call | solution.py:244
  24.1 0.1 collective-permute-start.8
  24.1 1.7 %collective-permute-done.6.own = bf16[14,56,128]{2,1,0:T(8,128)(2,1)S(1)} collective-permute-done((bf16[14,56,128]{2,1,0:T(8,128)(2,1)S(1)}, bf16[14,56,128]{2,1,0:T(8,128)(2,1)S(1)}, u32[]{:S(2)}, u32[]{:S(2)}) %collective-permute-start.6) | collective-permute-done | bytes 200736 | tf_op jit(solution)/shard_map/ppermute | solution.py:297
  25.8 0.4 %last_right.1.right = bf16[14,16,128]{2,1,0:T(8,128)(2,1)S(1)} custom-call(s32[1]{0:T(128)S(6)} %copy.11.length, f32[136,512]{1,0:T(8,128)S(1)} %copy-done, bf16[14,56,128]{2,1,0:T(8,128)(2,1)S(1)} %collective-permute-done.6.own), custom_call_target="tpu_custom_call" | custom-call | bytes 479236 | tf_op jit(solution)/shard_map/last_right/pallas_call | solution.py:244
  26.2 0.1 collective-permute-start.9
  26.3 0.0 collective-permute-done.8.given
  26.3 0.5 %last_left.1 = (f32[14,56,128]{2,1,0:T(8,128)S(1)}, f32[14,56,128]{2,1,0:T(8,128)S(1)}) custom-call(s32[1]{0:T(128)S(6)} %copy.11.length, f32[136,512]{1,0:T(8,128)S(1)} %copy-done, bf16[14,56,128]{2,1,0:T(8,128)(2,1)S(1)} %collective-permute-done.6.own, f32[14,56,128]{2,1,0:T(8,128)S(1)} %get-tuple-element.46.mine, ...), custom_call_target="tpu_custom_call" | custom-call | bytes 1081348 | tf_op jit(solution)/shard_map/last_left/pallas_call | solution.py:244
  26.8 0.7 %collective-permute-done.9.other = bf16[14,16,128]{2,1,0:T(8,128)(2,1)S(1)} collective-permute-done((bf16[14,16,128]{2,1,0:T(8,128)(2,1)S(1)}, bf16[14,16,128]{2,1,0:T(8,128)(2,1)S(1)}, u32[]{:S(2)}, u32[]{:S(2)}) %collective-permute-start.9) | collective-permute-done | bytes 57376 | tf_op jit(solution)/shard_map/ppermute | solution.py:300
  27.5 1.6 %finish.1 = bf16[14,56,128]{2,1,0:T(8,128)(2,1)} custom-call(f32[14,56,128]{2,1,0:T(8,128)S(1)} %get-tuple-element.48.left, bf16[14,16,128]{2,1,0:T(8,128)(2,1)S(1)} %last_right.1.right, bf16[14,16,128]{2,1,0:T(8,128)(2,1)S(1)} %collective-permute-done.9.other, f32[14,56,128]{2,1,0:T(8,128)S(1)} %get-tuple-element.49.mine, ...), custom_call_target="tpu_custom_call" | custom-call | flops 22478848 | bytes 1352192 | tf_op jit(solution)/shard_map/finish/pallas_call | solution.py:244
  (7 shorter events, 0.0 us)
Async XLA Ops:
  0.0 6.6 %collective-permute-start.1 = (bf16[14,56,128]{2,1,0:T(8,128)(2,1)}, bf16[14,56,128]{2,1,0:T(8,128)(2,1)S(1)}, u32[]{:S(2)}, u32[]{:S(2)}) collective-permute-start(bf16[14,56,128]{2,1,0:T(8,128)(2,1)} %bitcast.4), channel_id=1, source_target_pairs={{0,8},{8,0},{1,9},{9,1},{2,10},{10,2},{3,11},{11,3},{4,12},{12,4},... | collective-permute-start | bytes 602120 | tf_op jit(solution)/shard_map/ppermute | solution.py:300
  0.5 8.2 %collective-permute-start = (bf16[14,56,128]{2,1,0:T(8,128)(2,1)}, bf16[14,56,128]{2,1,0:T(8,128)(2,1)S(1)}, u32[]{:S(2)}, u32[]{:S(2)}) collective-permute-start(bf16[14,56,128]{2,1,0:T(8,128)(2,1)} %bitcast.5), channel_id=1, source_target_pairs={{0,2},{2,4},{4,6},{6,7},{7,5},{5,3},{3,1},{1,0},{8,9},{10,8},{12,1... | collective-permute-start | bytes 602120 | tf_op jit(solution)/shard_map/ppermute | solution.py:297
  3.0 7.1 %collective-permute-start.3 = (bf16[14,56,128]{2,1,0:T(8,128)(2,1)}, bf16[14,56,128]{2,1,0:T(8,128)(2,1)S(1)}, u32[]{:S(2)}, u32[]{:S(2)}) collective-permute-start(bf16[14,56,128]{2,1,0:T(8,128)(2,1)} %bitcast.6), channel_id=1, source_target_pairs={{0,9},{2,8},{4,10},{6,12},{7,14},{5,15},{3,13},{1,11},{8,2},{10,4}... | collective-permute-start | bytes 602120 | tf_op jit(solution)/shard_map/ppermute | solution.py:297
  5.0 1.6 %copy-start.1 = (bf16[56,14,128]{2,0,1:T(8,128)(2,1)S(1)}, bf16[56,14,128]{2,0,1:T(8,128)(2,1)}, u32[]{:S(2)}) copy-start(bf16[56,14,128]{2,0,1:T(8,128)(2,1)} %param.10) | copy-start | bytes 602116
  6.6 1.0 %copy-start = (f32[136,512]{1,0:T(8,128)S(1)}, f32[136,512]{1,0:T(8,128)}, u32[]{:S(2)}) copy-start(f32[136,512]{1,0:T(8,128)} %join.1.shared) | copy-start | bytes 835588
  7.6 4.1 %copy-start.2 = (bf16[128,128]{1,0:T(8,128)(2,1)S(1)}, bf16[128,128]{1,0:T(8,128)(2,1)}, u32[]{:S(2)}) copy-start(bf16[128,128]{1,0:T(8,128)(2,1)} %out_gate.1) | copy-start | bytes 98308
  7.6 4.1 %copy-start.3 = (bf16[128,128]{1,0:T(8,128)(2,1)S(1)}, bf16[128,128]{1,0:T(8,128)(2,1)}, u32[]{:S(2)}) copy-start(bf16[128,128]{1,0:T(8,128)(2,1)} %last_weight.1) | copy-start | bytes 98308
  8.6 3.1 %copy-start.4 = (f32[128]{0:T(128)S(1)}, f32[128]{0:T(128)}, u32[]{:S(2)}) copy-start(f32[128]{0:T(128)} %param.18) | copy-start | bytes 1540
  8.6 5.8 %collective-permute-start.2 = (bf16[14,56,128]{2,1,0:T(8,128)(2,1)S(1)}, bf16[14,56,128]{2,1,0:T(8,128)(2,1)S(1)}, u32[]{:S(2)}, u32[]{:S(2)}) collective-permute-start(bf16[14,56,128]{2,1,0:T(8,128)(2,1)S(1)} %collective-permute-done.own), channel_id=1, source_target_pairs={{0,2},{2,4},{4,6},{6,7},{7,5},{5,3},{3,1},{1,0},{8,9},{10,8},{12,1... | collective-permute-start | bytes 602120 | tf_op jit(solution)/shard_map/ppermute | solution.py:297
  10.1 6.4 %collective-permute-start.5 = (bf16[14,56,128]{2,1,0:T(8,128)(2,1)S(1)}, bf16[14,56,128]{2,1,0:T(8,128)(2,1)S(1)}, u32[]{:S(2)}, u32[]{:S(2)}) collective-permute-start(bf16[14,56,128]{2,1,0:T(8,128)(2,1)S(1)} %collective-permute-done.3.other), channel_id=1, source_target_pairs={{0,2},{2,4},{4,6},{6,7},{7,5},{5,3},{3,1},{1,0},{8,9},{10,8},{12,1... | collective-permute-start | bytes 602120 | tf_op jit(solution)/shard_map/ppermute | solution.py:297
  14.4 5.7 %collective-permute-start.4 = (bf16[14,56,128]{2,1,0:T(8,128)(2,1)S(1)}, bf16[14,56,128]{2,1,0:T(8,128)(2,1)S(1)}, u32[]{:S(2)}, u32[]{:S(2)}) collective-permute-start(bf16[14,56,128]{2,1,0:T(8,128)(2,1)S(1)} %collective-permute-done.2.own), channel_id=1, source_target_pairs={{0,2},{2,4},{4,6},{6,7},{7,5},{5,3},{3,1},{1,0},{8,9},{10,8},{12,1... | collective-permute-start | bytes 602120 | tf_op jit(solution)/shard_map/ppermute | solution.py:297
  16.5 5.7 %collective-permute-start.7 = (bf16[14,56,128]{2,1,0:T(8,128)(2,1)S(1)}, bf16[14,56,128]{2,1,0:T(8,128)(2,1)S(1)}, u32[]{:S(2)}, u32[]{:S(2)}) collective-permute-start(bf16[14,56,128]{2,1,0:T(8,128)(2,1)S(1)} %collective-permute-done.5.other), channel_id=1, source_target_pairs={{0,2},{2,4},{4,6},{6,7},{7,5},{5,3},{3,1},{1,0},{8,9},{10,8},{12,1... | collective-permute-start | bytes 602120 | tf_op jit(solution)/shard_map/ppermute | solution.py:297
  20.1 5.7 %collective-permute-start.6 = (bf16[14,56,128]{2,1,0:T(8,128)(2,1)S(1)}, bf16[14,56,128]{2,1,0:T(8,128)(2,1)S(1)}, u32[]{:S(2)}, u32[]{:S(2)}) collective-permute-start(bf16[14,56,128]{2,1,0:T(8,128)(2,1)S(1)} %collective-permute-done.4.own), channel_id=1, source_target_pairs={{0,2},{2,4},{4,6},{6,7},{7,5},{5,3},{3,1},{1,0},{8,9},{10,8},{12,1... | collective-permute-start | bytes 602120 | tf_op jit(solution)/shard_map/ppermute | solution.py:297
  24.1 2.2 %collective-permute-start.8 = (bf16[14,56,128]{2,1,0:T(8,128)(2,1)S(1)}, bf16[14,56,128]{2,1,0:T(8,128)(2,1)S(1)}, u32[]{:S(2)}, u32[]{:S(2)}) collective-permute-start(bf16[14,56,128]{2,1,0:T(8,128)(2,1)S(1)} %get-tuple-element.47), channel_id=1, source_target_pairs={{0,8},{8,0},{1,9},{9,1},{2,10},{10,2},{3,11},{11,3},{4,12},{12,4},... | collective-permute-start | bytes 602120 | tf_op jit(solution)/shard_map/ppermute | solution.py:300
  26.2 1.3 %collective-permute-start.9 = (bf16[14,16,128]{2,1,0:T(8,128)(2,1)S(1)}, bf16[14,16,128]{2,1,0:T(8,128)(2,1)S(1)}, u32[]{:S(2)}, u32[]{:S(2)}) collective-permute-start(bf16[14,16,128]{2,1,0:T(8,128)(2,1)S(1)} %last_right.1.right), channel_id=1, source_target_pairs={{0,8},{8,0},{1,9},{9,1},{2,10},{10,2},{3,11},{11,3},{4,12},{12,4},... | collective-permute-start | bytes 172040 | tf_op jit(solution)/shard_map/ppermute | solution.py:300

commit v25 on v16

--- a/solution.py
+++ b/solution.py
@@ -52,13 +52,12 @@
     return jnp.dot(left, right, preferred_element_type=F32)
 
 
-def gate(s, length, shared, pair, out_gate, last_gain, last_weight, gating, kept_gain, kept_weight):
-    gain = Shared(s, length, shared).gain
+def gate(s, gain, pair, out_gate, last_gain, last_weight, gating, kept_gain, kept_weight):
     kept_gain[...] = last_gain[...]
     kept_weight[...] = last_weight[...]
     for start in range(0, s.width, s.half):
         normed = [
-            normalise(pair[start + step].astype(F32)) * gain for step in range(s.half)
+            normalise(pair[start + step].astype(F32)) * gain[...] for step in range(s.half)
         ]
         value = sigmoid(dot(jnp.concatenate(normed, 0).astype(BF16), out_gate[...]))
         for step in range(s.half):
@@ -131,6 +130,10 @@
     for at, part in enumerate((left_gate, left_value, right_gate, right_value)):
         shared[: s.channels, at * h : (at + 1) * h] = part[...].astype(F32)
     shared[s.channels : s.channels + 1, : s.channels] = gain[...]
+
+
+def gain_of(s, length, shared, gain):
+    gain[...] = Shared(s, length, shared).gain
 
 
 def gated(s, rows, gain, weight, masks):
@@ -315,23 +318,28 @@
     far = s.cols // 2
     other = shift(pair, crossed=True)
     own = shift(pair)
-    total = add(0, pair, swap(pair), ())
-    other, own = in_turn(other, own, total)
+    given = swap(lax.optimization_barrier((pair, shared[1]))[0])
+    kept = call(functools.partial(gain_of, s), shape(gain.shape, F32), [], 0, *shared)
+    own, kept = lax.optimization_barrier((own, kept))
+    other = lax.optimization_barrier((other, own))[0]
     for distance in range(1, far - 1):
         ahead = [shift(other), shift(own)]
-        total = add(distance, own, other, total)
+        after = lax.optimization_barrier((pair, own))[0]
         if distance == 1:
+            total, gating = add(0, after, given, ()), ()
+        elif distance == 2:
             gating = call(
                 functools.partial(gate, s),
                 [sums, shape((1, hidden), F32), shape(out_weight.shape, BF16)],
                 [],
                 2 * height * width * channels * channels,
-                *shared,
-                pair,
+                kept,
+                after,
                 out_gate,
                 output_gain.reshape(1, hidden),
                 out_weight,
             )
+        total = add(distance, own, other, total)
         other, own = in_turn(*ahead, (total, gating))
     last = shift(own)
     mine, theirs = add(far - 1, own, other, total, narrow=True)

time: 29.3 us -> 30.1 us (1.027)
  starting transfers between devices: 11.8 us -> 12.9 us
    ppermute x3, starting transfers between devices: 0.59 us -> 1.15 us  [swap(): lax.ppermute(block, 'row', [(at, (at + 1) % s.rows) for at in range(s.row...]
    ppermute x7, starting transfers between devices: 11.2 us -> 11.7 us  [shift(): return lax.ppermute(block, ('row', 'col'), pairs)]
    pallas_call x9 -> x10, Pallas kernels: 10.9 us -> 10.9 us  [call(): pl.pallas_call(body, out_shape=out_shape, in_specs=[space(o) for o in ope...]
    unnamed x10 -> x12, local copies, waits for them, and re-layouts: 0.97 us -> 0.97 us
  transfers between devices with their start and end apart: 10 -> 10, of which waited for: 6 -> 5; matrix products, arithmetic and copies ran while one was open for 0% -> 0% of each run, Pallas kernels for 32% -> 31%
where the time goes in v25:
time: 30.1 us; the launch traced here: 29.9 us
  starting transfers between devices  12.9 us (43%)
  Pallas kernels  10.9 us (36%)
  waiting for transfers between devices  4.39 us (15%)
  local copies, waits for them, and re-layouts  0.97 us (3%)
  between operations  0.79 us (3%)
    ppermute x7, starting transfers between devices, shift(): return lax.ppermute(block, ('row', 'col'), pairs)  11.7 us
    pallas_call x10, Pallas kernels, call(): pl.pallas_call(body, out_shape=out_shape, in_specs=[space(o) for o in ope...  10.9 us
    ppermute x7, waiting for transfers between devices, shift(): return lax.ppermute(block, ('row', 'col'), pairs)  3.66 us
    ppermute x3, starting transfers between devices, swap(): lax.ppermute(block, 'row', [(at, (at + 1) % s.rows) for at in range(s.row...  1.15 us
    unnamed x12, local copies, waits for them, and re-layouts  0.97 us
    ppermute x3, waiting for transfers between devices, swap(): lax.ppermute(block, 'row', [(at, (at + 1) % s.rows) for at in range(s.row...  0.73 us
  transfers between devices with their start and end apart: 10, of which 5 were waited for; matrix products, arithmetic and copies ran while one was open for 0% of the time, Pallas kernels for 31%

profile of v25, /device:TPU:0, one launch (start us, length us, event | category | flops | bytes accessed | tf_op | source)
XLA Modules:
  0.0 29.9 jit_solution(8111583526619802387)
XLA Ops:
  0.0 3.0 %collective-permute-start = (bf16[14,56,128]{2,1,0:T(8,128)(2,1)}, bf16[14,56,128]{2,1,0:T(8,128)(2,1)S(1)}, u32[]{:S(2)}, u32[]{:S(2)}) collective-permute-start(bf16[14,56,128]{2,1,0:T(8,128)(2,1)} %bitcast.4), channel_id=1, source_target_pairs={{0,2},{2,4},{4,6},{6,7},{7,5},{5,3},{3,1},{1,0},{8,9},{10,8},{12,1... | collective-permute-start | bytes 602120 | tf_op jit(solution)/shard_map/ppermute | solution.py:288
  3.0 0.7 %collective-permute-start.2 = (bf16[14,56,128]{2,1,0:T(8,128)(2,1)}, bf16[14,56,128]{2,1,0:T(8,128)(2,1)S(1)}, u32[]{:S(2)}, u32[]{:S(2)}) collective-permute-start(bf16[14,56,128]{2,1,0:T(8,128)(2,1)} %bitcast.5), channel_id=1, source_target_pairs={{0,9},{2,8},{4,10},{6,12},{7,14},{5,15},{3,13},{1,11},{8,2},{10,4}... | collective-permute-start | bytes 602120 | tf_op jit(solution)/shard_map/ppermute | solution.py:288
  3.7 1.6 %join.1.shared = f32[136,512]{1,0:T(8,128)} custom-call(f32[1,128]{1,0:T(1,128)} %bitcast.10, bf16[128,128]{1,0:T(8,128)(2,1)} %left_gate.1, bf16[128,128]{1,0:T(8,128)(2,1)} %left_value.1, bf16[128,128]{1,0:T(8,128)(2,1)} %right_gate.1, bf16[128,128]{1,0:T(8,128)(2,1)} %right_value.1), custom_call_target="tpu_custom_call" | custom-call | bytes 131584 | tf_op jit(solution)/shard_map/join/pallas_call | solution.py:235
  5.3 1.0 %collective-permute-start.3 = (bf16[14,56,128]{2,1,0:T(8,128)(2,1)S(1)}, bf16[14,56,128]{2,1,0:T(8,128)(2,1)S(1)}, u32[]{:S(2)}, u32[]{:S(2)}) collective-permute-start(bf16[14,56,128]{2,1,0:T(8,128)(2,1)S(1)} %bitcast.6), channel_id=1, source_target_pairs={{0,8},{8,0},{1,9},{9,1},{2,10},{10,2},{3,11},{11,3},{4,12},{12,4},... | collective-permute-start | bytes 602120 | tf_op jit(solution)/shard_map/ppermute | solution.py:291
  7.0 0.9 %copy-done = f32[136,512]{1,0:T(8,128)S(1)} copy-done((f32[136,512]{1,0:T(8,128)S(1)}, f32[136,512]{1,0:T(8,128)}, u32[]{:S(2)}) %copy-start) | copy-done | bytes 278552
  7.9 0.0 collective-permute-done.own
  7.9 2.2 %collective-permute-start.1 = (bf16[14,56,128]{2,1,0:T(8,128)(2,1)S(1)}, bf16[14,56,128]{2,1,0:T(8,128)(2,1)S(1)}, u32[]{:S(2)}, u32[]{:S(2)}) collective-permute-start(bf16[14,56,128]{2,1,0:T(8,128)(2,1)S(1)} %collective-permute-done.own), channel_id=1, source_target_pairs={{0,2},{2,4},{4,6},{6,7},{7,5},{5,3},{3,1},{1,0},{8,9},{10,8},{12,1... | collective-permute-start | bytes 602120 | tf_op jit(solution)/shard_map/ppermute | solution.py:288
  10.1 0.0 collective-permute-done.2.other
  10.1 1.6 %collective-permute-start.5 = (bf16[14,56,128]{2,1,0:T(8,128)(2,1)S(1)}, bf16[14,56,128]{2,1,0:T(8,128)(2,1)S(1)}, u32[]{:S(2)}, u32[]{:S(2)}) collective-permute-start(bf16[14,56,128]{2,1,0:T(8,128)(2,1)S(1)} %collective-permute-done.2.other), channel_id=1, source_target_pairs={{0,2},{2,4},{4,6},{6,7},{7,5},{5,3},{3,1},{1,0},{8,9},{10,8},{12,1... | collective-permute-start | bytes 602120 | tf_op jit(solution)/shard_map/ppermute | solution.py:288
  11.7 0.0 collective-permute-done.3.other
  11.7 1.0 %add_both.4 = (f32[14,56,128]{2,1,0:T(8,128)S(1)}, f32[14,56,128]{2,1,0:T(8,128)S(1)}) custom-call(s32[1]{0:T(128)S(6)} %copy.11.length, f32[136,512]{1,0:T(8,128)S(1)} %copy-done, bf16[14,56,128]{2,1,0:T(8,128)(2,1)S(1)} %bitcast.7, bf16[14,56,128]{2,1,0:T(8,128)(2,1)S(1)} %collective-permute-done.3.other), custom_call_target="tpu_custom_call" | custom-call | flops 22478848 | bytes 679940 | tf_op jit(solution)/shard_map/add_both/pallas_call | solution.py:235
  12.7 0.0 copy-start.3
  12.7 0.0 copy-start.4
  12.7 1.8 %add_both.5 = (f32[14,56,128]{2,1,0:T(8,128)S(1)}, f32[14,56,128]{2,1,0:T(8,128)S(1)}) custom-call(s32[1]{0:T(128)S(6)} %copy.11.length, f32[136,512]{1,0:T(8,128)S(1)} %copy-done, bf16[14,56,128]{2,1,0:T(8,128)(2,1)S(1)} %collective-permute-done.own, bf16[14,56,128]{2,1,0:T(8,128)(2,1)S(1)} %collective-permute-done.2.other, ...), custom_call_target="tpu_custom_call" | custom-call | flops 44957696 | bytes 1482756 | tf_op jit(solution)/shard_map/add_both/pallas_call | solution.py:235
  14.5 0.2 collective-permute-done.1.own
  14.7 1.5 %collective-permute-start.4 = (bf16[14,56,128]{2,1,0:T(8,128)(2,1)S(1)}, bf16[14,56,128]{2,1,0:T(8,128)(2,1)S(1)}, u32[]{:S(2)}, u32[]{:S(2)}) collective-permute-start(bf16[14,56,128]{2,1,0:T(8,128)(2,1)S(1)} %collective-permute-done.1.own), channel_id=1, source_target_pairs={{0,2},{2,4},{4,6},{6,7},{7,5},{5,3},{3,1},{1,0},{8,9},{10,8},{12,1... | collective-permute-start | bytes 602120 | tf_op jit(solution)/shard_map/ppermute | solution.py:288
  16.2 0.6 %collective-permute-done.5.other = bf16[14,56,128]{2,1,0:T(8,128)(2,1)S(1)} collective-permute-done((bf16[14,56,128]{2,1,0:T(8,128)(2,1)S(1)}, bf16[14,56,128]{2,1,0:T(8,128)(2,1)S(1)}, u32[]{:S(2)}, u32[]{:S(2)}) %collective-permute-start.5) | collective-permute-done | bytes 200736 | tf_op jit(solution)/shard_map/ppermute | solution.py:288
  16.9 1.7 %collective-permute-start.7 = (bf16[14,56,128]{2,1,0:T(8,128)(2,1)S(1)}, bf16[14,56,128]{2,1,0:T(8,128)(2,1)S(1)}, u32[]{:S(2)}, u32[]{:S(2)}) collective-permute-start(bf16[14,56,128]{2,1,0:T(8,128)(2,1)S(1)} %collective-permute-done.5.other), channel_id=1, source_target_pairs={{0,2},{2,4},{4,6},{6,7},{7,5},{5,3},{3,1},{1,0},{8,9},{10,8},{12,1... | collective-permute-start | bytes 602120 | tf_op jit(solution)/shard_map/ppermute | solution.py:288
  18.6 0.5 %gate.1 = (f32[14,56,128]{2,1,0:T(8,128)S(1)}, f32[1,128]{1,0:T(1,128)S(1)}, bf16[128,128]{1,0:T(8,128)(2,1)S(1)}) custom-call(f32[1,128]{1,0:T(1,128)S(1)} %gain_of.1.gain, bf16[14,56,128]{2,1,0:T(8,128)(2,1)S(1)} %bitcast.8, bf16[128,128]{1,0:T(8,128)(2,1)S(1)} %copy-done.3, f32[1,128]{1,0:T(1,128)S(1)} %bitcast.9, bf16[128,128]{1,0:T(8,128)(2,1)S(1)} %copy-done.4), custom_call_target="tpu_custom_call" | custom-call | flops 25690112 | bytes 267264 | tf_op jit(solution)/shard_map/gate/pallas_call | solution.py:235
  19.1 1.8 %add_both.6 = (f32[14,56,128]{2,1,0:T(8,128)S(1)}, f32[14,56,128]{2,1,0:T(8,128)S(1)}) custom-call(s32[1]{0:T(128)S(6)} %copy.11.length, f32[136,512]{1,0:T(8,128)S(1)} %copy-done.1, bf16[14,56,128]{2,1,0:T(8,128)(2,1)S(1)} %collective-permute-done.1.own, bf16[14,56,128]{2,1,0:T(8,128)(2,1)S(1)} %collective-permute-done.5.other, ...), custom_call_target="tpu_custom_call" | custom-call | flops 44957696 | bytes 1482756 | tf_op jit(solution)/shard_map/add_both/pallas_call | solution.py:235
  20.8 0.0 collective-permute-done.4.own
  20.9 1.1 %collective-permute-start.6 = (bf16[14,56,128]{2,1,0:T(8,128)(2,1)S(1)}, bf16[14,56,128]{2,1,0:T(8,128)(2,1)S(1)}, u32[]{:S(2)}, u32[]{:S(2)}) collective-permute-start(bf16[14,56,128]{2,1,0:T(8,128)(2,1)S(1)} %collective-permute-done.4.own), channel_id=1, source_target_pairs={{0,2},{2,4},{4,6},{6,7},{7,5},{5,3},{3,1},{1,0},{8,9},{10,8},{12,1... | collective-permute-start | bytes 602120 | tf_op jit(solution)/shard_map/ppermute | solution.py:288
  21.9 0.6 %collective-permute-done.7.other = bf16[14,56,128]{2,1,0:T(8,128)(2,1)S(1)} collective-permute-done((bf16[14,56,128]{2,1,0:T(8,128)(2,1)S(1)}, bf16[14,56,128]{2,1,0:T(8,128)(2,1)S(1)}, u32[]{:S(2)}, u32[]{:S(2)}) %collective-permute-start.7) | collective-permute-done | bytes 200736 | tf_op jit(solution)/shard_map/ppermute | solution.py:288
  22.6 1.8 %add_both.7 = (f32[14,56,128]{2,1,0:T(8,128)S(1)}, bf16[14,56,128]{2,1,0:T(8,128)(2,1)S(1)}) custom-call(s32[1]{0:T(128)S(6)} %copy.11.length, f32[136,512]{1,0:T(8,128)S(1)} %copy-done.1, bf16[14,56,128]{2,1,0:T(8,128)(2,1)S(1)} %collective-permute-done.4.own, bf16[14,56,128]{2,1,0:T(8,128)(2,1)S(1)} %collective-permute-done.7.other, ...), custom_call_target="tpu_custom_call" | custom-call | flops 44957696 | bytes 1482756 | tf_op jit(solution)/shard_map/add_both/pallas_call | solution.py:235
  24.4 0.1 collective-permute-start.9
  24.4 2.2 %collective-permute-done.6.own = bf16[14,56,128]{2,1,0:T(8,128)(2,1)S(1)} collective-permute-done((bf16[14,56,128]{2,1,0:T(8,128)(2,1)S(1)}, bf16[14,56,128]{2,1,0:T(8,128)(2,1)S(1)}, u32[]{:S(2)}, u32[]{:S(2)}) %collective-permute-start.6) | collective-permute-done | bytes 200736 | tf_op jit(solution)/shard_map/ppermute | solution.py:288
  26.6 0.4 %last_right.1.right = bf16[14,16,128]{2,1,0:T(8,128)(2,1)S(1)} custom-call(s32[1]{0:T(128)S(6)} %copy.11.length, f32[136,512]{1,0:T(8,128)S(1)} %copy-done.1, bf16[14,56,128]{2,1,0:T(8,128)(2,1)S(1)} %collective-permute-done.6.own), custom_call_target="tpu_custom_call" | custom-call | bytes 479236 | tf_op jit(solution)/shard_map/last_right/pallas_call | solution.py:235
  27.0 0.1 collective-permute-start.8
  27.1 0.5 %last_left.1.left = f32[14,56,128]{2,1,0:T(8,128)S(1)} custom-call(s32[1]{0:T(128)S(6)} %copy.11.length, f32[136,512]{1,0:T(8,128)S(1)} %copy-done.1, bf16[14,56,128]{2,1,0:T(8,128)(2,1)S(1)} %collective-permute-done.6.own), custom_call_target="tpu_custom_call" | custom-call | bytes 479236 | tf_op jit(solution)/shard_map/last_left/pallas_call | solution.py:235
  27.6 0.0 collective-permute-done.9.given
  27.6 0.7 %collective-permute-done.8.other = bf16[14,16,128]{2,1,0:T(8,128)(2,1)S(1)} collective-permute-done((bf16[14,16,128]{2,1,0:T(8,128)(2,1)S(1)}, bf16[14,16,128]{2,1,0:T(8,128)(2,1)S(1)}, u32[]{:S(2)}, u32[]{:S(2)}) %collective-permute-start.8) | collective-permute-done | bytes 57376 | tf_op jit(solution)/shard_map/ppermute | solution.py:291
  28.3 1.6 %finish.1 = bf16[14,56,128]{2,1,0:T(8,128)(2,1)} custom-call(f32[14,56,128]{2,1,0:T(8,128)S(1)} %last_left.1.left, bf16[14,16,128]{2,1,0:T(8,128)(2,1)S(1)} %last_right.1.right, bf16[14,16,128]{2,1,0:T(8,128)(2,1)S(1)} %collective-permute-done.8.other, f32[14,56,128]{2,1,0:T(8,128)S(1)} %get-tuple-element.52.mine, ...), custom_call_target="tpu_custom_call" | custom-call | flops 22478848 | bytes 1552896 | tf_op jit(solution)/shard_map/finish/pallas_call | solution.py:235
  (10 shorter events, 0.0 us)
Async XLA Ops:
  0.0 7.9 %collective-permute-start = (bf16[14,56,128]{2,1,0:T(8,128)(2,1)}, bf16[14,56,128]{2,1,0:T(8,128)(2,1)S(1)}, u32[]{:S(2)}, u32[]{:S(2)}) collective-permute-start(bf16[14,56,128]{2,1,0:T(8,128)(2,1)} %bitcast.4), channel_id=1, source_target_pairs={{0,2},{2,4},{4,6},{6,7},{7,5},{5,3},{3,1},{1,0},{8,9},{10,8},{12,1... | collective-permute-start | bytes 602120 | tf_op jit(solution)/shard_map/ppermute | solution.py:288
  3.0 7.1 %collective-permute-start.2 = (bf16[14,56,128]{2,1,0:T(8,128)(2,1)}, bf16[14,56,128]{2,1,0:T(8,128)(2,1)S(1)}, u32[]{:S(2)}, u32[]{:S(2)}) collective-permute-start(bf16[14,56,128]{2,1,0:T(8,128)(2,1)} %bitcast.5), channel_id=1, source_target_pairs={{0,9},{2,8},{4,10},{6,12},{7,14},{5,15},{3,13},{1,11},{8,2},{10,4}... | collective-permute-start | bytes 602120 | tf_op jit(solution)/shard_map/ppermute | solution.py:288
  3.7 1.6 %copy-start.2 = (bf16[56,14,128]{2,0,1:T(8,128)(2,1)S(1)}, bf16[56,14,128]{2,0,1:T(8,128)(2,1)}, u32[]{:S(2)}) copy-start(bf16[56,14,128]{2,0,1:T(8,128)(2,1)} %param.10) | copy-start | bytes 602116
  5.3 6.4 %collective-permute-start.3 = (bf16[14,56,128]{2,1,0:T(8,128)(2,1)S(1)}, bf16[14,56,128]{2,1,0:T(8,128)(2,1)S(1)}, u32[]{:S(2)}, u32[]{:S(2)}) collective-permute-start(bf16[14,56,128]{2,1,0:T(8,128)(2,1)S(1)} %bitcast.6), channel_id=1, source_target_pairs={{0,8},{8,0},{1,9},{9,1},{2,10},{10,2},{3,11},{11,3},{4,12},{12,4},... | collective-permute-start | bytes 602120 | tf_op jit(solution)/shard_map/ppermute | solution.py:291
  7.0 1.0 %copy-start = (f32[136,512]{1,0:T(8,128)S(1)}, f32[136,512]{1,0:T(8,128)}, u32[]{:S(2)}) copy-start(f32[136,512]{1,0:T(8,128)} %join.1.shared) | copy-start | bytes 835588
  7.9 6.8 %collective-permute-start.1 = (bf16[14,56,128]{2,1,0:T(8,128)(2,1)S(1)}, bf16[14,56,128]{2,1,0:T(8,128)(2,1)S(1)}, u32[]{:S(2)}, u32[]{:S(2)}) collective-permute-start(bf16[14,56,128]{2,1,0:T(8,128)(2,1)S(1)} %collective-permute-done.own), channel_id=1, source_target_pairs={{0,2},{2,4},{4,6},{6,7},{7,5},{5,3},{3,1},{1,0},{8,9},{10,8},{12,1... | collective-permute-start | bytes 602120 | tf_op jit(solution)/shard_map/ppermute | solution.py:288
  10.1 6.8 %collective-permute-start.5 = (bf16[14,56,128]{2,1,0:T(8,128)(2,1)S(1)}, bf16[14,56,128]{2,1,0:T(8,128)(2,1)S(1)}, u32[]{:S(2)}, u32[]{:S(2)}) collective-permute-start(bf16[14,56,128]{2,1,0:T(8,128)(2,1)S(1)} %collective-permute-done.2.other), channel_id=1, source_target_pairs={{0,2},{2,4},{4,6},{6,7},{7,5},{5,3},{3,1},{1,0},{8,9},{10,8},{12,1... | collective-permute-start | bytes 602120 | tf_op jit(solution)/shard_map/ppermute | solution.py:288
  12.7 5.9 %copy-start.3 = (bf16[128,128]{1,0:T(8,128)(2,1)S(1)}, bf16[128,128]{1,0:T(8,128)(2,1)}, u32[]{:S(2)}) copy-start(bf16[128,128]{1,0:T(8,128)(2,1)} %out_gate.1) | copy-start | bytes 98308
  12.7 5.9 %copy-start.4 = (bf16[128,128]{1,0:T(8,128)(2,1)S(1)}, bf16[128,128]{1,0:T(8,128)(2,1)}, u32[]{:S(2)}) copy-start(bf16[128,128]{1,0:T(8,128)(2,1)} %last_weight.1) | copy-start | bytes 98308
  12.7 6.3 %copy-start.1 = (f32[136,512]{1,0:T(8,128)S(1)}, f32[136,512]{1,0:T(8,128)}, u32[]{:S(2)}) copy-start(f32[136,512]{1,0:T(8,128)} %join.1.shared) | copy-start | bytes 835588
  14.7 3.9 %copy-start.5 = (f32[128]{0:T(128)S(1)}, f32[128]{0:T(128)}, u32[]{:S(2)}) copy-start(f32[128]{0:T(128)} %param.18) | copy-start | bytes 1540
  14.7 6.1 %collective-permute-start.4 = (bf16[14,56,128]{2,1,0:T(8,128)(2,1)S(1)}, bf16[14,56,128]{2,1,0:T(8,128)(2,1)S(1)}, u32[]{:S(2)}, u32[]{:S(2)}) collective-permute-start(bf16[14,56,128]{2,1,0:T(8,128)(2,1)S(1)} %collective-permute-done.1.own), channel_id=1, source_target_pairs={{0,2},{2,4},{4,6},{6,7},{7,5},{5,3},{3,1},{1,0},{8,9},{10,8},{12,1... | collective-permute-start | bytes 602120 | tf_op jit(solution)/shard_map/ppermute | solution.py:288
  16.9 5.7 %collective-permute-start.7 = (bf16[14,56,128]{2,1,0:T(8,128)(2,1)S(1)}, bf16[14,56,128]{2,1,0:T(8,128)(2,1)S(1)}, u32[]{:S(2)}, u32[]{:S(2)}) collective-permute-start(bf16[14,56,128]{2,1,0:T(8,128)(2,1)S(1)} %collective-permute-done.5.other), channel_id=1, source_target_pairs={{0,2},{2,4},{4,6},{6,7},{7,5},{5,3},{3,1},{1,0},{8,9},{10,8},{12,1... | collective-permute-start | bytes 602120 | tf_op jit(solution)/shard_map/ppermute | solution.py:288
  20.9 5.8 %collective-permute-start.6 = (bf16[14,56,128]{2,1,0:T(8,128)(2,1)S(1)}, bf16[14,56,128]{2,1,0:T(8,128)(2,1)S(1)}, u32[]{:S(2)}, u32[]{:S(2)}) collective-permute-start(bf16[14,56,128]{2,1,0:T(8,128)(2,1)S(1)} %collective-permute-done.4.own), channel_id=1, source_target_pairs={{0,2},{2,4},{4,6},{6,7},{7,5},{5,3},{3,1},{1,0},{8,9},{10,8},{12,1... | collective-permute-start | bytes 602120 | tf_op jit(solution)/shard_map/ppermute | solution.py:288
  24.4 3.2 %collective-permute-start.9 = (bf16[14,56,128]{2,1,0:T(8,128)(2,1)S(1)}, bf16[14,56,128]{2,1,0:T(8,128)(2,1)S(1)}, u32[]{:S(2)}, u32[]{:S(2)}) collective-permute-start(bf16[14,56,128]{2,1,0:T(8,128)(2,1)S(1)} %get-tuple-element.53), channel_id=1, source_target_pairs={{0,8},{8,0},{1,9},{9,1},{2,10},{10,2},{3,11},{11,3},{4,12},{12,4},... | collective-permute-start | bytes 602120 | tf_op jit(solution)/shard_map/ppermute | solution.py:291
  27.0 1.3 %collective-permute-start.8 = (bf16[14,16,128]{2,1,0:T(8,128)(2,1)S(1)}, bf16[14,16,128]{2,1,0:T(8,128)(2,1)S(1)}, u32[]{:S(2)}, u32[]{:S(2)}) collective-permute-start(bf16[14,16,128]{2,1,0:T(8,128)(2,1)S(1)} %last_right.1.right), channel_id=1, source_target_pairs={{0,8},{8,0},{1,9},{9,1},{2,10},{10,2},{3,11},{11,3},{4,12},{12,4},... | collective-permute-start | bytes 172040 | tf_op jit(solution)/shard_map/ppermute | solution.py:291
